TPU v7x, 32 devices: a whole 2x2x4 slice. The times are simulated.
32 devices in a mesh: tp: 4 (over z), cp: 8 (over y, x, core).
Axes of the slice: x: 2, y: 2, z: 4, core: 2. Of those that a mesh axis runs over, the one named last changes fastest.
Arguments:
- layer_input: bfloat16 [1024, 1, 2048], P('cp'), may hold values from -6 to 6
- segment_ids: int32 [1024, 1], P('cp'), may hold values from 0 to 6, as said below
- qkv_weight: bfloat16 [2048, 3, 2048], P(None, None, 'tp'), may hold values from -0.125 to 0.125
- out_weight: bfloat16 [2048, 2048], P('tp'), may hold values from -0.125 to 0.125
- up_weight: bfloat16 [2048, 8192], P(None, 'tp'), may hold values from -0.125 to 0.125
- down_weight: bfloat16 [8192, 2048], P('tp'), may hold values from -0.0625 to 0.0625
- input_gain: float32 [2048], replicated, may hold values from 0.5 to 1.5
- heads_gain: float32 [2048], P('tp'), may hold values from 0.5 to 1.5
- middle_gain: float32 [2048], replicated, may hold values from 0.5 to 1.5
- hidden_gain: float32 [8192], P('tp'), may hold values from 0.5 to 1.5
- cotangent: bfloat16 [1024, 1, 2048], P('cp'), may hold values from -6 to 6
Outputs:
- layer_output: bfloat16 [1024, 1, 2048], P('cp')
- grad_input: bfloat16 [1024, 1, 2048], P('cp')
- grad_qkv: float32 [2048, 3, 2048], P('cp', None, 'tp')
- grad_out: float32 [2048, 2048], P(('tp', 'cp'))
- grad_up: float32 [2048, 8192], P('cp', 'tp')
- grad_down: float32 [8192, 2048], P(('tp', 'cp'))
- grad_input_gain: float32 [2048], P('cp')
- grad_heads_gain: float32 [2048], P(('tp', 'cp'))
- grad_middle_gain: float32 [2048], P('cp')
- grad_hidden_gain: float32 [8192], P(('tp', 'cp'))
Inputs may be any that keep to these rules, and one draw needn't show every extreme that they name: `segment_ids`: along the positions of a row the ids never fall; the first position has id 0 and the last id 6.
All inputs are finite; a program needn't handle non-finite values.
Results may differ from a plain program's by a relative error of at most 0.025.
Values may be sent and summed in bfloat16 or wider, within the bound.
No kernel may reach another device: no remote copies, remote signals or barrier semaphores. Data moves between devices by JAX's collectives and lax.ppermute only.
A program may use at most 192 MiB of HBM per device.

v0:
```python
import functools

import jax
import jax.numpy as jnp
import numpy as np
from jax import lax
from jax.experimental import pallas as pl
from jax.experimental.pallas import tpu as pltpu
from jax.sharding import PartitionSpec as P

HD = 64
D = 2048
FF = 8192

eps = 1e-05
scale_base = 512.0
masked_score = -1e30
f32 = jnp.float32
bf16 = jnp.bfloat16


def dot(a, b):
    return jnp.dot(a, b, preferred_element_type=f32)


def dot_t(a, b):
    return lax.dot_general(a, b, (((1,), (1,)), ((), ())), preferred_element_type=f32)


def t_dot(a, b):
    return lax.dot_general(a, b, (((0,), (0,)), ((), ())), preferred_element_type=f32)


def pairs(count, k):
    return [(i, i ^ k) for i in range(count)]


def swap_tp(value, k):
    return lax.ppermute(value, "tp", pairs(lax.axis_size("tp"), k))


def tp_order(value):
    count, me = lax.axis_size("tp"), lax.axis_index("tp")
    part = value.shape[0] // count
    return jnp.concatenate(
        [lax.dynamic_slice_in_dim(value, (me ^ k) * part, part, 0) for k in range(count)], axis=0
    )


def tp_scatter_sum(partial_sum):
    count = lax.axis_size("tp")
    part = partial_sum.shape[0] // count
    low = partial_sum.astype(bf16)
    total = partial_sum[:part]
    for k in range(1, count):
        total = total + swap_tp(low[k * part : (k + 1) * part], k).astype(f32)
    return total


def tp_gather(block):
    count = lax.axis_size("tp")
    return jnp.concatenate([block] + [swap_tp(block, k) for k in range(1, count)], axis=0)


def tp_sum(value):
    total = value
    for k in range(1, lax.axis_size("tp")):
        total = total + swap_tp(value, k)
    return total


def tp_token_sum(value):
    count = lax.axis_size("tp")
    blocks = value.reshape(value.shape[0], count, -1)
    total = blocks
    for k in range(1, count):
        got = swap_tp(blocks, k)
        total = total + jnp.stack([got[:, j ^ k] for j in range(count)], axis=1)
    return total.reshape(value.shape)


def cp_columns(value):
    return lax.all_to_all(value, "cp", split_axis=1, concat_axis=0, tiled=True)


def cp_gather(value):
    return lax.all_gather(value, "cp", axis=0, tiled=True)


def xpos_tables(positions):
    column = jnp.arange(HD // 2, dtype=f32)
    frequency = 10000.0 ** (-column / (HD // 2))
    zeta = (2.0 * column + 0.4 * HD) / (1.4 * HD)
    places = positions.astype(f32)[:, None]
    angle = places * frequency
    return (jnp.cos(angle), jnp.sin(angle), zeta ** (places / scale_base))


def turn(vector, cosine, sine, factor):
    paired = vector.reshape(vector.shape[:-1] + (HD // 2, 2))
    first, second = paired[..., 0], paired[..., 1]
    cosine, sine, factor = cosine[:, None], sine[:, None], factor[:, None]
    turned = jnp.stack(
        [(first * cosine - second * sine) * factor, (first * sine + second * cosine) * factor],
        axis=-1,
    )
    return turned.reshape(vector.shape)


def norm_rows(vector):
    center = jnp.mean(vector, axis=-1, keepdims=True)
    shifted = vector - center
    scaling = lax.rsqrt(jnp.mean(shifted * shifted, axis=-1, keepdims=True) + eps)
    return (shifted * scaling, scaling)


def norm_back(grad_result, gain, normed, scaling):
    grad_normed = grad_result * gain
    first = jnp.mean(grad_normed, axis=-1, keepdims=True)
    cross = jnp.mean(grad_normed * normed, axis=-1, keepdims=True)
    return scaling * (grad_normed - first - normed * cross)


def attend(queries, keys, values, allowed):
    scores = jnp.einsum("qhd,khd->hqk", queries, keys, preferred_element_type=f32) * HD**-0.5
    scores = jnp.where(allowed[None], scores, masked_score)
    top = jnp.max(scores, axis=-1, keepdims=True)
    exponent = jnp.where(allowed[None], jnp.exp(scores - top), 0.0)
    total = jnp.sum(exponent, axis=-1, keepdims=True)
    probability = (exponent / total).astype(bf16)
    mixed = jnp.einsum("hqk,khd->qhd", probability, values, preferred_element_type=f32)
    return (mixed, top + jnp.log(total))


def attend_back(queries, keys, values, allowed, lse, grad, delta):
    scores = jnp.einsum("qhd,khd->hqk", queries, keys, preferred_element_type=f32) * HD**-0.5
    probability = jnp.where(allowed[None], jnp.exp(scores - lse), 0.0)
    grad_prob = jnp.einsum("qhd,khd->hqk", grad, values, preferred_element_type=f32)
    grad_scores = (probability * (grad_prob - delta.T[:, :, None])).astype(bf16)
    grad_q = jnp.einsum("hqk,khd->qhd", grad_scores, keys, preferred_element_type=f32) * HD**-0.5
    grad_k = jnp.einsum("hqk,qhd->khd", grad_scores, queries, preferred_element_type=f32) * HD**-0.5
    grad_v = jnp.einsum(
        "hqk,qhd->khd", probability.astype(bf16), grad, preferred_element_type=f32
    )
    return (grad_q, grad_k, grad_v)


def body_general(
    layer_input,
    segment_ids,
    qkv_weight,
    out_weight,
    up_weight,
    down_weight,
    input_gain,
    heads_gain,
    middle_gain,
    hidden_gain,
    cotangent,
):
    local_len, row_count, width = layer_input.shape
    tp_count, cp_count = lax.axis_size("tp"), lax.axis_size("cp")
    me_tp, me_cp = lax.axis_index("tp"), lax.axis_index("cp")
    part = local_len // tp_count
    head_width = qkv_weight.shape[2]
    heads = head_width // HD
    by_head = heads % cp_count == 0
    own_heads = heads // cp_count if by_head else heads
    weight3 = jnp.transpose(qkv_weight, (1, 0, 2))

    x = tp_order(layer_input.reshape(local_len, width))
    gy = tp_order(cotangent.reshape(local_len, width))
    seg = tp_order(segment_ids)[:, 0]
    natural = tp_order(jnp.arange(local_len, dtype=jnp.int32))
    position = me_cp * local_len + natural
    position_all = (jnp.arange(cp_count, dtype=jnp.int32)[:, None] * local_len + natural).reshape(-1)

    stream = x.astype(f32)
    normed_one, scaling_one = norm_rows(stream)
    a = (normed_one * input_gain).astype(bf16)
    a_all = cp_gather(a)
    cosine, sine, factor = xpos_tables(position)
    raw_q = dot(a, weight3[0]).reshape(local_len, heads, HD)
    raw_k = dot(a, weight3[1]).reshape(local_len, heads, HD)
    raw_v = dot(a, weight3[2]).reshape(local_len, heads, HD)
    q = turn(raw_q, cosine, sine, factor).astype(bf16)
    k = turn(raw_k, cosine, sine, 1.0 / factor).astype(bf16)
    v = raw_v.astype(bf16)
    if by_head:
        extra = jnp.broadcast_to(seg.astype(bf16)[:, None, None], (local_len, cp_count, 16))
        sent = jnp.concatenate(
            [t.reshape(local_len, cp_count, own_heads * HD) for t in (q, k, v)] + [extra], axis=-1
        )
        got = lax.all_to_all(sent, "cp", split_axis=1, concat_axis=0, tiled=True)[:, 0]
        span = own_heads * HD
        q_all, k_all, v_all = (
            got[:, i * span : (i + 1) * span].reshape(-1, own_heads, HD) for i in range(3)
        )
        seg_all = got[:, 3 * span]
        seg_q, position_q = seg_all, position_all
    else:
        q_all, k_all, v_all = q, cp_gather(k), cp_gather(v)
        seg_all = cp_gather(seg.astype(bf16))
        seg_q, position_q = seg.astype(bf16), position
    allowed = (position_all[None, :] <= position_q[:, None]) & (seg_q[:, None] == seg_all[None, :])
    mixed, lse = attend(q_all, k_all, v_all, allowed)
    if by_head:
        attended = lax.all_to_all(
            mixed.astype(bf16).reshape(cp_count * local_len, own_heads * HD),
            "cp", split_axis=0, concat_axis=1, tiled=True,
        ).astype(f32)
    else:
        attended = mixed.reshape(local_len, head_width)

    sums = tp_token_sum(jnp.stack([jnp.sum(attended, axis=1), jnp.sum(attended * attended, axis=1)]))
    center = sums[0] / width
    scaling_h = lax.rsqrt(sums[1] / width - center * center + eps)[:, None]
    normed_h = (attended - center[:, None]) * scaling_h
    z = (normed_h * heads_gain).astype(bf16)
    gain_row = tp_sum(jnp.dot(heads_gain, out_weight.astype(f32)))
    branch = tp_scatter_sum(dot(z, out_weight))
    x1 = stream[:part] + branch
    normed_two, scaling_two = norm_rows(x1)
    u = tp_gather((normed_two * middle_gain).astype(bf16))

    grad_hid = dot_t(gy, down_weight)
    grad_normed = grad_hid * hidden_gain
    hidden = dot(u, up_weight)
    cdf = 0.5 * (1.0 + lax.erf(hidden * (0.5**0.5)))
    act = hidden * cdf
    slope = cdf + hidden * jnp.exp(-0.5 * hidden * hidden) * 0.3989422804014327
    sums = tp_token_sum(
        jnp.stack(
            [
                jnp.sum(act, axis=1),
                jnp.sum(act * act, axis=1),
                jnp.sum(grad_normed, axis=1),
                jnp.sum(grad_normed * act, axis=1),
            ]
        )
    )
    center = sums[0] / FF
    scaling_f = lax.rsqrt(sums[1] / FF - center * center + eps)
    first = sums[2] / FF
    cross = scaling_f * (sums[3] / FF - center * first)
    normed_f = (act - center[:, None]) * scaling_f[:, None]
    z2 = (normed_f * hidden_gain).astype(bf16)
    grad_act = scaling_f[:, None] * (grad_normed - first[:, None] - normed_f * cross[:, None])
    gh = (grad_act * slope).astype(bf16)
    hidden_gain_sum = jnp.sum(grad_hid * normed_f, axis=0)
    gu = tp_scatter_sum(dot_t(gh, up_weight))
    gx1 = gy[:part].astype(f32) + norm_back(gu, middle_gain, normed_two, scaling_two)
    middle_gain_sum = jnp.sum(gu * normed_two, axis=0)
    gb_own = gx1.astype(bf16)
    gb_f = gb_own.astype(f32)
    first = jnp.sum(gb_f * gain_row, axis=1) / width
    cross = jnp.sum(gb_f * branch, axis=1) / width
    gb = tp_gather(gb_own)
    stats = tp_gather(jnp.stack([first, cross], axis=1))

    gz = dot_t(gb, out_weight)
    heads_gain_sum = jnp.sum(gz * normed_h, axis=0)
    go = (scaling_h * (gz * heads_gain - stats[:, :1] - normed_h * stats[:, 1:])).astype(bf16)
    if by_head:
        grad_mixed = cp_columns(go).reshape(-1, own_heads, HD)
    else:
        grad_mixed = go.reshape(local_len, heads, HD)
    delta = jnp.sum(grad_mixed.astype(f32) * mixed, axis=-1)
    gq, gk, gv = attend_back(q_all, k_all, v_all, allowed, lse, grad_mixed, delta)
    if by_head:
        cos_all, sin_all, factor_all = xpos_tables(position_all)
    else:
        cos_all, sin_all, factor_all = cosine, sine, factor
        gk = lax.psum_scatter(gk.astype(bf16), "cp", scatter_dimension=0, tiled=True).astype(f32)
        gv = lax.psum_scatter(gv.astype(bf16), "cp", scatter_dimension=0, tiled=True).astype(f32)
    gq = turn(gq, cos_all, -sin_all, factor_all)
    gk = turn(gk, cos_all, -sin_all, 1.0 / factor_all)
    grads = jnp.stack([gq, gk, gv], axis=1).astype(bf16)
    if by_head:
        grads_own = grads.reshape(-1, 3 * own_heads * HD)
        grads = lax.all_to_all(
            grads.reshape(-1, 3, own_heads * HD), "cp", split_axis=0, concat_axis=2, tiled=True
        )
    else:
        grads = grads.reshape(local_len, 3, head_width)
        grads_own = lax.all_to_all(grads, "cp", split_axis=2, concat_axis=0, tiled=True)
        grads_own = grads_own.reshape(-1, 3 * head_width // cp_count)
    ga = (
        dot_t(grads[:, 0], weight3[0]) + dot_t(grads[:, 1], weight3[1]) + dot_t(grads[:, 2], weight3[2])
    )
    ga = tp_scatter_sum(ga)
    input_gain_sum = jnp.sum(ga * normed_one[:part], axis=0)
    grad_in = gx1 + norm_back(ga, input_gain, normed_one[:part], scaling_one[:part])

    y = (x1 + tp_scatter_sum(dot(z2, down_weight))).astype(bf16)
    layer_output = tp_order(tp_gather(y)).reshape(layer_input.shape)
    grad_input = tp_order(tp_gather(grad_in.astype(bf16))).reshape(layer_input.shape)

    grad_down = t_dot(cp_columns(z2), cp_gather(gy))
    grad_up = t_dot(cp_columns(u), cp_gather(gh))
    grad_out = t_dot(cp_columns(z), cp_gather(gb))
    grad_qkv = t_dot(a_all, grads_own).astype(bf16)
    grad_qkv = lax.all_to_all(
        grad_qkv.reshape(width, 3, head_width // cp_count), "cp", split_axis=0, concat_axis=2, tiled=True
    ).astype(f32)

    def cp_sum_own(vector):
        return jnp.sum(lax.all_to_all(vector.reshape(cp_count, -1), "cp", 0, 0, tiled=True), axis=0)

    def both_sum_own(vector):
        return tp_sum(cp_sum_own(vector))

    return (
        layer_output,
        grad_input,
        grad_qkv,
        grad_out,
        grad_up,
        grad_down,
        both_sum_own(input_gain_sum),
        cp_sum_own(heads_gain_sum),
        both_sum_own(middle_gain_sum),
        cp_sum_own(hidden_gain_sum),
    )


INTERPRET = False


def params(megabytes):
    return pltpu.CompilerParams(vmem_limit_bytes=megabytes * 1024 * 1024)


def shape(dims, kind):
    return jax.ShapeDtypeStruct(dims, kind)


def whole():
    return pl.BlockSpec(memory_space=pltpu.VMEM)


def scalars():
    return pl.BlockSpec(memory_space=pltpu.SMEM)


def call(kernel, outs, args, specs=None, out_specs=None, grid=None, scratch=(), mb=32, flops=0, after=()):
    specs = list(specs) if specs is not None else [whole() for _ in args]
    count = len(args)
    extra = len(after)

    def run(*refs):
        kernel(*refs[:count], *refs[count + extra :])

    moved = sum(int(np.prod(t.shape)) * t.dtype.itemsize for t in list(args) + list(outs))
    options = {} if grid is None else {"grid": grid}
    return pl.pallas_call(
        run,
        out_shape=tuple(outs),
        in_specs=specs + [pl.BlockSpec(memory_space=pl.ANY)] * extra,
        out_specs=tuple(out_specs) if out_specs is not None else tuple(whole() for _ in outs),
        scratch_shapes=list(scratch),
        compiler_params=params(mb),
        cost_estimate=pl.CostEstimate(flops=flops, bytes_accessed=moved, transcendentals=0),
        interpret=INTERPRET,
        **options,
    )(*args, *after)


def fixed(dims):
    return pl.BlockSpec(dims, lambda i: (0,) * len(dims))


def split_low(value):
    high = value.astype(bf16)
    return high, (value - high.astype(f32)).astype(bf16)


def lanes_of(columns, rows):
    lane = lax.broadcasted_iota(jnp.int32, (rows, 128), 1)
    out = jnp.zeros((rows, 128), f32)
    for i, column in enumerate(columns):
        out = jnp.where(lane == i, column.astype(f32), out)
    return out


def pair_sum(block, i):
    return block[:, i : i + 1].astype(f32) + block[:, i + 1 : i + 2].astype(f32)


def own_order(me, part, index):
    return ((index // part) ^ me) * part + index % part


def block_at(me, k, part):
    return pl.ds(pl.multiple_of((me ^ k) * part, part), part)


def swap_pairs(value, axis):
    size = value.shape[axis]
    place = lax.broadcasted_iota(jnp.int32, value.shape, axis)
    return jnp.where(
        place % 2 == 0, pltpu.roll(value, size - 1, axis), pltpu.roll(value, 1, axis)
    )


def tables(local_len, cp_count):
    column = np.arange(HD) // 2
    frequency = 10000.0 ** (-column / (HD // 2))
    zeta = (2.0 * column + 0.4 * HD) / (1.4 * HD)

    def of(places):
        angle = places[:, None] * frequency
        factor = zeta ** (places[:, None] / scale_base)
        return np.stack([np.cos(angle), np.sin(angle), factor, 1.0 / factor]).astype(np.float32)

    return of(np.arange(local_len)), of(np.arange(cp_count) * local_len)


def project_kernel(parts, ids, x, seg, gain, weight, inner, base, a, out, tab):
    step = pl.program_id(0)
    me, mine = ids[0], ids[1]
    rows, width = x.shape
    part = rows // parts
    heads = out.shape[0]

    @pl.when(step == 0)
    def _():
        for k in range(parts):
            block = x[block_at(me, k, part), :].astype(f32)
            normed, _ = norm_rows(block)
            a[k * part : (k + 1) * part, :] = (normed * gain[...]).astype(bf16)
            for kind in range(4):
                tab[kind, k * part : (k + 1) * part, :] = inner[kind, block_at(me, k, part), :]
        place = lax.broadcasted_iota(jnp.int32, (rows, rows), 1)
        source = lax.broadcasted_iota(jnp.int32, (rows, rows), 0)
        moved = (own_order(me, part, place) == source).astype(bf16)
        ids_row = jnp.broadcast_to(seg[...].astype(f32), (16, rows)).astype(bf16)
        ordered = dot(ids_row, moved).astype(bf16)
        for j in range(heads):
            out[j, 3 * HD : 3 * HD + 16, :] = ordered

    acc = dot(a[...], weight[0])
    here = [base[kind, pl.ds(mine, 1), :] for kind in range(4)]
    cosine = tab[0] * here[0] - tab[1] * here[1]
    sine = tab[1] * here[0] + tab[0] * here[1]
    factor = jnp.where(step == 0, tab[2] * here[2], tab[3] * here[3])
    lane = lax.broadcasted_iota(jnp.int32, cosine.shape, 1)
    sine = jnp.where(lane % 2 == 0, -sine, sine)
    cosine = jnp.where(step == 2, 1.0, cosine * factor)
    sine = jnp.where(step == 2, 0.0, sine * factor)
    for i in range(acc.shape[1] // 128):
        piece = acc[:, i * 128 : (i + 1) * 128]
        turned = (piece * cosine + swap_pairs(piece, 1) * sine).T.astype(bf16)
        for h in range(128 // HD):
            out[i * (128 // HD) + h, pl.ds(pl.multiple_of(step * HD, HD), HD), :] = turned[
                h * HD : (h + 1) * HD
            ]


def gather_heads(got, keys, ids_col, values=None):
    for j in range(got.shape[0]):
        rows = slice(j * got.shape[2], (j + 1) * got.shape[2])
        both = jnp.concatenate([got[j, HD : 3 * HD, :].astype(f32)], axis=0).T
        keys[rows, :] = both[:, :HD].astype(bf16)
        if values is not None:
            values[rows, :] = both[:, HD:].astype(bf16)
        ids_col[rows, :] = got[j, 3 * HD : 3 * HD + 16, :].astype(f32).T


def visible_scores(me, part, scores, ids_col, ids_row, count, first, group):
    same = ids_col[0:count, 0:1] == ids_row
    length = group
    key = lax.broadcasted_iota(jnp.int32, (length, length), 0)
    query = lax.broadcasted_iota(jnp.int32, (length, length), 1)
    rows = first
    own = lambda index: (index // rows) * rows + own_order(me, part, index % rows)
    earlier = own(key) <= own(query)
    if count > length:
        earlier = jnp.concatenate([jnp.ones((count - length, length), jnp.bool_), earlier], axis=0)
    return same & earlier


def attend_kernel(parts, ids, got, out, mixed, lse, keys, ids_col):
    me = ids[0]
    blocks, _, rows = got.shape
    part = rows // parts
    gather_heads(got, keys, ids_col)
    group = 2 if blocks % 2 == 0 else 1
    width = group * rows
    for i in range(blocks // group):
        mine = range(i * group, (i + 1) * group)
        query = jnp.concatenate([got[j, :HD, :] for j in mine], axis=1) * bf16(HD**-0.5)
        ids_row = jnp.concatenate([got[j, 3 * HD : 3 * HD + 1, :] for j in mine], axis=1).astype(f32)
        count = (i + 1) * width
        scores = dot(keys[0:count, :], query)
        allowed = visible_scores(me, part, scores, ids_col, ids_row, count, rows, width)
        scores = jnp.where(allowed, scores, masked_score)
        top = jnp.max(scores, axis=0, keepdims=True)
        exponent = jnp.exp(scores - top)
        total = jnp.sum(exponent, axis=0, keepdims=True)
        value = jnp.concatenate([got[j, 2 * HD : 3 * HD, :] for j in range((i + 1) * group)], axis=1)
        result = dot(value, exponent.astype(bf16)) / total
        mixed[:, i * width : (i + 1) * width] = result
        lse[:, i * width : (i + 1) * width] = top + jnp.log(total)
        for n, j in enumerate(mine):
            out[j] = result[:, n * rows : (n + 1) * rows].astype(bf16)


def store_pieces(total, own, pieces, part, extra=None):
    own[:, : total.shape[1]] = total[:part]
    for k, piece in enumerate(pieces, 1):
        piece[:, : total.shape[1]] = total[k * part : (k + 1) * part].astype(bf16)
    if extra is not None:
        own[:, total.shape[1] :] = extra[:part]
        for k, piece in enumerate(pieces, 1):
            piece[:, total.shape[1] :] = extra[k * part : (k + 1) * part].astype(bf16)


def out_kernel(parts, att, gain, weight, own, *pieces):
    blocks, _, rows = att.shape
    part = rows // parts
    value = jnp.concatenate([att[j].astype(f32) for j in range(blocks)], axis=0).T
    high, low = split_low(jnp.mean(value, axis=1, keepdims=True))
    centred = value - (high.astype(f32) + low.astype(f32))
    square = split_low(jnp.sum(centred * centred, axis=1, keepdims=True))
    total = dot((centred * gain[...]).astype(bf16), weight[...])
    store_pieces(total, own, pieces, part, lanes_of([high, low, *square], rows))


def middle_kernel(parts, head_width, ids, own, *refs):
    got, refs = refs[: parts - 1], refs[parts - 1 :]
    gain_rows, refs = refs[:parts], refs[parts:]
    x, gain, x1, u = refs
    part, width = x1.shape
    blocks = [own] + list(got)
    means = [pair_sum(b[:, width:], 0) for b in blocks]
    squares = [pair_sum(b[:, width:], 2) for b in blocks]
    mean = sum(means) / parts
    spread = sum(squares) + head_width * sum((m - mean) * (m - mean) for m in means)
    scaling = lax.rsqrt(spread / width + eps)
    total = sum(b[:, :width].astype(f32) for b in blocks)
    for m, row in zip(means, gain_rows):
        total = total + (m - mean) * row[...]
    value = x[block_at(ids[0], 0, part), :].astype(f32) + total * scaling
    x1[...] = value
    normed, _ = norm_rows(value)
    u[:, :width] = (normed * gain[...]).astype(bf16)
    u[:, width:] = lanes_of([*split_low(mean), *split_low(scaling)], part).astype(bf16)


def grad_hidden_kernel(parts, ids, gy, weight, heads_gain, out_weight, grad, gain_row, ordered):
    rows = gy.shape[0]
    part = rows // parts

    @pl.when(pl.program_id(0) == 0)
    def _():
        for k in range(parts):
            ordered[k * part : (k + 1) * part, :] = gy[block_at(ids[0], k, part), :]
        high, low = split_low(heads_gain[...])
        row = lax.broadcasted_iota(jnp.int32, (16, heads_gain.shape[1]), 0)
        both = jnp.where(row == 0, high.astype(f32), jnp.where(row == 1, low.astype(f32), 0.0))
        product = dot(both.astype(bf16), out_weight[...])
        gain_row[...] = product[0:1] + product[1:2]

    grad[...] = dot_t(ordered[...], weight[...])


def up_kernel(parts, own, *refs):
    got, refs = refs[: parts - 1], refs[parts - 1 :]
    weight, grad, gain, act, slope, u, stats, rows_u, sums = refs
    step = pl.program_id(0)
    part = own.shape[0]
    rows, width = rows_u.shape

    @pl.when(step == 0)
    def _():
        for k, block in enumerate([own] + list(got)):
            rows_u[k * part : (k + 1) * part, :] = block[:, :width]
        wide = u.shape[2]
        for j in range(u.shape[0]):
            u[j] = rows_u[:, j * wide : (j + 1) * wide]
        sums[...] = jnp.zeros_like(sums)

    hidden = dot(rows_u[...], weight[...])
    cdf = 0.5 * (1.0 + lax.erf(hidden * (0.5**0.5)))
    value = hidden * cdf
    act[...] = value
    slope[...] = cdf + hidden * jnp.exp(-0.5 * hidden * hidden) * 0.3989422804014327
    grad_normed = grad[...] * gain[...]
    columns = [value, value * value, grad_normed, grad_normed * value]
    sums[...] += lanes_of([jnp.sum(c, axis=1, keepdims=True) for c in columns], rows)

    @pl.when(step == pl.num_programs(0) - 1)
    def _():
        stats[...] = sums[...].T[:8, :]


def swap_lane_blocks(value, k, part):
    lanes = value.shape[1]
    lane = lax.broadcasted_iota(jnp.int32, value.shape, 1)
    distance = 1
    while distance <= k:
        if k & distance:
            move = distance * part
            value = jnp.where(
                (lane // move) % 2 == 0,
                pltpu.roll(value, lanes - move, 1),
                pltpu.roll(value, move, 1),
            )
        distance *= 2
    return value


def hidden_back_kernel(parts, full, own, *refs):
    got, refs = refs[: parts - 1], refs[parts - 1 :]
    act, slope, grad, gain, weight, gh, z2, gain_sum, own_out = refs[:9]
    pieces, (acc, cols) = refs[9 : 9 + parts - 1], refs[9 + parts - 1 :]
    step = pl.program_id(0)
    rows = act.shape[0]
    part = rows // parts

    @pl.when(step == 0)
    def _():
        total = own[...]
        for k, block in enumerate(got, 1):
            total = total + swap_lane_blocks(block[...], k, part)
        mean = total[0:1] / full
        scaling = lax.rsqrt(total[1:2] / full - mean * mean + eps)
        first = total[2:3] / full
        cross = scaling * (total[3:4] / full - mean * first)
        row = lax.broadcasted_iota(jnp.int32, (rows, rows), 0)
        table = jnp.zeros((rows, rows), f32)
        for i, value in enumerate([mean, scaling, first, cross]):
            table = jnp.where(row == i, value, table)
        cols[...] = table.T
        acc[...] = jnp.zeros_like(acc)

    mean, scaling, first, cross = (cols[:, i : i + 1] for i in range(4))
    normed = (act[...] - mean) * scaling
    low = (normed * gain[...]).astype(bf16)
    wide = z2.shape[2]
    for j in range(z2.shape[0]):
        z2[j] = low[:, j * wide : (j + 1) * wide]
    gain_sum[...] = jnp.sum(grad[...] * normed, axis=0, keepdims=True)
    value = (scaling * (grad[...] * gain[...] - first - normed * cross) * slope[...]).astype(bf16)
    gh[...] = value
    acc[...] += dot_t(value, weight[...])

    @pl.when(step == pl.num_programs(0) - 1)
    def _():
        store_pieces(acc[...], own_out, pieces, part)


def down_kernel(parts, z2, weight, own_out, *refs):
    pieces, (acc,) = refs[: parts - 1], refs[parts - 1 :]
    step = pl.program_id(0)

    @pl.when(step == 0)
    def _():
        acc[...] = jnp.zeros_like(acc)

    wide = z2.shape[2]
    for j in range(z2.shape[0]):
        acc[...] += dot(z2[j], weight[j * wide : (j + 1) * wide, :])

    @pl.when(step == pl.num_programs(0) - 1)
    def _():
        store_pieces(acc[...], own_out, pieces, acc.shape[0] // parts)


def middle_back_kernel(parts, ids, own, *refs):
    got, refs = refs[: parts - 1], refs[parts - 1 :]
    gain_rows, refs = refs[:parts], refs[parts:]
    x, x1, gy, gain, gx1, gb, gain_sum = refs
    part, width = x1.shape
    here = block_at(ids[0], 0, part)
    grad = own[...]
    for block in got:
        grad = grad + block[...].astype(f32)
    value = x1[...]
    normed, scaling = norm_rows(value)
    result = gy[here, :].astype(f32) + norm_back(grad, gain[...], normed, scaling)
    gx1[...] = result
    gain_sum[...] = jnp.sum(grad * normed, axis=0, keepdims=True)
    low = result.astype(bf16)
    gb[:, :width] = low
    low = low.astype(f32)
    gain_row = sum(row[...] for row in gain_rows)
    first = jnp.sum(low * gain_row, axis=1, keepdims=True) / width
    cross = jnp.sum(low * (value - x[here, :].astype(f32)), axis=1, keepdims=True) / width
    gb[:, width:] = lanes_of([*split_low(first), *split_low(cross)], part).astype(bf16)


def heads_back_kernel(parts, own, *refs):
    got, refs = refs[: parts - 1], refs[parts - 1 :]
    stats, refs = refs[:parts], refs[parts:]
    att, gain, weight, sent, gb, gain_sum = refs
    blocks, _, rows = att.shape
    part, width = own.shape[0], gb.shape[1]
    for k, block in enumerate([own] + list(got)):
        gb[k * part : (k + 1) * part, :] = block[:, :width]
    columns = jnp.concatenate([b[:, width:].astype(f32) for b in [own] + list(got)], axis=0).T
    first = columns[0:1] + columns[1:2]
    cross = columns[2:3] + columns[3:4]
    columns = jnp.concatenate([b[:, width:].astype(f32) for b in stats], axis=0).T
    mean = columns[0:1] + columns[1:2]
    scaling = columns[2:3] + columns[3:4]
    grad = dot_t(weight[...], gb[...])
    value = jnp.concatenate([att[j].astype(f32) for j in range(blocks)], axis=0)
    normed = (value - mean) * scaling
    gain_col = jnp.broadcast_to(gain[...], (8, gain.shape[1])).T[:, 0:1]
    gain_sum[...] = jnp.sum((grad * normed).T, axis=0, keepdims=True)
    go = (scaling * (grad * gain_col - first - normed * cross)).astype(bf16)
    z = (normed * gain_col).astype(bf16)
    for j in range(blocks):
        sent[j, :HD, :] = go[j * HD : (j + 1) * HD]
        sent[j, HD:, :] = z[j * HD : (j + 1) * HD]


def turn_back(grad, table, base, j, inverse):
    here = [base[kind, :, j : j + 1] for kind in range(4)]
    cosine = table[0] * here[0] - table[1] * here[1]
    sine = table[1] * here[0] + table[0] * here[1]
    factor = table[3] * here[3] if inverse else table[2] * here[2]
    row = lax.broadcasted_iota(jnp.int32, grad.shape, 0)
    sine = jnp.where(row % 2 == 0, sine, -sine)
    return (grad * cosine + swap_pairs(grad, 0) * sine) * factor


def attend_back_kernel(parts, ids, got, grads, mixed, lse, inner, base, out, keys, values, ids_col, gk, gv):
    me = ids[0]
    blocks, _, rows = got.shape
    part = rows // parts
    gather_heads(got, keys, ids_col, values)
    gk[...] = jnp.zeros_like(gk)
    gv[...] = jnp.zeros_like(gv)
    table = []
    for kind in range(4):
        ordered = jnp.concatenate(
            [inner[kind, block_at(me, k, part), :] for k in range(parts)], axis=0
        )
        table.append(ordered.T[:HD])
    group = 2 if blocks % 2 == 0 else 1
    width = group * rows
    for i in range(blocks // group):
        mine = range(i * group, (i + 1) * group)
        query = jnp.concatenate([got[j, :HD, :] for j in mine], axis=1) * bf16(HD**-0.5)
        ids_row = jnp.concatenate([got[j, 3 * HD : 3 * HD + 1, :] for j in mine], axis=1).astype(f32)
        go = jnp.concatenate([grads[j, :HD, :] for j in mine], axis=1)
        span = slice(i * width, (i + 1) * width)
        delta = jnp.sum(go.astype(f32) * mixed[:, span], axis=0, keepdims=True)
        count = (i + 1) * width
        scores = dot(keys[0:count, :], query)
        allowed = visible_scores(me, part, scores, ids_col, ids_row, count, rows, width)
        probability = jnp.where(allowed, jnp.exp(jnp.minimum(scores - lse[:, span], 0.5)), 0.0)
        grad_prob = dot(values[0:count, :], go)
        grad_scores = (probability * (grad_prob - delta)).astype(bf16)
        gv[:, 0:count] += dot_t(go, probability.astype(bf16))
        gk[:, 0:count] += dot_t(query, grad_scores)
        key = jnp.concatenate([got[j, HD : 2 * HD, :] for j in range((i + 1) * group)], axis=1)
        gq = dot(key, grad_scores) * HD**-0.5
        for n, j in enumerate(mine):
            piece = turn_back(gq[:, n * rows : (n + 1) * rows], table, base, j, False)
            out[j, :HD, :] = piece.astype(bf16)
    for j in range(blocks):
        span = slice(j * rows, (j + 1) * rows)
        out[j, HD : 2 * HD, :] = turn_back(gk[:, span], table, base, j, True).astype(bf16)
        out[j, 2 * HD :, :] = gv[:, span].astype(bf16)


def input_back_kernel(parts, got, weight, own_out, *refs):
    pieces, (acc,) = refs[: parts - 1], refs[parts - 1 :]
    step = pl.program_id(0)

    @pl.when(step == 0)
    def _():
        acc[...] = jnp.zeros_like(acc)

    here = pl.ds(pl.multiple_of(step * HD, HD), HD)
    grad = jnp.concatenate([got[j, here, :].astype(f32) for j in range(got.shape[0])], axis=0).T
    acc[...] += dot_t(grad.astype(bf16), weight[0])

    @pl.when(step == pl.num_programs(0) - 1)
    def _():
        store_pieces(acc[...], own_out, pieces, acc.shape[0] // parts)


def final_kernel(parts, ids, own, *refs):
    got, refs = refs[: parts - 1], refs[parts - 1 :]
    x, gx1, gain, out, gain_sum = refs
    part = gx1.shape[0]
    grad = own[...]
    for block in got:
        grad = grad + block[...].astype(f32)
    normed, scaling = norm_rows(x[block_at(ids[0], 0, part), :].astype(f32))
    out[...] = (gx1[...] + norm_back(grad, gain[...], normed, scaling)).astype(bf16)
    gain_sum[...] = jnp.sum(grad * normed, axis=0, keepdims=True)


def output_kernel(own, *refs):
    got, (x1, out) = refs[:-2], refs[-2:]
    total = own[...] + x1[...]
    for block in got:
        total = total + block[...].astype(f32)
    out[...] = total.astype(bf16)


def natural_kernel(ids, *refs):
    blocks, out = refs[:-1], refs[-1]
    part = blocks[0].shape[0]
    for k, block in enumerate(blocks):
        out[block_at(ids[0], k, part), :] = block[...]


def columns_grad_kernel(parts, reorder, ids, left, right, out, acc_left):
    @pl.when(pl.program_id(0) == 0)
    def _():
        blocks, rows, _ = left.shape
        part = rows // parts
        for j in range(blocks):
            for k in range(parts):
                if reorder:
                    to = pl.ds(pl.multiple_of(j * rows + (ids[0] ^ k) * part, part), part)
                else:
                    to = slice(j * rows + k * part, j * rows + (k + 1) * part)
                acc_left[to, :] = left[j, k * part : (k + 1) * part, :]

    out[...] = t_dot(acc_left[...], right[...])


def rows_grad_kernel(first, left, right, out):
    value = jnp.concatenate([left[j, first:, :] for j in range(left.shape[0])], axis=1)
    out[...] = dot(value, right[...])


def grad_qkv_kernel(left, right, out):
    value = jnp.concatenate([left[j] for j in range(left.shape[0])], axis=1)
    out[0] = dot(value, right[...]).astype(bf16)


def grad_qkv_place_kernel(got, out):
    for c in range(3):
        value = jnp.concatenate(
            [got[j, c * HD : (c + 1) * HD, :].astype(f32) for j in range(got.shape[0])], axis=0
        )
        out[c] = value.T


def body(
    layer_input,
    segment_ids,
    qkv_weight,
    out_weight,
    up_weight,
    down_weight,
    input_gain,
    heads_gain,
    middle_gain,
    hidden_gain,
    cotangent,
):
    rows, row_count, width = layer_input.shape
    T, C = lax.axis_size("tp"), lax.axis_size("cp")
    part = rows // T
    head_width = qkv_weight.shape[2]
    if head_width // HD != C or row_count != 1 or rows != 128 or part % 16 != 0:
        return body_general(
            layer_input, segment_ids, qkv_weight, out_weight, up_weight, down_weight,
            input_gain, heads_gain, middle_gain, hidden_gain, cotangent,
        )
    tokens = rows * C
    hidden = up_weight.shape[1]
    wide = width // C
    high = hidden // C
    ids = jnp.stack([lax.axis_index("tp"), lax.axis_index("cp")]).astype(jnp.int32)
    x = layer_input.reshape(rows, width)
    gy = cotangent.reshape(rows, width)
    weight3 = jnp.transpose(qkv_weight, (1, 0, 2))
    gain_in, gain_mid = input_gain.reshape(1, -1), middle_gain.reshape(1, -1)
    gain_heads, gain_hid = heads_gain.reshape(1, -1), hidden_gain.reshape(1, -1)
    inner, base = tables(rows, C)
    inner2 = jnp.asarray(np.concatenate([inner, inner], axis=2))
    base2 = jnp.asarray(np.concatenate([base, base], axis=2))
    base_t = np.zeros((4, HD, 128), np.float32)
    base_t[:, :, :C] = np.transpose(base, (0, 2, 1))
    base_t = jnp.asarray(base_t)
    wide_part = width + 128

    def piece_shapes(columns):
        return [shape((part, columns), f32)] + [shape((part, columns), bf16)] * (T - 1)

    def exchange(pieces):
        return [swap_tp(piece, k) for k, piece in enumerate(pieces, 1)]

    def spread(block):
        return [swap_tp(block, k) for k in range(1, T)]

    def to_cp(value):
        return lax.all_to_all(value, "cp", 0, 0, tiled=True)

    gy_all = cp_gather(gy)
    a, sent = call(
        functools.partial(project_kernel, T),
        [shape((rows, width), bf16), shape((C, 3 * HD + 16, rows), bf16)],
        [ids, x, segment_ids.reshape(1, rows), gain_in, weight3, inner2, base2],
        [scalars(), fixed((rows, width)), fixed((1, rows)), fixed((1, width)),
         pl.BlockSpec((1, width, head_width), lambda i: (i, 0, 0)), fixed((4, rows, 128)), fixed((4, C, 128))],
        [fixed((rows, width)), fixed((C, 3 * HD + 16, rows))],
        grid=(3,), scratch=[pltpu.VMEM((4, rows, 128), f32)],
        flops=2 * rows * width * 3 * head_width,
    )
    a_all = cp_gather(a)
    got = to_cp(sent)
    step = 512
    grad_hid, gain_row = call(
        functools.partial(grad_hidden_kernel, T),
        [shape((rows, hidden), f32), shape((1, width), f32)],
        [ids, gy, down_weight, gain_heads, out_weight],
        [scalars(), fixed((rows, width)), pl.BlockSpec((step, width), lambda i: (i, 0)),
         fixed((1, head_width)), fixed((head_width, width))],
        [pl.BlockSpec((rows, step), lambda i: (0, i)), fixed((1, width))],
        grid=(hidden // step,), scratch=[pltpu.VMEM((rows, width), bf16)],
        flops=2 * rows * width * hidden, after=[sent],
    )
    gain_rows = [gain_row] + spread(gain_row)
    back, mixed, lse = call(
        functools.partial(attend_kernel, T),
        [shape((C, HD, rows), bf16), shape((HD, tokens), f32), shape((1, tokens), f32)],
        [ids, got], [scalars(), whole()],
        scratch=[pltpu.VMEM((tokens, HD), bf16), pltpu.VMEM((tokens, 16), f32)],
        flops=4 * tokens * tokens * HD,
    )
    att = to_cp(back)

    own, *pieces = call(
        functools.partial(out_kernel, T), piece_shapes(wide_part), [att, gain_heads, out_weight],
        flops=2 * rows * width * head_width,
    )
    x1, u_own = call(
        functools.partial(middle_kernel, T, head_width),
        [shape((part, width), f32), shape((part, wide_part), bf16)],
        [ids, own, *exchange(pieces), *gain_rows, x, gain_mid],
        [scalars()] + [whole()] * (2 * T + 2),
    )
    u_blocks = [u_own] + spread(u_own)

    act, slope, u_cols, stats = call(
        functools.partial(up_kernel, T),
        [shape((rows, hidden), f32), shape((rows, hidden), f32), shape((C, rows, wide), bf16), shape((8, rows), f32)],
        [*u_blocks, up_weight, grad_hid, gain_hid],
        [fixed((part, wide_part))] * T
        + [pl.BlockSpec((width, step), lambda i: (0, i)), pl.BlockSpec((rows, step), lambda i: (0, i)),
           pl.BlockSpec((1, step), lambda i: (0, i))],
        [pl.BlockSpec((rows, step), lambda i: (0, i)), pl.BlockSpec((rows, step), lambda i: (0, i)),
         fixed((C, rows, wide)), fixed((8, rows))],
        grid=(hidden // step,), scratch=[pltpu.VMEM((rows, width), bf16), pltpu.VMEM((rows, 128), f32)],
        flops=2 * rows * width * hidden,
    )
    gh, z2, hidden_gain_sum, own, *pieces = call(
        functools.partial(hidden_back_kernel, T, FF),
        [shape((rows, hidden), bf16), shape((C, rows, high), bf16), shape((1, hidden), f32)] + piece_shapes(width),
        [stats, *spread(stats), act, slope, grad_hid, gain_hid, up_weight],
        [fixed((8, rows))] * T
        + [pl.BlockSpec((rows, step), lambda i: (0, i))] * 3
        + [pl.BlockSpec((1, step), lambda i: (0, i)), pl.BlockSpec((width, step), lambda i: (0, i))],
        [pl.BlockSpec((rows, step), lambda i: (0, i)),
         pl.BlockSpec((step // high, rows, high), lambda i: (i, 0, 0)),
         pl.BlockSpec((1, step), lambda i: (0, i))] + [fixed((part, width))] * T,
        grid=(hidden // step,), scratch=[pltpu.VMEM((rows, width), f32), pltpu.VMEM((rows, rows), f32)],
        flops=2 * rows * width * hidden,
    )
    gh_all = cp_gather(gh)
    gu_got = exchange(pieces)
    y_own, *y_pieces = call(
        functools.partial(down_kernel, T), piece_shapes(width), [z2, down_weight],
        [pl.BlockSpec((step // high, rows, high), lambda i: (i, 0, 0)), pl.BlockSpec((step, width), lambda i: (i, 0))],
        [fixed((part, width))] * T,
        grid=(hidden // step,), scratch=[pltpu.VMEM((rows, width), f32)],
        flops=2 * rows * width * hidden, after=[own],
    )
    gx1, gb_own, middle_gain_sum = call(
        functools.partial(middle_back_kernel, T),
        [shape((part, width), f32), shape((part, wide_part), bf16), shape((1, width), f32)],
        [ids, own, *gu_got, *gain_rows, x, x1, gy, gain_mid],
        [scalars()] + [whole()] * (2 * T + 4),
    )
    gb_blocks = [gb_own] + spread(gb_own)

    sent, gb, heads_gain_sum = call(
        functools.partial(heads_back_kernel, T),
        [shape((C, 2 * HD, rows), bf16), shape((rows, width), bf16), shape((1, head_width), f32)],
        [*gb_blocks, *u_blocks, att, gain_heads, out_weight],
        flops=2 * rows * width * head_width,
    )
    gb_all = cp_gather(gb)
    grads = to_cp(sent)
    (gq_sent,) = call(
        functools.partial(attend_back_kernel, T), [shape((C, 3 * HD, rows), bf16)],
        [ids, got, grads, mixed, lse, inner2, base_t], [scalars()] + [whole()] * 6,
        scratch=[pltpu.VMEM((tokens, HD), bf16), pltpu.VMEM((tokens, HD), bf16), pltpu.VMEM((tokens, 16), f32),
                 pltpu.VMEM((HD, tokens), f32), pltpu.VMEM((HD, tokens), f32)],
        flops=10 * tokens * tokens * HD,
    )
    gq = to_cp(gq_sent)
    own, *pieces = call(
        functools.partial(input_back_kernel, T), piece_shapes(width), [gq, weight3],
        [fixed((C, 3 * HD, rows)), pl.BlockSpec((1, width, head_width), lambda i: (i, 0, 0))],
        [fixed((part, width))] * T,
        grid=(3,), scratch=[pltpu.VMEM((rows, width), f32)],
        flops=2 * rows * width * 3 * head_width,
    )
    grad_in, input_gain_sum = call(
        functools.partial(final_kernel, T),
        [shape((part, width), bf16), shape((1, width), f32)],
        [ids, own, *exchange(pieces), x, gx1, gain_in],
        [scalars()] + [whole()] * (T + 3),
    )
    grad_blocks = [grad_in] + spread(grad_in)
    (grad_input,) = call(
        natural_kernel, [shape((rows, width), bf16)], [ids, *grad_blocks], [scalars()] + [whole()] * T
    )

    (y_low,) = call(output_kernel, [shape((part, width), bf16)], [y_own, *exchange(y_pieces), x1])
    y_blocks = [y_low] + spread(y_low)
    (layer_output,) = call(
        natural_kernel, [shape((rows, width), bf16)], [ids, *y_blocks], [scalars()] + [whole()] * T
    )

    def columns_grad(left, right, reorder):
        own_columns = left.shape[2]
        return call(
            functools.partial(columns_grad_kernel, T, reorder),
            [shape((own_columns, right.shape[1]), f32)], [ids, left, right],
            [scalars(), fixed(left.shape), pl.BlockSpec((tokens, step), lambda i: (0, i))],
            [pl.BlockSpec((own_columns, step), lambda i: (0, i))],
            grid=(right.shape[1] // step,), scratch=[pltpu.VMEM((tokens, own_columns), bf16)],
            flops=2 * tokens * own_columns * right.shape[1],
        )[0]

    grad_down = columns_grad(to_cp(z2), gy_all, True)
    grad_up = columns_grad(to_cp(u_cols), gh_all, False)
    (grad_out,) = call(
        functools.partial(rows_grad_kernel, HD), [shape((HD, width), f32)], [grads, gb_all],
        [fixed(grads.shape), pl.BlockSpec((tokens, step), lambda i: (0, i))],
        [pl.BlockSpec((HD, step), lambda i: (0, i))], grid=(width // step,),
        flops=2 * tokens * HD * width,
    )
    (grad_qkv,) = call(
        grad_qkv_kernel, [shape((C, 3 * HD, wide), bf16)], [gq_sent, a_all],
        [fixed(gq_sent.shape), pl.BlockSpec((tokens, wide), lambda i: (0, i))],
        [pl.BlockSpec((1, 3 * HD, wide), lambda i: (i, 0, 0))], grid=(C,),
        flops=2 * tokens * 3 * HD * width,
    )
    (grad_qkv,) = call(grad_qkv_place_kernel, [shape((3, wide, head_width), f32)], [to_cp(grad_qkv)])

    by_cp = jnp.concatenate([heads_gain_sum.reshape(C, -1), hidden_gain_sum.reshape(C, -1)], axis=1)
    by_cp = jnp.sum(to_cp(by_cp), axis=0)
    by_all = jnp.concatenate([input_gain_sum.reshape(C, -1), middle_gain_sum.reshape(C, -1)], axis=1)
    by_all = jnp.broadcast_to(by_all[None], (T, C, 2 * wide)).reshape(T * C, 2 * wide)
    by_all = jnp.sum(lax.all_to_all(by_all, ("tp", "cp"), 0, 0, tiled=True), axis=0)
    return (
        layer_output.reshape(layer_input.shape),
        grad_input.reshape(layer_input.shape),
        jnp.transpose(grad_qkv, (1, 0, 2)),
        grad_out,
        grad_up,
        grad_down,
        by_all[:wide],
        by_cp[: head_width // C],
        by_all[wide:],
        by_cp[head_width // C :],
    )


def solution(mesh):
    placed = (
        P("cp", None, None),
        P("cp", None),
        P(None, None, "tp"),
        P("tp", None),
        P(None, "tp"),
        P("tp", None),
        P(),
        P("tp"),
        P(),
        P("tp"),
        P("cp", None, None),
    )
    return jax.shard_map(
        body,
        mesh=mesh,
        in_specs=placed,
        out_specs=(
            P("cp", None, None),
            P("cp", None, None),
            P("cp", None, "tp"),
            P(("tp", "cp"), None),
            P("cp", "tp"),
            P(("tp", "cp"), None),
            P("cp"),
            P(("tp", "cp")),
            P("cp"),
            P(("tp", "cp")),
        ),
        check_vma=False,
    )
```

profile of v0, /device:TPU:0, one launch (start us, length us, event | category | flops | bytes accessed | tf_op | source)
XLA Modules:
  0.0 297.6 jit_solution(17302009462632508170)
XLA Ops:
  19.2 14.5 %all_to_all.53.refs_1_ = bf16[8,208,128]{2,1,0:T(8,128)(2,1)S(1)} all-to-all(bf16[8,208,128]{2,1,0:T(8,128)(2,1)S(1)} %get-tuple-element.50.refs_5_), channel_id=1, replica_groups=mesh['tp'=4,'cp'=8] {'cp'}, dimensions={0} | all-to-all | bytes 851968 | tf_op jit(solution)/shard_map/all_to_all | solution.py:899
  37.1 8.2 %all_to_all.54.refs_0_.refs_8_ = bf16[8,64,128]{2,1,0:T(8,128)(2,1)S(1)} all-to-all(bf16[8,64,128]{2,1,0:T(8,128)(2,1)S(1)} %get-tuple-element.51), channel_id=1, replica_groups=mesh['tp'=4,'cp'=8] {'cp'}, dimensions={0} | all-to-all | bytes 262144 | tf_op jit(solution)/shard_map/all_to_all | solution.py:899
  55.0 4.4 %shard_map.216 = (f32[128,2048]{1,0:T(8,128)S(1)}, f32[1,2048]{1,0:T(1,128)S(1)}) custom-call(s32[2]{0:T(128)S(1)} %pad_add_fusion.refs_0_, bf16[128,2048]{1,0:T(8,128)(2,1)S(1)} %bitcast.22, bf16[2048,2048]{1,0:T(8,128)(2,1)S(1)} %copy-done, f32[1,512]{1,0:T(1,128)S(1)} %bitcast.32, bf16[512,2048]{1,0:T(8,128)(2,1)S(1)} %copy-done.4, ...), custom_call_target="tpu_custom_call" | custom-call | flops 1073741824 | bytes 12068872 | tf_op jit(solution)/shard_map/pallas_call | solution.py:356
  60.1 3.8 %collective-permute-start.4 = (f32[1,2048]{1,0:T(1,128)S(1)}, f32[1,2048]{1,0:T(1,128)S(1)}, u32[]{:S(2)}, u32[]{:S(2)}) collective-permute-start(f32[1,2048]{1,0:T(1,128)S(1)} %get-tuple-element.56.refs_5_), channel_id=1, source_target_pairs={{0,16},{8,24},{16,0},{24,8},{1,17},{9,25},{17,1},{25,9},{2,18},{10... | collective-permute-start | bytes 24584 | tf_op jit(solution)/shard_map/ppermute | solution.py:39
  71.1 3.6 %collective-permute-start.7 = (bf16[32,2176]{1,0:T(8,128)(2,1)S(1)}, bf16[32,2176]{1,0:T(8,128)(2,1)S(1)}, u32[]{:S(2)}, u32[]{:S(2)}) collective-permute-start(bf16[32,2176]{1,0:T(8,128)(2,1)S(1)} %get-tuple-element.57.refs_0_.refs_4_), channel_id=1, source_target_pairs={{0,16},{8,24},{16,0},{24,8},{1,17},{9,25},{17,1},{25,9},{2,18},{10... | collective-permute-start | bytes 417800 | tf_op jit(solution)/shard_map/ppermute | solution.py:39
  78.4 3.9 %collective-permute-done.7.refs_2_.refs_6_ = bf16[32,2176]{1,0:T(8,128)(2,1)S(1)} collective-permute-done((bf16[32,2176]{1,0:T(8,128)(2,1)S(1)}, bf16[32,2176]{1,0:T(8,128)(2,1)S(1)}, u32[]{:S(2)}, u32[]{:S(2)}) %collective-permute-start.7) | collective-permute-done | bytes 139296 | tf_op jit(solution)/shard_map/ppermute | solution.py:39
  82.3 4.5 %shard_map.218 = (f32[128,2048]{1,0:T(8,128)S(1)}, f32[128,2048]{1,0:T(8,128)S(1)}, bf16[8,128,256]{2,1,0:T(8,128)(2,1)}, f32[8,128]{1,0:T(8,128)S(1)}) custom-call(bf16[32,2176]{1,0:T(8,128)(2,1)S(1)} %get-tuple-element.57.refs_0_.refs_4_, bf16[32,2176]{1,0:T(8,128)(2,1)S(1)} %collective-permute-done.6.refs_1_.refs_5_, ...), custom_call_target="tpu_custom_call" | custom-call | flops 1073741824 | bytes 12627968 | tf_op jit(solution)/shard_map/pallas_call | solution.py:356
  91.4 3.8 %collective-permute-done.11.refs_3_ = f32[8,128]{1,0:T(8,128)S(1)} collective-permute-done((f32[8,128]{1,0:T(8,128)S(1)}, f32[8,128]{1,0:T(8,128)S(1)}, u32[]{:S(2)}, u32[]{:S(2)}) %collective-permute-start.11) | collective-permute-done | bytes 4128 | tf_op jit(solution)/shard_map/ppermute | solution.py:39
  95.2 5.5 %shard_map.219 = (bf16[128,2048]{1,0:T(8,128)(2,1)S(1)}, bf16[8,128,256]{2,1,0:T(8,128)(2,1)}, f32[1,2048]{1,0:T(1,128)S(1)}, f32[32,2048]{1,0:T(8,128)S(1)}, bf...) custom-call(f32[8,128]{1,0:T(8,128)S(1)} %get-tuple-element.59.refs_0_, ...), custom_call_target="tpu_custom_call" | custom-call | flops 1073741824 | bytes 13271040 | tf_op jit(solution)/shard_map/pallas_call | solution.py:356
  126.6 5.0 %collective-permute-done.22.refs_2_ = bf16[32,2176]{1,0:T(8,128)(2,1)S(1)} collective-permute-done((bf16[32,2176]{1,0:T(8,128)(2,1)S(1)}, bf16[32,2176]{1,0:T(8,128)(2,1)S(1)}, u32[]{:S(2)}, u32[]{:S(2)}) %collective-permute-start.22) | collective-permute-done | bytes 139296 | tf_op jit(solution)/shard_map/ppermute | solution.py:39
  144.6 3.6 %all-to-all-done.2.refs_2_.refs_0_ = bf16[8,128,128]{2,1,0:T(8,128)(2,1)S(1)} async-done(((bf16[8,128,128]{2,1,0:T(8,128)(2,1)}), bf16[8,128,128]{2,1,0:T(8,128)(2,1)S(1)}, u32[]{:S(2)}, u32[]{:S(2)}) %all-to-all-start.2) | async-done | bytes 262176 | tf_op jit(solution)/shard_map/all_to_all | solution.py:899
  148.2 3.5 %all-to-all-start.8 = ((f32[8,1,320]{2,1,0:T(1,128)}), f32[8,1,320]{2,1,0:T(1,128)S(1)}, u32[]{:S(2)}, u32[]{:S(2)}) async-start(f32[8,1,320]{2,1,0:T(1,128)} %all_to_all.42), calls=%async_computation.8 | async-start | bytes 24576 | tf_op jit(solution)/shard_map/all_to_all | solution.py:899
  159.2 16.7 %all_to_all.55.refs_0_ = bf16[8,192,128]{2,1,0:T(8,128)(2,1)S(1)} all-to-all(bf16[8,192,128]{2,1,0:T(8,128)(2,1)S(1)} %shard_map.225.refs_0_), channel_id=1, replica_groups=mesh['tp'=4,'cp'=8] {'cp'}, dimensions={0} | all-to-all | bytes 786432 | tf_op jit(solution)/shard_map/all_to_all | solution.py:899
  176.0 3.5 %all-to-all-start.6 = ((bf16[8,128,256]{2,1,0:T(8,128)(2,1)}), bf16[8,128,256]{2,1,0:T(8,128)(2,1)S(1)}, u32[]{:S(2)}, u32[]{:S(2)}) async-start(bf16[8,128,256]{2,1,0:T(8,128)(2,1)} %get-tuple-element.62.refs_0_), calls=%async_computation.6 | async-start | bytes 1048576 | tf_op jit(solution)/shard_map/all_to_all | solution.py:899
  193.2 6.9 %collective-permute-done.25.refs_3_ = bf16[32,2048]{1,0:T(8,128)(2,1)S(1)} collective-permute-done((bf16[32,2048]{1,0:T(8,128)(2,1)S(1)}, bf16[32,2048]{1,0:T(8,128)(2,1)S(1)}, u32[]{:S(2)}, u32[]{:S(2)}) %collective-permute-start.25) | collective-permute-done | bytes 131104 | tf_op jit(solution)/shard_map/ppermute | solution.py:39
  202.4 5.8 %all-to-all-start.7 = ((f32[32,1,512]{2,1,0:T(1,128)}), f32[32,1,512]{2,1,0:T(1,128)S(1)}, u32[]{:S(2)}, u32[]{:S(2)}) async-start(f32[32,1,512]{2,1,0:T(1,128)} %all_to_all.40), calls=%async_computation.7 | async-start | bytes 131072 | tf_op jit(solution)/shard_map/all_to_all | solution.py:1060
  210.4 4.3 %shard_map.229 = bf16[8,192,256]{2,1,0:T(8,128)(2,1)} custom-call(bf16[8,192,128]{2,1,0:T(8,128)(2,1)S(1)} %shard_map.225.refs_0_, bf16[1024,2048]{1,0:T(8,128)(2,1)S(1)} %copy-done.10), custom_call_target="tpu_custom_call" | custom-call | flops 805306368 | bytes 5373952 | tf_op jit(solution)/shard_map/pallas_call | solution.py:356
  215.6 3.5 %all-to-all-start.4 = ((bf16[8,192,256]{2,1,0:T(8,128)(2,1)}), bf16[8,192,256]{2,1,0:T(8,128)(2,1)S(1)}, u32[]{:S(2)}, u32[]{:S(2)}) async-start(bf16[8,192,256]{2,1,0:T(8,128)(2,1)} %shard_map.229), calls=%async_computation.4 | async-start | bytes 1572864 | tf_op jit(solution)/shard_map/all_to_all | solution.py:899
  231.7 3.5 %all-to-all-start.5 = ((bf16[8,128,256]{2,1,0:T(8,128)(2,1)}), bf16[8,128,256]{2,1,0:T(8,128)(2,1)S(1)}, u32[]{:S(2)}, u32[]{:S(2)}) async-start(bf16[8,128,256]{2,1,0:T(8,128)(2,1)} %get-tuple-element.84), calls=%async_computation.5 | async-start | bytes 1048576 | tf_op jit(solution)/shard_map/all_to_all | solution.py:899
  235.2 4.7 %collective-permute-done.13.refs_2_ = bf16[32,2048]{1,0:T(8,128)(2,1)S(1)} collective-permute-done((bf16[32,2048]{1,0:T(8,128)(2,1)S(1)}, bf16[32,2048]{1,0:T(8,128)(2,1)S(1)}, u32[]{:S(2)}, u32[]{:S(2)}) %collective-permute-start.13) | collective-permute-done | bytes 131104 | tf_op jit(solution)/shard_map/ppermute | solution.py:39
  247.0 8.2 %collective-permute-done.16.refs_3_ = bf16[32,2048]{1,0:T(8,128)(2,1)S(1)} collective-permute-done((bf16[32,2048]{1,0:T(8,128)(2,1)S(1)}, bf16[32,2048]{1,0:T(8,128)(2,1)S(1)}, u32[]{:S(2)}, u32[]{:S(2)}) %collective-permute-start.16) | collective-permute-done | bytes 131104 | tf_op jit(solution)/shard_map/ppermute | solution.py:39
  264.1 7.5 %collective-permute-done.28.refs_3_ = bf16[32,2048]{1,0:T(8,128)(2,1)S(1)} collective-permute-done((bf16[32,2048]{1,0:T(8,128)(2,1)S(1)}, bf16[32,2048]{1,0:T(8,128)(2,1)S(1)}, u32[]{:S(2)}, u32[]{:S(2)}) %collective-permute-start.28) | collective-permute-done | bytes 131104 | tf_op jit(solution)/shard_map/ppermute | solution.py:39
  275.2 3.8 %shard_map.233 = f32[256,2048]{1,0:T(8,128)} custom-call(s32[2]{0:T(128)S(1)} %pad_add_fusion.refs_0_, bf16[8,128,256]{2,1,0:T(8,128)(2,1)S(1)} %all-to-all-done.6.refs_1_, bf16[1024,2048]{1,0:T(8,128)(2,1)S(1)} %bitcast.24), custom_call_target="tpu_custom_call" | custom-call | flops 1073741824 | bytes 6815752 | tf_op jit(solution)/shard_map/pallas_call | solution.py:356
  282.6 3.8 %shard_map.232 = f32[256,2048]{1,0:T(8,128)} custom-call(s32[2]{0:T(128)S(1)} %pad_add_fusion.refs_0_, bf16[8,128,256]{2,1,0:T(8,128)(2,1)S(1)} %all-to-all-done.5.refs_1_, bf16[1024,2048]{1,0:T(8,128)(2,1)S(1)} %copy-done.11), custom_call_target="tpu_custom_call" | custom-call | flops 1073741824 | bytes 6815752 | tf_op jit(solution)/shard_map/pallas_call | solution.py:356
  (235 shorter events, 146.9 us)
Async XLA Ops:
  7.2 201.0 %all-gather.6.cloned.1.call-start = ((), (), s32[]{:S(2)}) async-start(), calls=%async_computation.9 | async-start | bytes 4718592 | tf_op jit(solution)/shard_map/all_gather | solution.py:87
  18.4 254.5 %all-gather.12.cloned.1.call-start = ((), (), s32[]{:S(2)}) async-start(), calls=%async_computation.12 | async-start | bytes 4718592 | tf_op jit(solution)/shard_map/all_gather | solution.py:87
  19.2 261.2 %all-gather.10.cloned.1.call-start = ((), (), s32[]{:S(2)}) async-start(), calls=%async_computation.11 | async-start | bytes 4718592 | tf_op jit(solution)/shard_map/all_gather | solution.py:87
  45.9 23.5 %collective-permute-start = (bf16[32,2176]{1,0:T(8,128)(2,1)S(1)}, bf16[32,2176]{1,0:T(8,128)(2,1)S(1)}, u32[]{:S(2)}, u32[]{:S(2)}) collective-permute-start(bf16[32,2176]{1,0:T(8,128)(2,1)S(1)} %get-tuple-element.53), channel_id=1, source_target_pairs={{0,8},{8,0},{16,24},{24,16},{1,9},{9,1},{17,25},{25,17},{2,10},{10... | collective-permute-start | bytes 417800 | tf_op jit(solution)/shard_map/ppermute | solution.py:39
  47.6 21.7 %collective-permute-start.1 = (bf16[32,2176]{1,0:T(8,128)(2,1)S(1)}, bf16[32,2176]{1,0:T(8,128)(2,1)S(1)}, u32[]{:S(2)}, u32[]{:S(2)}) collective-permute-start(bf16[32,2176]{1,0:T(8,128)(2,1)S(1)} %get-tuple-element.54), channel_id=1, source_target_pairs={{0,16},{8,24},{16,0},{24,8},{1,17},{9,25},{17,1},{25,9},{2,18},{10... | collective-permute-start | bytes 417800 | tf_op jit(solution)/shard_map/ppermute | solution.py:39
  50.5 18.9 %collective-permute-start.2 = (bf16[32,2176]{1,0:T(8,128)(2,1)S(1)}, bf16[32,2176]{1,0:T(8,128)(2,1)S(1)}, u32[]{:S(2)}, u32[]{:S(2)}) collective-permute-start(bf16[32,2176]{1,0:T(8,128)(2,1)S(1)} %get-tuple-element.55), channel_id=1, source_target_pairs={{0,24},{8,16},{16,8},{24,0},{1,25},{9,17},{17,9},{25,1},{2,26},{10... | collective-permute-start | bytes 417800 | tf_op jit(solution)/shard_map/ppermute | solution.py:39
  71.1 11.1 %collective-permute-start.7 = (bf16[32,2176]{1,0:T(8,128)(2,1)S(1)}, bf16[32,2176]{1,0:T(8,128)(2,1)S(1)}, u32[]{:S(2)}, u32[]{:S(2)}) collective-permute-start(bf16[32,2176]{1,0:T(8,128)(2,1)S(1)} %get-tuple-element.57.refs_0_.refs_4_), channel_id=1, source_target_pairs={{0,16},{8,24},{16,0},{24,8},{1,17},{9,25},{17,1},{25,9},{2,18},{10... | collective-permute-start | bytes 417800 | tf_op jit(solution)/shard_map/ppermute | solution.py:39
  104.1 182.3 %all-gather.8.cloned.1.call-start = ((), (), s32[]{:S(2)}) async-start(), calls=%async_computation.10 | async-start | bytes 4718592 | tf_op jit(solution)/shard_map/all_gather | solution.py:87
  104.2 9.7 %collective-permute-start.19 = (bf16[32,2048]{1,0:T(8,128)(2,1)}, bf16[32,2048]{1,0:T(8,128)(2,1)S(1)}, u32[]{:S(2)}, u32[]{:S(2)}) collective-permute-start(bf16[32,2048]{1,0:T(8,128)(2,1)} %copy-done.55), channel_id=1, source_target_pairs={{0,16},{8,24},{16,0},{24,8},{1,17},{9,25},{17,1},{25,9},{2,18},{10... | collective-permute-start | bytes 393224 | tf_op jit(solution)/shard_map/ppermute | solution.py:39
  122.0 9.6 %collective-permute-start.22 = (bf16[32,2176]{1,0:T(8,128)(2,1)S(1)}, bf16[32,2176]{1,0:T(8,128)(2,1)S(1)}, u32[]{:S(2)}, u32[]{:S(2)}) collective-permute-start(bf16[32,2176]{1,0:T(8,128)(2,1)S(1)} %get-tuple-element.72.refs_0_), channel_id=1, source_target_pairs={{0,16},{8,24},{16,0},{24,8},{1,17},{9,25},{17,1},{25,9},{2,18},{10... | collective-permute-start | bytes 417800 | tf_op jit(solution)/shard_map/ppermute | solution.py:39
  137.9 10.3 %all-to-all-start.2 = ((bf16[8,128,128]{2,1,0:T(8,128)(2,1)}), bf16[8,128,128]{2,1,0:T(8,128)(2,1)S(1)}, u32[]{:S(2)}, u32[]{:S(2)}) async-start(bf16[8,128,128]{2,1,0:T(8,128)(2,1)} %copy-done.31), calls=%async_computation.2 | async-start | bytes 524288 | tf_op jit(solution)/shard_map/all_to_all | solution.py:899
  148.2 11.1 %all-to-all-start.8 = ((f32[8,1,320]{2,1,0:T(1,128)}), f32[8,1,320]{2,1,0:T(1,128)S(1)}, u32[]{:S(2)}, u32[]{:S(2)}) async-start(f32[8,1,320]{2,1,0:T(1,128)} %all_to_all.42), calls=%async_computation.8 | async-start | bytes 24576 | tf_op jit(solution)/shard_map/all_to_all | solution.py:899
  176.0 26.4 %all-to-all-start.6 = ((bf16[8,128,256]{2,1,0:T(8,128)(2,1)}), bf16[8,128,256]{2,1,0:T(8,128)(2,1)S(1)}, u32[]{:S(2)}, u32[]{:S(2)}) async-start(bf16[8,128,256]{2,1,0:T(8,128)(2,1)} %get-tuple-element.62.refs_0_), calls=%async_computation.6 | async-start | bytes 1048576 | tf_op jit(solution)/shard_map/all_to_all | solution.py:899
  187.1 12.9 %collective-permute-start.25 = (bf16[32,2048]{1,0:T(8,128)(2,1)S(1)}, bf16[32,2048]{1,0:T(8,128)(2,1)S(1)}, u32[]{:S(2)}, u32[]{:S(2)}) collective-permute-start(bf16[32,2048]{1,0:T(8,128)(2,1)S(1)} %get-tuple-element.78), channel_id=1, source_target_pairs={{0,16},{8,24},{16,0},{24,8},{1,17},{9,25},{17,1},{25,9},{2,18},{10... | collective-permute-start | bytes 393224 | tf_op jit(solution)/shard_map/ppermute | solution.py:39
  188.2 11.9 %collective-permute-start.26 = (bf16[32,2048]{1,0:T(8,128)(2,1)S(1)}, bf16[32,2048]{1,0:T(8,128)(2,1)S(1)}, u32[]{:S(2)}, u32[]{:S(2)}) collective-permute-start(bf16[32,2048]{1,0:T(8,128)(2,1)S(1)} %get-tuple-element.79), channel_id=1, source_target_pairs={{0,24},{8,16},{16,8},{24,0},{1,25},{9,17},{17,9},{25,1},{2,26},{10... | collective-permute-start | bytes 393224 | tf_op jit(solution)/shard_map/ppermute | solution.py:39
  202.4 13.2 %all-to-all-start.7 = ((f32[32,1,512]{2,1,0:T(1,128)}), f32[32,1,512]{2,1,0:T(1,128)S(1)}, u32[]{:S(2)}, u32[]{:S(2)}) async-start(f32[32,1,512]{2,1,0:T(1,128)} %all_to_all.40), calls=%async_computation.7 | async-start | bytes 131072 | tf_op jit(solution)/shard_map/all_to_all | solution.py:1060
  215.6 16.1 %all-to-all-start.4 = ((bf16[8,192,256]{2,1,0:T(8,128)(2,1)}), bf16[8,192,256]{2,1,0:T(8,128)(2,1)S(1)}, u32[]{:S(2)}, u32[]{:S(2)}) async-start(bf16[8,192,256]{2,1,0:T(8,128)(2,1)} %shard_map.229), calls=%async_computation.4 | async-start | bytes 1572864 | tf_op jit(solution)/shard_map/all_to_all | solution.py:899
  227.0 12.9 %collective-permute-start.13 = (bf16[32,2048]{1,0:T(8,128)(2,1)S(1)}, bf16[32,2048]{1,0:T(8,128)(2,1)S(1)}, u32[]{:S(2)}, u32[]{:S(2)}) collective-permute-start(bf16[32,2048]{1,0:T(8,128)(2,1)S(1)} %get-tuple-element.66), channel_id=1, source_target_pairs={{0,16},{8,24},{16,0},{24,8},{1,17},{9,25},{17,1},{25,9},{2,18},{10... | collective-permute-start | bytes 393224 | tf_op jit(solution)/shard_map/ppermute | solution.py:39
  229.5 10.4 %collective-permute-start.14 = (bf16[32,2048]{1,0:T(8,128)(2,1)S(1)}, bf16[32,2048]{1,0:T(8,128)(2,1)S(1)}, u32[]{:S(2)}, u32[]{:S(2)}) collective-permute-start(bf16[32,2048]{1,0:T(8,128)(2,1)S(1)} %get-tuple-element.67), channel_id=1, source_target_pairs={{0,24},{8,16},{16,8},{24,0},{1,25},{9,17},{17,9},{25,1},{2,26},{10... | collective-permute-start | bytes 393224 | tf_op jit(solution)/shard_map/ppermute | solution.py:39
  231.7 48.7 %all-to-all-start.5 = ((bf16[8,128,256]{2,1,0:T(8,128)(2,1)}), bf16[8,128,256]{2,1,0:T(8,128)(2,1)S(1)}, u32[]{:S(2)}, u32[]{:S(2)}) async-start(bf16[8,128,256]{2,1,0:T(8,128)(2,1)} %get-tuple-element.84), calls=%async_computation.5 | async-start | bytes 1048576 | tf_op jit(solution)/shard_map/all_to_all | solution.py:899
  242.7 12.5 %collective-permute-start.16 = (bf16[32,2048]{1,0:T(8,128)(2,1)S(1)}, bf16[32,2048]{1,0:T(8,128)(2,1)S(1)}, u32[]{:S(2)}, u32[]{:S(2)}) collective-permute-start(bf16[32,2048]{1,0:T(8,128)(2,1)S(1)} %shard_map.221.refs_1_), channel_id=1, source_target_pairs={{0,16},{8,24},{16,0},{24,8},{1,17},{9,25},{17,1},{25,9},{2,18},{10... | collective-permute-start | bytes 393224 | tf_op jit(solution)/shard_map/ppermute | solution.py:39
  243.7 11.5 %collective-permute-start.17 = (bf16[32,2048]{1,0:T(8,128)(2,1)S(1)}, bf16[32,2048]{1,0:T(8,128)(2,1)S(1)}, u32[]{:S(2)}, u32[]{:S(2)}) collective-permute-start(bf16[32,2048]{1,0:T(8,128)(2,1)S(1)} %shard_map.221.refs_1_), channel_id=1, source_target_pairs={{0,24},{8,16},{16,8},{24,0},{1,25},{9,17},{17,9},{25,1},{2,26},{10... | collective-permute-start | bytes 393224 | tf_op jit(solution)/shard_map/ppermute | solution.py:39
  259.7 11.9 %collective-permute-start.28 = (bf16[32,2048]{1,0:T(8,128)(2,1)S(1)}, bf16[32,2048]{1,0:T(8,128)(2,1)S(1)}, u32[]{:S(2)}, u32[]{:S(2)}) collective-permute-start(bf16[32,2048]{1,0:T(8,128)(2,1)S(1)} %get-tuple-element.81.refs_1_), channel_id=1, source_target_pairs={{0,16},{8,24},{16,0},{24,8},{1,17},{9,25},{17,1},{25,9},{2,18},{10... | collective-permute-start | bytes 393224 | tf_op jit(solution)/shard_map/ppermute | solution.py:39
  260.6 11.0 %collective-permute-start.29 = (bf16[32,2048]{1,0:T(8,128)(2,1)S(1)}, bf16[32,2048]{1,0:T(8,128)(2,1)S(1)}, u32[]{:S(2)}, u32[]{:S(2)}) collective-permute-start(bf16[32,2048]{1,0:T(8,128)(2,1)S(1)} %get-tuple-element.81.refs_1_), channel_id=1, source_target_pairs={{0,24},{8,16},{16,8},{24,0},{1,25},{9,17},{17,9},{25,1},{2,26},{10... | collective-permute-start | bytes 393224 | tf_op jit(solution)/shard_map/ppermute | solution.py:39
  (81 other events, 676.2 us)
Sparse Core Ops, SparseCore 0:
  18.6 39.9 all-gather.5
  60.5 36.6 all-gather.11
  104.2 34.5 all-gather.9
  140.5 41.0 all-gather.7
where the time goes:
time: 299 us; the launch traced here: 298 us
  starting transfers between devices  71.8 us (24%)
  waiting for transfers between devices  64.6 us (22%)
  Pallas kernels  53 us (18%)
  local copies, waits for them, and re-layouts  50 us (17%)
  blocking collectives  39.4 us (13%)
  between operations  14.3 us (5%)
  other arithmetic  4.42 us (1%)
    ppermute x30, waiting for transfers between devices, swap_tp(): return lax.ppermute(value, 'tp', pairs(lax.axis_size('tp'), k))  58.1 us
    pallas_call x21, Pallas kernels, call(): pl.pallas_call(run, out_shape=tuple(outs), in_specs=specs + [pl.BlockSpec...  53 us
    ppermute x30, starting transfers between devices, swap_tp(): return lax.ppermute(value, 'tp', pairs(lax.axis_size('tp'), k))  48.4 us
    unnamed x130, local copies, waits for them, and re-layouts  46.3 us
    all_to_all x3, blocking collectives, to_cp(): return lax.all_to_all(value, 'cp', 0, 0, tiled=True)  39.4 us
    all_to_all x5, starting transfers between devices, to_cp(): return lax.all_to_all(value, 'cp', 0, 0, tiled=True)  17.5 us
  transfers between devices with their start and end apart: 40, of which 19 were waited for; matrix products, arithmetic and copies ran while one was open for 2% of the time, Pallas kernels for 16%

commit v1 on v0

--- a/solution.py
+++ b/solution.py
@@ -343,27 +343,135 @@
     return pl.BlockSpec(memory_space=pltpu.SMEM)
 
 
-def call(kernel, outs, args, specs=None, out_specs=None, grid=None, scratch=(), mb=32, flops=0, after=()):
+class Pin:
+    def __init__(self, value):
+        self.value = value
+
+
+class Far(Pin):
+    def __init__(self, value, dims=None, block=None):
+        super().__init__(value)
+        self.dims = tuple(value.shape) if dims is None else dims
+        self.block = block
+
+
+class Near:
+    def __init__(self, value):
+        self.value = value
+
+
+class Fetched:
+    def __init__(self, ref, copy):
+        self.ref, self.copy, self.shape = ref, copy, ref.shape
+
+    def ready(self):
+        if self.copy is not None:
+            self.copy.wait()
+            self.copy = None
+
+    def __getitem__(self, index):
+        self.ready()
+        return self.ref[index]
+
+
+def pinned(value):
+    return value if INTERPRET else pltpu.with_memory_space_constraint(value, pltpu.HBM)
+
+
+def call(
+    kernel, outs, args, specs=None, out_specs=None, grid=None, scratch=(), mb=8, flops=0, after=(), carry=(), prefetch=0
+):
     specs = list(specs) if specs is not None else [whole() for _ in args]
-    count = len(args)
-    extra = len(after)
+    out_specs = list(out_specs) if out_specs is not None else [whole() for _ in outs]
+    count, extra, kept, made = len(args), len(after), len(carry), len(outs)
+    anywhere = pl.BlockSpec(memory_space=pl.ANY)
+    far_in = [i for i, t in enumerate(args) if isinstance(t, Far)]
+    far_out = [i for i, t in enumerate(outs) if isinstance(t, Far)]
+    for i in far_in:
+        specs[i] = anywhere
+    for i in far_out:
+        out_specs[i] = anywhere
+    moving = [pltpu.VMEM(args[i].dims, args[i].value.dtype) for i in far_in]
+    moving += [pltpu.VMEM(outs[i].dims, outs[i].value.dtype) for i in far_out]
+    moving += [pltpu.SemaphoreType.DMA] * (len(far_in) + len(far_out))
+    own_scratch = len(scratch)
 
     def run(*refs):
-        kernel(*refs[:count], *refs[count + extra :])
-
-    moved = sum(int(np.prod(t.shape)) * t.dtype.itemsize for t in list(args) + list(outs))
-    options = {} if grid is None else {"grid": grid}
+        ins = list(refs[:count])
+        results = refs[count + extra + kept :]
+        products = list(results[:made])
+        rest = results[made + kept :]
+        slots, sems = rest[own_scratch : own_scratch + len(far_in) + len(far_out)], rest[own_scratch + len(far_in) + len(far_out) :]
+        for i, slot, sem in zip(far_in, slots, sems):
+            source = refs[i]
+            if args[i].block is not None:
+                source = source.at[args[i].block(refs[0])]
+            copy = pltpu.make_async_copy(source, slot, sem)
+            copy.start()
+            ins[i] = Fetched(slot, copy)
+        for i, slot in zip(far_out, slots[len(far_in) :]):
+            products[i] = slot
+        kernel(*ins, *products, *rest[:own_scratch])
+        for i in far_in:
+            ins[i].ready()
+        copies = [
+            pltpu.make_async_copy(slot, results[i], sem)
+            for i, slot, sem in zip(far_out, slots[len(far_in) :], sems[len(far_in) :])
+        ]
+        for copy in copies:
+            copy.start()
+        for copy in copies:
+            copy.wait()
+
+    def plain(value):
+        return value.value if isinstance(value, (Pin, Near)) else value
+
+    def result(value):
+        dims = plain(value)
+        if INTERPRET or value is dims:
+            return dims
+        return (pltpu.HBM if isinstance(value, Pin) else pltpu.VMEM)(dims.shape, dims.dtype)
+
+    moved = sum(int(np.prod(plain(t).shape)) * plain(t).dtype.itemsize for t in list(args) + list(outs))
+    where = dict(
+        in_specs=specs + [anywhere] * (extra + kept),
+        out_specs=tuple(out_specs + [anywhere] * kept),
+        scratch_shapes=list(scratch) + moving,
+    )
+    if prefetch:
+        where["in_specs"] = where["in_specs"][prefetch:]
+        where = {"grid_spec": pltpu.PrefetchScalarGridSpec(num_scalar_prefetch=prefetch, grid=grid, **where)}
+    elif grid is not None:
+        where["grid"] = grid
     return pl.pallas_call(
         run,
-        out_shape=tuple(outs),
-        in_specs=specs + [pl.BlockSpec(memory_space=pl.ANY)] * extra,
-        out_specs=tuple(out_specs) if out_specs is not None else tuple(whole() for _ in outs),
-        scratch_shapes=list(scratch),
+        out_shape=tuple(result(t) for t in outs) + tuple(result(Pin(shape(t.shape, t.dtype))) for t in carry),
+        input_output_aliases={count + extra + i: made + i for i in range(kept)},
         compiler_params=params(mb),
-        cost_estimate=pl.CostEstimate(flops=flops, bytes_accessed=moved, transcendentals=0),
+        cost_estimate=pl.CostEstimate(flops=5000000000, bytes_accessed=0, transcendentals=0),
         interpret=INTERPRET,
-        **options,
-    )(*args, *after)
+        **where,
+    )(*[pinned(t.value) if isinstance(t, Pin) else t for t in list(args) + list(after)], *[pinned(t) for t in carry])
+
+
+def bring(items, ids, after=()):
+    def kernel(ids, *refs):
+        sources, slots, sems = refs[: len(items)], refs[len(items) : 2 * len(items)], refs[2 * len(items) :]
+        copies = []
+        for (_, _, block), source, slot, sem in zip(items, sources, slots, sems):
+            copies.append(pltpu.make_async_copy(source if block is None else source.at[block(ids)], slot, sem))
+        for copy in copies:
+            copy.start()
+        for copy in copies:
+            copy.wait()
+
+    return call(
+        kernel,
+        [Near(shape(dims, array.dtype)) for array, dims, _ in items],
+        [ids] + [Pin(array) for array, _, _ in items],
+        [scalars()] + [pl.BlockSpec(memory_space=pl.ANY)] * len(items),
+        scratch=[pltpu.SemaphoreType.DMA] * len(items), after=after, mb=2,
+    )
 
 
 def fixed(dims):
@@ -416,7 +524,7 @@
     return of(np.arange(local_len)), of(np.arange(cp_count) * local_len)
 
 
-def project_kernel(parts, ids, x, seg, gain, weight, inner, base, a, out, tab):
+def project_kernel(parts, ids, x, gy, seg, gain, weight, inner, base, a, gy_out, out, tab):
     step = pl.program_id(0)
     me, mine = ids[0], ids[1]
     rows, width = x.shape
@@ -429,6 +537,7 @@
             block = x[block_at(me, k, part), :].astype(f32)
             normed, _ = norm_rows(block)
             a[k * part : (k + 1) * part, :] = (normed * gain[...]).astype(bf16)
+            gy_out[k * part : (k + 1) * part, :] = gy[block_at(me, k, part), :]
             for kind in range(4):
                 tab[kind, k * part : (k + 1) * part, :] = inner[kind, block_at(me, k, part), :]
         place = lax.broadcasted_iota(jnp.int32, (rows, rows), 1)
@@ -480,8 +589,9 @@
     return same & earlier
 
 
-def attend_kernel(parts, ids, got, out, mixed, lse, keys, ids_col):
+def attend_kernel(parts, ids, got, out, mixed, lse, kept, keys, ids_col):
     me = ids[0]
+    kept[...] = got[...]
     blocks, _, rows = got.shape
     part = rows // parts
     gather_heads(got, keys, ids_col)
@@ -516,83 +626,100 @@
             piece[:, total.shape[1] :] = extra[k * part : (k + 1) * part].astype(bf16)
 
 
-def out_kernel(parts, att, gain, weight, own, *pieces):
+def fold_row(row, part):
+    block = jnp.concatenate([row[:, i : i + 128] for i in range(0, row.shape[1], 128)], axis=0)
+    return jnp.concatenate(split_low(block), axis=0)
+
+
+def unfold_row(block):
+    half = block.shape[0] // 2
+    total = block[:half].astype(f32) + block[half:].astype(f32)
+    return jnp.concatenate([total[i : i + 1] for i in range(half)], axis=1)
+
+
+def out_kernel(parts, att, gain, weight, own, *refs):
+    pieces, kept = refs[:-1], refs[-1]
+    kept[...] = att[...]
     blocks, _, rows = att.shape
-    part = rows // parts
+    part, width = rows // parts, weight.shape[1]
     value = jnp.concatenate([att[j].astype(f32) for j in range(blocks)], axis=0).T
     high, low = split_low(jnp.mean(value, axis=1, keepdims=True))
     centred = value - (high.astype(f32) + low.astype(f32))
     square = split_low(jnp.sum(centred * centred, axis=1, keepdims=True))
-    total = dot((centred * gain[...]).astype(bf16), weight[...])
-    store_pieces(total, own, pieces, part, lanes_of([high, low, *square], rows))
-
-
-def middle_kernel(parts, head_width, ids, own, *refs):
-    got, refs = refs[: parts - 1], refs[parts - 1 :]
-    gain_rows, refs = refs[:parts], refs[parts:]
-    x, gain, x1, u = refs
+    gains = gain[...]
+    row = lax.broadcasted_iota(jnp.int32, (16, gains.shape[1]), 0)
+    gain_high, gain_low = (t.astype(f32) for t in split_low(gains))
+    gain_rows = jnp.where(row == 0, gain_high, jnp.where(row == 1, gain_low, 0.0))
+    left = jnp.concatenate([(centred * gains).astype(bf16), gain_rows.astype(bf16)], axis=0)
+    total = dot(left, weight[...])
+    folded = fold_row(total[rows : rows + 1] + total[rows + 1 : rows + 2], part)
+    stats = lanes_of([high, low, *square], rows).astype(bf16)
+    own[:, :width] = total[:part]
+    own[:, width : width + 128] = stats[:part].astype(f32)
+    own[:, width + 128 :] = folded.astype(f32)
+    for k, piece in enumerate(pieces, 1):
+        here = slice(k * part, (k + 1) * part)
+        piece[:, :width] = total[here].astype(bf16)
+        piece[:, width : width + 128] = stats[here]
+        piece[:, width + 128 :] = folded
+
+
+def middle_kernel(parts, head_width, own, *refs):
+    got, (x, gain, x1, u, gain_row) = refs[: parts - 1], refs[parts - 1 :]
     part, width = x1.shape
     blocks = [own] + list(got)
-    means = [pair_sum(b[:, width:], 0) for b in blocks]
-    squares = [pair_sum(b[:, width:], 2) for b in blocks]
+    stats = [b[:, width : width + 128] for b in blocks]
+    means = [pair_sum(b, 0) for b in stats]
+    squares = [pair_sum(b, 2) for b in stats]
+    rows = [unfold_row(b[:, width + 128 :]) for b in blocks]
+    gain_row[...] = sum(rows)
     mean = sum(means) / parts
     spread = sum(squares) + head_width * sum((m - mean) * (m - mean) for m in means)
     scaling = lax.rsqrt(spread / width + eps)
     total = sum(b[:, :width].astype(f32) for b in blocks)
-    for m, row in zip(means, gain_rows):
-        total = total + (m - mean) * row[...]
-    value = x[block_at(ids[0], 0, part), :].astype(f32) + total * scaling
+    for m, row in zip(means, rows):
+        total = total + (m - mean) * row
+    value = x[...].astype(f32) + total * scaling
     x1[...] = value
     normed, _ = norm_rows(value)
     u[:, :width] = (normed * gain[...]).astype(bf16)
     u[:, width:] = lanes_of([*split_low(mean), *split_low(scaling)], part).astype(bf16)
 
 
-def grad_hidden_kernel(parts, ids, gy, weight, heads_gain, out_weight, grad, gain_row, ordered):
-    rows = gy.shape[0]
-    part = rows // parts
-
-    @pl.when(pl.program_id(0) == 0)
-    def _():
-        for k in range(parts):
-            ordered[k * part : (k + 1) * part, :] = gy[block_at(ids[0], k, part), :]
-        high, low = split_low(heads_gain[...])
-        row = lax.broadcasted_iota(jnp.int32, (16, heads_gain.shape[1]), 0)
-        both = jnp.where(row == 0, high.astype(f32), jnp.where(row == 1, low.astype(f32), 0.0))
-        product = dot(both.astype(bf16), out_weight[...])
-        gain_row[...] = product[0:1] + product[1:2]
-
-    grad[...] = dot_t(ordered[...], weight[...])
-
-
-def up_kernel(parts, own, *refs):
+def grad_hidden_kernel(gy, weight, grad):
+    grad[...] = dot_t(gy[...], weight[...])
+
+
+def flip_kernel(weight, out):
+    out[...] = weight[...].T
+
+
+def up_kernel(parts, step, own, *refs):
     got, refs = refs[: parts - 1], refs[parts - 1 :]
-    weight, grad, gain, act, slope, u, stats, rows_u, sums = refs
-    step = pl.program_id(0)
+    weight, grad, gain, act, slope, u, stats, tail, rows_u = refs
     part = own.shape[0]
     rows, width = rows_u.shape
-
-    @pl.when(step == 0)
-    def _():
-        for k, block in enumerate([own] + list(got)):
-            rows_u[k * part : (k + 1) * part, :] = block[:, :width]
-        wide = u.shape[2]
-        for j in range(u.shape[0]):
-            u[j] = rows_u[:, j * wide : (j + 1) * wide]
-        sums[...] = jnp.zeros_like(sums)
-
-    hidden = dot(rows_u[...], weight[...])
-    cdf = 0.5 * (1.0 + lax.erf(hidden * (0.5**0.5)))
-    value = hidden * cdf
-    act[...] = value
-    slope[...] = cdf + hidden * jnp.exp(-0.5 * hidden * hidden) * 0.3989422804014327
-    grad_normed = grad[...] * gain[...]
-    columns = [value, value * value, grad_normed, grad_normed * value]
-    sums[...] += lanes_of([jnp.sum(c, axis=1, keepdims=True) for c in columns], rows)
-
-    @pl.when(step == pl.num_programs(0) - 1)
-    def _():
-        stats[...] = sums[...].T[:8, :]
+    for k, block in enumerate([own] + list(got)):
+        rows_u[k * part : (k + 1) * part, :] = block[:, :width]
+        tail[k * part : (k + 1) * part, :] = block[:, width:].astype(f32)
+    wide = u.shape[2]
+    for j in range(u.shape[0]):
+        u[j] = rows_u[:, j * wide : (j + 1) * wide]
+    total = [jnp.zeros((rows, 128), f32)] * 4
+    for i in range(0, weight.shape[1], step):
+        here = slice(i, i + step)
+        hidden = dot(rows_u[...], weight[:, here])
+        cdf = 0.5 * (1.0 + lax.erf(hidden * (0.5**0.5)))
+        value = hidden * cdf
+        act[:, here] = value
+        slope[:, here] = cdf + hidden * jnp.exp(-0.5 * hidden * hidden) * 0.3989422804014327
+        grad_normed = grad[:, here] * gain[:, here]
+        columns = [value, value * value, grad_normed, grad_normed * value]
+        for n, column in enumerate(columns):
+            for j in range(0, step, 128):
+                total[n] = total[n] + column[:, j : j + 128]
+    sums = lanes_of([jnp.sum(t, axis=1, keepdims=True) for t in total], rows)
+    stats[...] = sums.T[:8, :]
 
 
 def swap_lane_blocks(value, k, part):
@@ -611,90 +738,80 @@
     return value
 
 
-def hidden_back_kernel(parts, full, own, *refs):
+def hidden_back_kernel(parts, full, step, own, *refs):
     got, refs = refs[: parts - 1], refs[parts - 1 :]
-    act, slope, grad, gain, weight, gh, z2, gain_sum, own_out = refs[:9]
-    pieces, (acc, cols) = refs[9 : 9 + parts - 1], refs[9 + parts - 1 :]
-    step = pl.program_id(0)
+    act, slope, grad, gain, weight, gh, z2, own_out = refs[:8]
+    pieces = refs[8:]
     rows = act.shape[0]
     part = rows // parts
-
-    @pl.when(step == 0)
-    def _():
-        total = own[...]
-        for k, block in enumerate(got, 1):
-            total = total + swap_lane_blocks(block[...], k, part)
-        mean = total[0:1] / full
-        scaling = lax.rsqrt(total[1:2] / full - mean * mean + eps)
-        first = total[2:3] / full
-        cross = scaling * (total[3:4] / full - mean * first)
-        row = lax.broadcasted_iota(jnp.int32, (rows, rows), 0)
-        table = jnp.zeros((rows, rows), f32)
-        for i, value in enumerate([mean, scaling, first, cross]):
-            table = jnp.where(row == i, value, table)
-        cols[...] = table.T
-        acc[...] = jnp.zeros_like(acc)
-
+    total = own[...]
+    for k, block in enumerate(got, 1):
+        total = total + swap_lane_blocks(block[...], k, part)
+    mean = total[0:1] / full
+    scaling = lax.rsqrt(total[1:2] / full - mean * mean + eps)
+    first = total[2:3] / full
+    cross = scaling * (total[3:4] / full - mean * first)
+    row = lax.broadcasted_iota(jnp.int32, (rows, rows), 0)
+    table = jnp.zeros((rows, rows), f32)
+    for i, value in enumerate([mean, scaling, first, cross]):
+        table = jnp.where(row == i, value, table)
+    cols = table.T
     mean, scaling, first, cross = (cols[:, i : i + 1] for i in range(4))
-    normed = (act[...] - mean) * scaling
-    low = (normed * gain[...]).astype(bf16)
     wide = z2.shape[2]
-    for j in range(z2.shape[0]):
-        z2[j] = low[:, j * wide : (j + 1) * wide]
-    gain_sum[...] = jnp.sum(grad[...] * normed, axis=0, keepdims=True)
-    value = (scaling * (grad[...] * gain[...] - first - normed * cross) * slope[...]).astype(bf16)
-    gh[...] = value
-    acc[...] += dot_t(value, weight[...])
-
-    @pl.when(step == pl.num_programs(0) - 1)
-    def _():
-        store_pieces(acc[...], own_out, pieces, part)
-
-
-def down_kernel(parts, z2, weight, own_out, *refs):
-    pieces, (acc,) = refs[: parts - 1], refs[parts - 1 :]
-    step = pl.program_id(0)
-
-    @pl.when(step == 0)
-    def _():
-        acc[...] = jnp.zeros_like(acc)
-
+    for i in range(0, act.shape[1], step):
+        here = slice(i, i + step)
+        normed = (act[:, here] - mean) * scaling
+        low = (normed * gain[:, here]).astype(bf16)
+        for j in range(0, step, wide):
+            z2[(i + j) // wide] = low[:, j : j + wide]
+        value = scaling * (grad[:, here] * gain[:, here] - first - normed * cross) * slope[:, here]
+        gh[:, here] = value.astype(bf16)
+    width = weight.shape[1]
+    for i in range(0, width, step):
+        here = slice(i, i + step)
+        result = dot(gh[...], weight[:, here])
+        own_out[:, here] = result[:part]
+        for k, piece in enumerate(pieces, 1):
+            piece[:, here] = result[k * part : (k + 1) * part].astype(bf16)
+
+
+def down_kernel(parts, step, z2, gh, weight, own_out, *refs):
+    pieces, gh_out = refs[: parts - 1], refs[parts - 1]
+    gh_out[...] = gh[...]
     wide = z2.shape[2]
-    for j in range(z2.shape[0]):
-        acc[...] += dot(z2[j], weight[j * wide : (j + 1) * wide, :])
-
-    @pl.when(step == pl.num_programs(0) - 1)
-    def _():
-        store_pieces(acc[...], own_out, pieces, acc.shape[0] // parts)
-
-
-def middle_back_kernel(parts, ids, own, *refs):
+    part = own_out.shape[0]
+    for i in range(0, weight.shape[1], step):
+        here = slice(i, i + step)
+        result = sum(
+            dot(z2[j], weight[j * wide : (j + 1) * wide, here]) for j in range(z2.shape[0])
+        )
+        own_out[:, here] = result[:part]
+        for k, piece in enumerate(pieces, 1):
+            piece[:, here] = result[k * part : (k + 1) * part].astype(bf16)
+
+
+def middle_back_kernel(parts, own, *refs):
     got, refs = refs[: parts - 1], refs[parts - 1 :]
-    gain_rows, refs = refs[:parts], refs[parts:]
-    x, x1, gy, gain, gx1, gb, gain_sum = refs
+    gain_row, x, x1, gy, gain, gx1, gb = refs
     part, width = x1.shape
-    here = block_at(ids[0], 0, part)
     grad = own[...]
     for block in got:
         grad = grad + block[...].astype(f32)
     value = x1[...]
     normed, scaling = norm_rows(value)
-    result = gy[here, :].astype(f32) + norm_back(grad, gain[...], normed, scaling)
+    result = gy[...].astype(f32) + norm_back(grad, gain[...], normed, scaling)
     gx1[...] = result
-    gain_sum[...] = jnp.sum(grad * normed, axis=0, keepdims=True)
     low = result.astype(bf16)
     gb[:, :width] = low
     low = low.astype(f32)
-    gain_row = sum(row[...] for row in gain_rows)
-    first = jnp.sum(low * gain_row, axis=1, keepdims=True) / width
-    cross = jnp.sum(low * (value - x[here, :].astype(f32)), axis=1, keepdims=True) / width
+    first = jnp.sum(low * gain_row[...], axis=1, keepdims=True) / width
+    cross = jnp.sum(low * (value - x[...].astype(f32)), axis=1, keepdims=True) / width
     gb[:, width:] = lanes_of([*split_low(first), *split_low(cross)], part).astype(bf16)
 
 
 def heads_back_kernel(parts, own, *refs):
     got, refs = refs[: parts - 1], refs[parts - 1 :]
-    stats, refs = refs[:parts], refs[parts:]
-    att, gain, weight, sent, gb, gain_sum = refs
+    stats, att, gain, weight, sent, gb = refs
     blocks, _, rows = att.shape
     part, width = own.shape[0], gb.shape[1]
     for k, block in enumerate([own] + list(got)):
@@ -702,19 +819,22 @@
     columns = jnp.concatenate([b[:, width:].astype(f32) for b in [own] + list(got)], axis=0).T
     first = columns[0:1] + columns[1:2]
     cross = columns[2:3] + columns[3:4]
-    columns = jnp.concatenate([b[:, width:].astype(f32) for b in stats], axis=0).T
+    columns = stats[...].T
     mean = columns[0:1] + columns[1:2]
     scaling = columns[2:3] + columns[3:4]
     grad = dot_t(weight[...], gb[...])
     value = jnp.concatenate([att[j].astype(f32) for j in range(blocks)], axis=0)
     normed = (value - mean) * scaling
     gain_col = jnp.broadcast_to(gain[...], (8, gain.shape[1])).T[:, 0:1]
-    gain_sum[...] = jnp.sum((grad * normed).T, axis=0, keepdims=True)
     go = (scaling * (grad * gain_col - first - normed * cross)).astype(bf16)
     z = (normed * gain_col).astype(bf16)
     for j in range(blocks):
         sent[j, :HD, :] = go[j * HD : (j + 1) * HD]
         sent[j, HD:, :] = z[j * HD : (j + 1) * HD]
+
+
+def hand_on_kernel(value, out):
+    out[...] = value[...]
 
 
 def turn_back(grad, table, base, j, inverse):
@@ -768,33 +888,29 @@
         out[j, 2 * HD :, :] = gv[:, span].astype(bf16)
 
 
-def input_back_kernel(parts, got, weight, own_out, *refs):
-    pieces, (acc,) = refs[: parts - 1], refs[parts - 1 :]
-    step = pl.program_id(0)
-
-    @pl.when(step == 0)
-    def _():
-        acc[...] = jnp.zeros_like(acc)
-
-    here = pl.ds(pl.multiple_of(step * HD, HD), HD)
-    grad = jnp.concatenate([got[j, here, :].astype(f32) for j in range(got.shape[0])], axis=0).T
-    acc[...] += dot_t(grad.astype(bf16), weight[0])
-
-    @pl.when(step == pl.num_programs(0) - 1)
-    def _():
-        store_pieces(acc[...], own_out, pieces, acc.shape[0] // parts)
-
-
-def final_kernel(parts, ids, own, *refs):
+def input_back_kernel(parts, step, got, weight, own_out, *pieces):
+    part, width = own_out.shape
+    grads = []
+    for c in range(3):
+        here = slice(c * HD, (c + 1) * HD)
+        grad = jnp.concatenate([got[j, here, :].astype(f32) for j in range(got.shape[0])], axis=0)
+        grads.append(grad.T.astype(bf16))
+    for i in range(0, width, step):
+        here = slice(i, i + step)
+        result = sum(dot_t(grads[c], weight[c, here, :]) for c in range(3))
+        own_out[:, here] = result[:part]
+        for k, piece in enumerate(pieces, 1):
+            piece[:, here] = result[k * part : (k + 1) * part].astype(bf16)
+
+
+def final_kernel(parts, own, *refs):
     got, refs = refs[: parts - 1], refs[parts - 1 :]
-    x, gx1, gain, out, gain_sum = refs
-    part = gx1.shape[0]
+    x, gx1, gain, out = refs
     grad = own[...]
     for block in got:
         grad = grad + block[...].astype(f32)
-    normed, scaling = norm_rows(x[block_at(ids[0], 0, part), :].astype(f32))
+    normed, scaling = norm_rows(x[...].astype(f32))
     out[...] = (gx1[...] + norm_back(grad, gain[...], normed, scaling)).astype(bf16)
-    gain_sum[...] = jnp.sum(grad * normed, axis=0, keepdims=True)
 
 
 def output_kernel(own, *refs):
@@ -812,25 +928,49 @@
         out[block_at(ids[0], k, part), :] = block[...]
 
 
-def columns_grad_kernel(parts, reorder, ids, left, right, out, acc_left):
-    @pl.when(pl.program_id(0) == 0)
+def own_row(table, index):
+    row = lax.broadcasted_iota(jnp.int32, table.shape, 0)
+    return jnp.sum(jnp.where(row == index, table[...], 0.0), axis=0, keepdims=True)
+
+
+def row_of(column, columns):
+    return jnp.broadcast_to(column, (columns, 128)).T[:1, :]
+
+
+def columns_grad_kernel(ids, left, right, weight, gain, out, gain_grad, left_all, sums):
+    step = pl.program_id(0)
+
+    @pl.when(step == 0)
     def _():
-        blocks, rows, _ = left.shape
-        part = rows // parts
-        for j in range(blocks):
-            for k in range(parts):
-                if reorder:
-                    to = pl.ds(pl.multiple_of(j * rows + (ids[0] ^ k) * part, part), part)
-                else:
-                    to = slice(j * rows + k * part, j * rows + (k + 1) * part)
-                acc_left[to, :] = left[j, k * part : (k + 1) * part, :]
-
-    out[...] = t_dot(acc_left[...], right[...])
-
-
-def rows_grad_kernel(first, left, right, out):
+        rows = left.shape[1]
+        for j in range(left.shape[0]):
+            left_all[j * rows : (j + 1) * rows, :] = left[j]
+        sums[...] = jnp.zeros_like(sums)
+
+    grad = t_dot(left_all[...], right[...])
+    out[...] = grad
+    sums[...] += jnp.sum(grad * weight[...].astype(f32), axis=1, keepdims=True)
+
+    @pl.when(step == pl.num_programs(0) - 1)
+    def _():
+        gain_grad[...] = row_of(sums[...], sums.shape[0]) / own_row(gain, ids[1])
+
+
+def rows_grad_kernel(first, ids, left, right, weight, gain, out, gain_grad, sums):
+    step = pl.program_id(0)
+
+    @pl.when(step == 0)
+    def _():
+        sums[...] = jnp.zeros_like(sums)
+
     value = jnp.concatenate([left[j, first:, :] for j in range(left.shape[0])], axis=1)
-    out[...] = dot(value, right[...])
+    grad = dot(value, right[...])
+    out[...] = grad
+    sums[...] += jnp.sum(grad * weight[...].astype(f32), axis=1, keepdims=True)
+
+    @pl.when(step == pl.num_programs(0) - 1)
+    def _():
+        gain_grad[...] = row_of(sums[...], sums.shape[0]) / own_row(gain, ids[1])
 
 
 def grad_qkv_kernel(left, right, out):
@@ -838,12 +978,24 @@
     out[0] = dot(value, right[...]).astype(bf16)
 
 
-def grad_qkv_place_kernel(got, out):
+def grad_qkv_place_kernel(ids, got, weight, gain, up_gain, out, gain_grads):
+    total = 0.0
     for c in range(3):
         value = jnp.concatenate(
             [got[j, c * HD : (c + 1) * HD, :].astype(f32) for j in range(got.shape[0])], axis=0
-        )
-        out[c] = value.T
+        ).T
+        out[c] = value
+        total = total + jnp.sum(value * weight[c].astype(f32), axis=1, keepdims=True)
+    first = row_of(total, total.shape[0]) / own_row(gain, ids[1])
+    row = lax.broadcasted_iota(jnp.int32, gain_grads.shape, 0)
+    gain_grads[...] = jnp.where(row == 0, first, up_gain[...])
+
+
+def gain_sum_kernel(*refs):
+    blocks, (first, second) = refs[:-2], refs[-2:]
+    total = sum(b[...] for b in blocks)
+    first[...] = total[0:1]
+    second[...] = total[1:2]
 
 
 def body(
@@ -863,7 +1015,7 @@
     T, C = lax.axis_size("tp"), lax.axis_size("cp")
     part = rows // T
     head_width = qkv_weight.shape[2]
-    if head_width // HD != C or row_count != 1 or rows != 128 or part % 16 != 0:
+    if head_width // HD != C or row_count != 1 or rows != 128 or 64 * part != width:
         return body_general(
             layer_input, segment_ids, qkv_weight, out_weight, up_weight, down_weight,
             input_gain, heads_gain, middle_gain, hidden_gain, cotangent,
@@ -885,6 +1037,7 @@
     base_t[:, :, :C] = np.transpose(base, (0, 2, 1))
     base_t = jnp.asarray(base_t)
     wide_part = width + 128
+    step = 512
 
     def piece_shapes(columns):
         return [shape((part, columns), f32)] + [shape((part, columns), bf16)] * (T - 1)
@@ -898,166 +1051,176 @@
     def to_cp(value):
         return lax.all_to_all(value, "cp", 0, 0, tiled=True)
 
-    gy_all = cp_gather(gy)
-    a, sent = call(
+    def entire(value):
+        return (value, value.shape, None)
+
+    def own_rows(value):
+        return (value, (part, width), lambda ids: (block_at(ids[0], 0, part), slice(None)))
+
+    cols, first_rows = lambda i, *_: (0, i), lambda i, *_: (i, 0)
+    origin2, origin3 = lambda i, *_: (0, 0), lambda i, *_: (0, 0, 0)
+
+    a, gy_x, sent = call(
         functools.partial(project_kernel, T),
-        [shape((rows, width), bf16), shape((C, 3 * HD + 16, rows), bf16)],
-        [ids, x, segment_ids.reshape(1, rows), gain_in, weight3, inner2, base2],
-        [scalars(), fixed((rows, width)), fixed((1, rows)), fixed((1, width)),
+        [Pin(shape((rows, width), bf16)), Pin(shape((rows, width), bf16)), Pin(shape((C, 3 * HD + 16, rows), bf16))],
+        [ids, Pin(x), Pin(gy), Pin(segment_ids.reshape(1, rows)), Pin(gain_in), Pin(weight3), Pin(inner2), Pin(base2)],
+        [scalars(), fixed((rows, width)), fixed((rows, width)), fixed((1, rows)), fixed((1, width)),
          pl.BlockSpec((1, width, head_width), lambda i: (i, 0, 0)), fixed((4, rows, 128)), fixed((4, C, 128))],
-        [fixed((rows, width)), fixed((C, 3 * HD + 16, rows))],
-        grid=(3,), scratch=[pltpu.VMEM((4, rows, 128), f32)],
-        flops=2 * rows * width * 3 * head_width,
-    )
-    a_all = cp_gather(a)
+        [fixed((rows, width)), fixed((rows, width)), fixed((C, 3 * HD + 16, rows))],
+        grid=(3,), scratch=[pltpu.VMEM((4, rows, 128), f32)], mb=14,
+    )
     got = to_cp(sent)
-    step = 512
-    grad_hid, gain_row = call(
-        functools.partial(grad_hidden_kernel, T),
-        [shape((rows, hidden), f32), shape((1, width), f32)],
-        [ids, gy, down_weight, gain_heads, out_weight],
-        [scalars(), fixed((rows, width)), pl.BlockSpec((step, width), lambda i: (i, 0)),
-         fixed((1, head_width)), fixed((head_width, width))],
-        [pl.BlockSpec((rows, step), lambda i: (0, i)), fixed((1, width))],
-        grid=(hidden // step,), scratch=[pltpu.VMEM((rows, width), bf16)],
-        flops=2 * rows * width * hidden, after=[sent],
-    )
-    gain_rows = [gain_row] + spread(gain_row)
-    back, mixed, lse = call(
+    near_up, near_out, near_x, near_gy, near_mid, near_heads, near_hid, near_in = bring(
+        [entire(up_weight), entire(out_weight), own_rows(x), own_rows(gy), entire(gain_mid), entire(gain_heads),
+         entire(gain_hid), entire(gain_in)],
+        ids, after=[Pin(sent)],
+    )
+    back, mixed, lse, near_got, gy_x = call(
         functools.partial(attend_kernel, T),
-        [shape((C, HD, rows), bf16), shape((HD, tokens), f32), shape((1, tokens), f32)],
+        [Far(shape((C, HD, rows), bf16)), Near(shape((HD, tokens), f32)), Near(shape((1, tokens), f32)),
+         Near(shape((C, 3 * HD + 16, rows), bf16))],
         [ids, got], [scalars(), whole()],
         scratch=[pltpu.VMEM((tokens, HD), bf16), pltpu.VMEM((tokens, 16), f32)],
-        flops=4 * tokens * tokens * HD,
+        mb=10, after=[near_heads], carry=[gy_x],
     )
     att = to_cp(back)
-
-    own, *pieces = call(
-        functools.partial(out_kernel, T), piece_shapes(wide_part), [att, gain_heads, out_weight],
-        flops=2 * rows * width * head_width,
-    )
-    x1, u_own = call(
+    gy_all = cp_gather(gy_x)
+
+    own, *pieces, near_att, a = call(
+        functools.partial(out_kernel, T),
+        piece_shapes(width + 256) + [Near(shape((C, HD, rows), bf16))],
+        [att, near_heads, near_out], carry=[a],
+    )
+    a_all = cp_gather(a)
+    grad_hid, near_token = call(
+        lambda gy_ref, weight, grad, token: (
+            grad_hidden_kernel(gy_ref, weight, grad), hand_on_kernel(jnp.zeros((8, 128), f32), token)),
+        [Near(shape((rows, hidden), f32)), shape((8, 128), f32)],
+        [Pin(gy_x), Pin(down_weight)],
+        [fixed((rows, width)), pl.BlockSpec((step, width), first_rows)],
+        [pl.BlockSpec((rows, step), cols), fixed((8, 128))],
+        grid=(hidden // step,), after=[own], mb=10,
+    )
+    x1, u_own, gain_row = call(
         functools.partial(middle_kernel, T, head_width),
-        [shape((part, width), f32), shape((part, wide_part), bf16)],
-        [ids, own, *exchange(pieces), *gain_rows, x, gain_mid],
-        [scalars()] + [whole()] * (2 * T + 2),
+        [Near(shape((part, width), f32)), shape((part, wide_part), bf16), Near(shape((1, width), f32))],
+        [own, *exchange(pieces), near_x, near_mid], after=[near_token],
     )
     u_blocks = [u_own] + spread(u_own)
-
-    act, slope, u_cols, stats = call(
-        functools.partial(up_kernel, T),
-        [shape((rows, hidden), f32), shape((rows, hidden), f32), shape((C, rows, wide), bf16), shape((8, rows), f32)],
-        [*u_blocks, up_weight, grad_hid, gain_hid],
-        [fixed((part, wide_part))] * T
-        + [pl.BlockSpec((width, step), lambda i: (0, i)), pl.BlockSpec((rows, step), lambda i: (0, i)),
-           pl.BlockSpec((1, step), lambda i: (0, i))],
-        [pl.BlockSpec((rows, step), lambda i: (0, i)), pl.BlockSpec((rows, step), lambda i: (0, i)),
-         fixed((C, rows, wide)), fixed((8, rows))],
-        grid=(hidden // step,), scratch=[pltpu.VMEM((rows, width), bf16), pltpu.VMEM((rows, 128), f32)],
-        flops=2 * rows * width * hidden,
-    )
-    gh, z2, hidden_gain_sum, own, *pieces = call(
-        functools.partial(hidden_back_kernel, T, FF),
-        [shape((rows, hidden), bf16), shape((C, rows, high), bf16), shape((1, hidden), f32)] + piece_shapes(width),
-        [stats, *spread(stats), act, slope, grad_hid, gain_hid, up_weight],
-        [fixed((8, rows))] * T
-        + [pl.BlockSpec((rows, step), lambda i: (0, i))] * 3
-        + [pl.BlockSpec((1, step), lambda i: (0, i)), pl.BlockSpec((width, step), lambda i: (0, i))],
-        [pl.BlockSpec((rows, step), lambda i: (0, i)),
-         pl.BlockSpec((step // high, rows, high), lambda i: (i, 0, 0)),
-         pl.BlockSpec((1, step), lambda i: (0, i))] + [fixed((part, width))] * T,
-        grid=(hidden // step,), scratch=[pltpu.VMEM((rows, width), f32), pltpu.VMEM((rows, rows), f32)],
-        flops=2 * rows * width * hidden,
-    )
-    gh_all = cp_gather(gh)
+    (near_down,) = bring([entire(down_weight)], ids, after=[u_own])
+    (near_flip,) = call(flip_kernel, [Near(shape((hidden, width), bf16))], [near_up], after=[u_own], mb=16)
+
+    act, slope, u_cols, stats, near_tail = call(
+        functools.partial(up_kernel, T, step),
+        [Near(shape((rows, hidden), f32)), Near(shape((rows, hidden), f32)), Near(shape((C, rows, wide), bf16)),
+         shape((8, rows), f32), Near(shape((rows, 128), f32))],
+        [*u_blocks, near_up, grad_hid, near_hid],
+        scratch=[pltpu.VMEM((rows, width), bf16)], mb=8, after=[near_flip, near_down],
+    )
+    gh, z2, own, *pieces = call(
+        functools.partial(hidden_back_kernel, T, FF, step),
+        [Near(shape((rows, hidden), bf16)), Near(shape((C, rows, high), bf16))] + piece_shapes(width),
+        [stats, *spread(stats), act, slope, grad_hid, near_hid, near_flip], mb=8,
+    )
     gu_got = exchange(pieces)
-    y_own, *y_pieces = call(
-        functools.partial(down_kernel, T), piece_shapes(width), [z2, down_weight],
-        [pl.BlockSpec((step // high, rows, high), lambda i: (i, 0, 0)), pl.BlockSpec((step, width), lambda i: (i, 0))],
-        [fixed((part, width))] * T,
-        grid=(hidden // step,), scratch=[pltpu.VMEM((rows, width), f32)],
-        flops=2 * rows * width * hidden, after=[own],
-    )
-    gx1, gb_own, middle_gain_sum = call(
+    (z2_sent,) = call(hand_on_kernel, [Far(shape(z2.shape, bf16))], [z2], after=[own])
+    z2_got = to_cp(z2_sent)
+    y_own, *y_pieces, gh_out, u_sent = call(
+        lambda z2_ref, gh_ref, w_ref, u_ref, *outs: (
+            down_kernel(T, step, z2_ref, gh_ref, w_ref, *outs[:-1]), hand_on_kernel(u_ref, outs[-1])),
+        [Near(t) for t in piece_shapes(width)] + [Far(shape((rows, hidden), bf16)), Far(shape(u_cols.shape, bf16))],
+        [z2, gh, near_down, u_cols], after=[own, Pin(z2_sent)],
+    )
+    gh_all = cp_gather(gh_out)
+    u_got = to_cp(u_sent)
+    gx1, gb_own = call(
         functools.partial(middle_back_kernel, T),
-        [shape((part, width), f32), shape((part, wide_part), bf16), shape((1, width), f32)],
-        [ids, own, *gu_got, *gain_rows, x, x1, gy, gain_mid],
-        [scalars()] + [whole()] * (2 * T + 4),
+        [Near(shape((part, width), f32)), shape((part, wide_part), bf16)],
+        [own, *gu_got, gain_row, near_x, x1, near_gy, near_mid], after=[Pin(gh_out)],
     )
     gb_blocks = [gb_own] + spread(gb_own)
 
-    sent, gb, heads_gain_sum = call(
+    def columns_grad(left, right, weight, gain, after):
+        own_columns = left.shape[2]
+        return call(
+            columns_grad_kernel,
+            [Pin(shape((own_columns, right.shape[1]), f32)), shape((1, own_columns), f32)],
+            [ids, Pin(left), Pin(right), Pin(weight), gain.reshape(C, -1)],
+            [scalars(), pl.BlockSpec(left.shape, origin3), pl.BlockSpec((tokens, step), cols),
+             pl.BlockSpec((own_columns, step), lambda i, ids: (ids[1], i)), pl.BlockSpec((C, own_columns), origin2)],
+            [pl.BlockSpec((own_columns, step), cols), pl.BlockSpec((1, own_columns), origin2)],
+            grid=(right.shape[1] // step,),
+            scratch=[pltpu.VMEM((tokens, own_columns), bf16), pltpu.VMEM((own_columns, 1), f32)],
+            after=after, prefetch=1, mb=10,
+        )
+
+    grad_down, hidden_gain_grad = columns_grad(z2_got, gy_all, down_weight, hidden_gain, [gb_own])
+    near_three, near_inner, near_base = bring(
+        [entire(weight3), entire(inner2), entire(base_t)], ids, after=[Pin(grad_down)]
+    )
+    sent, gb, *y_pieces = call(
         functools.partial(heads_back_kernel, T),
-        [shape((C, 2 * HD, rows), bf16), shape((rows, width), bf16), shape((1, head_width), f32)],
-        [*gb_blocks, *u_blocks, att, gain_heads, out_weight],
-        flops=2 * rows * width * head_width,
-    )
-    gb_all = cp_gather(gb)
+        [Far(shape((C, 2 * HD, rows), bf16)), Near(shape((rows, width), bf16))],
+        [*gb_blocks, near_tail, near_att, near_heads, near_out], after=[near_base], carry=y_pieces,
+    )
+    y_got = exchange(y_pieces)
     grads = to_cp(sent)
+    (gb_out,) = call(hand_on_kernel, [Far(shape((rows, width), bf16))], [gb], after=[Pin(sent)])
+    gb_all = cp_gather(gb_out)
     (gq_sent,) = call(
-        functools.partial(attend_back_kernel, T), [shape((C, 3 * HD, rows), bf16)],
-        [ids, got, grads, mixed, lse, inner2, base_t], [scalars()] + [whole()] * 6,
+        functools.partial(attend_back_kernel, T), [Far(shape((C, 3 * HD, rows), bf16))],
+        [ids, near_got, grads, mixed, lse, near_inner, near_base], [scalars()] + [whole()] * 6,
         scratch=[pltpu.VMEM((tokens, HD), bf16), pltpu.VMEM((tokens, HD), bf16), pltpu.VMEM((tokens, 16), f32),
                  pltpu.VMEM((HD, tokens), f32), pltpu.VMEM((HD, tokens), f32)],
-        flops=10 * tokens * tokens * HD,
+        mb=12, after=[Pin(gb_out), y_got[0]],
     )
     gq = to_cp(gq_sent)
-    own, *pieces = call(
-        functools.partial(input_back_kernel, T), piece_shapes(width), [gq, weight3],
-        [fixed((C, 3 * HD, rows)), pl.BlockSpec((1, width, head_width), lambda i: (i, 0, 0))],
-        [fixed((part, width))] * T,
-        grid=(3,), scratch=[pltpu.VMEM((rows, width), f32)],
-        flops=2 * rows * width * 3 * head_width,
-    )
-    grad_in, input_gain_sum = call(
+    (y_low,) = call(output_kernel, [shape((part, width), bf16)], [y_own, *y_got, x1], after=[Pin(gq_sent)])
+    y_blocks = [y_low] + spread(y_low)
+    (grad_qkv,) = call(
+        grad_qkv_kernel, [Pin(shape((C, 3 * HD, wide), bf16))], [Pin(gq_sent), Pin(a_all)],
+        [fixed(gq_sent.shape), pl.BlockSpec((tokens, wide), cols)],
+        [pl.BlockSpec((1, 3 * HD, wide), lambda i: (i, 0, 0))], grid=(C,), after=[y_low],
+    )
+    own, *pieces, grad_qkv = call(
+        functools.partial(input_back_kernel, T, step), piece_shapes(width), [gq, near_three], carry=[grad_qkv],
+    )
+    ga_got = exchange(pieces)
+    grad_qkv_got = to_cp(grad_qkv)
+    grad_up, up_gain = columns_grad(u_got, gh_all, up_weight, middle_gain, [own])
+    (layer_output,) = call(
+        natural_kernel, [Far(shape((rows, width), bf16))], [ids, *y_blocks], [scalars()] + [whole()] * T, after=[own]
+    )
+    (grad_in,) = call(
         functools.partial(final_kernel, T),
-        [shape((part, width), bf16), shape((1, width), f32)],
-        [ids, own, *exchange(pieces), x, gx1, gain_in],
-        [scalars()] + [whole()] * (T + 3),
+        [shape((part, width), bf16)],
+        [own, *ga_got, near_x, gx1, near_in], after=[Pin(layer_output), Pin(grad_up)],
     )
     grad_blocks = [grad_in] + spread(grad_in)
+
+    own_wide = lambda ids: (slice(None), pl.ds(pl.multiple_of(ids[1] * wide, wide), wide), slice(None))
+    grad_out, heads_gain_grad = call(
+        functools.partial(rows_grad_kernel, HD),
+        [Pin(shape((HD, width), f32)), shape((1, HD), f32)],
+        [ids, Pin(grads), Pin(gb_all), Pin(out_weight), heads_gain.reshape(C, -1)],
+        [scalars(), pl.BlockSpec(grads.shape, origin3), pl.BlockSpec((tokens, step), cols),
+         pl.BlockSpec((HD, step), lambda i, ids: (ids[1], i)), pl.BlockSpec((C, HD), origin2)],
+        [pl.BlockSpec((HD, step), cols), pl.BlockSpec((1, HD), origin2)], grid=(width // step,),
+        scratch=[pltpu.VMEM((HD, 1), f32)], after=[grad_in], prefetch=1,
+    )
+    grad_qkv, gains = call(
+        grad_qkv_place_kernel,
+        [Far(shape((3, wide, head_width), f32)), shape((8, wide), f32)],
+        [ids, grad_qkv_got, Far(weight3, (3, wide, head_width), own_wide), input_gain.reshape(C, -1), up_gain],
+        [scalars()] + [whole()] * 4, after=[Pin(grad_out)],
+    )
     (grad_input,) = call(
-        natural_kernel, [shape((rows, width), bf16)], [ids, *grad_blocks], [scalars()] + [whole()] * T
-    )
-
-    (y_low,) = call(output_kernel, [shape((part, width), bf16)], [y_own, *exchange(y_pieces), x1])
-    y_blocks = [y_low] + spread(y_low)
-    (layer_output,) = call(
-        natural_kernel, [shape((rows, width), bf16)], [ids, *y_blocks], [scalars()] + [whole()] * T
-    )
-
-    def columns_grad(left, right, reorder):
-        own_columns = left.shape[2]
-        return call(
-            functools.partial(columns_grad_kernel, T, reorder),
-            [shape((own_columns, right.shape[1]), f32)], [ids, left, right],
-            [scalars(), fixed(left.shape), pl.BlockSpec((tokens, step), lambda i: (0, i))],
-            [pl.BlockSpec((own_columns, step), lambda i: (0, i))],
-            grid=(right.shape[1] // step,), scratch=[pltpu.VMEM((tokens, own_columns), bf16)],
-            flops=2 * tokens * own_columns * right.shape[1],
-        )[0]
-
-    grad_down = columns_grad(to_cp(z2), gy_all, True)
-    grad_up = columns_grad(to_cp(u_cols), gh_all, False)
-    (grad_out,) = call(
-        functools.partial(rows_grad_kernel, HD), [shape((HD, width), f32)], [grads, gb_all],
-        [fixed(grads.shape), pl.BlockSpec((tokens, step), lambda i: (0, i))],
-        [pl.BlockSpec((HD, step), lambda i: (0, i))], grid=(width // step,),
-        flops=2 * tokens * HD * width,
-    )
-    (grad_qkv,) = call(
-        grad_qkv_kernel, [shape((C, 3 * HD, wide), bf16)], [gq_sent, a_all],
-        [fixed(gq_sent.shape), pl.BlockSpec((tokens, wide), lambda i: (0, i))],
-        [pl.BlockSpec((1, 3 * HD, wide), lambda i: (i, 0, 0))], grid=(C,),
-        flops=2 * tokens * 3 * HD * width,
-    )
-    (grad_qkv,) = call(grad_qkv_place_kernel, [shape((3, wide, head_width), f32)], [to_cp(grad_qkv)])
-
-    by_cp = jnp.concatenate([heads_gain_sum.reshape(C, -1), hidden_gain_sum.reshape(C, -1)], axis=1)
-    by_cp = jnp.sum(to_cp(by_cp), axis=0)
-    by_all = jnp.concatenate([input_gain_sum.reshape(C, -1), middle_gain_sum.reshape(C, -1)], axis=1)
-    by_all = jnp.broadcast_to(by_all[None], (T, C, 2 * wide)).reshape(T * C, 2 * wide)
-    by_all = jnp.sum(lax.all_to_all(by_all, ("tp", "cp"), 0, 0, tiled=True), axis=0)
+        natural_kernel, [Far(shape((rows, width), bf16))], [ids, *grad_blocks], [scalars()] + [whole()] * T,
+        after=[Pin(grad_qkv)],
+    )
+    input_gain_grad, middle_gain_grad = call(
+        gain_sum_kernel, [shape((1, wide), f32), shape((1, wide), f32)], [gains, *spread(gains)]
+    )
     return (
         layer_output.reshape(layer_input.shape),
         grad_input.reshape(layer_input.shape),
@@ -1065,10 +1228,10 @@
         grad_out,
         grad_up,
         grad_down,
-        by_all[:wide],
-        by_cp[: head_width // C],
-        by_all[wide:],
-        by_cp[head_width // C :],
+        input_gain_grad.reshape(-1),
+        heads_gain_grad.reshape(-1),
+        middle_gain_grad.reshape(-1),
+        hidden_gain_grad.reshape(-1),
     )
 
 

time: 299 us -> 229 us (0.77)
  local copies, waits for them, and re-layouts: 50 us -> 14.8 us
  blocking collectives: 39.4 us -> 9.68 us
  Pallas kernels: 53 us -> 78.9 us
  waiting for transfers between devices: 64.6 us -> 41.7 us
  other arithmetic: 4.42 us -> 0.08 us
  starting transfers between devices: 71.8 us -> 68.5 us
    ppermute x30, waiting for transfers between devices: 58.1 us -> 24.8 us  [swap_tp(): return lax.ppermute(value, 'tp', pairs(lax.axis_size('tp'), k))]
    unnamed x130 -> x42, local copies, waits for them, and re-layouts: 46.3 us -> 14.7 us
    all_to_all x3 -> x1, blocking collectives: 39.4 us -> 9.68 us  [to_cp(): return lax.all_to_all(value, 'cp', 0, 0, tiled=True)]
    pallas_call x21 -> x28, Pallas kernels: 53 us -> 78.9 us  [call(): pl.pallas_call(run, out_shape=tuple((result(t) for t in outs)) + tuple((r...]
    all_to_all x5 -> x6, starting transfers between devices: 17.5 us -> 23.8 us  [to_cp(): return lax.all_to_all(value, 'cp', 0, 0, tiled=True)]
    all_to_all x5 -> x6, waiting for transfers between devices: 4.86 us -> 11 us  [to_cp(): return lax.all_to_all(value, 'cp', 0, 0, tiled=True)]
    all_gather x4, waiting for transfers between devices: 0.03 us -> 5.8 us  [cp_gather(): return lax.all_gather(value, 'cp', axis=0, tiled=True)]
    all_to_all x1 -> x0, starting transfers between devices: 5.76 us -> none  [body(): lax.all_to_all(by_all, ('tp', 'cp'), 0, 0, tiled=True)]
  transfers between devices with their start and end apart: 40 -> 40, of which waited for: 19 -> 12; matrix products, arithmetic and copies ran while one was open for 2% -> 0% of each run, Pallas kernels for 16% -> 30%
where the time goes in v1:
time: 229 us; the launch traced here: 228 us
  Pallas kernels  78.9 us (34%)
  starting transfers between devices  68.5 us (30%)
  waiting for transfers between devices  41.7 us (18%)
  local copies, waits for them, and re-layouts  14.8 us (6%)
  between operations  14.2 us (6%)
  blocking collectives  9.68 us (4%)
    pallas_call x28, Pallas kernels, call(): pl.pallas_call(run, out_shape=tuple((result(t) for t in outs)) + tuple((r...  78.9 us
    ppermute x30, starting transfers between devices, swap_tp(): return lax.ppermute(value, 'tp', pairs(lax.axis_size('tp'), k))  44.4 us
    ppermute x30, waiting for transfers between devices, swap_tp(): return lax.ppermute(value, 'tp', pairs(lax.axis_size('tp'), k))  24.8 us
    all_to_all x6, starting transfers between devices, to_cp(): return lax.all_to_all(value, 'cp', 0, 0, tiled=True)  23.8 us
    unnamed x42, local copies, waits for them, and re-layouts  14.7 us
    all_to_all x6, waiting for transfers between devices, to_cp(): return lax.all_to_all(value, 'cp', 0, 0, tiled=True)  11 us
    all_to_all x1, blocking collectives, to_cp(): return lax.all_to_all(value, 'cp', 0, 0, tiled=True)  9.68 us
    all_gather x4, waiting for transfers between devices, cp_gather(): return lax.all_gather(value, 'cp', axis=0, tiled=True)  5.8 us
  transfers between devices with their start and end apart: 40, of which 12 were waited for; matrix products, arithmetic and copies ran while one was open for 0% of the time, Pallas kernels for 30%

profile of v1, /device:TPU:0, one launch (start us, length us, event | category | flops | bytes accessed | tf_op | source)
XLA Modules:
  0.0 227.8 jit_solution(12872606658876385052)
XLA Ops:
  7.3 6.4 %shard_map.213 = (bf16[128,2048]{1,0:T(8,128)(2,1)}, bf16[128,2048]{1,0:T(8,128)(2,1)}, bf16[8,208,128]{2,1,0:T(8,128)(2,1)}) custom-call(s32[2]{0:T(128)S(1)} %pad_add_fusion.refs_0_, bf16[128,2048]{1,0:T(8,128)(2,1)} %bitcast.27, bf16[128,2048]{1,0:T(8,128)(2,1)} %bitcast.29, s32[1,128]{1,0:T(1,128)} %bitcast.31, f32[1,2048]{1,0:T(1,128)} %bitcast.21, ...), custom_call_target="tpu_custom_call" | custom-call | flops 5000000000 | tf_op jit(solution)/shard_map/pallas_call | solution.py:446
  13.6 5.2 %all-to-all-start = ((bf16[8,208,128]{2,1,0:T(8,128)(2,1)}), bf16[8,208,128]{2,1,0:T(8,128)(2,1)S(1)}, u32[]{:S(2)}, u32[]{:S(2)}) async-start(bf16[8,208,128]{2,1,0:T(8,128)(2,1)} %get-tuple-element.79.refs_9_), calls=%async_computation | async-start | bytes 851968 | tf_op jit(solution)/shard_map/all_to_all | solution.py:1052
  18.9 4.7 %shard_map.214 = (bf16[2048,2048]{1,0:T(8,128)(2,1)S(1)}, bf16[512,2048]{1,0:T(8,128)(2,1)S(1)}, bf16[32,2048]{1,0:T(8,128)(2,1)S(1)}, bf16[32,2048]{1,0:T(8,128...) custom-call(s32[2]{0:T(128)S(1)} %pad_add_fusion.refs_0_, ...), custom_call_target="tpu_custom_call" | custom-call | flops 5000000000 | tf_op jit(solution)/shard_map/pallas_call | solution.py:446
  23.5 3.3 %copy-done = bf16[2048,2048]{1,0:T(8,128)(2,1)} copy-done((bf16[2048,2048]{1,0:T(8,128)(2,1)}, bf16[2048,2048]{1,0:T(8,128)(2,1)S(1)}, u32[]{:S(2)}) %copy-start) | copy-done | bytes 8388632
  31.6 9.7 %all_to_all.35.refs_0_ = bf16[8,64,128]{2,1,0:T(8,128)(2,1)S(1)} all-to-all(bf16[8,64,128]{2,1,0:T(8,128)(2,1)} %get-tuple-element.82), channel_id=1, replica_groups=mesh['tp'=4,'cp'=8] {'cp'}, dimensions={0} | all-to-all | bytes 262144 | tf_op jit(solution)/shard_map/all_to_all | solution.py:1052
  48.3 6.0 %shard_map.217 = (f32[128,2048]{1,0:T(8,128)S(1)}, f32[8,128]{1,0:T(8,128)S(1)}) custom-call(bf16[128,2048]{1,0:T(8,128)(2,1)} %get-tuple-element.91.refs_0_, bf16[2048,2048]{1,0:T(8,128)(2,1)} %refs_3_.4, f32[32,2304]{1,0:T(8,128)S(1)} %get-tuple-element.85.refs_2_.refs_0_), custom_call_target="tpu_custom_call" | custom-call | flops 5000000000 | tf_op jit(solution)/shard_map/pallas_call | solution.py:446
  54.3 5.1 %collective-permute-done.1.refs_2_ = bf16[32,2304]{1,0:T(8,128)(2,1)S(1)} collective-permute-done((bf16[32,2304]{1,0:T(8,128)(2,1)S(1)}, bf16[32,2304]{1,0:T(8,128)(2,1)S(1)}, u32[]{:S(2)}, u32[]{:S(2)}) %collective-permute-start.1) | collective-permute-done | bytes 147488 | tf_op jit(solution)/shard_map/ppermute | solution.py:39
  64.6 4.0 %shard_map.220.refs_8_.refs_2_ = bf16[2048,2048]{1,0:T(8,128)(2,1)S(1)} custom-call(s32[2]{0:T(128)S(1)} %pad_add_fusion.refs_0_, bf16[2048,2048]{1,0:T(8,128)(2,1)} %refs_3_.4, bf16[32,2176]{1,0:T(8,128)(2,1)S(1)} %get-tuple-element.93.refs_1_.refs_2_.refs_0_), custom_call_target="tpu_custom_call" | custom-call | flops 5000000000 | tf_op jit(solution)/shard_map/pallas_call | solution.py:446
  71.2 3.3 %collective-permute-done.4.refs_2_ = bf16[32,2176]{1,0:T(8,128)(2,1)S(1)} collective-permute-done((bf16[32,2176]{1,0:T(8,128)(2,1)S(1)}, bf16[32,2176]{1,0:T(8,128)(2,1)S(1)}, u32[]{:S(2)}, u32[]{:S(2)}) %collective-permute-start.4) | collective-permute-done | bytes 139296 | tf_op jit(solution)/shard_map/ppermute | solution.py:39
  95.6 3.5 %all-to-all-start.2 = ((bf16[8,128,256]{2,1,0:T(8,128)(2,1)}), bf16[8,128,256]{2,1,0:T(8,128)(2,1)S(1)}, u32[]{:S(2)}, u32[]{:S(2)}) async-start(bf16[8,128,256]{2,1,0:T(8,128)(2,1)} %shard_map.223.refs_5_), calls=%async_computation.2 | async-start | bytes 1048576 | tf_op jit(solution)/shard_map/all_to_all | solution.py:1052
  107.9 6.2 %all-to-all-done.2.refs_1_ = bf16[8,128,256]{2,1,0:T(8,128)(2,1)S(1)} async-done(((bf16[8,128,256]{2,1,0:T(8,128)(2,1)}), bf16[8,128,256]{2,1,0:T(8,128)(2,1)S(1)}, u32[]{:S(2)}, u32[]{:S(2)}) %all-to-all-start.2) | async-done | bytes 524320 | tf_op jit(solution)/shard_map/all_to_all | solution.py:1052
  114.9 6.2 %shard_map.226 = (f32[256,2048]{1,0:T(8,128)}, f32[1,256]{1,0:T(1,128)}) custom-call(s32[2]{0:T(128)S(1)} %pad_add_fusion.refs_0_, bf16[8,128,256]{2,1,0:T(8,128)(2,1)} %copy-done.13, bf16[1024,2048]{1,0:T(8,128)(2,1)} %all-gather.5.cloned.1.call-done.refs_2_, bf16[2048,2048]{1,0:T(8,128)(2,1)} %refs_3_.4, f32[8,256]{1,0:T(8,128)S(1)} %reshape.78.refs_4_, ...), custom_call_target="tpu_custom_call" | custom-call | flops 5000000000 | tf_op jit(solution)/shard_map/pallas_call | solution.py:446
  121.1 3.8 %shard_map.227 = (bf16[3,2048,512]{2,1,0:T(8,128)(2,1)S(1)}, f32[4,128,128]{2,1,0:T(8,128)S(1)}, f32[4,64,128]{2,1,0:T(8,128)S(1)}) custom-call(s32[2]{0:T(128)S(1)} %pad_add_fusion.refs_0_, bf16[3,2048,512]{2,1,0:T(8,128)(2,1)} %bitcast.25, f32[4,128,128]{2,1,0:T(8,128)} %constant.14.clone.refs_6_.refs_2_, f32[4,64,128]{2,1,0:T(8,128)} %constant.16.clone.refs_3_, ...), custom_call_target="tpu_custom_call" | custom-call | flops 5000000000 | tf_op jit(solution)/shard_map/pallas_call | solution.py:446
  130.0 3.6 %all-to-all-start.3 = ((bf16[8,128,128]{2,1,0:T(8,128)(2,1)}), bf16[8,128,128]{2,1,0:T(8,128)(2,1)S(1)}, u32[]{:S(2)}, u32[]{:S(2)}) async-start(bf16[8,128,128]{2,1,0:T(8,128)(2,1)} %get-tuple-element.124.refs_1_), calls=%async_computation.3 | async-start | bytes 524288 | tf_op jit(solution)/shard_map/all_to_all | solution.py:1052
  140.5 3.8 %shard_map.230.refs_5_.refs_0_ = bf16[8,192,128]{2,1,0:T(8,128)(2,1)} custom-call(s32[2]{0:T(128)S(1)} %pad_add_fusion.refs_0_, bf16[8,208,128]{2,1,0:T(8,128)(2,1)S(1)} %get-tuple-element.123.refs_1_, bf16[8,128,128]{2,1,0:T(8,128)(2,1)S(1)} %all-to-all-done.3.refs_2_.refs_1_, f32[64,1024]{1,0:T(8,128)S(1)} %get-tuple-element.125.refs_3_, ...), custom_call_target="tpu_custom_call" | custom-call | flops 5000000000 | tf_op jit(solution)/shard_map/pallas_call | solution.py:446
  144.2 3.9 %all-to-all-start.4 = ((bf16[8,192,128]{2,1,0:T(8,128)(2,1)}), bf16[8,192,128]{2,1,0:T(8,128)(2,1)S(1)}, u32[]{:S(2)}, u32[]{:S(2)}) async-start(bf16[8,192,128]{2,1,0:T(8,128)(2,1)} %shard_map.230.refs_5_.refs_0_), calls=%async_computation.4 | async-start | bytes 786432 | tf_op jit(solution)/shard_map/all_to_all | solution.py:1052
  152.9 6.9 %shard_map.232.refs_2_ = bf16[8,192,256]{2,1,0:T(8,128)(2,1)} custom-call(bf16[8,192,128]{2,1,0:T(8,128)(2,1)} %shard_map.230.refs_5_.refs_0_, bf16[1024,2048]{1,0:T(8,128)(2,1)} %all-gather.7.cloned.1.call-done.refs_1_, bf16[32,2048]{1,0:T(8,128)(2,1)S(1)} %shard_map.231.refs_2_.refs_1_), custom_call_target="tpu_custom_call" | custom-call | flops 5000000000 | tf_op jit(solution)/shard_map/pallas_call | solution.py:446
  159.8 4.0 %all-to-all-start.5 = ((bf16[8,128,256]{2,1,0:T(8,128)(2,1)}), bf16[8,128,256]{2,1,0:T(8,128)(2,1)S(1)}, u32[]{:S(2)}, u32[]{:S(2)}) async-start(bf16[8,128,256]{2,1,0:T(8,128)(2,1)} %get-tuple-element.137), calls=%async_computation.5 | async-start | bytes 1048576 | tf_op jit(solution)/shard_map/all_to_all | solution.py:1052
  171.8 4.8 %all-to-all-done.5.refs_1_ = bf16[8,128,256]{2,1,0:T(8,128)(2,1)S(1)} async-done(((bf16[8,128,256]{2,1,0:T(8,128)(2,1)}), bf16[8,128,256]{2,1,0:T(8,128)(2,1)S(1)}, u32[]{:S(2)}, u32[]{:S(2)}) %all-to-all-start.5) | async-done | bytes 524320 | tf_op jit(solution)/shard_map/all_to_all | solution.py:1052
  176.6 3.5 %all-to-all-start.6 = ((bf16[8,192,256]{2,1,0:T(8,128)(2,1)}), bf16[8,192,256]{2,1,0:T(8,128)(2,1)S(1)}, u32[]{:S(2)}, u32[]{:S(2)}) async-start(bf16[8,192,256]{2,1,0:T(8,128)(2,1)} %get-tuple-element.139), calls=%async_computation.6 | async-start | bytes 1572864 | tf_op jit(solution)/shard_map/all_to_all | solution.py:1052
  180.1 6.2 %shard_map.235 = (f32[256,2048]{1,0:T(8,128)}, f32[1,256]{1,0:T(1,128)S(1)}) custom-call(s32[2]{0:T(128)S(1)} %pad_add_fusion.refs_0_, bf16[8,128,256]{2,1,0:T(8,128)(2,1)} %copy-done.14, bf16[1024,2048]{1,0:T(8,128)(2,1)} %all-gather.9.cloned.1.call-done.refs_2_, bf16[2048,2048]{1,0:T(8,128)(2,1)} %refs_3_.5, f32[8,256]{1,0:T(8,128)S(1)} %reshape.80.refs_4_, ...), custom_call_target="tpu_custom_call" | custom-call | flops 5000000000 | tf_op jit(solution)/shard_map/pallas_call | solution.py:446
  189.3 4.8 %collective-permute-done.23.refs_3_ = bf16[32,2048]{1,0:T(8,128)(2,1)S(1)} collective-permute-done((bf16[32,2048]{1,0:T(8,128)(2,1)S(1)}, bf16[32,2048]{1,0:T(8,128)(2,1)S(1)}, u32[]{:S(2)}, u32[]{:S(2)}) %collective-permute-start.23) | collective-permute-done | bytes 131104 | tf_op jit(solution)/shard_map/ppermute | solution.py:39
  198.9 5.8 %all-gather.11.cloned.1.call-done.refs_2_ = bf16[1024,2048]{1,0:T(8,128)(2,1)} async-done(((bf16[128,2048]{1,0:T(8,128)(2,1)}), bf16[1024,2048]{1,0:T(8,128)(2,1)}) %all-gather.11.cloned.1.call-update) | async-done | bytes 4194320 | tf_op jit(solution)/shard_map/all_gather | solution.py:87
  204.7 5.4 %shard_map.237 = (f32[64,2048]{1,0:T(8,128)}, f32[1,64]{1,0:T(1,128)}) custom-call(s32[2]{0:T(128)S(1)} %pad_add_fusion.refs_0_, bf16[8,128,128]{2,1,0:T(8,128)(2,1)} %copy-done.1, bf16[1024,2048]{1,0:T(8,128)(2,1)} %all-gather.11.cloned.1.call-done.refs_2_, bf16[512,2048]{1,0:T(8,128)(2,1)} %refs_3_.6, f32[8,64]{1,0:T(8,128)S(1)} %reshape.82.refs_4_, ...), custom_call_target="tpu_custom_call" | custom-call | flops 5000000000 | tf_op jit(solution)/shard_map/pallas_call | solution.py:446
  (137 shorter events, 93.5 us)
Async XLA Ops:
  13.6 14.6 %all-to-all-start = ((bf16[8,208,128]{2,1,0:T(8,128)(2,1)}), bf16[8,208,128]{2,1,0:T(8,128)(2,1)S(1)}, u32[]{:S(2)}, u32[]{:S(2)}) async-start(bf16[8,208,128]{2,1,0:T(8,128)(2,1)} %get-tuple-element.79.refs_9_), calls=%async_computation | async-start | bytes 851968 | tf_op jit(solution)/shard_map/all_to_all | solution.py:1052
  18.8 95.3 %all-gather.5.cloned.1.call-start = ((), (), s32[]{:S(2)}) async-start(), calls=%async_computation.7 | async-start | bytes 4718592 | tf_op jit(solution)/shard_map/all_gather | solution.py:87
  31.5 121.4 %all-gather.7.cloned.1.call-start = ((), (), s32[]{:S(2)}) async-start(), calls=%async_computation.8 | async-start | bytes 4718592 | tf_op jit(solution)/shard_map/all_gather | solution.py:87
  43.6 136.5 %all-gather.9.cloned.1.call-start = ((), (), s32[]{:S(2)}) async-start(), calls=%async_computation.9 | async-start | bytes 4718592 | tf_op jit(solution)/shard_map/all_gather | solution.py:87
  45.6 13.9 %collective-permute-start.1 = (bf16[32,2304]{1,0:T(8,128)(2,1)S(1)}, bf16[32,2304]{1,0:T(8,128)(2,1)S(1)}, u32[]{:S(2)}, u32[]{:S(2)}) collective-permute-start(bf16[32,2304]{1,0:T(8,128)(2,1)S(1)} %get-tuple-element.87), channel_id=1, source_target_pairs={{0,16},{8,24},{16,0},{24,8},{1,17},{9,25},{17,1},{25,9},{2,18},{10... | collective-permute-start | bytes 442376 | tf_op jit(solution)/shard_map/ppermute | solution.py:39
  62.2 12.3 %collective-permute-start.4 = (bf16[32,2176]{1,0:T(8,128)(2,1)S(1)}, bf16[32,2176]{1,0:T(8,128)(2,1)S(1)}, u32[]{:S(2)}, u32[]{:S(2)}) collective-permute-start(bf16[32,2176]{1,0:T(8,128)(2,1)S(1)} %get-tuple-element.93.refs_1_.refs_2_.refs_0_), channel_id=1, source_target_pairs={{0,16},{8,24},{16,0},{24,8},{1,17},{9,25},{17,1},{25,9},{2,18},{10... | collective-permute-start | bytes 417800 | tf_op jit(solution)/shard_map/ppermute | solution.py:39
  95.6 18.5 %all-to-all-start.2 = ((bf16[8,128,256]{2,1,0:T(8,128)(2,1)}), bf16[8,128,256]{2,1,0:T(8,128)(2,1)S(1)}, u32[]{:S(2)}, u32[]{:S(2)}) async-start(bf16[8,128,256]{2,1,0:T(8,128)(2,1)} %shard_map.223.refs_5_), calls=%async_computation.2 | async-start | bytes 1048576 | tf_op jit(solution)/shard_map/all_to_all | solution.py:1052
  99.1 105.6 %all-gather.11.cloned.1.call-start = ((), (), s32[]{:S(2)}) async-start(), calls=%async_computation.10 | async-start | bytes 4718592 | tf_op jit(solution)/shard_map/all_gather | solution.py:87
  103.3 24.2 %collective-permute-start.12 = (bf16[32,2176]{1,0:T(8,128)(2,1)S(1)}, bf16[32,2176]{1,0:T(8,128)(2,1)S(1)}, u32[]{:S(2)}, u32[]{:S(2)}) collective-permute-start(bf16[32,2176]{1,0:T(8,128)(2,1)S(1)} %get-tuple-element.112.refs_5_.refs_0_), channel_id=1, source_target_pairs={{0,8},{8,0},{16,24},{24,16},{1,9},{9,1},{17,25},{25,17},{2,10},{10... | collective-permute-start | bytes 417800 | tf_op jit(solution)/shard_map/ppermute | solution.py:39
  105.5 22.1 %collective-permute-start.13 = (bf16[32,2176]{1,0:T(8,128)(2,1)S(1)}, bf16[32,2176]{1,0:T(8,128)(2,1)S(1)}, u32[]{:S(2)}, u32[]{:S(2)}) collective-permute-start(bf16[32,2176]{1,0:T(8,128)(2,1)S(1)} %get-tuple-element.112.refs_5_.refs_0_), channel_id=1, source_target_pairs={{0,16},{8,24},{16,0},{24,8},{1,17},{9,25},{17,1},{25,9},{2,18},{10... | collective-permute-start | bytes 417800 | tf_op jit(solution)/shard_map/ppermute | solution.py:39
  105.6 21.9 %collective-permute-start.14 = (bf16[32,2176]{1,0:T(8,128)(2,1)S(1)}, bf16[32,2176]{1,0:T(8,128)(2,1)S(1)}, u32[]{:S(2)}, u32[]{:S(2)}) collective-permute-start(bf16[32,2176]{1,0:T(8,128)(2,1)S(1)} %get-tuple-element.112.refs_5_.refs_0_), channel_id=1, source_target_pairs={{0,24},{8,16},{16,8},{24,0},{1,25},{9,17},{17,9},{25,1},{2,26},{10... | collective-permute-start | bytes 417800 | tf_op jit(solution)/shard_map/ppermute | solution.py:39
  135.2 13.0 %collective-permute-start.16 = (bf16[32,2048]{1,0:T(8,128)(2,1)S(1)}, bf16[32,2048]{1,0:T(8,128)(2,1)S(1)}, u32[]{:S(2)}, u32[]{:S(2)}) collective-permute-start(bf16[32,2048]{1,0:T(8,128)(2,1)S(1)} %copy-done.5), channel_id=1, source_target_pairs={{0,16},{8,24},{16,0},{24,8},{1,17},{9,25},{17,1},{25,9},{2,18},{10... | collective-permute-start | bytes 393224 | tf_op jit(solution)/shard_map/ppermute | solution.py:39
  136.1 12.1 %collective-permute-start.17 = (bf16[32,2048]{1,0:T(8,128)(2,1)S(1)}, bf16[32,2048]{1,0:T(8,128)(2,1)S(1)}, u32[]{:S(2)}, u32[]{:S(2)}) collective-permute-start(bf16[32,2048]{1,0:T(8,128)(2,1)S(1)} %copy-done.7), channel_id=1, source_target_pairs={{0,24},{8,16},{16,8},{24,0},{1,25},{9,17},{17,9},{25,1},{2,26},{10... | collective-permute-start | bytes 393224 | tf_op jit(solution)/shard_map/ppermute | solution.py:39
  144.2 15.6 %all-to-all-start.4 = ((bf16[8,192,128]{2,1,0:T(8,128)(2,1)}), bf16[8,192,128]{2,1,0:T(8,128)(2,1)S(1)}, u32[]{:S(2)}, u32[]{:S(2)}) async-start(bf16[8,192,128]{2,1,0:T(8,128)(2,1)} %shard_map.230.refs_5_.refs_0_), calls=%async_computation.4 | async-start | bytes 786432 | tf_op jit(solution)/shard_map/all_to_all | solution.py:1052
  148.3 38.1 %collective-permute-start.18 = (bf16[32,2048]{1,0:T(8,128)(2,1)S(1)}, bf16[32,2048]{1,0:T(8,128)(2,1)S(1)}, u32[]{:S(2)}, u32[]{:S(2)}) collective-permute-start(bf16[32,2048]{1,0:T(8,128)(2,1)S(1)} %shard_map.231.refs_2_.refs_1_), channel_id=1, source_target_pairs={{0,8},{8,0},{16,24},{24,16},{1,9},{9,1},{17,25},{25,17},{2,10},{10... | collective-permute-start | bytes 393224 | tf_op jit(solution)/shard_map/ppermute | solution.py:39
  150.5 37.4 %collective-permute-start.19 = (bf16[32,2048]{1,0:T(8,128)(2,1)S(1)}, bf16[32,2048]{1,0:T(8,128)(2,1)S(1)}, u32[]{:S(2)}, u32[]{:S(2)}) collective-permute-start(bf16[32,2048]{1,0:T(8,128)(2,1)S(1)} %shard_map.231.refs_2_.refs_1_), channel_id=1, source_target_pairs={{0,16},{8,24},{16,0},{24,8},{1,17},{9,25},{17,1},{25,9},{2,18},{10... | collective-permute-start | bytes 393224 | tf_op jit(solution)/shard_map/ppermute | solution.py:39
  151.3 36.6 %collective-permute-start.20 = (bf16[32,2048]{1,0:T(8,128)(2,1)S(1)}, bf16[32,2048]{1,0:T(8,128)(2,1)S(1)}, u32[]{:S(2)}, u32[]{:S(2)}) collective-permute-start(bf16[32,2048]{1,0:T(8,128)(2,1)S(1)} %shard_map.231.refs_2_.refs_1_), channel_id=1, source_target_pairs={{0,24},{8,16},{16,8},{24,0},{1,25},{9,17},{17,9},{25,1},{2,26},{10... | collective-permute-start | bytes 393224 | tf_op jit(solution)/shard_map/ppermute | solution.py:39
  159.8 16.7 %all-to-all-start.5 = ((bf16[8,128,256]{2,1,0:T(8,128)(2,1)}), bf16[8,128,256]{2,1,0:T(8,128)(2,1)S(1)}, u32[]{:S(2)}, u32[]{:S(2)}) async-start(bf16[8,128,256]{2,1,0:T(8,128)(2,1)} %get-tuple-element.137), calls=%async_computation.5 | async-start | bytes 1048576 | tf_op jit(solution)/shard_map/all_to_all | solution.py:1052
  168.9 20.4 %collective-permute-start.21 = (bf16[32,2048]{1,0:T(8,128)(2,1)S(1)}, bf16[32,2048]{1,0:T(8,128)(2,1)S(1)}, u32[]{:S(2)}, u32[]{:S(2)}) collective-permute-start(bf16[32,2048]{1,0:T(8,128)(2,1)S(1)} %get-tuple-element.132), channel_id=1, source_target_pairs={{0,8},{8,0},{16,24},{24,16},{1,9},{9,1},{17,25},{25,17},{2,10},{10... | collective-permute-start | bytes 393224 | tf_op jit(solution)/shard_map/ppermute | solution.py:39
  169.8 19.4 %collective-permute-start.22 = (bf16[32,2048]{1,0:T(8,128)(2,1)S(1)}, bf16[32,2048]{1,0:T(8,128)(2,1)S(1)}, u32[]{:S(2)}, u32[]{:S(2)}) collective-permute-start(bf16[32,2048]{1,0:T(8,128)(2,1)S(1)} %get-tuple-element.133), channel_id=1, source_target_pairs={{0,16},{8,24},{16,0},{24,8},{1,17},{9,25},{17,1},{25,9},{2,18},{10... | collective-permute-start | bytes 393224 | tf_op jit(solution)/shard_map/ppermute | solution.py:39
  176.6 33.5 %all-to-all-start.6 = ((bf16[8,192,256]{2,1,0:T(8,128)(2,1)}), bf16[8,192,256]{2,1,0:T(8,128)(2,1)S(1)}, u32[]{:S(2)}, u32[]{:S(2)}) async-start(bf16[8,192,256]{2,1,0:T(8,128)(2,1)} %get-tuple-element.139), calls=%async_computation.6 | async-start | bytes 1572864 | tf_op jit(solution)/shard_map/all_to_all | solution.py:1052
  194.4 20.8 %collective-permute-start.24 = (bf16[32,2048]{1,0:T(8,128)(2,1)S(1)}, bf16[32,2048]{1,0:T(8,128)(2,1)S(1)}, u32[]{:S(2)}, u32[]{:S(2)}) collective-permute-start(bf16[32,2048]{1,0:T(8,128)(2,1)S(1)} %shard_map.236.refs_5_.refs_1_), channel_id=1, source_target_pairs={{0,8},{8,0},{16,24},{24,16},{1,9},{9,1},{17,25},{25,17},{2,10},{10... | collective-permute-start | bytes 393224 | tf_op jit(solution)/shard_map/ppermute | solution.py:39
  196.4 21.3 %collective-permute-start.25 = (bf16[32,2048]{1,0:T(8,128)(2,1)S(1)}, bf16[32,2048]{1,0:T(8,128)(2,1)S(1)}, u32[]{:S(2)}, u32[]{:S(2)}) collective-permute-start(bf16[32,2048]{1,0:T(8,128)(2,1)S(1)} %shard_map.236.refs_5_.refs_1_), channel_id=1, source_target_pairs={{0,16},{8,24},{16,0},{24,8},{1,17},{9,25},{17,1},{25,9},{2,18},{10... | collective-permute-start | bytes 393224 | tf_op jit(solution)/shard_map/ppermute | solution.py:39
  196.5 21.1 %collective-permute-start.26 = (bf16[32,2048]{1,0:T(8,128)(2,1)S(1)}, bf16[32,2048]{1,0:T(8,128)(2,1)S(1)}, u32[]{:S(2)}, u32[]{:S(2)}) collective-permute-start(bf16[32,2048]{1,0:T(8,128)(2,1)S(1)} %shard_map.236.refs_5_.refs_1_), channel_id=1, source_target_pairs={{0,24},{8,16},{16,8},{24,0},{1,25},{9,17},{17,9},{25,1},{2,26},{10... | collective-permute-start | bytes 393224 | tf_op jit(solution)/shard_map/ppermute | solution.py:39
  (37 other events, 217.9 us)
Sparse Core Ops, SparseCore 0:
  31.7 38.3 all-gather.4
  72.6 41.9 all-gather.6
  116.5 37.6 all-gather.8
  156.5 48.1 all-gather.10

commit v2 on v1

--- a/solution.py
+++ b/solution.py
@@ -374,12 +374,32 @@
         return self.ref[index]
 
 
+class Stored:
+    def __init__(self, ref, copy):
+        self.ref, self.copy, self.shape, self.sent = ref, copy, ref.shape, False
+
+    def send(self):
+        if not self.sent:
+            self.copy.start()
+            self.sent = True
+
+    def __getitem__(self, index):
+        return self.ref[index]
+
+    def __setitem__(self, index, value):
+        self.ref[index] = value
+
+
+def plain(value):
+    return value.value if isinstance(value, (Pin, Near)) else value
+
+
 def pinned(value):
     return value if INTERPRET else pltpu.with_memory_space_constraint(value, pltpu.HBM)
 
 
 def call(
-    kernel, outs, args, specs=None, out_specs=None, grid=None, scratch=(), mb=8, flops=0, after=(), carry=(), prefetch=0
+    kernel, outs, args, specs=None, out_specs=None, grid=None, scratch=(), mb=8, cost=0.3, after=(), carry=(), prefetch=0
 ):
     specs = list(specs) if specs is not None else [whole() for _ in args]
     out_specs = list(out_specs) if out_specs is not None else [whole() for _ in outs]
@@ -409,22 +429,19 @@
             copy = pltpu.make_async_copy(source, slot, sem)
             copy.start()
             ins[i] = Fetched(slot, copy)
-        for i, slot in zip(far_out, slots[len(far_in) :]):
-            products[i] = slot
+        stored = [
+            Stored(slot, pltpu.make_async_copy(slot, results[i], sem))
+            for i, slot, sem in zip(far_out, slots[len(far_in) :], sems[len(far_in) :])
+        ]
+        for i, product in zip(far_out, stored):
+            products[i] = product
         kernel(*ins, *products, *rest[:own_scratch])
         for i in far_in:
             ins[i].ready()
-        copies = [
-            pltpu.make_async_copy(slot, results[i], sem)
-            for i, slot, sem in zip(far_out, slots[len(far_in) :], sems[len(far_in) :])
-        ]
-        for copy in copies:
-            copy.start()
-        for copy in copies:
-            copy.wait()
-
-    def plain(value):
-        return value.value if isinstance(value, (Pin, Near)) else value
+        for product in stored:
+            product.send()
+        for product in stored:
+            product.copy.wait()
 
     def result(value):
         dims = plain(value)
@@ -432,7 +449,6 @@
             return dims
         return (pltpu.HBM if isinstance(value, Pin) else pltpu.VMEM)(dims.shape, dims.dtype)
 
-    moved = sum(int(np.prod(plain(t).shape)) * plain(t).dtype.itemsize for t in list(args) + list(outs))
     where = dict(
         in_specs=specs + [anywhere] * (extra + kept),
         out_specs=tuple(out_specs + [anywhere] * kept),
@@ -448,13 +464,13 @@
         out_shape=tuple(result(t) for t in outs) + tuple(result(Pin(shape(t.shape, t.dtype))) for t in carry),
         input_output_aliases={count + extra + i: made + i for i in range(kept)},
         compiler_params=params(mb),
-        cost_estimate=pl.CostEstimate(flops=5000000000, bytes_accessed=0, transcendentals=0),
+        cost_estimate=pl.CostEstimate(flops=int(cost * 1e9), bytes_accessed=0, transcendentals=0),
         interpret=INTERPRET,
         **where,
     )(*[pinned(t.value) if isinstance(t, Pin) else t for t in list(args) + list(after)], *[pinned(t) for t in carry])
 
 
-def bring(items, ids, after=()):
+def bring(items, ids, after=(), carry=(), cost=0.3):
     def kernel(ids, *refs):
         sources, slots, sems = refs[: len(items)], refs[len(items) : 2 * len(items)], refs[2 * len(items) :]
         copies = []
@@ -470,7 +486,7 @@
         [Near(shape(dims, array.dtype)) for array, dims, _ in items],
         [ids] + [Pin(array) for array, _, _ in items],
         [scalars()] + [pl.BlockSpec(memory_space=pl.ANY)] * len(items),
-        scratch=[pltpu.SemaphoreType.DMA] * len(items), after=after, mb=2,
+        scratch=[pltpu.SemaphoreType.DMA] * len(items), after=after, carry=carry, mb=2, cost=cost,
     )
 
 
@@ -524,46 +540,48 @@
     return of(np.arange(local_len)), of(np.arange(cp_count) * local_len)
 
 
-def project_kernel(parts, ids, x, gy, seg, gain, weight, inner, base, a, gy_out, out, tab):
-    step = pl.program_id(0)
+def project_kernel(parts, ids, x, gain, inner, base, seg, w0, w1, w2, gy, pair, gy_out, out):
     me, mine = ids[0], ids[1]
-    rows, width = x.shape
+    rows, width = pair.shape[1:]
     part = rows // parts
     heads = out.shape[0]
-
-    @pl.when(step == 0)
-    def _():
-        for k in range(parts):
-            block = x[block_at(me, k, part), :].astype(f32)
-            normed, _ = norm_rows(block)
-            a[k * part : (k + 1) * part, :] = (normed * gain[...]).astype(bf16)
-            gy_out[k * part : (k + 1) * part, :] = gy[block_at(me, k, part), :]
-            for kind in range(4):
-                tab[kind, k * part : (k + 1) * part, :] = inner[kind, block_at(me, k, part), :]
-        place = lax.broadcasted_iota(jnp.int32, (rows, rows), 1)
-        source = lax.broadcasted_iota(jnp.int32, (rows, rows), 0)
-        moved = (own_order(me, part, place) == source).astype(bf16)
-        ids_row = jnp.broadcast_to(seg[...].astype(f32), (16, rows)).astype(bf16)
-        ordered = dot(ids_row, moved).astype(bf16)
-        for j in range(heads):
-            out[j, 3 * HD : 3 * HD + 16, :] = ordered
-
-    acc = dot(a[...], weight[0])
+    x.ready()
+    for k in range(parts):
+        normed, _ = norm_rows(x.ref[block_at(me, k, part), :].astype(f32))
+        pair[0, k * part : (k + 1) * part, :] = (normed * gain[...]).astype(bf16)
+    inner.ready()
     here = [base[kind, pl.ds(mine, 1), :] for kind in range(4)]
-    cosine = tab[0] * here[0] - tab[1] * here[1]
-    sine = tab[1] * here[0] + tab[0] * here[1]
-    factor = jnp.where(step == 0, tab[2] * here[2], tab[3] * here[3])
+    table = [
+        jnp.concatenate([inner.ref[kind, block_at(me, k, part), :] for k in range(parts)], axis=0)
+        for kind in range(4)
+    ]
+    cosine = table[0] * here[0] - table[1] * here[1]
+    sine = table[1] * here[0] + table[0] * here[1]
     lane = lax.broadcasted_iota(jnp.int32, cosine.shape, 1)
     sine = jnp.where(lane % 2 == 0, -sine, sine)
-    cosine = jnp.where(step == 2, 1.0, cosine * factor)
-    sine = jnp.where(step == 2, 0.0, sine * factor)
-    for i in range(acc.shape[1] // 128):
-        piece = acc[:, i * 128 : (i + 1) * 128]
-        turned = (piece * cosine + swap_pairs(piece, 1) * sine).T.astype(bf16)
-        for h in range(128 // HD):
-            out[i * (128 // HD) + h, pl.ds(pl.multiple_of(step * HD, HD), HD), :] = turned[
-                h * HD : (h + 1) * HD
-            ]
+    place = lax.broadcasted_iota(jnp.int32, (rows, rows), 1)
+    source = lax.broadcasted_iota(jnp.int32, (rows, rows), 0)
+    moved = (own_order(me, part, place) == source).astype(bf16)
+    ids_row = jnp.broadcast_to(seg[...].astype(f32), (16, rows)).astype(bf16)
+    ordered = dot(ids_row, moved).astype(bf16)
+    for j in range(heads):
+        out[j, 3 * HD : 3 * HD + 16, :] = ordered
+    for c, weight in enumerate((w0, w1, w2)):
+        acc = dot(pair[0], weight[0])
+        factor = (table[2] * here[2], table[3] * here[3], None)[c]
+        for i in range(acc.shape[1] // 128):
+            piece = acc[:, i * 128 : (i + 1) * 128]
+            if c < 2:
+                piece = piece * (cosine * factor) + swap_pairs(piece, 1) * (sine * factor)
+            turned = piece.T.astype(bf16)
+            for h in range(128 // HD):
+                out[i * (128 // HD) + h, c * HD : (c + 1) * HD, :] = turned[h * HD : (h + 1) * HD]
+    out.send()
+    gy.ready()
+    for k in range(parts):
+        block = gy.ref[block_at(me, k, part), :]
+        pair[1, k * part : (k + 1) * part, :] = block
+        gy_out[k * part : (k + 1) * part, :] = block
 
 
 def gather_heads(got, keys, ids_col, values=None):
@@ -592,6 +610,7 @@
 def attend_kernel(parts, ids, got, out, mixed, lse, kept, keys, ids_col):
     me = ids[0]
     kept[...] = got[...]
+    kept.send()
     blocks, _, rows = got.shape
     part = rows // parts
     gather_heads(got, keys, ids_col)
@@ -614,6 +633,7 @@
         lse[:, i * width : (i + 1) * width] = top + jnp.log(total)
         for n, j in enumerate(mine):
             out[j] = result[:, n * rows : (n + 1) * rows].astype(bf16)
+    out.send()
 
 
 def store_pieces(total, own, pieces, part, extra=None):
@@ -690,8 +710,16 @@
     grad[...] = dot_t(gy[...], weight[...])
 
 
-def flip_kernel(weight, out):
-    out[...] = weight[...].T
+def prepare_kernel(step, up, down, near_up, flipped, near_down, up_sems, down_sem):
+    chunks = [slice(i, i + step) for i in range(0, up.shape[0], step)]
+    copies = [pltpu.make_async_copy(up.at[c, :], near_up.at[c, :], up_sems.at[i]) for i, c in enumerate(chunks)]
+    last = pltpu.make_async_copy(down, near_down, down_sem)
+    for copy in copies + [last]:
+        copy.start()
+    for copy, chunk in zip(copies, chunks):
+        copy.wait()
+        flipped[:, chunk] = near_up[chunk, :].T
+    last.wait()
 
 
 def up_kernel(parts, step, own, *refs):
@@ -775,9 +803,13 @@
             piece[:, here] = result[k * part : (k + 1) * part].astype(bf16)
 
 
-def down_kernel(parts, step, z2, gh, weight, own_out, *refs):
-    pieces, gh_out = refs[: parts - 1], refs[parts - 1]
+def down_kernel(parts, step, z2, gh, u, weight, own_out, *refs):
+    pieces, (both_out, gh_out) = refs[: parts - 1], refs[parts - 1 :]
+    both_out[:, :, : u.shape[2]] = u[...]
+    both_out[:, :, u.shape[2] :] = z2[...]
+    both_out.send()
     gh_out[...] = gh[...]
+    gh_out.send()
     wide = z2.shape[2]
     part = own_out.shape[0]
     for i in range(0, weight.shape[1], step):
@@ -816,6 +848,7 @@
     part, width = own.shape[0], gb.shape[1]
     for k, block in enumerate([own] + list(got)):
         gb[k * part : (k + 1) * part, :] = block[:, :width]
+    gb.send()
     columns = jnp.concatenate([b[:, width:].astype(f32) for b in [own] + list(got)], axis=0).T
     first = columns[0:1] + columns[1:2]
     cross = columns[2:3] + columns[3:4]
@@ -833,10 +866,6 @@
         sent[j, HD:, :] = z[j * HD : (j + 1) * HD]
 
 
-def hand_on_kernel(value, out):
-    out[...] = value[...]
-
-
 def turn_back(grad, table, base, j, inverse):
     here = [base[kind, :, j : j + 1] for kind in range(4)]
     cosine = table[0] * here[0] - table[1] * here[1]
@@ -847,8 +876,11 @@
     return (grad * cosine + swap_pairs(grad, 0) * sine) * factor
 
 
-def attend_back_kernel(parts, ids, got, grads, mixed, lse, inner, base, out, keys, values, ids_col, gk, gv):
+def attend_back_kernel(parts, ids, got, grads, mixed, lse, inner, base, out, z, keys, values, ids_col, gk, gv):
     me = ids[0]
+    for j in range(grads.shape[0]):
+        z[j] = grads[j, HD:, :]
+    z.send()
     blocks, _, rows = got.shape
     part = rows // parts
     gather_heads(got, keys, ids_col, values)
@@ -888,29 +920,33 @@
         out[j, 2 * HD :, :] = gv[:, span].astype(bf16)
 
 
-def input_back_kernel(parts, step, got, weight, own_out, *pieces):
+def input_back_kernel(parts, step, got, w0, w1, w2, own_out, *pieces):
     part, width = own_out.shape
     grads = []
     for c in range(3):
         here = slice(c * HD, (c + 1) * HD)
         grad = jnp.concatenate([got[j, here, :].astype(f32) for j in range(got.shape[0])], axis=0)
         grads.append(grad.T.astype(bf16))
-    for i in range(0, width, step):
-        here = slice(i, i + step)
-        result = sum(dot_t(grads[c], weight[c, here, :]) for c in range(3))
-        own_out[:, here] = result[:part]
-        for k, piece in enumerate(pieces, 1):
-            piece[:, here] = result[k * part : (k + 1) * part].astype(bf16)
+    result = dot_t(grads[0], w0[0]) + dot_t(grads[1], w1[0]) + dot_t(grads[2], w2[0])
+    own_out[...] = result[:part]
+    for k, piece in enumerate(pieces, 1):
+        piece[...] = result[k * part : (k + 1) * part].astype(bf16)
 
 
 def final_kernel(parts, own, *refs):
     got, refs = refs[: parts - 1], refs[parts - 1 :]
-    x, gx1, gain, out = refs
+    x, gx1, gain, y_own = refs[:4]
+    y_got, (x1, out) = refs[4 : parts + 3], refs[parts + 3 :]
+    width = x.shape[1]
     grad = own[...]
     for block in got:
         grad = grad + block[...].astype(f32)
     normed, scaling = norm_rows(x[...].astype(f32))
-    out[...] = (gx1[...] + norm_back(grad, gain[...], normed, scaling)).astype(bf16)
+    out[:, :width] = (gx1[...] + norm_back(grad, gain[...], normed, scaling)).astype(bf16)
+    total = y_own[...] + x1[...]
+    for block in y_got:
+        total = total + block[...].astype(f32)
+    out[:, width:] = total.astype(bf16)
 
 
 def output_kernel(own, *refs):
@@ -937,45 +973,76 @@
     return jnp.broadcast_to(column, (columns, 128)).T[:1, :]
 
 
-def columns_grad_kernel(ids, left, right, weight, gain, out, gain_grad, left_all, sums):
-    step = pl.program_id(0)
-
-    @pl.when(step == 0)
-    def _():
-        rows = left.shape[1]
-        for j in range(left.shape[0]):
-            left_all[j * rows : (j + 1) * rows, :] = left[j]
-        sums[...] = jnp.zeros_like(sums)
-
-    grad = t_dot(left_all[...], right[...])
-    out[...] = grad
-    sums[...] += jnp.sum(grad * weight[...].astype(f32), axis=1, keepdims=True)
-
-    @pl.when(step == pl.num_programs(0) - 1)
-    def _():
-        gain_grad[...] = row_of(sums[...], sums.shape[0]) / own_row(gain, ids[1])
-
-
-def rows_grad_kernel(first, ids, left, right, weight, gain, out, gain_grad, sums):
-    step = pl.program_id(0)
-
-    @pl.when(step == 0)
-    def _():
-        sums[...] = jnp.zeros_like(sums)
-
-    value = jnp.concatenate([left[j, first:, :] for j in range(left.shape[0])], axis=1)
-    grad = dot(value, right[...])
-    out[...] = grad
-    sums[...] += jnp.sum(grad * weight[...].astype(f32), axis=1, keepdims=True)
-
-    @pl.when(step == pl.num_programs(0) - 1)
-    def _():
-        gain_grad[...] = row_of(sums[...], sums.shape[0]) / own_row(gain, ids[1])
-
-
-def grad_qkv_kernel(left, right, out):
-    value = jnp.concatenate([left[j] for j in range(left.shape[0])], axis=1)
-    out[0] = dot(value, right[...]).astype(bf16)
+def product_kernel(step, columns, which, offset, ids, left, right, *refs):
+    count = left.shape[0]
+    gains = len(refs) > 7
+    if gains:
+        (weight, gain, out, gain_grad), refs = refs[:4], refs[4:]
+        (near_weight, weight_sem), refs = refs[-2:], refs[:-2]
+    else:
+        out, refs = refs[0], refs[1:]
+    left_all, right_all, result, left_sems, right_sems, out_sems = refs
+    rows, size = right.shape[-2:]
+    own = result.shape[0]
+    tokens = count * rows
+    chunks = [slice(i, i + step) for i in range(0, size, step)]
+
+    first = []
+    for r in range(count):
+        source = left.at[r]
+        if columns:
+            source, place = source.at[:, pl.ds(offset, own)], left_all.at[pl.ds(r * rows, rows), :]
+        else:
+            source, place = source.at[pl.ds(offset, own), :], left_all.at[r]
+        first.append(pltpu.make_async_copy(source, place, left_sems.at[r]))
+    side = right if which is None else right.at[:, which]
+    later = [
+        [pltpu.make_async_copy(side.at[:, :, c], right_all.at[:, :, c], right_sems.at[i])] for i, c in enumerate(chunks)
+    ]
+    for copy in first + later[0]:
+        copy.start()
+    if gains:
+        fetch = pltpu.make_async_copy(
+            weight.at[pl.ds(pl.multiple_of(ids[1] * own, own), own), :], near_weight, weight_sem
+        )
+        fetch.start()
+    for copies in later[1:]:
+        for copy in copies:
+            copy.start()
+    for copy in first:
+        copy.wait()
+    if not columns:
+        value = jnp.concatenate([left_all[r] for r in range(count)], axis=1)
+    sums = jnp.zeros((own, 128), f32)
+    sent = []
+    for i, (c, copies) in enumerate(zip(chunks, later)):
+        for copy in copies:
+            copy.wait()
+        block = right_all[:, :, c].reshape(tokens, step)
+        grad = t_dot(left_all[...], block) if columns else dot(value, block)
+        result[:, c] = grad.astype(result.dtype)
+        if gains:
+            if i == 0:
+                fetch.wait()
+            product = grad * near_weight[:, c].astype(f32)
+            for j in range(0, step, 128):
+                sums = sums + product[:, j : j + 128]
+            moves = [pltpu.make_async_copy(result.at[:, c], out.at[:, c], out_sems.at[i, 0])]
+        else:
+            wide = out.shape[2]
+            moves = [
+                pltpu.make_async_copy(
+                    result.at[:, pl.ds(j, wide)], out.at[j // wide], out_sems.at[i, (j - c.start) // wide]
+                )
+                for j in range(c.start, c.stop, wide)
+            ]
+        for move in moves:
+            move.start()
+        sent.extend(moves)
+    if gains:
+        gain_grad[...] = row_of(jnp.sum(sums, axis=1, keepdims=True), own) / own_row(gain, ids[1])
+    for copy in sent:
+        copy.wait()
 
 
 def grad_qkv_place_kernel(ids, got, weight, gain, up_gain, out, gain_grads):
@@ -986,14 +1053,19 @@
         ).T
         out[c] = value
         total = total + jnp.sum(value * weight[c].astype(f32), axis=1, keepdims=True)
+    out.send()
     first = row_of(total, total.shape[0]) / own_row(gain, ids[1])
     row = lax.broadcasted_iota(jnp.int32, gain_grads.shape, 0)
     gain_grads[...] = jnp.where(row == 0, first, up_gain[...])
 
 
-def gain_sum_kernel(*refs):
-    blocks, (first, second) = refs[:-2], refs[-2:]
-    total = sum(b[...] for b in blocks)
+def outputs_kernel(parts, ids, *refs):
+    blocks, gains, (out, y, first, second) = refs[:parts], refs[parts : 2 * parts], refs[2 * parts :]
+    part, width = blocks[0].shape[0], out.shape[1]
+    for k, block in enumerate(blocks):
+        out[block_at(ids[0], k, part), :] = block[:, :width]
+        y[block_at(ids[0], k, part), :] = block[:, width:]
+    total = sum(b[...] for b in gains)
     first[...] = total[0:1]
     second[...] = total[1:2]
 
@@ -1057,65 +1129,67 @@
     def own_rows(value):
         return (value, (part, width), lambda ids: (block_at(ids[0], 0, part), slice(None)))
 
+    def third(c):
+        return lambda ids: (pl.ds(c, 1), slice(None), slice(None))
+
     cols, first_rows = lambda i, *_: (0, i), lambda i, *_: (i, 0)
     origin2, origin3 = lambda i, *_: (0, 0), lambda i, *_: (0, 0, 0)
-
-    a, gy_x, sent = call(
+    weight_thirds = [Far(weight3, (1, width, head_width), third(c)) for c in range(3)]
+
+    pair, gy_x, sent = call(
         functools.partial(project_kernel, T),
-        [Pin(shape((rows, width), bf16)), Pin(shape((rows, width), bf16)), Pin(shape((C, 3 * HD + 16, rows), bf16))],
-        [ids, Pin(x), Pin(gy), Pin(segment_ids.reshape(1, rows)), Pin(gain_in), Pin(weight3), Pin(inner2), Pin(base2)],
-        [scalars(), fixed((rows, width)), fixed((rows, width)), fixed((1, rows)), fixed((1, width)),
-         pl.BlockSpec((1, width, head_width), lambda i: (i, 0, 0)), fixed((4, rows, 128)), fixed((4, C, 128))],
-        [fixed((rows, width)), fixed((rows, width)), fixed((C, 3 * HD + 16, rows))],
-        grid=(3,), scratch=[pltpu.VMEM((4, rows, 128), f32)], mb=14,
+        [Far(shape((2, rows, width), bf16)), Far(shape((rows, width), bf16)), Far(shape((C, 3 * HD + 16, rows), bf16))],
+        [ids, Far(x), Far(gain_in), Far(inner2), Far(base2), Far(segment_ids.reshape(1, rows)), *weight_thirds, Far(gy)],
+        [scalars()] + [whole()] * 9, mb=14,
     )
     got = to_cp(sent)
-    near_up, near_out, near_x, near_gy, near_mid, near_heads, near_hid, near_in = bring(
-        [entire(up_weight), entire(out_weight), own_rows(x), own_rows(gy), entire(gain_mid), entire(gain_heads),
+    near_out, near_x, near_gy, near_mid, near_heads, near_hid, near_in = bring(
+        [entire(out_weight), own_rows(x), own_rows(gy), entire(gain_mid), entire(gain_heads),
          entire(gain_hid), entire(gain_in)],
         ids, after=[Pin(sent)],
     )
-    back, mixed, lse, near_got, gy_x = call(
+    back, mixed, lse, far_got, pair = call(
         functools.partial(attend_kernel, T),
-        [Far(shape((C, HD, rows), bf16)), Near(shape((HD, tokens), f32)), Near(shape((1, tokens), f32)),
-         Near(shape((C, 3 * HD + 16, rows), bf16))],
+        [Far(shape((C, HD, rows), bf16)), Far(shape((HD, tokens), f32)), Far(shape((1, tokens), f32)),
+         Far(shape((C, 3 * HD + 16, rows), bf16))],
         [ids, got], [scalars(), whole()],
         scratch=[pltpu.VMEM((tokens, HD), bf16), pltpu.VMEM((tokens, 16), f32)],
-        mb=10, after=[near_heads], carry=[gy_x],
+        mb=10, after=[near_heads], carry=[pair],
     )
     att = to_cp(back)
-    gy_all = cp_gather(gy_x)
-
-    own, *pieces, near_att, a = call(
+    early = lax.all_gather(pair, "cp", axis=0)
+
+    own, *pieces, near_att = call(
         functools.partial(out_kernel, T),
         piece_shapes(width + 256) + [Near(shape((C, HD, rows), bf16))],
-        [att, near_heads, near_out], carry=[a],
-    )
-    a_all = cp_gather(a)
-    grad_hid, near_token = call(
-        lambda gy_ref, weight, grad, token: (
-            grad_hidden_kernel(gy_ref, weight, grad), hand_on_kernel(jnp.zeros((8, 128), f32), token)),
-        [Near(shape((rows, hidden), f32)), shape((8, 128), f32)],
+        [att, near_heads, near_out],
+    )
+    (grad_hid,) = call(
+        grad_hidden_kernel, [Near(shape((rows, hidden), f32))],
         [Pin(gy_x), Pin(down_weight)],
         [fixed((rows, width)), pl.BlockSpec((step, width), first_rows)],
-        [pl.BlockSpec((rows, step), cols), fixed((8, 128))],
-        grid=(hidden // step,), after=[own], mb=10,
+        [pl.BlockSpec((rows, step), cols)],
+        grid=(hidden // step,), after=[own], mb=10, cost=3,
     )
     x1, u_own, gain_row = call(
         functools.partial(middle_kernel, T, head_width),
         [Near(shape((part, width), f32)), shape((part, wide_part), bf16), Near(shape((1, width), f32))],
-        [own, *exchange(pieces), near_x, near_mid], after=[near_token],
+        [own, *exchange(pieces), near_x, near_mid], after=[grad_hid],
     )
     u_blocks = [u_own] + spread(u_own)
-    (near_down,) = bring([entire(down_weight)], ids, after=[u_own])
-    (near_flip,) = call(flip_kernel, [Near(shape((hidden, width), bf16))], [near_up], after=[u_own], mb=16)
+    near_up, near_flip, near_down = call(
+        functools.partial(prepare_kernel, 256),
+        [Near(shape((width, hidden), bf16)), Near(shape((hidden, width), bf16)), Near(shape((hidden, width), bf16))],
+        [Pin(up_weight), Pin(down_weight)], [pl.BlockSpec(memory_space=pl.ANY)] * 2,
+        scratch=[pltpu.SemaphoreType.DMA((width // 256,)), pltpu.SemaphoreType.DMA], after=[u_own], mb=6,
+    )
 
     act, slope, u_cols, stats, near_tail = call(
         functools.partial(up_kernel, T, step),
         [Near(shape((rows, hidden), f32)), Near(shape((rows, hidden), f32)), Near(shape((C, rows, wide), bf16)),
          shape((8, rows), f32), Near(shape((rows, 128), f32))],
         [*u_blocks, near_up, grad_hid, near_hid],
-        scratch=[pltpu.VMEM((rows, width), bf16)], mb=8, after=[near_flip, near_down],
+        scratch=[pltpu.VMEM((rows, width), bf16)], mb=8, after=[near_flip],
     )
     gh, z2, own, *pieces = call(
         functools.partial(hidden_back_kernel, T, FF, step),
@@ -1123,103 +1197,93 @@
         [stats, *spread(stats), act, slope, grad_hid, near_hid, near_flip], mb=8,
     )
     gu_got = exchange(pieces)
-    (z2_sent,) = call(hand_on_kernel, [Far(shape(z2.shape, bf16))], [z2], after=[own])
-    z2_got = to_cp(z2_sent)
-    y_own, *y_pieces, gh_out, u_sent = call(
-        lambda z2_ref, gh_ref, w_ref, u_ref, *outs: (
-            down_kernel(T, step, z2_ref, gh_ref, w_ref, *outs[:-1]), hand_on_kernel(u_ref, outs[-1])),
-        [Near(t) for t in piece_shapes(width)] + [Far(shape((rows, hidden), bf16)), Far(shape(u_cols.shape, bf16))],
-        [z2, gh, near_down, u_cols], after=[own, Pin(z2_sent)],
-    )
-    gh_all = cp_gather(gh_out)
-    u_got = to_cp(u_sent)
+    y_own, *y_pieces, both_sent, gh_out = call(
+        functools.partial(down_kernel, T, step),
+        [Far(t) for t in piece_shapes(width)]
+        + [Far(shape((C, rows, wide + high), bf16)), Far(shape((rows, hidden), bf16))],
+        [z2, gh, u_cols, near_down], after=[own], cost=20,
+    )
+    both_got = to_cp(both_sent)
+    gh_all = lax.all_gather(gh_out, "cp", axis=0)
     gx1, gb_own = call(
         functools.partial(middle_back_kernel, T),
         [Near(shape((part, width), f32)), shape((part, wide_part), bf16)],
-        [own, *gu_got, gain_row, near_x, x1, near_gy, near_mid], after=[Pin(gh_out)],
+        [own, *gu_got, gain_row, near_x, x1, near_gy, near_mid], after=[Pin(gh_out)], cost=8,
     )
     gb_blocks = [gb_own] + spread(gb_own)
-
-    def columns_grad(left, right, weight, gain, after):
-        own_columns = left.shape[2]
+    (near_out,) = bring([entire(out_weight)], ids, after=[gb_own])
+
+    def product(left, right, columns, which, offset, own, after, weight=None, gain=None, cost=20):
+        anywhere = pl.BlockSpec(memory_space=pl.ANY)
+        size = right.shape[-1]
+        chunk = 2 * step
+        left_dims = (tokens, own) if columns else (C, own, rows)
+        if weight is not None:
+            outs = [Pin(shape((own, size), f32)), shape((1, own), f32)]
+            more, more_specs = [Pin(weight), gain.reshape(C, -1)], [anywhere, whole()]
+            out_specs, extra = [anywhere, whole()], [pltpu.VMEM((own, size), bf16), pltpu.SemaphoreType.DMA]
+        else:
+            outs, out_specs = [Pin(shape((C, own, size // C), bf16))], [anywhere]
+            more, more_specs, extra = [], [], []
         return call(
-            columns_grad_kernel,
-            [Pin(shape((own_columns, right.shape[1]), f32)), shape((1, own_columns), f32)],
-            [ids, Pin(left), Pin(right), Pin(weight), gain.reshape(C, -1)],
-            [scalars(), pl.BlockSpec(left.shape, origin3), pl.BlockSpec((tokens, step), cols),
-             pl.BlockSpec((own_columns, step), lambda i, ids: (ids[1], i)), pl.BlockSpec((C, own_columns), origin2)],
-            [pl.BlockSpec((own_columns, step), cols), pl.BlockSpec((1, own_columns), origin2)],
-            grid=(right.shape[1] // step,),
-            scratch=[pltpu.VMEM((tokens, own_columns), bf16), pltpu.VMEM((own_columns, 1), f32)],
-            after=after, prefetch=1, mb=10,
+            functools.partial(product_kernel, chunk, columns, which, offset), outs,
+            [ids, Pin(left), Pin(right), *more], [scalars()] + [anywhere] * 2 + more_specs, out_specs,
+            scratch=[pltpu.VMEM(left_dims, bf16), pltpu.VMEM((C, rows, size), bf16),
+                     pltpu.VMEM((own, size), plain(outs[0]).dtype),
+                     pltpu.SemaphoreType.DMA((C,)), pltpu.SemaphoreType.DMA((size // chunk,)),
+                     pltpu.SemaphoreType.DMA((size // chunk, chunk * C // size))] + extra,
+            mb=14, after=after, cost=cost,
         )
 
-    grad_down, hidden_gain_grad = columns_grad(z2_got, gy_all, down_weight, hidden_gain, [gb_own])
-    near_three, near_inner, near_base = bring(
-        [entire(weight3), entire(inner2), entire(base_t)], ids, after=[Pin(grad_down)]
-    )
-    sent, gb, *y_pieces = call(
+    sent, gb, *kept = call(
         functools.partial(heads_back_kernel, T),
-        [Far(shape((C, 2 * HD, rows), bf16)), Near(shape((rows, width), bf16))],
-        [*gb_blocks, near_tail, near_att, near_heads, near_out], after=[near_base], carry=y_pieces,
-    )
+        [Far(shape((C, 2 * HD, rows), bf16)), Far(shape((rows, width), bf16))],
+        [*gb_blocks, near_tail, near_att, near_heads, near_out], after=[Pin(both_got)], carry=y_pieces,
+    )
+    y_pieces = kept
+    gb_all = lax.all_gather(gb, "cp", axis=0)
     y_got = exchange(y_pieces)
     grads = to_cp(sent)
-    (gb_out,) = call(hand_on_kernel, [Far(shape((rows, width), bf16))], [gb], after=[Pin(sent)])
-    gb_all = cp_gather(gb_out)
-    (gq_sent,) = call(
-        functools.partial(attend_back_kernel, T), [Far(shape((C, 3 * HD, rows), bf16))],
-        [ids, near_got, grads, mixed, lse, near_inner, near_base], [scalars()] + [whole()] * 6,
+    near_got, near_mixed, near_lse, near_inner, near_base = bring(
+        [entire(far_got), entire(mixed), entire(lse), entire(inner2), entire(base_t)], ids, after=[Pin(sent)]
+    )
+    gq_sent, z = call(
+        functools.partial(attend_back_kernel, T),
+        [Far(shape((C, 3 * HD, rows), bf16)), Far(shape((C, HD, rows), bf16))],
+        [ids, near_got, grads, near_mixed, near_lse, near_inner, near_base], [scalars()] + [whole()] * 6,
         scratch=[pltpu.VMEM((tokens, HD), bf16), pltpu.VMEM((tokens, HD), bf16), pltpu.VMEM((tokens, 16), f32),
                  pltpu.VMEM((HD, tokens), f32), pltpu.VMEM((HD, tokens), f32)],
-        mb=12, after=[Pin(gb_out), y_got[0]],
+        mb=12, cost=8,
     )
     gq = to_cp(gq_sent)
-    (y_low,) = call(output_kernel, [shape((part, width), bf16)], [y_own, *y_got, x1], after=[Pin(gq_sent)])
-    y_blocks = [y_low] + spread(y_low)
-    (grad_qkv,) = call(
-        grad_qkv_kernel, [Pin(shape((C, 3 * HD, wide), bf16))], [Pin(gq_sent), Pin(a_all)],
-        [fixed(gq_sent.shape), pl.BlockSpec((tokens, wide), cols)],
-        [pl.BlockSpec((1, 3 * HD, wide), lambda i: (i, 0, 0))], grid=(C,), after=[y_low],
-    )
-    own, *pieces, grad_qkv = call(
-        functools.partial(input_back_kernel, T, step), piece_shapes(width), [gq, near_three], carry=[grad_qkv],
-    )
+    (grad_qkv,) = product(gq_sent, early, False, 0, 0, 3 * HD, [Pin(gq_sent)])
+    own, *pieces = call(
+        functools.partial(input_back_kernel, T, step), piece_shapes(width), [gq, *weight_thirds], mb=10, carry=[grad_qkv],
+    )
+    pieces, grad_qkv = pieces[: T - 1], pieces[T - 1]
     ga_got = exchange(pieces)
     grad_qkv_got = to_cp(grad_qkv)
-    grad_up, up_gain = columns_grad(u_got, gh_all, up_weight, middle_gain, [own])
-    (layer_output,) = call(
-        natural_kernel, [Far(shape((rows, width), bf16))], [ids, *y_blocks], [scalars()] + [whole()] * T, after=[own]
-    )
-    (grad_in,) = call(
+    grad_up, up_gain = product(both_got, gh_all, True, None, 0, wide, [own], up_weight, middle_gain)
+    (final,) = call(
         functools.partial(final_kernel, T),
-        [shape((part, width), bf16)],
-        [own, *ga_got, near_x, gx1, near_in], after=[Pin(layer_output), Pin(grad_up)],
-    )
-    grad_blocks = [grad_in] + spread(grad_in)
-
+        [shape((part, 2 * width), bf16)],
+        [own, *ga_got, near_x, gx1, near_in, Far(y_own), *y_got, x1], after=[Pin(grad_up)],
+    )
+    final_blocks = [final] + spread(final)
     own_wide = lambda ids: (slice(None), pl.ds(pl.multiple_of(ids[1] * wide, wide), wide), slice(None))
-    grad_out, heads_gain_grad = call(
-        functools.partial(rows_grad_kernel, HD),
-        [Pin(shape((HD, width), f32)), shape((1, HD), f32)],
-        [ids, Pin(grads), Pin(gb_all), Pin(out_weight), heads_gain.reshape(C, -1)],
-        [scalars(), pl.BlockSpec(grads.shape, origin3), pl.BlockSpec((tokens, step), cols),
-         pl.BlockSpec((HD, step), lambda i, ids: (ids[1], i)), pl.BlockSpec((C, HD), origin2)],
-        [pl.BlockSpec((HD, step), cols), pl.BlockSpec((1, HD), origin2)], grid=(width // step,),
-        scratch=[pltpu.VMEM((HD, 1), f32)], after=[grad_in], prefetch=1,
-    )
     grad_qkv, gains = call(
         grad_qkv_place_kernel,
         [Far(shape((3, wide, head_width), f32)), shape((8, wide), f32)],
         [ids, grad_qkv_got, Far(weight3, (3, wide, head_width), own_wide), input_gain.reshape(C, -1), up_gain],
-        [scalars()] + [whole()] * 4, after=[Pin(grad_out)],
-    )
-    (grad_input,) = call(
-        natural_kernel, [Far(shape((rows, width), bf16))], [ids, *grad_blocks], [scalars()] + [whole()] * T,
-        after=[Pin(grad_qkv)],
-    )
-    input_gain_grad, middle_gain_grad = call(
-        gain_sum_kernel, [shape((1, wide), f32), shape((1, wide), f32)], [gains, *spread(gains)]
+        [scalars()] + [whole()] * 4, after=[final], cost=20,
+    )
+    gain_blocks = [gains] + spread(gains)
+    grad_down, hidden_gain_grad = product(both_got, early, True, 1, wide, high, [gains], down_weight, hidden_gain)
+    grad_out, heads_gain_grad = product(z, gb_all, False, None, 0, HD, [Pin(grad_down)], out_weight, heads_gain)
+    grad_input, layer_output, input_gain_grad, middle_gain_grad = call(
+        functools.partial(outputs_kernel, T),
+        [Far(shape((rows, width), bf16))] * 2 + [shape((1, wide), f32), shape((1, wide), f32)],
+        [ids, *final_blocks, *gain_blocks], [scalars()] + [whole()] * (2 * T), after=[Pin(grad_out)],
     )
     return (
         layer_output.reshape(layer_input.shape),

time: 229 us -> 202 us (0.88)
  local copies, waits for them, and re-layouts: 14.8 us -> 0.79 us
  starting transfers between devices: 68.5 us -> 59.9 us
  Pallas kernels: 78.9 us -> 73.4 us
  waiting for transfers between devices: 41.7 us -> 44 us
    unnamed x42 -> x10, local copies, waits for them, and re-layouts: 14.7 us -> 0.02 us
    all_to_all x6 -> x5, waiting for transfers between devices: 11 us -> 19.4 us  [to_cp(): return lax.all_to_all(value, 'cp', 0, 0, tiled=True)]
    all_gather x4 -> x3, waiting for transfers between devices: 5.8 us -> 0.02 us  [the longest x1 0.02 us: body(): early = lax.all_gather(pair, 'cp', axis=0)]
    pallas_call x28 -> x23, Pallas kernels: 78.9 us -> 73.4 us  [call(): pl.pallas_call(run, out_shape=tuple((result(t) for t in outs)) + tuple((r...]
    ppermute x30 -> x27, starting transfers between devices: 44.4 us -> 39.7 us  [swap_tp(): return lax.ppermute(value, 'tp', pairs(lax.axis_size('tp'), k))]
    all_to_all x6 -> x5, starting transfers between devices: 23.8 us -> 19.9 us  [to_cp(): return lax.all_to_all(value, 'cp', 0, 0, tiled=True)]
    ppermute x30 -> x27, waiting for transfers between devices: 24.8 us -> 24.6 us  [swap_tp(): return lax.ppermute(value, 'tp', pairs(lax.axis_size('tp'), k))]
  transfers between devices with their start and end apart: 40 -> 35, of which waited for: 12 -> 13; matrix products, arithmetic and copies ran while one was open for 0% -> 0% of each run, Pallas kernels for 30% -> 31%
where the time goes in v2:
time: 202 us; the launch traced here: 201 us
  Pallas kernels  73.4 us (36%)
  starting transfers between devices  59.9 us (30%)
  waiting for transfers between devices  44 us (22%)
  between operations  14.2 us (7%)
  blocking collectives  8.82 us (4%)
    pallas_call x23, Pallas kernels, call(): pl.pallas_call(run, out_shape=tuple((result(t) for t in outs)) + tuple((r...  73.4 us
    ppermute x27, starting transfers between devices, swap_tp(): return lax.ppermute(value, 'tp', pairs(lax.axis_size('tp'), k))  39.7 us
    ppermute x27, waiting for transfers between devices, swap_tp(): return lax.ppermute(value, 'tp', pairs(lax.axis_size('tp'), k))  24.6 us
    all_to_all x5, starting transfers between devices, to_cp(): return lax.all_to_all(value, 'cp', 0, 0, tiled=True)  19.9 us
    all_to_all x5, waiting for transfers between devices, to_cp(): return lax.all_to_all(value, 'cp', 0, 0, tiled=True)  19.4 us
    all_to_all x1, blocking collectives, to_cp(): return lax.all_to_all(value, 'cp', 0, 0, tiled=True)  8.82 us
  transfers between devices with their start and end apart: 35, of which 13 were waited for; matrix products, arithmetic and copies ran while one was open for 0% of the time, Pallas kernels for 31%

profile of v2, /device:TPU:0, one launch (start us, length us, event | category | flops | bytes accessed | tf_op | source)
XLA Modules:
  0.0 201.2 jit_solution(4614089675889782741)
XLA Ops:
  7.3 6.1 %shard_map.213 = (bf16[2,128,2048]{2,1,0:T(8,128)(2,1)}, bf16[128,2048]{1,0:T(8,128)(2,1)}, bf16[8,208,128]{2,1,0:T(8,128)(2,1)}) custom-call(s32[2]{0:T(128)S(1)} %pad_add_fusion.refs_0_, bf16[128,2048]{1,0:T(8,128)(2,1)} %bitcast.27, f32[1,2048]{1,0:T(1,128)} %bitcast.31, f32[4,128,128]{2,1,0:T(8,128)} %constant.14.clone.refs_3_.refs_4_, ...), custom_call_target="tpu_custom_call" | custom-call | flops 300000000 | tf_op jit(solution)/shard_map/pallas_call | solution.py:462
  13.3 5.2 %all-to-all-start = ((bf16[8,208,128]{2,1,0:T(8,128)(2,1)}), bf16[8,208,128]{2,1,0:T(8,128)(2,1)S(1)}, u32[]{:S(2)}, u32[]{:S(2)}) async-start(bf16[8,208,128]{2,1,0:T(8,128)(2,1)} %get-tuple-element.84.refs_8_), calls=%async_computation | async-start | bytes 851968 | tf_op jit(solution)/shard_map/all_to_all | solution.py:1124
  20.8 6.4 %all-to-all-done.refs_1_ = bf16[8,208,128]{2,1,0:T(8,128)(2,1)S(1)} async-done(((bf16[8,208,128]{2,1,0:T(8,128)(2,1)}), bf16[8,208,128]{2,1,0:T(8,128)(2,1)S(1)}, u32[]{:S(2)}, u32[]{:S(2)}) %all-to-all-start) | async-done | bytes 426016 | tf_op jit(solution)/shard_map/all_to_all | solution.py:1124
  27.2 3.5 %shard_map.215 = (bf16[8,64,128]{2,1,0:T(8,128)(2,1)}, f32[64,1024]{1,0:T(8,128)}, f32[1,1024]{1,0:T(1,128)}, bf16[8,208,128]{2,1,0:T(8,128)(2,1)}, bf16[2,128,2048]{2,1,0:T(8,128)(2,1)}) custom-call(s32[2]{0:T(128)S(1)} %pad_add_fusion.refs_0_, bf16[8,208,128]{2,1,0:T(8,128)(2,1)S(1)} %all-to-all-done.refs_1_, ...), custom_call_target="tpu_custom_call", output_to_operand_aliasing={{4}: (3, {})} | custom-call | flops 300000000 | tf_op jit(solution)/shard_map/pallas_call | solution.py:462
  30.7 8.8 %all_to_all.30.refs_0_ = bf16[8,64,128]{2,1,0:T(8,128)(2,1)S(1)} all-to-all(bf16[8,64,128]{2,1,0:T(8,128)(2,1)} %get-tuple-element.90), channel_id=1, replica_groups=mesh['tp'=4,'cp'=8] {'cp'}, dimensions={0} | all-to-all | bytes 262144 | tf_op jit(solution)/shard_map/all_to_all | solution.py:1124
  44.7 6.0 %shard_map.217.refs_6_.refs_5_ = f32[128,2048]{1,0:T(8,128)S(1)} custom-call(bf16[128,2048]{1,0:T(8,128)(2,1)} %get-tuple-element.98.refs_0_, bf16[2048,2048]{1,0:T(8,128)(2,1)} %refs_3_.5, f32[32,2304]{1,0:T(8,128)S(1)} %get-tuple-element.92.refs_2_.refs_0_), custom_call_target="tpu_custom_call" | custom-call | flops 3000000000 | tf_op jit(solution)/shard_map/pallas_call | solution.py:462
  50.7 5.2 %collective-permute-done.1.refs_2_ = bf16[32,2304]{1,0:T(8,128)(2,1)S(1)} collective-permute-done((bf16[32,2304]{1,0:T(8,128)(2,1)S(1)}, bf16[32,2304]{1,0:T(8,128)(2,1)S(1)}, u32[]{:S(2)}, u32[]{:S(2)}) %collective-permute-start.1) | collective-permute-done | bytes 147488 | tf_op jit(solution)/shard_map/ppermute | solution.py:39
  61.0 6.0 %shard_map.219 = (bf16[2048,2048]{1,0:T(8,128)(2,1)S(1)}, bf16[2048,2048]{1,0:T(8,128)(2,1)S(1)}, bf16[2048,2048]{1,0:T(8,128)(2,1)S(1)}) custom-call(bf16[2048,2048]{1,0:T(8,128)(2,1)} %refs_3_.4, bf16[2048,2048]{1,0:T(8,128)(2,1)} %refs_3_.5, bf16[32,2176]{1,0:T(8,128)(2,1)S(1)} %get-tuple-element.99.refs_2_.refs_0_), custom_call_target="tpu_custom_call" | custom-call | flops 300000000 | tf_op jit(solution)/shard_map/pallas_call | solution.py:462
  67.0 3.7 %collective-permute-done.4.refs_2_ = bf16[32,2176]{1,0:T(8,128)(2,1)S(1)} collective-permute-done((bf16[32,2176]{1,0:T(8,128)(2,1)S(1)}, bf16[32,2176]{1,0:T(8,128)(2,1)S(1)}, u32[]{:S(2)}, u32[]{:S(2)}) %collective-permute-start.4) | collective-permute-done | bytes 139296 | tf_op jit(solution)/shard_map/ppermute | solution.py:39
  83.2 2.7 %shard_map.222 = (f32[32,2048]{1,0:T(8,128)}, bf16[32,2048]{1,0:T(8,128)(2,1)}, bf16[32,2048]{1,0:T(8,128)(2,1)}, bf16[32,2048]{1,0:T(8,128)(2,1)}, bf16[8,128,5...) custom-call(bf16[8,128,256]{2,1,0:T(8,128)(2,1)S(1)} %get-tuple-element.113.refs_0_, ...), custom_call_target="tpu_custom_call" | custom-call | flops 20000000000 | tf_op jit(solution)/shard_map/pallas_call | solution.py:462
  89.5 4.2 %all-to-all-start.2 = ((bf16[8,128,512]{2,1,0:T(8,128)(2,1)}), bf16[8,128,512]{2,1,0:T(8,128)(2,1)}, u32[]{:S(2)}, u32[]{:S(2)}) async-start(bf16[8,128,512]{2,1,0:T(8,128)(2,1)} %get-tuple-element.121), calls=%async_computation.2 | async-start | bytes 2097152 | tf_op jit(solution)/shard_map/all_to_all | solution.py:1124
  104.2 8.1 %collective-permute-done.13.refs_2_ = bf16[32,2176]{1,0:T(8,128)(2,1)S(1)} collective-permute-done((bf16[32,2176]{1,0:T(8,128)(2,1)S(1)}, bf16[32,2176]{1,0:T(8,128)(2,1)S(1)}, u32[]{:S(2)}, u32[]{:S(2)}) %collective-permute-start.13) | collective-permute-done | bytes 139296 | tf_op jit(solution)/shard_map/ppermute | solution.py:39
  116.2 3.4 %all-to-all-start.3 = ((bf16[8,128,128]{2,1,0:T(8,128)(2,1)}), bf16[8,128,128]{2,1,0:T(8,128)(2,1)S(1)}, u32[]{:S(2)}, u32[]{:S(2)}) async-start(bf16[8,128,128]{2,1,0:T(8,128)(2,1)} %get-tuple-element.125.refs_6_), calls=%async_computation.3 | async-start | bytes 524288 | tf_op jit(solution)/shard_map/all_to_all | solution.py:1124
  129.7 3.7 %shard_map.227 = (bf16[8,192,128]{2,1,0:T(8,128)(2,1)}, bf16[8,64,128]{2,1,0:T(8,128)(2,1)}) custom-call(s32[2]{0:T(128)S(1)} %pad_add_fusion.refs_0_, bf16[8,208,128]{2,1,0:T(8,128)(2,1)S(1)} %get-tuple-element.126.refs_1_, bf16[8,128,128]{2,1,0:T(8,128)(2,1)S(1)} %all-to-all-done.3.refs_2_, f32[64,1024]{1,0:T(8,128)S(1)} %get-tuple-element.127.refs_3_, ...), custom_call_target="tpu_custom_call" | custom-call | flops 8000000000 | tf_op jit(solution)/shard_map/pallas_call | solution.py:462
  133.4 3.5 %all-to-all-start.4 = ((bf16[8,192,128]{2,1,0:T(8,128)(2,1)}), bf16[8,192,128]{2,1,0:T(8,128)(2,1)S(1)}, u32[]{:S(2)}, u32[]{:S(2)}) async-start(bf16[8,192,128]{2,1,0:T(8,128)(2,1)} %get-tuple-element.131.refs_1_.refs_3_), calls=%async_computation.4 | async-start | bytes 786432 | tf_op jit(solution)/shard_map/all_to_all | solution.py:1124
  136.9 4.5 %shard_map.228.refs_4_ = bf16[8,192,256]{2,1,0:T(8,128)(2,1)} custom-call(s32[2]{0:T(128)S(1)} %pad_add_fusion.refs_0_, bf16[8,192,128]{2,1,0:T(8,128)(2,1)} %get-tuple-element.131.refs_1_.refs_3_, bf16[8,2,128,2048]{3,2,1,0:T(8,128)(2,1)} %bitcast.37, bf16[8,192,128]{2,1,0:T(8,128)(2,1)} %get-tuple-element.131.refs_1_.refs_3_), custom_call_target="tpu_custom_call" | custom-call | flops 20000000000 | tf_op jit(solution)/shard_map/pallas_call | solution.py:462
  141.4 3.7 %all-to-all-done.4.refs_0_ = bf16[8,192,128]{2,1,0:T(8,128)(2,1)S(1)} async-done(((bf16[8,192,128]{2,1,0:T(8,128)(2,1)}), bf16[8,192,128]{2,1,0:T(8,128)(2,1)S(1)}, u32[]{:S(2)}, u32[]{:S(2)}) %all-to-all-start.4) | async-done | bytes 393248 | tf_op jit(solution)/shard_map/all_to_all | solution.py:1124
  145.2 4.7 %shard_map.229 = (f32[32,2048]{1,0:T(8,128)S(1)}, bf16[32,2048]{1,0:T(8,128)(2,1)S(1)}, bf16[32,2048]{1,0:T(8,128)(2,1)S(1)}, bf16[32,2048]{1,0:T(8,128)(2,1)S(1)}, bf16[8,192,256]{2,1,0:T(8,128)(2,1)}) custom-call(bf16[8,192,128]{2,1,0:T(8,128)(2,1)S(1)} %all-to-all-done.4.refs_0_, bf16[3,2048,512]{2,1,0:T(8,128)(2,1)} %bitcast.23, ...), custom_call_target="tpu_custom_call", output_to_operand_aliasing={{4}: (4, {})} | custom-call | flops 300000000 | tf_op jit(solution)/shard_map/pallas_call | solution.py:462
  151.9 3.5 %all-to-all-start.5 = ((bf16[8,192,256]{2,1,0:T(8,128)(2,1)}), bf16[8,192,256]{2,1,0:T(8,128)(2,1)S(1)}, u32[]{:S(2)}, u32[]{:S(2)}) async-start(bf16[8,192,256]{2,1,0:T(8,128)(2,1)} %get-tuple-element.144), calls=%async_computation.5 | async-start | bytes 1572864 | tf_op jit(solution)/shard_map/all_to_all | solution.py:1124
  157.9 6.1 %shard_map.230 = (f32[256,2048]{1,0:T(8,128)}, f32[1,256]{1,0:T(1,128)S(1)}) custom-call(s32[2]{0:T(128)S(1)} %pad_add_fusion.refs_0_, bf16[8,128,512]{2,1,0:T(8,128)(2,1)} %all-to-all-done.2.refs_8_.refs_1_, bf16[8,128,2048]{2,1,0:T(8,128)(2,1)} %bitcast.39, bf16[2048,2048]{1,0:T(8,128)(2,1)} %refs_3_.4, f32[8,256]{1,0:T(8,128)S(1)} %reshape.78.refs_4_, ...), custom_call_target="tpu_custom_call" | custom-call | flops 20000000000 | tf_op jit(solution)/shard_map/pallas_call | solution.py:462
  169.7 4.0 %all-to-all-done.5.refs_1_ = bf16[8,192,256]{2,1,0:T(8,128)(2,1)S(1)} async-done(((bf16[8,192,256]{2,1,0:T(8,128)(2,1)}), bf16[8,192,256]{2,1,0:T(8,128)(2,1)S(1)}, u32[]{:S(2)}, u32[]{:S(2)}) %all-to-all-start.5) | async-done | bytes 786464 | tf_op jit(solution)/shard_map/all_to_all | solution.py:1124
  173.8 3.1 %shard_map.232 = (f32[3,256,512]{2,1,0:T(8,128)}, f32[8,256]{1,0:T(8,128)S(1)}) custom-call(s32[2]{0:T(128)S(1)} %pad_add_fusion.refs_0_, bf16[8,192,256]{2,1,0:T(8,128)(2,1)S(1)} %all-to-all-done.5.refs_1_, bf16[3,2048,512]{2,1,0:T(8,128)(2,1)} %bitcast.26, f32[8,256]{1,0:T(8,128)S(1)} %reshape.79.refs_3_, f32[1,256]{1,0:T(1,128)S(1)} %get-tuple-element.145.refs_4_, ...), custom_call_target="tpu_custom_call" | custom-call | flops 20000000000 | tf_op jit(solution)/shard_map/pallas_call | solution.py:462
  179.1 5.8 %shard_map.233 = (f32[256,2048]{1,0:T(8,128)}, f32[1,256]{1,0:T(1,128)}) custom-call(s32[2]{0:T(128)S(1)} %pad_add_fusion.refs_0_, bf16[8,128,512]{2,1,0:T(8,128)(2,1)} %all-to-all-done.2.refs_8_.refs_1_, bf16[8,2,128,2048]{3,2,1,0:T(8,128)(2,1)} %bitcast.38, bf16[2048,2048]{1,0:T(8,128)(2,1)} %refs_3_.5, f32[8,256]{1,0:T(8,128)S(1)} %reshape.81.refs_4_, ...), custom_call_target="tpu_custom_call" | custom-call | flops 20000000000 | tf_op jit(solution)/shard_map/pallas_call | solution.py:462
  187.3 4.8 %shard_map.234 = (f32[64,2048]{1,0:T(8,128)}, f32[1,64]{1,0:T(1,128)}) custom-call(s32[2]{0:T(128)S(1)} %pad_add_fusion.refs_0_, bf16[8,64,128]{2,1,0:T(8,128)(2,1)} %get-tuple-element.147.refs_1_, bf16[8,128,2048]{2,1,0:T(8,128)(2,1)} %bitcast.40, bf16[512,2048]{1,0:T(8,128)(2,1)} %refs_3_.6, f32[8,64]{1,0:T(8,128)S(1)} %reshape.80.refs_4_, ...), custom_call_target="tpu_custom_call" | custom-call | flops 20000000000 | tf_op jit(solution)/shard_map/pallas_call | solution.py:462
  (88 shorter events, 70.3 us)
Async XLA Ops:
  13.3 13.9 %all-to-all-start = ((bf16[8,208,128]{2,1,0:T(8,128)(2,1)}), bf16[8,208,128]{2,1,0:T(8,128)(2,1)S(1)}, u32[]{:S(2)}, u32[]{:S(2)}) async-start(bf16[8,208,128]{2,1,0:T(8,128)(2,1)} %get-tuple-element.84.refs_8_), calls=%async_computation | async-start | bytes 851968 | tf_op jit(solution)/shard_map/all_to_all | solution.py:1124
  18.5 118.4 %all-gather.7.cloned.1.call-start = ((), (), s32[]{:S(2)}) async-start(), calls=%async_computation.6 | async-start | bytes 9437184 | tf_op jit(solution)/shard_map/all_gather | solution.py:1160
  30.7 127.2 %all-gather.9.cloned.1.call-start = ((), (), s32[]{:S(2)}) async-start(), calls=%async_computation.7 | async-start | bytes 4718592 | tf_op jit(solution)/shard_map/all_gather | solution.py:1207
  41.8 14.0 %collective-permute-start.1 = (bf16[32,2304]{1,0:T(8,128)(2,1)S(1)}, bf16[32,2304]{1,0:T(8,128)(2,1)S(1)}, u32[]{:S(2)}, u32[]{:S(2)}) collective-permute-start(bf16[32,2304]{1,0:T(8,128)(2,1)S(1)} %get-tuple-element.94), channel_id=1, source_target_pairs={{0,16},{8,24},{16,0},{24,8},{1,17},{9,25},{17,1},{25,9},{2,18},{10... | collective-permute-start | bytes 442376 | tf_op jit(solution)/shard_map/ppermute | solution.py:39
  44.4 11.4 %collective-permute-start.2 = (bf16[32,2304]{1,0:T(8,128)(2,1)S(1)}, bf16[32,2304]{1,0:T(8,128)(2,1)S(1)}, u32[]{:S(2)}, u32[]{:S(2)}) collective-permute-start(bf16[32,2304]{1,0:T(8,128)(2,1)S(1)} %get-tuple-element.95), channel_id=1, source_target_pairs={{0,24},{8,16},{16,8},{24,0},{1,25},{9,17},{17,9},{25,1},{2,26},{10... | collective-permute-start | bytes 442376 | tf_op jit(solution)/shard_map/ppermute | solution.py:39
  58.5 12.2 %collective-permute-start.4 = (bf16[32,2176]{1,0:T(8,128)(2,1)S(1)}, bf16[32,2176]{1,0:T(8,128)(2,1)S(1)}, u32[]{:S(2)}, u32[]{:S(2)}) collective-permute-start(bf16[32,2176]{1,0:T(8,128)(2,1)S(1)} %get-tuple-element.99.refs_2_.refs_0_), channel_id=1, source_target_pairs={{0,16},{8,24},{16,0},{24,8},{1,17},{9,25},{17,1},{25,9},{2,18},{10... | collective-permute-start | bytes 417800 | tf_op jit(solution)/shard_map/ppermute | solution.py:39
  59.6 11.2 %collective-permute-start.5 = (bf16[32,2176]{1,0:T(8,128)(2,1)S(1)}, bf16[32,2176]{1,0:T(8,128)(2,1)S(1)}, u32[]{:S(2)}, u32[]{:S(2)}) collective-permute-start(bf16[32,2176]{1,0:T(8,128)(2,1)S(1)} %get-tuple-element.99.refs_2_.refs_0_), channel_id=1, source_target_pairs={{0,24},{8,16},{16,8},{24,0},{1,25},{9,17},{17,9},{25,1},{2,26},{10... | collective-permute-start | bytes 417800 | tf_op jit(solution)/shard_map/ppermute | solution.py:39
  89.5 25.2 %all-to-all-start.2 = ((bf16[8,128,512]{2,1,0:T(8,128)(2,1)}), bf16[8,128,512]{2,1,0:T(8,128)(2,1)}, u32[]{:S(2)}, u32[]{:S(2)}) async-start(bf16[8,128,512]{2,1,0:T(8,128)(2,1)} %get-tuple-element.121), calls=%async_computation.2 | async-start | bytes 2097152 | tf_op jit(solution)/shard_map/all_to_all | solution.py:1124
  99.6 12.7 %collective-permute-start.13 = (bf16[32,2176]{1,0:T(8,128)(2,1)S(1)}, bf16[32,2176]{1,0:T(8,128)(2,1)S(1)}, u32[]{:S(2)}, u32[]{:S(2)}) collective-permute-start(bf16[32,2176]{1,0:T(8,128)(2,1)S(1)} %get-tuple-element.118.refs_2_.refs_0_), channel_id=1, source_target_pairs={{0,16},{8,24},{16,0},{24,8},{1,17},{9,25},{17,1},{25,9},{2,18},{10... | collective-permute-start | bytes 417800 | tf_op jit(solution)/shard_map/ppermute | solution.py:39
  99.6 12.6 %collective-permute-start.14 = (bf16[32,2176]{1,0:T(8,128)(2,1)S(1)}, bf16[32,2176]{1,0:T(8,128)(2,1)S(1)}, u32[]{:S(2)}, u32[]{:S(2)}) collective-permute-start(bf16[32,2176]{1,0:T(8,128)(2,1)S(1)} %get-tuple-element.118.refs_2_.refs_0_), channel_id=1, source_target_pairs={{0,24},{8,16},{16,8},{24,0},{1,25},{9,17},{17,9},{25,1},{2,26},{10... | collective-permute-start | bytes 417800 | tf_op jit(solution)/shard_map/ppermute | solution.py:39
  116.2 13.4 %all-to-all-start.3 = ((bf16[8,128,128]{2,1,0:T(8,128)(2,1)}), bf16[8,128,128]{2,1,0:T(8,128)(2,1)S(1)}, u32[]{:S(2)}, u32[]{:S(2)}) async-start(bf16[8,128,128]{2,1,0:T(8,128)(2,1)} %get-tuple-element.125.refs_6_), calls=%async_computation.3 | async-start | bytes 524288 | tf_op jit(solution)/shard_map/all_to_all | solution.py:1124
  119.7 67.6 %all-gather.11.cloned.1.call-start = ((), (), s32[]{:S(2)}) async-start(), calls=%async_computation.8 | async-start | bytes 4718592 | tf_op jit(solution)/shard_map/all_gather | solution.py:1244
  120.8 34.7 %collective-permute-start.18 = (bf16[32,2048]{1,0:T(8,128)(2,1)}, bf16[32,2048]{1,0:T(8,128)(2,1)S(1)}, u32[]{:S(2)}, u32[]{:S(2)}) collective-permute-start(bf16[32,2048]{1,0:T(8,128)(2,1)} %get-tuple-element.140), channel_id=1, source_target_pairs={{0,8},{8,0},{16,24},{24,16},{1,9},{9,1},{17,25},{25,17},{2,10},{10... | collective-permute-start | bytes 393224 | tf_op jit(solution)/shard_map/ppermute | solution.py:39
  121.8 42.2 %collective-permute-start.19 = (bf16[32,2048]{1,0:T(8,128)(2,1)}, bf16[32,2048]{1,0:T(8,128)(2,1)S(1)}, u32[]{:S(2)}, u32[]{:S(2)}) collective-permute-start(bf16[32,2048]{1,0:T(8,128)(2,1)} %get-tuple-element.141), channel_id=1, source_target_pairs={{0,16},{8,24},{16,0},{24,8},{1,17},{9,25},{17,1},{25,9},{2,18},{10... | collective-permute-start | bytes 393224 | tf_op jit(solution)/shard_map/ppermute | solution.py:39
  122.8 41.2 %collective-permute-start.20 = (bf16[32,2048]{1,0:T(8,128)(2,1)}, bf16[32,2048]{1,0:T(8,128)(2,1)S(1)}, u32[]{:S(2)}, u32[]{:S(2)}) collective-permute-start(bf16[32,2048]{1,0:T(8,128)(2,1)} %get-tuple-element.142), channel_id=1, source_target_pairs={{0,24},{8,16},{16,8},{24,0},{1,25},{9,17},{17,9},{25,1},{2,26},{10... | collective-permute-start | bytes 393224 | tf_op jit(solution)/shard_map/ppermute | solution.py:39
  133.4 11.7 %all-to-all-start.4 = ((bf16[8,192,128]{2,1,0:T(8,128)(2,1)}), bf16[8,192,128]{2,1,0:T(8,128)(2,1)S(1)}, u32[]{:S(2)}, u32[]{:S(2)}) async-start(bf16[8,192,128]{2,1,0:T(8,128)(2,1)} %get-tuple-element.131.refs_1_.refs_3_), calls=%async_computation.4 | async-start | bytes 786432 | tf_op jit(solution)/shard_map/all_to_all | solution.py:1124
  149.8 14.2 %collective-permute-start.15 = (bf16[32,2048]{1,0:T(8,128)(2,1)S(1)}, bf16[32,2048]{1,0:T(8,128)(2,1)S(1)}, u32[]{:S(2)}, u32[]{:S(2)}) collective-permute-start(bf16[32,2048]{1,0:T(8,128)(2,1)S(1)} %get-tuple-element.134), channel_id=1, source_target_pairs={{0,8},{8,0},{16,24},{24,16},{1,9},{9,1},{17,25},{25,17},{2,10},{10... | collective-permute-start | bytes 393224 | tf_op jit(solution)/shard_map/ppermute | solution.py:39
  151.1 13.0 %collective-permute-start.16 = (bf16[32,2048]{1,0:T(8,128)(2,1)S(1)}, bf16[32,2048]{1,0:T(8,128)(2,1)S(1)}, u32[]{:S(2)}, u32[]{:S(2)}) collective-permute-start(bf16[32,2048]{1,0:T(8,128)(2,1)S(1)} %get-tuple-element.135), channel_id=1, source_target_pairs={{0,16},{8,24},{16,0},{24,8},{1,17},{9,25},{17,1},{25,9},{2,18},{10... | collective-permute-start | bytes 393224 | tf_op jit(solution)/shard_map/ppermute | solution.py:39
  151.9 21.9 %all-to-all-start.5 = ((bf16[8,192,256]{2,1,0:T(8,128)(2,1)}), bf16[8,192,256]{2,1,0:T(8,128)(2,1)S(1)}, u32[]{:S(2)}, u32[]{:S(2)}) async-start(bf16[8,192,256]{2,1,0:T(8,128)(2,1)} %get-tuple-element.144), calls=%async_computation.5 | async-start | bytes 1572864 | tf_op jit(solution)/shard_map/all_to_all | solution.py:1124
  165.3 19.7 %collective-permute-start.21 = (bf16[32,4096]{1,0:T(8,128)(2,1)S(1)}, bf16[32,4096]{1,0:T(8,128)(2,1)S(1)}, u32[]{:S(2)}, u32[]{:S(2)}) collective-permute-start(bf16[32,4096]{1,0:T(8,128)(2,1)S(1)} %shard_map.231.refs_5_.refs_1_), channel_id=1, source_target_pairs={{0,8},{8,0},{16,24},{24,16},{1,9},{9,1},{17,25},{25,17},{2,10},{10... | collective-permute-start | bytes 786440 | tf_op jit(solution)/shard_map/ppermute | solution.py:39
  166.5 25.6 %collective-permute-start.22 = (bf16[32,4096]{1,0:T(8,128)(2,1)S(1)}, bf16[32,4096]{1,0:T(8,128)(2,1)S(1)}, u32[]{:S(2)}, u32[]{:S(2)}) collective-permute-start(bf16[32,4096]{1,0:T(8,128)(2,1)S(1)} %shard_map.231.refs_5_.refs_1_), channel_id=1, source_target_pairs={{0,16},{8,24},{16,0},{24,8},{1,17},{9,25},{17,1},{25,9},{2,18},{10... | collective-permute-start | bytes 786440 | tf_op jit(solution)/shard_map/ppermute | solution.py:39
  167.6 24.5 %collective-permute-start.23 = (bf16[32,4096]{1,0:T(8,128)(2,1)S(1)}, bf16[32,4096]{1,0:T(8,128)(2,1)S(1)}, u32[]{:S(2)}, u32[]{:S(2)}) collective-permute-start(bf16[32,4096]{1,0:T(8,128)(2,1)S(1)} %shard_map.231.refs_5_.refs_1_), channel_id=1, source_target_pairs={{0,24},{8,16},{16,8},{24,0},{1,25},{9,17},{17,9},{25,1},{2,26},{10... | collective-permute-start | bytes 786440 | tf_op jit(solution)/shard_map/ppermute | solution.py:39
  176.9 15.2 %collective-permute-start.24 = (f32[8,256]{1,0:T(8,128)S(1)}, f32[8,256]{1,0:T(8,128)S(1)}, u32[]{:S(2)}, u32[]{:S(2)}) collective-permute-start(f32[8,256]{1,0:T(8,128)S(1)} %get-tuple-element.146.refs_5_), channel_id=1, source_target_pairs={{0,8},{8,0},{16,24},{24,16},{1,9},{9,1},{17,25},{25,17},{2,10},{10... | collective-permute-start | bytes 24584 | tf_op jit(solution)/shard_map/ppermute | solution.py:39
  177.8 14.7 %collective-permute-start.25 = (f32[8,256]{1,0:T(8,128)S(1)}, f32[8,256]{1,0:T(8,128)S(1)}, u32[]{:S(2)}, u32[]{:S(2)}) collective-permute-start(f32[8,256]{1,0:T(8,128)S(1)} %get-tuple-element.146.refs_5_), channel_id=1, source_target_pairs={{0,16},{8,24},{16,0},{24,8},{1,17},{9,25},{17,1},{25,9},{2,18},{10... | collective-permute-start | bytes 24584 | tf_op jit(solution)/shard_map/ppermute | solution.py:39
  (16 other events, 186.7 us)
Sparse Core Ops, SparseCore 0:
  30.8 53.7 all-gather.6
  87.1 48.0 all-gather.8
  137.7 42.2 all-gather.10

commit v3 on v2

--- a/solution.py
+++ b/solution.py
@@ -388,6 +388,10 @@
 
     def __setitem__(self, index, value):
         self.ref[index] = value
+
+    @property
+    def dtype(self):
+        return self.ref.dtype
 
 
 def plain(value):
@@ -685,7 +689,7 @@
 
 
 def middle_kernel(parts, head_width, own, *refs):
-    got, (x, gain, x1, u, gain_row) = refs[: parts - 1], refs[parts - 1 :]
+    got, (x, gain, x1, u, gain_row) = refs[: parts - 1][::-1], refs[parts - 1 :]
     part, width = x1.shape
     blocks = [own] + list(got)
     stats = [b[:, width : width + 128] for b in blocks]
@@ -710,20 +714,18 @@
     grad[...] = dot_t(gy[...], weight[...])
 
 
-def prepare_kernel(step, up, down, near_up, flipped, near_down, up_sems, down_sem):
+def prepare_kernel(step, up, near_up, flipped, up_sems):
     chunks = [slice(i, i + step) for i in range(0, up.shape[0], step)]
     copies = [pltpu.make_async_copy(up.at[c, :], near_up.at[c, :], up_sems.at[i]) for i, c in enumerate(chunks)]
-    last = pltpu.make_async_copy(down, near_down, down_sem)
-    for copy in copies + [last]:
+    for copy in copies:
         copy.start()
     for copy, chunk in zip(copies, chunks):
         copy.wait()
         flipped[:, chunk] = near_up[chunk, :].T
-    last.wait()
 
 
 def up_kernel(parts, step, own, *refs):
-    got, refs = refs[: parts - 1], refs[parts - 1 :]
+    got, refs = refs[: parts - 1][::-1], refs[parts - 1 :]
     weight, grad, gain, act, slope, u, stats, tail, rows_u = refs
     part = own.shape[0]
     rows, width = rows_u.shape
@@ -767,9 +769,11 @@
 
 
 def hidden_back_kernel(parts, full, step, own, *refs):
-    got, refs = refs[: parts - 1], refs[parts - 1 :]
-    act, slope, grad, gain, weight, gh, z2, own_out = refs[:8]
-    pieces = refs[8:]
+    got, refs = refs[: parts - 1][::-1], refs[parts - 1 :]
+    act, slope, grad, gain, weight, u, gh, both, own_out = refs[:9]
+    pieces = refs[9:]
+    first_wide = u.shape[2]
+    both[:, :, :first_wide] = u[...]
     rows = act.shape[0]
     part = rows // parts
     total = own[...]
@@ -785,15 +789,17 @@
         table = jnp.where(row == i, value, table)
     cols = table.T
     mean, scaling, first, cross = (cols[:, i : i + 1] for i in range(4))
-    wide = z2.shape[2]
+    wide = both.shape[2] - first_wide
     for i in range(0, act.shape[1], step):
         here = slice(i, i + step)
         normed = (act[:, here] - mean) * scaling
         low = (normed * gain[:, here]).astype(bf16)
         for j in range(0, step, wide):
-            z2[(i + j) // wide] = low[:, j : j + wide]
+            both[(i + j) // wide, :, first_wide:] = low[:, j : j + wide]
         value = scaling * (grad[:, here] * gain[:, here] - first - normed * cross) * slope[:, here]
         gh[:, here] = value.astype(bf16)
+    both.send()
+    gh.send()
     width = weight.shape[1]
     for i in range(0, width, step):
         here = slice(i, i + step)
@@ -803,27 +809,23 @@
             piece[:, here] = result[k * part : (k + 1) * part].astype(bf16)
 
 
-def down_kernel(parts, step, z2, gh, u, weight, own_out, *refs):
-    pieces, (both_out, gh_out) = refs[: parts - 1], refs[parts - 1 :]
-    both_out[:, :, : u.shape[2]] = u[...]
-    both_out[:, :, u.shape[2] :] = z2[...]
-    both_out.send()
-    gh_out[...] = gh[...]
-    gh_out.send()
-    wide = z2.shape[2]
+def down_kernel(parts, z2, *refs):
+    count = len(refs) - parts
+    weights, own_out, pieces = refs[:count], refs[count], refs[count + 1 :]
+    blocks, _, wide = z2.shape
     part = own_out.shape[0]
-    for i in range(0, weight.shape[1], step):
-        here = slice(i, i + step)
-        result = sum(
-            dot(z2[j], weight[j * wide : (j + 1) * wide, here]) for j in range(z2.shape[0])
-        )
-        own_out[:, here] = result[:part]
-        for k, piece in enumerate(pieces, 1):
-            piece[:, here] = result[k * part : (k + 1) * part].astype(bf16)
+    total = 0.0
+    for i, weight in enumerate(weights):
+        rows = weight.shape[0]
+        left = jnp.concatenate([z2[j] for j in range(i * rows // wide, (i + 1) * rows // wide)], axis=1)
+        total = total + dot(left, weight[...])
+    own_out[...] = total[:part]
+    for k, piece in enumerate(pieces, 1):
+        piece[...] = total[k * part : (k + 1) * part].astype(bf16)
 
 
 def middle_back_kernel(parts, own, *refs):
-    got, refs = refs[: parts - 1], refs[parts - 1 :]
+    got, refs = refs[: parts - 1][::-1], refs[parts - 1 :]
     gain_row, x, x1, gy, gain, gx1, gb = refs
     part, width = x1.shape
     grad = own[...]
@@ -842,7 +844,7 @@
 
 
 def heads_back_kernel(parts, own, *refs):
-    got, refs = refs[: parts - 1], refs[parts - 1 :]
+    got, refs = refs[: parts - 1][::-1], refs[parts - 1 :]
     stats, att, gain, weight, sent, gb = refs
     blocks, _, rows = att.shape
     part, width = own.shape[0], gb.shape[1]
@@ -934,19 +936,12 @@
 
 
 def final_kernel(parts, own, *refs):
-    got, refs = refs[: parts - 1], refs[parts - 1 :]
-    x, gx1, gain, y_own = refs[:4]
-    y_got, (x1, out) = refs[4 : parts + 3], refs[parts + 3 :]
-    width = x.shape[1]
+    got, (x, gx1, gain, out) = refs[: parts - 1][::-1], refs[parts - 1 :]
     grad = own[...]
     for block in got:
         grad = grad + block[...].astype(f32)
     normed, scaling = norm_rows(x[...].astype(f32))
-    out[:, :width] = (gx1[...] + norm_back(grad, gain[...], normed, scaling)).astype(bf16)
-    total = y_own[...] + x1[...]
-    for block in y_got:
-        total = total + block[...].astype(f32)
-    out[:, width:] = total.astype(bf16)
+    out[...] = (gx1[...] + norm_back(grad, gain[...], normed, scaling)).astype(bf16)
 
 
 def output_kernel(own, *refs):
@@ -964,9 +959,11 @@
         out[block_at(ids[0], k, part), :] = block[...]
 
 
-def own_row(table, index):
-    row = lax.broadcasted_iota(jnp.int32, table.shape, 0)
-    return jnp.sum(jnp.where(row == index, table[...], 0.0), axis=0, keepdims=True)
+def own_row(gain, index, own):
+    total = jnp.zeros((1, own), f32)
+    for j in range(gain.shape[1] // own):
+        total = jnp.where(index == j, gain[:, j * own : (j + 1) * own], total)
+    return total
 
 
 def row_of(column, columns):
@@ -1040,7 +1037,7 @@
             move.start()
         sent.extend(moves)
     if gains:
-        gain_grad[...] = row_of(jnp.sum(sums, axis=1, keepdims=True), own) / own_row(gain, ids[1])
+        gain_grad[...] = row_of(jnp.sum(sums, axis=1, keepdims=True), own) / own_row(gain, ids[1], own)
     for copy in sent:
         copy.wait()
 
@@ -1054,17 +1051,20 @@
         out[c] = value
         total = total + jnp.sum(value * weight[c].astype(f32), axis=1, keepdims=True)
     out.send()
-    first = row_of(total, total.shape[0]) / own_row(gain, ids[1])
+    first = row_of(total, total.shape[0]) / own_row(gain, ids[1], total.shape[0])
     row = lax.broadcasted_iota(jnp.int32, gain_grads.shape, 0)
     gain_grads[...] = jnp.where(row == 0, first, up_gain[...])
 
 
 def outputs_kernel(parts, ids, *refs):
-    blocks, gains, (out, y, first, second) = refs[:parts], refs[parts : 2 * parts], refs[2 * parts :]
-    part, width = blocks[0].shape[0], out.shape[1]
-    for k, block in enumerate(blocks):
-        out[block_at(ids[0], k, part), :] = block[:, :width]
-        y[block_at(ids[0], k, part), :] = block[:, width:]
+    blocks, y_blocks, gains = (refs[i * parts : (i + 1) * parts] for i in range(3))
+    out, y, first, second = refs[3 * parts :]
+    part = blocks[0].shape[0]
+    for k in range(parts):
+        out[block_at(ids[0], k, part), :] = blocks[-k % parts][...]
+        y[block_at(ids[0], k, part), :] = y_blocks[-k % parts][...]
+    out.send()
+    y.send()
     total = sum(b[...] for b in gains)
     first[...] = total[0:1]
     second[...] = total[1:2]
@@ -1115,10 +1115,10 @@
         return [shape((part, columns), f32)] + [shape((part, columns), bf16)] * (T - 1)
 
     def exchange(pieces):
-        return [swap_tp(piece, k) for k, piece in enumerate(pieces, 1)]
+        return [swap_tp(pieces[k - 1], k) for k in range(T - 1, 0, -1)]
 
     def spread(block):
-        return [swap_tp(block, k) for k in range(1, T)]
+        return exchange([block] * (T - 1))
 
     def to_cp(value):
         return lax.all_to_all(value, "cp", 0, 0, tiled=True)
@@ -1177,11 +1177,11 @@
         [own, *exchange(pieces), near_x, near_mid], after=[grad_hid],
     )
     u_blocks = [u_own] + spread(u_own)
-    near_up, near_flip, near_down = call(
+    near_up, near_flip = call(
         functools.partial(prepare_kernel, 256),
-        [Near(shape((width, hidden), bf16)), Near(shape((hidden, width), bf16)), Near(shape((hidden, width), bf16))],
-        [Pin(up_weight), Pin(down_weight)], [pl.BlockSpec(memory_space=pl.ANY)] * 2,
-        scratch=[pltpu.SemaphoreType.DMA((width // 256,)), pltpu.SemaphoreType.DMA], after=[u_own], mb=6,
+        [Near(shape((width, hidden), bf16)), Near(shape((hidden, width), bf16))],
+        [Pin(up_weight)], [pl.BlockSpec(memory_space=pl.ANY)],
+        scratch=[pltpu.SemaphoreType.DMA((width // 256,))], after=[u_own], mb=6,
     )
 
     act, slope, u_cols, stats, near_tail = call(
@@ -1191,24 +1191,28 @@
         [*u_blocks, near_up, grad_hid, near_hid],
         scratch=[pltpu.VMEM((rows, width), bf16)], mb=8, after=[near_flip],
     )
-    gh, z2, own, *pieces = call(
+    gh, both, own, *pieces = call(
         functools.partial(hidden_back_kernel, T, FF, step),
-        [Near(shape((rows, hidden), bf16)), Near(shape((C, rows, high), bf16))] + piece_shapes(width),
-        [stats, *spread(stats), act, slope, grad_hid, near_hid, near_flip], mb=8,
+        [Far(shape((rows, hidden), bf16)), Far(shape((C, rows, wide + high), bf16))] + piece_shapes(width),
+        [stats, *spread(stats), act, slope, grad_hid, near_hid, near_flip, u_cols], mb=10,
     )
     gu_got = exchange(pieces)
-    y_own, *y_pieces, both_sent, gh_out = call(
-        functools.partial(down_kernel, T, step),
-        [Far(t) for t in piece_shapes(width)]
-        + [Far(shape((C, rows, wide + high), bf16)), Far(shape((rows, hidden), bf16))],
-        [z2, gh, u_cols, near_down], after=[own], cost=20,
-    )
-    both_got = to_cp(both_sent)
-    gh_all = lax.all_gather(gh_out, "cp", axis=0)
+    both_got = to_cp(both)
+    gh_all = lax.all_gather(gh, "cp", axis=0)
+    down_parts = [
+        Far(down_weight, (step, width), (lambda at: lambda ids: (pl.ds(at, step), slice(None)))(i))
+        for i in range(0, hidden, step)
+    ]
+    y_own, *y_pieces = call(
+        functools.partial(down_kernel, T),
+        [Far(t) for t in piece_shapes(width)],
+        [Far(both, (C, rows, high), lambda ids: (slice(None), slice(None), pl.ds(wide, high))), *down_parts],
+        after=[own], cost=20, mb=14,
+    )
     gx1, gb_own = call(
         functools.partial(middle_back_kernel, T),
         [Near(shape((part, width), f32)), shape((part, wide_part), bf16)],
-        [own, *gu_got, gain_row, near_x, x1, near_gy, near_mid], after=[Pin(gh_out)], cost=8,
+        [own, *gu_got, gain_row, near_x, x1, near_gy, near_mid], after=[Pin(y_own)], cost=8,
     )
     gb_blocks = [gb_own] + spread(gb_own)
     (near_out,) = bring([entire(out_weight)], ids, after=[gb_own])
@@ -1220,7 +1224,7 @@
         left_dims = (tokens, own) if columns else (C, own, rows)
         if weight is not None:
             outs = [Pin(shape((own, size), f32)), shape((1, own), f32)]
-            more, more_specs = [Pin(weight), gain.reshape(C, -1)], [anywhere, whole()]
+            more, more_specs = [Pin(weight), gain], [anywhere, whole()]
             out_specs, extra = [anywhere, whole()], [pltpu.VMEM((own, size), bf16), pltpu.SemaphoreType.DMA]
         else:
             outs, out_specs = [Pin(shape((C, own, size // C), bf16))], [anywhere]
@@ -1235,6 +1239,7 @@
             mb=14, after=after, cost=cost,
         )
 
+
     sent, gb, *kept = call(
         functools.partial(heads_back_kernel, T),
         [Far(shape((C, 2 * HD, rows), bf16)), Far(shape((rows, width), bf16))],
@@ -1247,43 +1252,46 @@
     near_got, near_mixed, near_lse, near_inner, near_base = bring(
         [entire(far_got), entire(mixed), entire(lse), entire(inner2), entire(base_t)], ids, after=[Pin(sent)]
     )
+    grad_down, hidden_gain_grad = product(both_got, early, True, 1, wide, high, [Pin(sent)], down_weight, gain_hid)
     gq_sent, z = call(
         functools.partial(attend_back_kernel, T),
         [Far(shape((C, 3 * HD, rows), bf16)), Far(shape((C, HD, rows), bf16))],
         [ids, near_got, grads, near_mixed, near_lse, near_inner, near_base], [scalars()] + [whole()] * 6,
         scratch=[pltpu.VMEM((tokens, HD), bf16), pltpu.VMEM((tokens, HD), bf16), pltpu.VMEM((tokens, 16), f32),
                  pltpu.VMEM((HD, tokens), f32), pltpu.VMEM((HD, tokens), f32)],
-        mb=12, cost=8,
+        mb=12, cost=8, after=[Pin(grad_down)],
     )
     gq = to_cp(gq_sent)
-    (grad_qkv,) = product(gq_sent, early, False, 0, 0, 3 * HD, [Pin(gq_sent)])
+    (y_low,) = call(
+        output_kernel, [shape((part, width), bf16)], [Far(y_own), *y_got, x1], after=[Pin(gq_sent)]
+    )
+    y_blocks = [y_low] + spread(y_low)
+    (grad_qkv,) = product(gq_sent, early, False, 0, 0, 3 * HD, [y_low])
     own, *pieces = call(
-        functools.partial(input_back_kernel, T, step), piece_shapes(width), [gq, *weight_thirds], mb=10, carry=[grad_qkv],
-    )
-    pieces, grad_qkv = pieces[: T - 1], pieces[T - 1]
+        functools.partial(input_back_kernel, T, step), piece_shapes(width), [gq, *weight_thirds], mb=10, cost=10,
+    )
     ga_got = exchange(pieces)
     grad_qkv_got = to_cp(grad_qkv)
-    grad_up, up_gain = product(both_got, gh_all, True, None, 0, wide, [own], up_weight, middle_gain)
+    grad_up, up_gain = product(both_got, gh_all, True, None, 0, wide, [own], up_weight, gain_mid)
     (final,) = call(
         functools.partial(final_kernel, T),
-        [shape((part, 2 * width), bf16)],
-        [own, *ga_got, near_x, gx1, near_in, Far(y_own), *y_got, x1], after=[Pin(grad_up)],
+        [shape((part, width), bf16)],
+        [own, *ga_got, near_x, gx1, near_in], after=[Pin(grad_up)],
     )
     final_blocks = [final] + spread(final)
     own_wide = lambda ids: (slice(None), pl.ds(pl.multiple_of(ids[1] * wide, wide), wide), slice(None))
     grad_qkv, gains = call(
         grad_qkv_place_kernel,
         [Far(shape((3, wide, head_width), f32)), shape((8, wide), f32)],
-        [ids, grad_qkv_got, Far(weight3, (3, wide, head_width), own_wide), input_gain.reshape(C, -1), up_gain],
+        [ids, grad_qkv_got, Far(weight3, (3, wide, head_width), own_wide), gain_in, up_gain],
         [scalars()] + [whole()] * 4, after=[final], cost=20,
     )
     gain_blocks = [gains] + spread(gains)
-    grad_down, hidden_gain_grad = product(both_got, early, True, 1, wide, high, [gains], down_weight, hidden_gain)
-    grad_out, heads_gain_grad = product(z, gb_all, False, None, 0, HD, [Pin(grad_down)], out_weight, heads_gain)
+    grad_out, heads_gain_grad = product(z, gb_all, False, None, 0, HD, [gains], out_weight, gain_heads)
     grad_input, layer_output, input_gain_grad, middle_gain_grad = call(
         functools.partial(outputs_kernel, T),
         [Far(shape((rows, width), bf16))] * 2 + [shape((1, wide), f32), shape((1, wide), f32)],
-        [ids, *final_blocks, *gain_blocks], [scalars()] + [whole()] * (2 * T), after=[Pin(grad_out)],
+        [ids, *final_blocks, *y_blocks, *gain_blocks], [scalars()] + [whole()] * (3 * T), after=[Pin(grad_out)],
     )
     return (
         layer_output.reshape(layer_input.shape),

time: 202 us -> 195 us (0.965)
  waiting for transfers between devices: 44 us -> 30.5 us
  starting transfers between devices: 59.9 us -> 66.2 us
    all_to_all x5, waiting for transfers between devices: 19.4 us -> 7.48 us  [to_cp(): return lax.all_to_all(value, 'cp', 0, 0, tiled=True)]
    ppermute x27 -> x30, starting transfers between devices: 39.7 us -> 45.2 us  [swap_tp(): return lax.ppermute(value, 'tp', pairs(lax.axis_size('tp'), k))]
    ppermute x27 -> x30, waiting for transfers between devices: 24.6 us -> 22.9 us  [swap_tp(): return lax.ppermute(value, 'tp', pairs(lax.axis_size('tp'), k))]
    pallas_call x23 -> x24, Pallas kernels: 73.4 us -> 74.7 us  [call(): pl.pallas_call(run, out_shape=tuple((result(t) for t in outs)) + tuple((r...]
  transfers between devices with their start and end apart: 35 -> 38, of which waited for: 13 -> 10; matrix products, arithmetic and copies ran while one was open for 0% -> 0% of each run, Pallas kernels for 31% -> 32%
where the time goes in v3:
time: 195 us; the launch traced here: 194 us
  Pallas kernels  74.7 us (38%)
  starting transfers between devices  66.2 us (34%)
  waiting for transfers between devices  30.5 us (16%)
  between operations  14.2 us (7%)
  blocking collectives  8.82 us (5%)
    pallas_call x24, Pallas kernels, call(): pl.pallas_call(run, out_shape=tuple((result(t) for t in outs)) + tuple((r...  74.7 us
    ppermute x30, starting transfers between devices, swap_tp(): return lax.ppermute(value, 'tp', pairs(lax.axis_size('tp'), k))  45.2 us
    ppermute x30, waiting for transfers between devices, swap_tp(): return lax.ppermute(value, 'tp', pairs(lax.axis_size('tp'), k))  22.9 us
    all_to_all x5, starting transfers between devices, to_cp(): return lax.all_to_all(value, 'cp', 0, 0, tiled=True)  20.6 us
    all_to_all x1, blocking collectives, to_cp(): return lax.all_to_all(value, 'cp', 0, 0, tiled=True)  8.82 us
    all_to_all x5, waiting for transfers between devices, to_cp(): return lax.all_to_all(value, 'cp', 0, 0, tiled=True)  7.48 us
  transfers between devices with their start and end apart: 38, of which 10 were waited for; matrix products, arithmetic and copies ran while one was open for 0% of the time, Pallas kernels for 32%

profile of v3, /device:TPU:0, one launch (start us, length us, event | category | flops | bytes accessed | tf_op | source)
XLA Modules:
  0.0 194.4 jit_solution(11163496163948500532)
XLA Ops:
  7.3 6.1 %shard_map.213 = (bf16[2,128,2048]{2,1,0:T(8,128)(2,1)}, bf16[128,2048]{1,0:T(8,128)(2,1)}, bf16[8,208,128]{2,1,0:T(8,128)(2,1)}) custom-call(s32[2]{0:T(128)S(1)} %pad_add_fusion.refs_0_, bf16[128,2048]{1,0:T(8,128)(2,1)} %bitcast.36, f32[1,2048]{1,0:T(1,128)} %bitcast.20, f32[4,128,128]{2,1,0:T(8,128)} %constant.14.clone.refs_3_.refs_4_, ...), custom_call_target="tpu_custom_call" | custom-call | flops 300000000 | tf_op jit(solution)/shard_map/pallas_call | solution.py:466
  13.3 5.2 %all-to-all-start = ((bf16[8,208,128]{2,1,0:T(8,128)(2,1)}), bf16[8,208,128]{2,1,0:T(8,128)(2,1)S(1)}, u32[]{:S(2)}, u32[]{:S(2)}) async-start(bf16[8,208,128]{2,1,0:T(8,128)(2,1)} %get-tuple-element.80.refs_8_), calls=%async_computation | async-start | bytes 851968 | tf_op jit(solution)/shard_map/all_to_all | solution.py:1124
  20.8 6.4 %all-to-all-done.refs_1_ = bf16[8,208,128]{2,1,0:T(8,128)(2,1)S(1)} async-done(((bf16[8,208,128]{2,1,0:T(8,128)(2,1)}), bf16[8,208,128]{2,1,0:T(8,128)(2,1)S(1)}, u32[]{:S(2)}, u32[]{:S(2)}) %all-to-all-start) | async-done | bytes 426016 | tf_op jit(solution)/shard_map/all_to_all | solution.py:1124
  27.2 3.5 %shard_map.215 = (bf16[8,64,128]{2,1,0:T(8,128)(2,1)}, f32[64,1024]{1,0:T(8,128)}, f32[1,1024]{1,0:T(1,128)}, bf16[8,208,128]{2,1,0:T(8,128)(2,1)}, bf16[2,128,2048]{2,1,0:T(8,128)(2,1)}) custom-call(s32[2]{0:T(128)S(1)} %pad_add_fusion.refs_0_, bf16[8,208,128]{2,1,0:T(8,128)(2,1)S(1)} %all-to-all-done.refs_1_, ...), custom_call_target="tpu_custom_call", output_to_operand_aliasing={{4}: (3, {})} | custom-call | flops 300000000 | tf_op jit(solution)/shard_map/pallas_call | solution.py:466
  30.7 8.8 %all_to_all.30.refs_0_ = bf16[8,64,128]{2,1,0:T(8,128)(2,1)S(1)} all-to-all(bf16[8,64,128]{2,1,0:T(8,128)(2,1)} %get-tuple-element.86), channel_id=1, replica_groups=mesh['tp'=4,'cp'=8] {'cp'}, dimensions={0} | all-to-all | bytes 262144 | tf_op jit(solution)/shard_map/all_to_all | solution.py:1124
  40.2 3.7 %collective-permute-start = (bf16[32,2304]{1,0:T(8,128)(2,1)S(1)}, bf16[32,2304]{1,0:T(8,128)(2,1)S(1)}, u32[]{:S(2)}, u32[]{:S(2)}) collective-permute-start(bf16[32,2304]{1,0:T(8,128)(2,1)S(1)} %get-tuple-element.89), channel_id=1, source_target_pairs={{0,24},{8,16},{16,8},{24,0},{1,25},{9,17},{17,9},{25,1},{2,26},{10... | collective-permute-start | bytes 442376 | tf_op jit(solution)/shard_map/ppermute | solution.py:39
  44.7 6.0 %shard_map.217.refs_6_.refs_5_ = f32[128,2048]{1,0:T(8,128)S(1)} custom-call(bf16[128,2048]{1,0:T(8,128)(2,1)} %get-tuple-element.94.refs_0_, bf16[2048,2048]{1,0:T(8,128)(2,1)} %refs_3_.6, f32[32,2304]{1,0:T(8,128)S(1)} %get-tuple-element.88.refs_2_.refs_0_), custom_call_target="tpu_custom_call" | custom-call | flops 3000000000 | tf_op jit(solution)/shard_map/pallas_call | solution.py:466
  50.7 5.5 %collective-permute-done.1.refs_2_ = bf16[32,2304]{1,0:T(8,128)(2,1)S(1)} collective-permute-done((bf16[32,2304]{1,0:T(8,128)(2,1)S(1)}, bf16[32,2304]{1,0:T(8,128)(2,1)S(1)}, u32[]{:S(2)}, u32[]{:S(2)}) %collective-permute-start.1) | collective-permute-done | bytes 147488 | tf_op jit(solution)/shard_map/ppermute | solution.py:39
  61.1 4.1 %shard_map.219 = (bf16[2048,2048]{1,0:T(8,128)(2,1)S(1)}, bf16[2048,2048]{1,0:T(8,128)(2,1)S(1)}) custom-call(bf16[2048,2048]{1,0:T(8,128)(2,1)} %refs_3_.7, bf16[32,2176]{1,0:T(8,128)(2,1)S(1)} %get-tuple-element.95.refs_1_.refs_0_), custom_call_target="tpu_custom_call" | custom-call | flops 300000000 | tf_op jit(solution)/shard_map/pallas_call | solution.py:466
  65.2 4.6 %collective-permute-done.4.refs_2_ = bf16[32,2176]{1,0:T(8,128)(2,1)S(1)} collective-permute-done((bf16[32,2176]{1,0:T(8,128)(2,1)S(1)}, bf16[32,2176]{1,0:T(8,128)(2,1)S(1)}, u32[]{:S(2)}, u32[]{:S(2)}) %collective-permute-start.4) | collective-permute-done | bytes 139296 | tf_op jit(solution)/shard_map/ppermute | solution.py:39
  85.2 4.2 %all-to-all-start.2 = ((bf16[8,128,512]{2,1,0:T(8,128)(2,1)}), bf16[8,128,512]{2,1,0:T(8,128)(2,1)}, u32[]{:S(2)}, u32[]{:S(2)}) async-start(bf16[8,128,512]{2,1,0:T(8,128)(2,1)} %get-tuple-element.110.refs_0_), calls=%async_computation.2 | async-start | bytes 2097152 | tf_op jit(solution)/shard_map/all_to_all | solution.py:1124
  89.4 5.0 %shard_map.222 = (f32[32,2048]{1,0:T(8,128)}, bf16[32,2048]{1,0:T(8,128)(2,1)}, bf16[32,2048]{1,0:T(8,128)(2,1)}, bf16[32,2048]{1,0:T(8,128)(2,1)}) custom-call(bf16[8,128,512]{2,1,0:T(8,128)(2,1)} %get-tuple-element.110.refs_0_, bf16[2048,2048]{1,0:T(8,128)(2,1)} %refs_3_.6, bf16[2048,2048]{1,0:T(8,128)(2,1)} %refs_3_.6, bf16[2048,2048]{1,0:T(8,128)(2,1)} %refs_3_.6, ...), custom_call_target="tpu_custom_call" | custom-call | flops 20000000000 | tf_op jit(solution)/shard_map/pallas_call | solution.py:466
  103.4 6.9 %collective-permute-done.13.refs_2_ = bf16[32,2176]{1,0:T(8,128)(2,1)S(1)} collective-permute-done((bf16[32,2176]{1,0:T(8,128)(2,1)S(1)}, bf16[32,2176]{1,0:T(8,128)(2,1)S(1)}, u32[]{:S(2)}, u32[]{:S(2)}) %collective-permute-start.13) | collective-permute-done | bytes 139296 | tf_op jit(solution)/shard_map/ppermute | solution.py:39
  112.0 3.8 %all-to-all-start.3 = ((bf16[8,128,128]{2,1,0:T(8,128)(2,1)}), bf16[8,128,128]{2,1,0:T(8,128)(2,1)S(1)}, u32[]{:S(2)}, u32[]{:S(2)}) async-start(bf16[8,128,128]{2,1,0:T(8,128)(2,1)} %get-tuple-element.118.refs_6_.refs_5_), calls=%async_computation.3 | async-start | bytes 524288 | tf_op jit(solution)/shard_map/all_to_all | solution.py:1124
  122.3 5.9 %shard_map.227 = (f32[256,2048]{1,0:T(8,128)}, f32[1,256]{1,0:T(1,128)}) custom-call(s32[2]{0:T(128)S(1)} %pad_add_fusion.refs_0_, bf16[8,128,512]{2,1,0:T(8,128)(2,1)} %all-to-all-done.2.refs_8_.refs_1_, bf16[8,2,128,2048]{3,2,1,0:T(8,128)(2,1)} %bitcast.41, bf16[2048,2048]{1,0:T(8,128)(2,1)} %refs_3_.6, f32[1,2048]{1,0:T(1,128)S(1)} %bitcast.24, ...), custom_call_target="tpu_custom_call" | custom-call | flops 20000000000 | tf_op jit(solution)/shard_map/pallas_call | solution.py:466
  128.2 3.7 %shard_map.228 = (bf16[8,192,128]{2,1,0:T(8,128)(2,1)}, bf16[8,64,128]{2,1,0:T(8,128)(2,1)}) custom-call(s32[2]{0:T(128)S(1)} %pad_add_fusion.refs_0_, bf16[8,208,128]{2,1,0:T(8,128)(2,1)S(1)} %get-tuple-element.119.refs_1_, bf16[8,128,128]{2,1,0:T(8,128)(2,1)S(1)} %all-to-all-done.3.refs_2_, f32[64,1024]{1,0:T(8,128)S(1)} %get-tuple-element.120.refs_3_, ...), custom_call_target="tpu_custom_call" | custom-call | flops 8000000000 | tf_op jit(solution)/shard_map/pallas_call | solution.py:466
  132.0 3.9 %all-to-all-start.4 = ((bf16[8,192,128]{2,1,0:T(8,128)(2,1)}), bf16[8,192,128]{2,1,0:T(8,128)(2,1)S(1)}, u32[]{:S(2)}, u32[]{:S(2)}) async-start(bf16[8,192,128]{2,1,0:T(8,128)(2,1)} %get-tuple-element.126.refs_5_.refs_1_), calls=%async_computation.4 | async-start | bytes 786432 | tf_op jit(solution)/shard_map/all_to_all | solution.py:1124
  136.9 4.5 %shard_map.233 = bf16[8,192,256]{2,1,0:T(8,128)(2,1)} custom-call(s32[2]{0:T(128)S(1)} %pad_add_fusion.refs_0_, bf16[8,192,128]{2,1,0:T(8,128)(2,1)} %get-tuple-element.126.refs_5_.refs_1_, bf16[8,2,128,2048]{3,2,1,0:T(8,128)(2,1)} %bitcast.42, bf16[32,2048]{1,0:T(8,128)(2,1)S(1)} %shard_map.232.refs_3_.refs_5_), custom_call_target="tpu_custom_call" | custom-call | flops 20000000000 | tf_op jit(solution)/shard_map/pallas_call | solution.py:466
  144.2 3.5 %all-to-all-start.5 = ((bf16[8,192,256]{2,1,0:T(8,128)(2,1)}), bf16[8,192,256]{2,1,0:T(8,128)(2,1)S(1)}, u32[]{:S(2)}, u32[]{:S(2)}) async-start(bf16[8,192,256]{2,1,0:T(8,128)(2,1)} %shard_map.233), calls=%async_computation.5 | async-start | bytes 1572864 | tf_op jit(solution)/shard_map/all_to_all | solution.py:1124
  147.8 4.5 %shard_map.229 = (f32[32,2048]{1,0:T(8,128)S(1)}, bf16[32,2048]{1,0:T(8,128)(2,1)S(1)}, bf16[32,2048]{1,0:T(8,128)(2,1)S(1)}, bf16[32,2048]{1,0:T(8,128)(2,1)S(1)}) custom-call(bf16[8,192,128]{2,1,0:T(8,128)(2,1)S(1)} %all-to-all-done.4.refs_0_, bf16[3,2048,512]{2,1,0:T(8,128)(2,1)} %bitcast.32, bf16[3,2048,512]{2,1,0:T(8,128)(2,1)} %bitcast.33, ...), custom_call_target="tpu_custom_call" | custom-call | flops 10000000000 | tf_op jit(solution)/shard_map/pallas_call | solution.py:466
  156.8 6.1 %shard_map.230 = (f32[256,2048]{1,0:T(8,128)}, f32[1,256]{1,0:T(1,128)S(1)}) custom-call(s32[2]{0:T(128)S(1)} %pad_add_fusion.refs_0_, bf16[8,128,512]{2,1,0:T(8,128)(2,1)} %all-to-all-done.2.refs_8_.refs_1_, bf16[8,128,2048]{2,1,0:T(8,128)(2,1)} %bitcast.43, bf16[2048,2048]{1,0:T(8,128)(2,1)} %refs_3_.7, f32[1,2048]{1,0:T(1,128)S(1)} %bitcast.26, ...), custom_call_target="tpu_custom_call" | custom-call | flops 20000000000 | tf_op jit(solution)/shard_map/pallas_call | solution.py:466
  162.9 3.3 %collective-permute-start.26 = (bf16[32,2048]{1,0:T(8,128)(2,1)S(1)}, bf16[32,2048]{1,0:T(8,128)(2,1)S(1)}, u32[]{:S(2)}, u32[]{:S(2)}) collective-permute-start(bf16[32,2048]{1,0:T(8,128)(2,1)S(1)} %shard_map.232.refs_3_.refs_5_), channel_id=1, source_target_pairs={{0,8},{8,0},{16,24},{24,16},{1,9},{9,1},{17,25},{25,17},{2,10},{10... | collective-permute-start | bytes 393224 | tf_op jit(solution)/shard_map/ppermute | solution.py:39
  170.8 3.1 %shard_map.234 = (f32[3,256,512]{2,1,0:T(8,128)}, f32[8,256]{1,0:T(8,128)S(1)}) custom-call(s32[2]{0:T(128)S(1)} %pad_add_fusion.refs_0_, bf16[8,192,256]{2,1,0:T(8,128)(2,1)S(1)} %all-to-all-done.5.refs_1_, bf16[3,2048,512]{2,1,0:T(8,128)(2,1)} %bitcast.35, f32[1,2048]{1,0:T(1,128)S(1)} %bitcast.22, f32[1,256]{1,0:T(1,128)S(1)} %get-tuple-element.138.refs_4_, ...), custom_call_target="tpu_custom_call" | custom-call | flops 20000000000 | tf_op jit(solution)/shard_map/pallas_call | solution.py:466
  180.9 4.8 %shard_map.235 = (f32[64,2048]{1,0:T(8,128)}, f32[1,64]{1,0:T(1,128)}) custom-call(s32[2]{0:T(128)S(1)} %pad_add_fusion.refs_0_, bf16[8,64,128]{2,1,0:T(8,128)(2,1)} %get-tuple-element.140.refs_1_, bf16[8,128,2048]{2,1,0:T(8,128)(2,1)} %bitcast.44, bf16[512,2048]{1,0:T(8,128)(2,1)} %refs_3_.8, f32[1,512]{1,0:T(1,128)S(1)} %bitcast.28, ...), custom_call_target="tpu_custom_call" | custom-call | flops 20000000000 | tf_op jit(solution)/shard_map/pallas_call | solution.py:466
  (89 shorter events, 63.3 us)
Async XLA Ops:
  13.3 13.9 %all-to-all-start = ((bf16[8,208,128]{2,1,0:T(8,128)(2,1)}), bf16[8,208,128]{2,1,0:T(8,128)(2,1)S(1)}, u32[]{:S(2)}, u32[]{:S(2)}) async-start(bf16[8,208,128]{2,1,0:T(8,128)(2,1)} %get-tuple-element.80.refs_8_), calls=%async_computation | async-start | bytes 851968 | tf_op jit(solution)/shard_map/all_to_all | solution.py:1124
  18.5 103.8 %all-gather.7.cloned.1.call-start = ((), (), s32[]{:S(2)}) async-start(), calls=%async_computation.6 | async-start | bytes 9437184 | tf_op jit(solution)/shard_map/all_gather | solution.py:1160
  30.7 126.1 %all-gather.9.cloned.1.call-start = ((), (), s32[]{:S(2)}) async-start(), calls=%async_computation.7 | async-start | bytes 4718592 | tf_op jit(solution)/shard_map/all_gather | solution.py:1201
  43.9 12.3 %collective-permute-start.1 = (bf16[32,2304]{1,0:T(8,128)(2,1)S(1)}, bf16[32,2304]{1,0:T(8,128)(2,1)S(1)}, u32[]{:S(2)}, u32[]{:S(2)}) collective-permute-start(bf16[32,2304]{1,0:T(8,128)(2,1)S(1)} %get-tuple-element.90), channel_id=1, source_target_pairs={{0,16},{8,24},{16,0},{24,8},{1,17},{9,25},{17,1},{25,9},{2,18},{10... | collective-permute-start | bytes 442376 | tf_op jit(solution)/shard_map/ppermute | solution.py:39
  43.9 12.3 %collective-permute-start.2 = (bf16[32,2304]{1,0:T(8,128)(2,1)S(1)}, bf16[32,2304]{1,0:T(8,128)(2,1)S(1)}, u32[]{:S(2)}, u32[]{:S(2)}) collective-permute-start(bf16[32,2304]{1,0:T(8,128)(2,1)S(1)} %get-tuple-element.91), channel_id=1, source_target_pairs={{0,8},{8,0},{16,24},{24,16},{1,9},{9,1},{17,25},{25,17},{2,10},{10... | collective-permute-start | bytes 442376 | tf_op jit(solution)/shard_map/ppermute | solution.py:39
  80.7 13.7 %collective-permute-start.10 = (bf16[32,2048]{1,0:T(8,128)(2,1)S(1)}, bf16[32,2048]{1,0:T(8,128)(2,1)S(1)}, u32[]{:S(2)}, u32[]{:S(2)}) collective-permute-start(bf16[32,2048]{1,0:T(8,128)(2,1)S(1)} %get-tuple-element.105), channel_id=1, source_target_pairs={{0,16},{8,24},{16,0},{24,8},{1,17},{9,25},{17,1},{25,9},{2,18},{10... | collective-permute-start | bytes 393224 | tf_op jit(solution)/shard_map/ppermute | solution.py:39
  82.8 11.6 %collective-permute-start.11 = (bf16[32,2048]{1,0:T(8,128)(2,1)S(1)}, bf16[32,2048]{1,0:T(8,128)(2,1)S(1)}, u32[]{:S(2)}, u32[]{:S(2)}) collective-permute-start(bf16[32,2048]{1,0:T(8,128)(2,1)S(1)} %get-tuple-element.106), channel_id=1, source_target_pairs={{0,8},{8,0},{16,24},{24,16},{1,9},{9,1},{17,25},{25,17},{2,10},{10... | collective-permute-start | bytes 393224 | tf_op jit(solution)/shard_map/ppermute | solution.py:39
  85.2 25.3 %all-to-all-start.2 = ((bf16[8,128,512]{2,1,0:T(8,128)(2,1)}), bf16[8,128,512]{2,1,0:T(8,128)(2,1)}, u32[]{:S(2)}, u32[]{:S(2)}) async-start(bf16[8,128,512]{2,1,0:T(8,128)(2,1)} %get-tuple-element.110.refs_0_), calls=%async_computation.2 | async-start | bytes 2097152 | tf_op jit(solution)/shard_map/all_to_all | solution.py:1124
  97.2 13.1 %collective-permute-start.13 = (bf16[32,2176]{1,0:T(8,128)(2,1)S(1)}, bf16[32,2176]{1,0:T(8,128)(2,1)S(1)}, u32[]{:S(2)}, u32[]{:S(2)}) collective-permute-start(bf16[32,2176]{1,0:T(8,128)(2,1)S(1)} %get-tuple-element.112.refs_2_.refs_0_), channel_id=1, source_target_pairs={{0,16},{8,24},{16,0},{24,8},{1,17},{9,25},{17,1},{25,9},{2,18},{10... | collective-permute-start | bytes 417800 | tf_op jit(solution)/shard_map/ppermute | solution.py:39
  97.5 12.9 %collective-permute-start.14 = (bf16[32,2176]{1,0:T(8,128)(2,1)S(1)}, bf16[32,2176]{1,0:T(8,128)(2,1)S(1)}, u32[]{:S(2)}, u32[]{:S(2)}) collective-permute-start(bf16[32,2176]{1,0:T(8,128)(2,1)S(1)} %get-tuple-element.112.refs_2_.refs_0_), channel_id=1, source_target_pairs={{0,8},{8,0},{16,24},{24,16},{1,9},{9,1},{17,25},{25,17},{2,10},{10... | collective-permute-start | bytes 417800 | tf_op jit(solution)/shard_map/ppermute | solution.py:39
  112.0 16.2 %all-to-all-start.3 = ((bf16[8,128,128]{2,1,0:T(8,128)(2,1)}), bf16[8,128,128]{2,1,0:T(8,128)(2,1)S(1)}, u32[]{:S(2)}, u32[]{:S(2)}) async-start(bf16[8,128,128]{2,1,0:T(8,128)(2,1)} %get-tuple-element.118.refs_6_.refs_5_), calls=%async_computation.3 | async-start | bytes 524288 | tf_op jit(solution)/shard_map/all_to_all | solution.py:1124
  115.7 65.1 %all-gather.11.cloned.1.call-start = ((), (), s32[]{:S(2)}) async-start(), calls=%async_computation.8 | async-start | bytes 4718592 | tf_op jit(solution)/shard_map/all_gather | solution.py:1249
  116.0 19.9 %collective-permute-start.21 = (bf16[32,2048]{1,0:T(8,128)(2,1)}, bf16[32,2048]{1,0:T(8,128)(2,1)S(1)}, u32[]{:S(2)}, u32[]{:S(2)}) collective-permute-start(bf16[32,2048]{1,0:T(8,128)(2,1)} %get-tuple-element.135), channel_id=1, source_target_pairs={{0,24},{8,16},{16,8},{24,0},{1,25},{9,17},{17,9},{25,1},{2,26},{10... | collective-permute-start | bytes 393224 | tf_op jit(solution)/shard_map/ppermute | solution.py:39
  118.0 17.9 %collective-permute-start.22 = (bf16[32,2048]{1,0:T(8,128)(2,1)}, bf16[32,2048]{1,0:T(8,128)(2,1)S(1)}, u32[]{:S(2)}, u32[]{:S(2)}) collective-permute-start(bf16[32,2048]{1,0:T(8,128)(2,1)} %get-tuple-element.136), channel_id=1, source_target_pairs={{0,16},{8,24},{16,0},{24,8},{1,17},{9,25},{17,1},{25,9},{2,18},{10... | collective-permute-start | bytes 393224 | tf_op jit(solution)/shard_map/ppermute | solution.py:39
  118.2 17.7 %collective-permute-start.23 = (bf16[32,2048]{1,0:T(8,128)(2,1)}, bf16[32,2048]{1,0:T(8,128)(2,1)S(1)}, u32[]{:S(2)}, u32[]{:S(2)}) collective-permute-start(bf16[32,2048]{1,0:T(8,128)(2,1)} %get-tuple-element.137), channel_id=1, source_target_pairs={{0,8},{8,0},{16,24},{24,16},{1,9},{9,1},{17,25},{25,17},{2,10},{10... | collective-permute-start | bytes 393224 | tf_op jit(solution)/shard_map/ppermute | solution.py:39
  132.0 12.3 %all-to-all-start.4 = ((bf16[8,192,128]{2,1,0:T(8,128)(2,1)}), bf16[8,192,128]{2,1,0:T(8,128)(2,1)S(1)}, u32[]{:S(2)}, u32[]{:S(2)}) async-start(bf16[8,192,128]{2,1,0:T(8,128)(2,1)} %get-tuple-element.126.refs_5_.refs_1_), calls=%async_computation.4 | async-start | bytes 786432 | tf_op jit(solution)/shard_map/all_to_all | solution.py:1124
  141.4 32.4 %collective-permute-start.24 = (bf16[32,2048]{1,0:T(8,128)(2,1)S(1)}, bf16[32,2048]{1,0:T(8,128)(2,1)S(1)}, u32[]{:S(2)}, u32[]{:S(2)}) collective-permute-start(bf16[32,2048]{1,0:T(8,128)(2,1)S(1)} %shard_map.232.refs_3_.refs_5_), channel_id=1, source_target_pairs={{0,24},{8,16},{16,8},{24,0},{1,25},{9,17},{17,9},{25,1},{2,26},{10... | collective-permute-start | bytes 393224 | tf_op jit(solution)/shard_map/ppermute | solution.py:39
  143.3 33.2 %collective-permute-start.25 = (bf16[32,2048]{1,0:T(8,128)(2,1)S(1)}, bf16[32,2048]{1,0:T(8,128)(2,1)S(1)}, u32[]{:S(2)}, u32[]{:S(2)}) collective-permute-start(bf16[32,2048]{1,0:T(8,128)(2,1)S(1)} %shard_map.232.refs_3_.refs_5_), channel_id=1, source_target_pairs={{0,16},{8,24},{16,0},{24,8},{1,17},{9,25},{17,1},{25,9},{2,18},{10... | collective-permute-start | bytes 393224 | tf_op jit(solution)/shard_map/ppermute | solution.py:39
  144.2 26.5 %all-to-all-start.5 = ((bf16[8,192,256]{2,1,0:T(8,128)(2,1)}), bf16[8,192,256]{2,1,0:T(8,128)(2,1)S(1)}, u32[]{:S(2)}, u32[]{:S(2)}) async-start(bf16[8,192,256]{2,1,0:T(8,128)(2,1)} %shard_map.233), calls=%async_computation.5 | async-start | bytes 1572864 | tf_op jit(solution)/shard_map/all_to_all | solution.py:1124
  154.1 14.3 %collective-permute-start.16 = (bf16[32,2048]{1,0:T(8,128)(2,1)S(1)}, bf16[32,2048]{1,0:T(8,128)(2,1)S(1)}, u32[]{:S(2)}, u32[]{:S(2)}) collective-permute-start(bf16[32,2048]{1,0:T(8,128)(2,1)S(1)} %get-tuple-element.129), channel_id=1, source_target_pairs={{0,16},{8,24},{16,0},{24,8},{1,17},{9,25},{17,1},{25,9},{2,18},{10... | collective-permute-start | bytes 393224 | tf_op jit(solution)/shard_map/ppermute | solution.py:39
  156.1 12.3 %collective-permute-start.17 = (bf16[32,2048]{1,0:T(8,128)(2,1)S(1)}, bf16[32,2048]{1,0:T(8,128)(2,1)S(1)}, u32[]{:S(2)}, u32[]{:S(2)}) collective-permute-start(bf16[32,2048]{1,0:T(8,128)(2,1)S(1)} %get-tuple-element.130), channel_id=1, source_target_pairs={{0,8},{8,0},{16,24},{24,16},{1,9},{9,1},{17,25},{25,17},{2,10},{10... | collective-permute-start | bytes 393224 | tf_op jit(solution)/shard_map/ppermute | solution.py:39
  162.9 15.5 %collective-permute-start.26 = (bf16[32,2048]{1,0:T(8,128)(2,1)S(1)}, bf16[32,2048]{1,0:T(8,128)(2,1)S(1)}, u32[]{:S(2)}, u32[]{:S(2)}) collective-permute-start(bf16[32,2048]{1,0:T(8,128)(2,1)S(1)} %shard_map.232.refs_3_.refs_5_), channel_id=1, source_target_pairs={{0,8},{8,0},{16,24},{24,16},{1,9},{9,1},{17,25},{25,17},{2,10},{10... | collective-permute-start | bytes 393224 | tf_op jit(solution)/shard_map/ppermute | solution.py:39
  170.7 14.9 %collective-permute-start.19 = (bf16[32,2048]{1,0:T(8,128)(2,1)S(1)}, bf16[32,2048]{1,0:T(8,128)(2,1)S(1)}, u32[]{:S(2)}, u32[]{:S(2)}) collective-permute-start(bf16[32,2048]{1,0:T(8,128)(2,1)S(1)} %shard_map.231.refs_5_.refs_1_), channel_id=1, source_target_pairs={{0,16},{8,24},{16,0},{24,8},{1,17},{9,25},{17,1},{25,9},{2,18},{10... | collective-permute-start | bytes 393224 | tf_op jit(solution)/shard_map/ppermute | solution.py:39
  173.9 11.8 %collective-permute-start.20 = (bf16[32,2048]{1,0:T(8,128)(2,1)S(1)}, bf16[32,2048]{1,0:T(8,128)(2,1)S(1)}, u32[]{:S(2)}, u32[]{:S(2)}) collective-permute-start(bf16[32,2048]{1,0:T(8,128)(2,1)S(1)} %shard_map.231.refs_5_.refs_1_), channel_id=1, source_target_pairs={{0,8},{8,0},{16,24},{24,16},{1,9},{9,1},{17,25},{25,17},{2,10},{10... | collective-permute-start | bytes 393224 | tf_op jit(solution)/shard_map/ppermute | solution.py:39
  (18 other events, 172.0 us)
Sparse Core Ops, SparseCore 0:
  30.8 53.7 all-gather.6
  87.1 44.6 all-gather.8
  134.2 39.9 all-gather.10

commit v4 on v3

--- a/solution.py
+++ b/solution.py
@@ -544,7 +544,7 @@
     return of(np.arange(local_len)), of(np.arange(cp_count) * local_len)
 
 
-def project_kernel(parts, ids, x, gain, inner, base, seg, w0, w1, w2, gy, pair, gy_out, out):
+def project_kernel(parts, ids, x, gain, gy, inner, base, seg, w0, w1, w2, pair, gy_out, out):
     me, mine = ids[0], ids[1]
     rows, width = pair.shape[1:]
     part = rows // parts
@@ -553,6 +553,13 @@
     for k in range(parts):
         normed, _ = norm_rows(x.ref[block_at(me, k, part), :].astype(f32))
         pair[0, k * part : (k + 1) * part, :] = (normed * gain[...]).astype(bf16)
+    gy.ready()
+    for k in range(parts):
+        block = gy.ref[block_at(me, k, part), :]
+        pair[1, k * part : (k + 1) * part, :] = block
+        gy_out[k * part : (k + 1) * part, :] = block
+    pair.send()
+    gy_out.send()
     inner.ready()
     here = [base[kind, pl.ds(mine, 1), :] for kind in range(4)]
     table = [
@@ -581,11 +588,6 @@
             for h in range(128 // HD):
                 out[i * (128 // HD) + h, c * HD : (c + 1) * HD, :] = turned[h * HD : (h + 1) * HD]
     out.send()
-    gy.ready()
-    for k in range(parts):
-        block = gy.ref[block_at(me, k, part), :]
-        pair[1, k * part : (k + 1) * part, :] = block
-        gy_out[k * part : (k + 1) * part, :] = block
 
 
 def gather_heads(got, keys, ids_col, values=None):
@@ -809,19 +811,30 @@
             piece[:, here] = result[k * part : (k + 1) * part].astype(bf16)
 
 
-def down_kernel(parts, z2, *refs):
-    count = len(refs) - parts
-    weights, own_out, pieces = refs[:count], refs[count], refs[count + 1 :]
-    blocks, _, wide = z2.shape
-    part = own_out.shape[0]
+def down_kernel(z2, *refs):
+    weights, (own, second, odd) = refs[:-3], refs[-3:]
+    _, _, wide = z2.shape
+    part = own.shape[0]
     total = 0.0
     for i, weight in enumerate(weights):
         rows = weight.shape[0]
         left = jnp.concatenate([z2[j] for j in range(i * rows // wide, (i + 1) * rows // wide)], axis=1)
         total = total + dot(left, weight[...])
-    own_out[...] = total[:part]
-    for k, piece in enumerate(pieces, 1):
-        piece[...] = total[k * part : (k + 1) * part].astype(bf16)
+    own[...] = total[:part]
+    second[...] = total[2 * part : 3 * part]
+    odd[:part, :] = total[part : 2 * part].astype(bf16)
+    odd[part:, :] = total[3 * part :].astype(bf16)
+
+
+def half_kernel(second, got, out):
+    part = second.shape[0]
+    out[...] = (second[...] + got[part:, :].astype(f32)).astype(bf16)
+
+
+def join_kernel(first, second, out):
+    part = first.shape[0]
+    out[:part, :] = first[...]
+    out[part:, :] = second[...]
 
 
 def middle_back_kernel(parts, own, *refs):
@@ -936,20 +949,24 @@
 
 
 def final_kernel(parts, own, *refs):
-    got, (x, gx1, gain, out) = refs[: parts - 1][::-1], refs[parts - 1 :]
+    got, (x, gx1, gain, gains, out) = refs[: parts - 1][::-1], refs[parts - 1 :]
+    part, width = gx1.shape
     grad = own[...]
     for block in got:
         grad = grad + block[...].astype(f32)
     normed, scaling = norm_rows(x[...].astype(f32))
-    out[...] = (gx1[...] + norm_back(grad, gain[...], normed, scaling)).astype(bf16)
-
-
-def output_kernel(own, *refs):
-    got, (x1, out) = refs[:-2], refs[-2:]
-    total = own[...] + x1[...]
-    for block in got:
-        total = total + block[...].astype(f32)
-    out[...] = total.astype(bf16)
+    out[:, :width] = (gx1[...] + norm_back(grad, gain[...], normed, scaling)).astype(bf16)
+    rows = gains[0:2]
+    pieces = [rows[n : n + 1, i : i + 128] for n in range(2) for i in range(0, rows.shape[1], 128)]
+    high, low = split_low(jnp.concatenate(pieces, axis=0))
+    empty = jnp.zeros((part - 2 * len(pieces), 128), f32)
+    tail = jnp.concatenate([high.astype(f32), low.astype(f32), empty], axis=0)
+    out[:, width:] = tail.astype(bf16)
+
+
+def output_kernel(own, got, last, x1, out):
+    total = own[...] + x1[...] + got[: out.shape[0], :].astype(f32)
+    out[...] = (total + last[...].astype(f32)).astype(bf16)
 
 
 def natural_kernel(ids, *refs):
@@ -1057,17 +1074,20 @@
 
 
 def outputs_kernel(parts, ids, *refs):
-    blocks, y_blocks, gains = (refs[i * parts : (i + 1) * parts] for i in range(3))
-    out, y, first, second = refs[3 * parts :]
-    part = blocks[0].shape[0]
+    blocks, (y_even, y_odd, out, y, first, second) = refs[:parts], refs[parts:]
+    part, width = blocks[0].shape[0], out.shape[1]
     for k in range(parts):
-        out[block_at(ids[0], k, part), :] = blocks[-k % parts][...]
-        y[block_at(ids[0], k, part), :] = y_blocks[-k % parts][...]
+        out[block_at(ids[0], k, part), :] = blocks[-k % parts][:, :width]
+        both = y_odd if k % 2 else y_even
+        y[block_at(ids[0], k, part), :] = both[k // 2 * part : (k // 2 + 1) * part, :]
     out.send()
     y.send()
-    total = sum(b[...] for b in gains)
-    first[...] = total[0:1]
-    second[...] = total[1:2]
+    count = first.shape[1] // 128
+    total = sum(b[:, width:].astype(f32) for b in blocks)
+    total = total[: 2 * count] + total[2 * count : 4 * count]
+    for i in range(count):
+        first[:, i * 128 : (i + 1) * 128] = total[i : i + 1]
+        second[:, i * 128 : (i + 1) * 128] = total[count + i : count + i + 1]
 
 
 def body(
@@ -1087,7 +1107,7 @@
     T, C = lax.axis_size("tp"), lax.axis_size("cp")
     part = rows // T
     head_width = qkv_weight.shape[2]
-    if head_width // HD != C or row_count != 1 or rows != 128 or 64 * part != width:
+    if head_width // HD != C or row_count != 1 or rows != 128 or T != 4 or 64 * part != width:
         return body_general(
             layer_input, segment_ids, qkv_weight, out_weight, up_weight, down_weight,
             input_gain, heads_gain, middle_gain, hidden_gain, cotangent,
@@ -1139,7 +1159,7 @@
     pair, gy_x, sent = call(
         functools.partial(project_kernel, T),
         [Far(shape((2, rows, width), bf16)), Far(shape((rows, width), bf16)), Far(shape((C, 3 * HD + 16, rows), bf16))],
-        [ids, Far(x), Far(gain_in), Far(inner2), Far(base2), Far(segment_ids.reshape(1, rows)), *weight_thirds, Far(gy)],
+        [ids, Far(x), Far(gain_in), Far(gy), Far(inner2), Far(base2), Far(segment_ids.reshape(1, rows)), *weight_thirds],
         [scalars()] + [whole()] * 9, mb=14,
     )
     got = to_cp(sent)
@@ -1203,18 +1223,18 @@
         Far(down_weight, (step, width), (lambda at: lambda ids: (pl.ds(at, step), slice(None)))(i))
         for i in range(0, hidden, step)
     ]
-    y_own, *y_pieces = call(
-        functools.partial(down_kernel, T),
-        [Far(t) for t in piece_shapes(width)],
-        [Far(both, (C, rows, high), lambda ids: (slice(None), slice(None), pl.ds(wide, high))), *down_parts],
-        after=[own], cost=20, mb=14,
-    )
     gx1, gb_own = call(
         functools.partial(middle_back_kernel, T),
         [Near(shape((part, width), f32)), shape((part, wide_part), bf16)],
-        [own, *gu_got, gain_row, near_x, x1, near_gy, near_mid], after=[Pin(y_own)], cost=8,
+        [own, *gu_got, gain_row, near_x, x1, near_gy, near_mid], cost=8,
     )
     gb_blocks = [gb_own] + spread(gb_own)
+    y_own, y_second, y_odd = call(
+        down_kernel,
+        [Far(shape((part, width), f32)), Far(shape((part, width), f32)), Far(shape((2 * part, width), bf16))],
+        [Far(both, (C, rows, high), lambda ids: (slice(None), slice(None), pl.ds(wide, high))), *down_parts],
+        after=[gb_own], cost=20, mb=14,
+    )
     (near_out,) = bring([entire(out_weight)], ids, after=[gb_own])
 
     def product(left, right, columns, which, offset, own, after, weight=None, gain=None, cost=20):
@@ -1240,58 +1260,60 @@
         )
 
 
-    sent, gb, *kept = call(
+    sent, gb, y_odd = call(
         functools.partial(heads_back_kernel, T),
         [Far(shape((C, 2 * HD, rows), bf16)), Far(shape((rows, width), bf16))],
-        [*gb_blocks, near_tail, near_att, near_heads, near_out], after=[Pin(both_got)], carry=y_pieces,
-    )
-    y_pieces = kept
+        [*gb_blocks, near_tail, near_att, near_heads, near_out], after=[Pin(both_got)], carry=[y_odd],
+    )
+    y_got = swap_tp(y_odd, 1)
     gb_all = lax.all_gather(gb, "cp", axis=0)
-    y_got = exchange(y_pieces)
     grads = to_cp(sent)
     near_got, near_mixed, near_lse, near_inner, near_base = bring(
         [entire(far_got), entire(mixed), entire(lse), entire(inner2), entire(base_t)], ids, after=[Pin(sent)]
     )
     grad_down, hidden_gain_grad = product(both_got, early, True, 1, wide, high, [Pin(sent)], down_weight, gain_hid)
+    (y_half,) = call(half_kernel, [shape((part, width), bf16)], [Far(y_second), y_got], after=[Pin(sent)])
+    y_last = swap_tp(y_half, 2)
     gq_sent, z = call(
         functools.partial(attend_back_kernel, T),
         [Far(shape((C, 3 * HD, rows), bf16)), Far(shape((C, HD, rows), bf16))],
         [ids, near_got, grads, near_mixed, near_lse, near_inner, near_base], [scalars()] + [whole()] * 6,
         scratch=[pltpu.VMEM((tokens, HD), bf16), pltpu.VMEM((tokens, HD), bf16), pltpu.VMEM((tokens, 16), f32),
                  pltpu.VMEM((HD, tokens), f32), pltpu.VMEM((HD, tokens), f32)],
-        mb=12, cost=8, after=[Pin(grad_down)],
+        mb=12, cost=8, after=[Pin(grad_down), y_half],
     )
     gq = to_cp(gq_sent)
     (y_low,) = call(
-        output_kernel, [shape((part, width), bf16)], [Far(y_own), *y_got, x1], after=[Pin(gq_sent)]
-    )
-    y_blocks = [y_low] + spread(y_low)
+        output_kernel, [shape((part, width), bf16)], [Far(y_own), y_got, y_last, x1], after=[Pin(gq_sent)]
+    )
+    y_even = swap_tp(y_low, 2)
     (grad_qkv,) = product(gq_sent, early, False, 0, 0, 3 * HD, [y_low])
     own, *pieces = call(
         functools.partial(input_back_kernel, T, step), piece_shapes(width), [gq, *weight_thirds], mb=10, cost=10,
     )
     ga_got = exchange(pieces)
+    (y_even,) = call(join_kernel, [shape((2 * part, width), bf16)], [y_low, y_even], after=[own])
+    y_odd = swap_tp(y_even, 1)
     grad_qkv_got = to_cp(grad_qkv)
     grad_up, up_gain = product(both_got, gh_all, True, None, 0, wide, [own], up_weight, gain_mid)
-    (final,) = call(
-        functools.partial(final_kernel, T),
-        [shape((part, width), bf16)],
-        [own, *ga_got, near_x, gx1, near_in], after=[Pin(grad_up)],
-    )
-    final_blocks = [final] + spread(final)
     own_wide = lambda ids: (slice(None), pl.ds(pl.multiple_of(ids[1] * wide, wide), wide), slice(None))
     grad_qkv, gains = call(
         grad_qkv_place_kernel,
         [Far(shape((3, wide, head_width), f32)), shape((8, wide), f32)],
         [ids, grad_qkv_got, Far(weight3, (3, wide, head_width), own_wide), gain_in, up_gain],
-        [scalars()] + [whole()] * 4, after=[final], cost=20,
-    )
-    gain_blocks = [gains] + spread(gains)
-    grad_out, heads_gain_grad = product(z, gb_all, False, None, 0, HD, [gains], out_weight, gain_heads)
+        [scalars()] + [whole()] * 4, after=[own], cost=20,
+    )
+    (final,) = call(
+        functools.partial(final_kernel, T),
+        [shape((part, wide_part), bf16)],
+        [own, *ga_got, near_x, gx1, near_in, gains], after=[Pin(grad_up)],
+    )
+    final_blocks = [final] + spread(final)
+    grad_out, heads_gain_grad = product(z, gb_all, False, None, 0, HD, [final], out_weight, gain_heads)
     grad_input, layer_output, input_gain_grad, middle_gain_grad = call(
         functools.partial(outputs_kernel, T),
         [Far(shape((rows, width), bf16))] * 2 + [shape((1, wide), f32), shape((1, wide), f32)],
-        [ids, *final_blocks, *y_blocks, *gain_blocks], [scalars()] + [whole()] * (3 * T), after=[Pin(grad_out)],
+        [ids, *final_blocks, y_even, y_odd], [scalars()] + [whole()] * (T + 2), after=[Pin(grad_out)],
     )
     return (
         layer_output.reshape(layer_input.shape),

time: 195 us -> 191 us (0.979)
  starting transfers between devices: 66.2 us -> 56.2 us
  waiting for transfers between devices: 30.5 us -> 35.5 us
    ppermute x30 -> x25, starting transfers between devices: 45.2 us -> 35.3 us  [swap_tp(): return lax.ppermute(value, 'tp', pairs(lax.axis_size('tp'), k))]
    all_to_all x5, waiting for transfers between devices: 7.48 us -> 11.5 us  [to_cp(): return lax.all_to_all(value, 'cp', 0, 0, tiled=True)]
    all_gather x1, waiting for transfers between devices: 0.01 us -> 3.74 us  [body(): gb_all = lax.all_gather(gb, 'cp', axis=0)]
    ppermute x30 -> x25, waiting for transfers between devices: 22.9 us -> 19.7 us  [swap_tp(): return lax.ppermute(value, 'tp', pairs(lax.axis_size('tp'), k))]
    pallas_call x24 -> x26, Pallas kernels: 74.7 us -> 74.9 us  [call(): pl.pallas_call(run, out_shape=tuple((result(t) for t in outs)) + tuple((r...]
  transfers between devices with their start and end apart: 38 -> 33, of which waited for: 10 -> 13; matrix products, arithmetic and copies ran while one was open for 0% -> 0% of each run, Pallas kernels for 32% -> 33%
where the time goes in v4:
time: 191 us; the launch traced here: 190 us
  Pallas kernels  74.9 us (39%)
  starting transfers between devices  56.2 us (29%)
  waiting for transfers between devices  35.5 us (19%)
  between operations  14.1 us (7%)
  blocking collectives  8.82 us (5%)
    pallas_call x26, Pallas kernels, call(): pl.pallas_call(run, out_shape=tuple((result(t) for t in outs)) + tuple((r...  74.9 us
    ppermute x25, starting transfers between devices, swap_tp(): return lax.ppermute(value, 'tp', pairs(lax.axis_size('tp'), k))  35.3 us
    all_to_all x5, starting transfers between devices, to_cp(): return lax.all_to_all(value, 'cp', 0, 0, tiled=True)  20.6 us
    ppermute x25, waiting for transfers between devices, swap_tp(): return lax.ppermute(value, 'tp', pairs(lax.axis_size('tp'), k))  19.7 us
    all_to_all x5, waiting for transfers between devices, to_cp(): return lax.all_to_all(value, 'cp', 0, 0, tiled=True)  11.5 us
    all_to_all x1, blocking collectives, to_cp(): return lax.all_to_all(value, 'cp', 0, 0, tiled=True)  8.82 us
  transfers between devices with their start and end apart: 33, of which 13 were waited for; matrix products, arithmetic and copies ran while one was open for 0% of the time, Pallas kernels for 33%

profile of v4, /device:TPU:0, one launch (start us, length us, event | category | flops | bytes accessed | tf_op | source)
XLA Modules:
  0.0 189.7 jit_solution(11845766459839771226)
XLA Ops:
  7.3 5.8 %shard_map.213 = (bf16[2,128,2048]{2,1,0:T(8,128)(2,1)}, bf16[128,2048]{1,0:T(8,128)(2,1)}, bf16[8,208,128]{2,1,0:T(8,128)(2,1)}) custom-call(s32[2]{0:T(128)S(1)} %pad_add_fusion.refs_0_, bf16[128,2048]{1,0:T(8,128)(2,1)} %bitcast.36, f32[1,2048]{1,0:T(1,128)} %bitcast.20, bf16[128,2048]{1,0:T(8,128)(2,1)} %bitcast.38, ...), custom_call_target="tpu_custom_call" | custom-call | flops 300000000 | tf_op jit(solution)/shard_map/pallas_call | solution.py:466
  13.1 5.2 %all-to-all-start = ((bf16[8,208,128]{2,1,0:T(8,128)(2,1)}), bf16[8,208,128]{2,1,0:T(8,128)(2,1)S(1)}, u32[]{:S(2)}, u32[]{:S(2)}) async-start(bf16[8,208,128]{2,1,0:T(8,128)(2,1)} %get-tuple-element.77.refs_8_), calls=%async_computation | async-start | bytes 851968 | tf_op jit(solution)/shard_map/all_to_all | solution.py:1144
  20.5 6.4 %all-to-all-done.refs_1_ = bf16[8,208,128]{2,1,0:T(8,128)(2,1)S(1)} async-done(((bf16[8,208,128]{2,1,0:T(8,128)(2,1)}), bf16[8,208,128]{2,1,0:T(8,128)(2,1)S(1)}, u32[]{:S(2)}, u32[]{:S(2)}) %all-to-all-start) | async-done | bytes 426016 | tf_op jit(solution)/shard_map/all_to_all | solution.py:1144
  26.9 3.4 %shard_map.215 = (bf16[8,64,128]{2,1,0:T(8,128)(2,1)}, f32[64,1024]{1,0:T(8,128)}, f32[1,1024]{1,0:T(1,128)}, bf16[8,208,128]{2,1,0:T(8,128)(2,1)}, bf16[2,128,2048]{2,1,0:T(8,128)(2,1)}) custom-call(s32[2]{0:T(128)S(1)} %pad_add_fusion.refs_0_, bf16[8,208,128]{2,1,0:T(8,128)(2,1)S(1)} %all-to-all-done.refs_1_, ...), custom_call_target="tpu_custom_call", output_to_operand_aliasing={{4}: (3, {})} | custom-call | flops 300000000 | tf_op jit(solution)/shard_map/pallas_call | solution.py:466
  30.5 8.8 %all_to_all.30.refs_0_ = bf16[8,64,128]{2,1,0:T(8,128)(2,1)S(1)} all-to-all(bf16[8,64,128]{2,1,0:T(8,128)(2,1)} %get-tuple-element.83), channel_id=1, replica_groups=mesh['tp'=4,'cp'=8] {'cp'}, dimensions={0} | all-to-all | bytes 262144 | tf_op jit(solution)/shard_map/all_to_all | solution.py:1144
  39.9 3.7 %collective-permute-start = (bf16[32,2304]{1,0:T(8,128)(2,1)S(1)}, bf16[32,2304]{1,0:T(8,128)(2,1)S(1)}, u32[]{:S(2)}, u32[]{:S(2)}) collective-permute-start(bf16[32,2304]{1,0:T(8,128)(2,1)S(1)} %get-tuple-element.86), channel_id=1, source_target_pairs={{0,24},{8,16},{16,8},{24,0},{1,25},{9,17},{17,9},{25,1},{2,26},{10... | collective-permute-start | bytes 442376 | tf_op jit(solution)/shard_map/ppermute | solution.py:39
  44.4 6.0 %shard_map.217.refs_6_.refs_5_ = f32[128,2048]{1,0:T(8,128)S(1)} custom-call(bf16[128,2048]{1,0:T(8,128)(2,1)} %get-tuple-element.91.refs_0_, bf16[2048,2048]{1,0:T(8,128)(2,1)} %refs_3_.5, f32[32,2304]{1,0:T(8,128)S(1)} %get-tuple-element.85.refs_2_.refs_0_), custom_call_target="tpu_custom_call" | custom-call | flops 3000000000 | tf_op jit(solution)/shard_map/pallas_call | solution.py:466
  50.4 5.5 %collective-permute-done.1.refs_2_ = bf16[32,2304]{1,0:T(8,128)(2,1)S(1)} collective-permute-done((bf16[32,2304]{1,0:T(8,128)(2,1)S(1)}, bf16[32,2304]{1,0:T(8,128)(2,1)S(1)}, u32[]{:S(2)}, u32[]{:S(2)}) %collective-permute-start.1) | collective-permute-done | bytes 147488 | tf_op jit(solution)/shard_map/ppermute | solution.py:39
  60.8 4.1 %shard_map.219 = (bf16[2048,2048]{1,0:T(8,128)(2,1)S(1)}, bf16[2048,2048]{1,0:T(8,128)(2,1)S(1)}) custom-call(bf16[2048,2048]{1,0:T(8,128)(2,1)} %refs_3_.6, bf16[32,2176]{1,0:T(8,128)(2,1)S(1)} %get-tuple-element.92.refs_1_.refs_0_), custom_call_target="tpu_custom_call" | custom-call | flops 300000000 | tf_op jit(solution)/shard_map/pallas_call | solution.py:466
  65.0 4.6 %collective-permute-done.4.refs_2_ = bf16[32,2176]{1,0:T(8,128)(2,1)S(1)} collective-permute-done((bf16[32,2176]{1,0:T(8,128)(2,1)S(1)}, bf16[32,2176]{1,0:T(8,128)(2,1)S(1)}, u32[]{:S(2)}, u32[]{:S(2)}) %collective-permute-start.4) | collective-permute-done | bytes 139296 | tf_op jit(solution)/shard_map/ppermute | solution.py:39
  84.9 4.2 %all-to-all-start.2 = ((bf16[8,128,512]{2,1,0:T(8,128)(2,1)}), bf16[8,128,512]{2,1,0:T(8,128)(2,1)}, u32[]{:S(2)}, u32[]{:S(2)}) async-start(bf16[8,128,512]{2,1,0:T(8,128)(2,1)} %get-tuple-element.110.refs_0_), calls=%async_computation.2 | async-start | bytes 2097152 | tf_op jit(solution)/shard_map/all_to_all | solution.py:1144
  97.2 5.0 %shard_map.224 = (f32[32,2048]{1,0:T(8,128)}, f32[32,2048]{1,0:T(8,128)}, bf16[64,2048]{1,0:T(8,128)(2,1)}) custom-call(bf16[8,128,512]{2,1,0:T(8,128)(2,1)} %get-tuple-element.110.refs_0_, bf16[2048,2048]{1,0:T(8,128)(2,1)} %refs_3_.5, bf16[2048,2048]{1,0:T(8,128)(2,1)} %refs_3_.5, bf16[2048,2048]{1,0:T(8,128)(2,1)} %refs_3_.5, bf16[2048,2048]{1,0:T(8,128)(2,1)} %refs_3_.5, ...), custom_call_target="tpu_custom_call" | custom-call | flops 20000000000 | tf_op jit(solution)/shard_map/pallas_call | solution.py:466
  106.7 3.5 %all-to-all-done.2.refs_8_.refs_1_ = bf16[8,128,512]{2,1,0:T(8,128)(2,1)} async-done(((bf16[8,128,512]{2,1,0:T(8,128)(2,1)}), bf16[8,128,512]{2,1,0:T(8,128)(2,1)}, u32[]{:S(2)}, u32[]{:S(2)}) %all-to-all-start.2) | async-done | bytes 1048608 | tf_op jit(solution)/shard_map/all_to_all | solution.py:1144
  112.8 3.4 %all-to-all-start.3 = ((bf16[8,128,128]{2,1,0:T(8,128)(2,1)}), bf16[8,128,128]{2,1,0:T(8,128)(2,1)S(1)}, u32[]{:S(2)}, u32[]{:S(2)}) async-start(bf16[8,128,128]{2,1,0:T(8,128)(2,1)} %get-tuple-element.112.refs_6_.refs_5_.refs_2_), calls=%async_computation.3 | async-start | bytes 524288 | tf_op jit(solution)/shard_map/all_to_all | solution.py:1144
  121.6 5.8 %shard_map.227 = (f32[256,2048]{1,0:T(8,128)}, f32[1,256]{1,0:T(1,128)}) custom-call(s32[2]{0:T(128)S(1)} %pad_add_fusion.refs_0_, bf16[8,128,512]{2,1,0:T(8,128)(2,1)} %all-to-all-done.2.refs_8_.refs_1_, bf16[8,2,128,2048]{3,2,1,0:T(8,128)(2,1)} %bitcast.41, bf16[2048,2048]{1,0:T(8,128)(2,1)} %refs_3_.5, f32[1,2048]{1,0:T(1,128)S(1)} %bitcast.24, ...), custom_call_target="tpu_custom_call" | custom-call | flops 20000000000 | tf_op jit(solution)/shard_map/pallas_call | solution.py:466
  127.5 3.7 %shard_map.229 = (bf16[8,192,128]{2,1,0:T(8,128)(2,1)}, bf16[8,64,128]{2,1,0:T(8,128)(2,1)}) custom-call(s32[2]{0:T(128)S(1)} %pad_add_fusion.refs_0_, bf16[8,208,128]{2,1,0:T(8,128)(2,1)S(1)} %get-tuple-element.113.refs_1_, bf16[8,128,128]{2,1,0:T(8,128)(2,1)S(1)} %all-to-all-done.3.refs_2_, f32[64,1024]{1,0:T(8,128)S(1)} %get-tuple-element.114.refs_3_, ...), custom_call_target="tpu_custom_call" | custom-call | flops 8000000000 | tf_op jit(solution)/shard_map/pallas_call | solution.py:466
  131.2 4.2 %all-to-all-start.4 = ((bf16[8,192,128]{2,1,0:T(8,128)(2,1)}), bf16[8,192,128]{2,1,0:T(8,128)(2,1)S(1)}, u32[]{:S(2)}, u32[]{:S(2)}) async-start(bf16[8,192,128]{2,1,0:T(8,128)(2,1)} %get-tuple-element.122.refs_4_.refs_1_), calls=%async_computation.4 | async-start | bytes 786432 | tf_op jit(solution)/shard_map/all_to_all | solution.py:1144
  136.4 4.5 %shard_map.232 = bf16[8,192,256]{2,1,0:T(8,128)(2,1)} custom-call(s32[2]{0:T(128)S(1)} %pad_add_fusion.refs_0_, bf16[8,192,128]{2,1,0:T(8,128)(2,1)} %get-tuple-element.122.refs_4_.refs_1_, bf16[8,2,128,2048]{3,2,1,0:T(8,128)(2,1)} %bitcast.42, bf16[32,2048]{1,0:T(8,128)(2,1)S(1)} %shard_map.231.refs_3_.refs_0_), custom_call_target="tpu_custom_call" | custom-call | flops 20000000000 | tf_op jit(solution)/shard_map/pallas_call | solution.py:466
  143.8 3.5 %all-to-all-start.5 = ((bf16[8,192,256]{2,1,0:T(8,128)(2,1)}), bf16[8,192,256]{2,1,0:T(8,128)(2,1)S(1)}, u32[]{:S(2)}, u32[]{:S(2)}) async-start(bf16[8,192,256]{2,1,0:T(8,128)(2,1)} %shard_map.232), calls=%async_computation.5 | async-start | bytes 1572864 | tf_op jit(solution)/shard_map/all_to_all | solution.py:1144
  147.3 4.5 %shard_map.230 = (f32[32,2048]{1,0:T(8,128)S(1)}, bf16[32,2048]{1,0:T(8,128)(2,1)S(1)}, bf16[32,2048]{1,0:T(8,128)(2,1)S(1)}, bf16[32,2048]{1,0:T(8,128)(2,1)S(1)}) custom-call(bf16[8,192,128]{2,1,0:T(8,128)(2,1)S(1)} %all-to-all-done.4.refs_0_, bf16[3,2048,512]{2,1,0:T(8,128)(2,1)} %bitcast.32, bf16[3,2048,512]{2,1,0:T(8,128)(2,1)} %bitcast.33, ...), custom_call_target="tpu_custom_call" | custom-call | flops 10000000000 | tf_op jit(solution)/shard_map/pallas_call | solution.py:466
  156.5 5.6 %shard_map.233 = (f32[256,2048]{1,0:T(8,128)}, f32[1,256]{1,0:T(1,128)S(1)}) custom-call(s32[2]{0:T(128)S(1)} %pad_add_fusion.refs_0_, bf16[8,128,512]{2,1,0:T(8,128)(2,1)} %all-to-all-done.2.refs_8_.refs_1_, bf16[8,128,2048]{2,1,0:T(8,128)(2,1)} %bitcast.43, bf16[2048,2048]{1,0:T(8,128)(2,1)} %refs_3_.6, f32[1,2048]{1,0:T(1,128)S(1)} %bitcast.26, ...), custom_call_target="tpu_custom_call" | custom-call | flops 20000000000 | tf_op jit(solution)/shard_map/pallas_call | solution.py:466
  162.1 3.1 %shard_map.234 = (f32[3,256,512]{2,1,0:T(8,128)}, f32[8,256]{1,0:T(8,128)S(1)}) custom-call(s32[2]{0:T(128)S(1)} %pad_add_fusion.refs_0_, bf16[8,192,256]{2,1,0:T(8,128)(2,1)S(1)} %all-to-all-done.5.refs_1_, bf16[3,2048,512]{2,1,0:T(8,128)(2,1)} %bitcast.35, f32[1,2048]{1,0:T(1,128)S(1)} %bitcast.22, f32[1,256]{1,0:T(1,128)S(1)} %get-tuple-element.131.refs_4_, ...), custom_call_target="tpu_custom_call" | custom-call | flops 20000000000 | tf_op jit(solution)/shard_map/pallas_call | solution.py:466
  170.8 3.7 %all-gather.11.cloned.1.call-done = bf16[1024,2048]{1,0:T(8,128)(2,1)} async-done(((bf16[128,2048]{1,0:T(8,128)(2,1)}), bf16[1024,2048]{1,0:T(8,128)(2,1)}) %all-gather.11.cloned.1.call-update) | async-done | bytes 4194320 | tf_op jit(solution)/shard_map/all_gather | solution.py:1269
  174.5 4.8 %shard_map.237 = (f32[64,2048]{1,0:T(8,128)}, f32[1,64]{1,0:T(1,128)}) custom-call(s32[2]{0:T(128)S(1)} %pad_add_fusion.refs_0_, bf16[8,64,128]{2,1,0:T(8,128)(2,1)} %get-tuple-element.134.refs_1_, bf16[8,128,2048]{2,1,0:T(8,128)(2,1)} %bitcast.44, bf16[512,2048]{1,0:T(8,128)(2,1)} %refs_3_.7, f32[1,512]{1,0:T(1,128)S(1)} %bitcast.28, ...), custom_call_target="tpu_custom_call" | custom-call | flops 20000000000 | tf_op jit(solution)/shard_map/pallas_call | solution.py:466
  (81 shorter events, 62.3 us)
Async XLA Ops:
  13.1 13.9 %all-to-all-start = ((bf16[8,208,128]{2,1,0:T(8,128)(2,1)}), bf16[8,208,128]{2,1,0:T(8,128)(2,1)S(1)}, u32[]{:S(2)}, u32[]{:S(2)}) async-start(bf16[8,208,128]{2,1,0:T(8,128)(2,1)} %get-tuple-element.77.refs_8_), calls=%async_computation | async-start | bytes 851968 | tf_op jit(solution)/shard_map/all_to_all | solution.py:1144
  18.2 103.4 %all-gather.7.cloned.1.call-start = ((), (), s32[]{:S(2)}) async-start(), calls=%async_computation.6 | async-start | bytes 9437184 | tf_op jit(solution)/shard_map/all_gather | solution.py:1180
  30.4 126.0 %all-gather.9.cloned.1.call-start = ((), (), s32[]{:S(2)}) async-start(), calls=%async_computation.7 | async-start | bytes 4718592 | tf_op jit(solution)/shard_map/all_gather | solution.py:1221
  39.9 10.4 %collective-permute-start = (bf16[32,2304]{1,0:T(8,128)(2,1)S(1)}, bf16[32,2304]{1,0:T(8,128)(2,1)S(1)}, u32[]{:S(2)}, u32[]{:S(2)}) collective-permute-start(bf16[32,2304]{1,0:T(8,128)(2,1)S(1)} %get-tuple-element.86), channel_id=1, source_target_pairs={{0,24},{8,16},{16,8},{24,0},{1,25},{9,17},{17,9},{25,1},{2,26},{10... | collective-permute-start | bytes 442376 | tf_op jit(solution)/shard_map/ppermute | solution.py:39
  43.6 12.3 %collective-permute-start.1 = (bf16[32,2304]{1,0:T(8,128)(2,1)S(1)}, bf16[32,2304]{1,0:T(8,128)(2,1)S(1)}, u32[]{:S(2)}, u32[]{:S(2)}) collective-permute-start(bf16[32,2304]{1,0:T(8,128)(2,1)S(1)} %get-tuple-element.87), channel_id=1, source_target_pairs={{0,16},{8,24},{16,0},{24,8},{1,17},{9,25},{17,1},{25,9},{2,18},{10... | collective-permute-start | bytes 442376 | tf_op jit(solution)/shard_map/ppermute | solution.py:39
  43.6 12.3 %collective-permute-start.2 = (bf16[32,2304]{1,0:T(8,128)(2,1)S(1)}, bf16[32,2304]{1,0:T(8,128)(2,1)S(1)}, u32[]{:S(2)}, u32[]{:S(2)}) collective-permute-start(bf16[32,2304]{1,0:T(8,128)(2,1)S(1)} %get-tuple-element.88), channel_id=1, source_target_pairs={{0,8},{8,0},{16,24},{24,16},{1,9},{9,1},{17,25},{25,17},{2,10},{10... | collective-permute-start | bytes 442376 | tf_op jit(solution)/shard_map/ppermute | solution.py:39
  59.0 10.6 %collective-permute-start.4 = (bf16[32,2176]{1,0:T(8,128)(2,1)S(1)}, bf16[32,2176]{1,0:T(8,128)(2,1)S(1)}, u32[]{:S(2)}, u32[]{:S(2)}) collective-permute-start(bf16[32,2176]{1,0:T(8,128)(2,1)S(1)} %get-tuple-element.92.refs_1_.refs_0_), channel_id=1, source_target_pairs={{0,16},{8,24},{16,0},{24,8},{1,17},{9,25},{17,1},{25,9},{2,18},{10... | collective-permute-start | bytes 417800 | tf_op jit(solution)/shard_map/ppermute | solution.py:39
  59.0 10.6 %collective-permute-start.5 = (bf16[32,2176]{1,0:T(8,128)(2,1)S(1)}, bf16[32,2176]{1,0:T(8,128)(2,1)S(1)}, u32[]{:S(2)}, u32[]{:S(2)}) collective-permute-start(bf16[32,2176]{1,0:T(8,128)(2,1)S(1)} %get-tuple-element.92.refs_1_.refs_0_), channel_id=1, source_target_pairs={{0,8},{8,0},{16,24},{24,16},{1,9},{9,1},{17,25},{25,17},{2,10},{10... | collective-permute-start | bytes 417800 | tf_op jit(solution)/shard_map/ppermute | solution.py:39
  84.9 25.3 %all-to-all-start.2 = ((bf16[8,128,512]{2,1,0:T(8,128)(2,1)}), bf16[8,128,512]{2,1,0:T(8,128)(2,1)}, u32[]{:S(2)}, u32[]{:S(2)}) async-start(bf16[8,128,512]{2,1,0:T(8,128)(2,1)} %get-tuple-element.110.refs_0_), calls=%async_computation.2 | async-start | bytes 2097152 | tf_op jit(solution)/shard_map/all_to_all | solution.py:1144
  92.8 11.7 %collective-permute-start.12 = (bf16[32,2176]{1,0:T(8,128)(2,1)S(1)}, bf16[32,2176]{1,0:T(8,128)(2,1)S(1)}, u32[]{:S(2)}, u32[]{:S(2)}) collective-permute-start(bf16[32,2176]{1,0:T(8,128)(2,1)S(1)} %get-tuple-element.107.refs_2_.refs_5_.refs_0_), channel_id=1, source_target_pairs={{0,24},{8,16},{16,8},{24,0},{1,25},{9,17},{17,9},{25,1},{2,26},{10... | collective-permute-start | bytes 417800 | tf_op jit(solution)/shard_map/ppermute | solution.py:39
  94.9 11.8 %collective-permute-start.13 = (bf16[32,2176]{1,0:T(8,128)(2,1)S(1)}, bf16[32,2176]{1,0:T(8,128)(2,1)S(1)}, u32[]{:S(2)}, u32[]{:S(2)}) collective-permute-start(bf16[32,2176]{1,0:T(8,128)(2,1)S(1)} %get-tuple-element.107.refs_2_.refs_5_.refs_0_), channel_id=1, source_target_pairs={{0,16},{8,24},{16,0},{24,8},{1,17},{9,25},{17,1},{25,9},{2,18},{10... | collective-permute-start | bytes 417800 | tf_op jit(solution)/shard_map/ppermute | solution.py:39
  112.8 14.7 %all-to-all-start.3 = ((bf16[8,128,128]{2,1,0:T(8,128)(2,1)}), bf16[8,128,128]{2,1,0:T(8,128)(2,1)S(1)}, u32[]{:S(2)}, u32[]{:S(2)}) async-start(bf16[8,128,128]{2,1,0:T(8,128)(2,1)} %get-tuple-element.112.refs_6_.refs_5_.refs_2_), calls=%async_computation.3 | async-start | bytes 524288 | tf_op jit(solution)/shard_map/all_to_all | solution.py:1144
  116.2 58.3 %all-gather.11.cloned.1.call-start = ((), (), s32[]{:S(2)}) async-start(), calls=%async_computation.8 | async-start | bytes 4718592 | tf_op jit(solution)/shard_map/all_gather | solution.py:1269
  119.8 15.6 %collective-permute-start.19 = (bf16[32,2048]{1,0:T(8,128)(2,1)S(1)}, bf16[32,2048]{1,0:T(8,128)(2,1)S(1)}, u32[]{:S(2)}, u32[]{:S(2)}) collective-permute-start(bf16[32,2048]{1,0:T(8,128)(2,1)S(1)} %shard_map.228.refs_8_), channel_id=1, source_target_pairs={{0,16},{8,24},{16,0},{24,8},{1,17},{9,25},{17,1},{25,9},{2,18},{10... | collective-permute-start | bytes 393224 | tf_op jit(solution)/shard_map/ppermute | solution.py:39
  131.2 12.5 %all-to-all-start.4 = ((bf16[8,192,128]{2,1,0:T(8,128)(2,1)}), bf16[8,192,128]{2,1,0:T(8,128)(2,1)S(1)}, u32[]{:S(2)}, u32[]{:S(2)}) async-start(bf16[8,192,128]{2,1,0:T(8,128)(2,1)} %get-tuple-element.122.refs_4_.refs_1_), calls=%async_computation.4 | async-start | bytes 786432 | tf_op jit(solution)/shard_map/all_to_all | solution.py:1144
  140.9 15.4 %collective-permute-start.23 = (bf16[32,2048]{1,0:T(8,128)(2,1)S(1)}, bf16[32,2048]{1,0:T(8,128)(2,1)S(1)}, u32[]{:S(2)}, u32[]{:S(2)}) collective-permute-start(bf16[32,2048]{1,0:T(8,128)(2,1)S(1)} %shard_map.231.refs_3_.refs_0_), channel_id=1, source_target_pairs={{0,16},{8,24},{16,0},{24,8},{1,17},{9,25},{17,1},{25,9},{2,18},{10... | collective-permute-start | bytes 393224 | tf_op jit(solution)/shard_map/ppermute | solution.py:39
  143.8 18.3 %all-to-all-start.5 = ((bf16[8,192,256]{2,1,0:T(8,128)(2,1)}), bf16[8,192,256]{2,1,0:T(8,128)(2,1)S(1)}, u32[]{:S(2)}, u32[]{:S(2)}) async-start(bf16[8,192,256]{2,1,0:T(8,128)(2,1)} %shard_map.232), calls=%async_computation.5 | async-start | bytes 1572864 | tf_op jit(solution)/shard_map/all_to_all | solution.py:1144
  151.8 13.4 %collective-permute-start.16 = (bf16[32,2048]{1,0:T(8,128)(2,1)S(1)}, bf16[32,2048]{1,0:T(8,128)(2,1)S(1)}, u32[]{:S(2)}, u32[]{:S(2)}) collective-permute-start(bf16[32,2048]{1,0:T(8,128)(2,1)S(1)} %get-tuple-element.124), channel_id=1, source_target_pairs={{0,24},{8,16},{16,8},{24,0},{1,25},{9,17},{17,9},{25,1},{2,26},{10... | collective-permute-start | bytes 393224 | tf_op jit(solution)/shard_map/ppermute | solution.py:39
  153.4 12.5 %collective-permute-start.17 = (bf16[32,2048]{1,0:T(8,128)(2,1)S(1)}, bf16[32,2048]{1,0:T(8,128)(2,1)S(1)}, u32[]{:S(2)}, u32[]{:S(2)}) collective-permute-start(bf16[32,2048]{1,0:T(8,128)(2,1)S(1)} %get-tuple-element.125), channel_id=1, source_target_pairs={{0,16},{8,24},{16,0},{24,8},{1,17},{9,25},{17,1},{25,9},{2,18},{10... | collective-permute-start | bytes 393224 | tf_op jit(solution)/shard_map/ppermute | solution.py:39
  153.6 12.3 %collective-permute-start.18 = (bf16[32,2048]{1,0:T(8,128)(2,1)S(1)}, bf16[32,2048]{1,0:T(8,128)(2,1)S(1)}, u32[]{:S(2)}, u32[]{:S(2)}) collective-permute-start(bf16[32,2048]{1,0:T(8,128)(2,1)S(1)} %get-tuple-element.126), channel_id=1, source_target_pairs={{0,8},{8,0},{16,24},{24,16},{1,9},{9,1},{17,25},{25,17},{2,10},{10... | collective-permute-start | bytes 393224 | tf_op jit(solution)/shard_map/ppermute | solution.py:39
  156.3 23.0 %collective-permute-start.24 = (bf16[64,2048]{1,0:T(8,128)(2,1)S(1)}, bf16[64,2048]{1,0:T(8,128)(2,1)S(1)}, u32[]{:S(2)}, u32[]{:S(2)}) collective-permute-start(bf16[64,2048]{1,0:T(8,128)(2,1)S(1)} %shard_map.236.refs_5_), channel_id=1, source_target_pairs={{0,8},{8,0},{16,24},{24,16},{1,9},{9,1},{17,25},{25,17},{2,10},{10... | collective-permute-start | bytes 786440 | tf_op jit(solution)/shard_map/ppermute | solution.py:39
  166.3 13.0 %collective-permute-start.20 = (bf16[32,2176]{1,0:T(8,128)(2,1)S(1)}, bf16[32,2176]{1,0:T(8,128)(2,1)S(1)}, u32[]{:S(2)}, u32[]{:S(2)}) collective-permute-start(bf16[32,2176]{1,0:T(8,128)(2,1)S(1)} %shard_map.235.refs_5_.refs_1_), channel_id=1, source_target_pairs={{0,24},{8,16},{16,8},{24,0},{1,25},{9,17},{17,9},{25,1},{2,26},{10... | collective-permute-start | bytes 417800 | tf_op jit(solution)/shard_map/ppermute | solution.py:39
  168.7 12.3 %collective-permute-start.21 = (bf16[32,2176]{1,0:T(8,128)(2,1)S(1)}, bf16[32,2176]{1,0:T(8,128)(2,1)S(1)}, u32[]{:S(2)}, u32[]{:S(2)}) collective-permute-start(bf16[32,2176]{1,0:T(8,128)(2,1)S(1)} %shard_map.235.refs_5_.refs_1_), channel_id=1, source_target_pairs={{0,16},{8,24},{16,0},{24,8},{1,17},{9,25},{17,1},{25,9},{2,18},{10... | collective-permute-start | bytes 417800 | tf_op jit(solution)/shard_map/ppermute | solution.py:39
  169.2 11.8 %collective-permute-start.22 = (bf16[32,2176]{1,0:T(8,128)(2,1)S(1)}, bf16[32,2176]{1,0:T(8,128)(2,1)S(1)}, u32[]{:S(2)}, u32[]{:S(2)}) collective-permute-start(bf16[32,2176]{1,0:T(8,128)(2,1)S(1)} %shard_map.235.refs_5_.refs_1_), channel_id=1, source_target_pairs={{0,8},{8,0},{16,24},{24,16},{1,9},{9,1},{17,25},{25,17},{2,10},{10... | collective-permute-start | bytes 417800 | tf_op jit(solution)/shard_map/ppermute | solution.py:39
  (13 other events, 112.2 us)
Sparse Core Ops, SparseCore 0:
  30.5 53.7 all-gather.6
  86.8 44.6 all-gather.8
  133.9 40.5 all-gather.10

commit v5 on v4

--- a/solution.py
+++ b/solution.py
@@ -620,12 +620,12 @@
     blocks, _, rows = got.shape
     part = rows // parts
     gather_heads(got, keys, ids_col)
-    group = 2 if blocks % 2 == 0 else 1
+    group = 4 if blocks % 4 == 0 else 1
     width = group * rows
     for i in range(blocks // group):
         mine = range(i * group, (i + 1) * group)
         query = jnp.concatenate([got[j, :HD, :] for j in mine], axis=1) * bf16(HD**-0.5)
-        ids_row = jnp.concatenate([got[j, 3 * HD : 3 * HD + 1, :] for j in mine], axis=1).astype(f32)
+        ids_row = jnp.concatenate([got[j, 3 * HD : 3 * HD + 16, :].astype(f32)[:1] for j in mine], axis=1)
         count = (i + 1) * width
         scores = dot(keys[0:count, :], query)
         allowed = visible_scores(me, part, scores, ids_col, ids_row, count, rows, width)
@@ -650,17 +650,6 @@
         own[:, total.shape[1] :] = extra[:part]
         for k, piece in enumerate(pieces, 1):
             piece[:, total.shape[1] :] = extra[k * part : (k + 1) * part].astype(bf16)
-
-
-def fold_row(row, part):
-    block = jnp.concatenate([row[:, i : i + 128] for i in range(0, row.shape[1], 128)], axis=0)
-    return jnp.concatenate(split_low(block), axis=0)
-
-
-def unfold_row(block):
-    half = block.shape[0] // 2
-    total = block[:half].astype(f32) + block[half:].astype(f32)
-    return jnp.concatenate([total[i : i + 1] for i in range(half)], axis=1)
 
 
 def out_kernel(parts, att, gain, weight, own, *refs):
@@ -678,26 +667,33 @@
     gain_rows = jnp.where(row == 0, gain_high, jnp.where(row == 1, gain_low, 0.0))
     left = jnp.concatenate([(centred * gains).astype(bf16), gain_rows.astype(bf16)], axis=0)
     total = dot(left, weight[...])
-    folded = fold_row(total[rows : rows + 1] + total[rows + 1 : rows + 2], part)
-    stats = lanes_of([high, low, *square], rows).astype(bf16)
+    gain_row = total[rows : rows + 1] + total[rows + 1 : rows + 2]
+    gain_block = jnp.concatenate([gain_row[:, i : i + 128] for i in range(0, width, 128)], axis=0)
+    stats = lanes_of([high, low, *square], rows).T
+    empty = jnp.zeros((part - gain_block.shape[0] - 1, 128), f32)
+
+    def extra(k):
+        row = jnp.concatenate([stats[i : i + 1, k * part : (k + 1) * part] for i in range(4)], axis=1)
+        return jnp.concatenate([gain_block, row, empty], axis=0).astype(bf16)
+
     own[:, :width] = total[:part]
-    own[:, width : width + 128] = stats[:part].astype(f32)
-    own[:, width + 128 :] = folded.astype(f32)
+    own[:, width:] = extra(0).astype(f32)
     for k, piece in enumerate(pieces, 1):
         here = slice(k * part, (k + 1) * part)
         piece[:, :width] = total[here].astype(bf16)
-        piece[:, width : width + 128] = stats[here]
-        piece[:, width + 128 :] = folded
+        piece[:, width:] = extra(k)
 
 
 def middle_kernel(parts, head_width, own, *refs):
-    got, (x, gain, x1, u, gain_row) = refs[: parts - 1][::-1], refs[parts - 1 :]
+    got, (x, gain, x1, u, gain_row, norms) = refs[: parts - 1][::-1], refs[parts - 1 :]
     part, width = x1.shape
     blocks = [own] + list(got)
-    stats = [b[:, width : width + 128] for b in blocks]
-    means = [pair_sum(b, 0) for b in stats]
-    squares = [pair_sum(b, 2) for b in stats]
-    rows = [unfold_row(b[:, width + 128 :]) for b in blocks]
+    extras = [b[:, width:].astype(f32) for b in blocks]
+    count = width // 128
+    rows = [jnp.concatenate([e[i : i + 1] for i in range(count)], axis=1) for e in extras]
+    columns = [jnp.broadcast_to(e[count : count + 1], (128, 128)).T[:, 0:1] for e in extras]
+    means = [c[:part] + c[part : 2 * part] for c in columns]
+    squares = [c[2 * part : 3 * part] + c[3 * part :] for c in columns]
     gain_row[...] = sum(rows)
     mean = sum(means) / parts
     spread = sum(squares) + head_width * sum((m - mean) * (m - mean) for m in means)
@@ -708,8 +704,9 @@
     value = x[...].astype(f32) + total * scaling
     x1[...] = value
     normed, _ = norm_rows(value)
-    u[:, :width] = (normed * gain[...]).astype(bf16)
-    u[:, width:] = lanes_of([*split_low(mean), *split_low(scaling)], part).astype(bf16)
+    u[...] = (normed * gain[...]).astype(bf16)
+    norms[...] = jnp.zeros_like(norms)
+    norms[0:2, :part] = lanes_of([mean, scaling], part).T[0:2, :]
 
 
 def grad_hidden_kernel(gy, weight, grad):
@@ -728,12 +725,11 @@
 
 def up_kernel(parts, step, own, *refs):
     got, refs = refs[: parts - 1][::-1], refs[parts - 1 :]
-    weight, grad, gain, act, slope, u, stats, tail, rows_u = refs
+    weight, grad, gain, norms, act, slope, u, stats, rows_u = refs
     part = own.shape[0]
     rows, width = rows_u.shape
     for k, block in enumerate([own] + list(got)):
-        rows_u[k * part : (k + 1) * part, :] = block[:, :width]
-        tail[k * part : (k + 1) * part, :] = block[:, width:].astype(f32)
+        rows_u[k * part : (k + 1) * part, :] = block[...]
     wide = u.shape[2]
     for j in range(u.shape[0]):
         u[j] = rows_u[:, j * wide : (j + 1) * wide]
@@ -752,6 +748,7 @@
                 total[n] = total[n] + column[:, j : j + 128]
     sums = lanes_of([jnp.sum(t, axis=1, keepdims=True) for t in total], rows)
     stats[...] = sums.T[:8, :]
+    stats[4:6, :] = norms[0:2, :]
 
 
 def swap_lane_blocks(value, k, part):
@@ -772,8 +769,8 @@
 
 def hidden_back_kernel(parts, full, step, own, *refs):
     got, refs = refs[: parts - 1][::-1], refs[parts - 1 :]
-    act, slope, grad, gain, weight, u, gh, both, own_out = refs[:9]
-    pieces = refs[9:]
+    act, slope, grad, gain, weight, u, gh, both, norms, own_out = refs[:10]
+    pieces = refs[10:]
     first_wide = u.shape[2]
     both[:, :, :first_wide] = u[...]
     rows = act.shape[0]
@@ -781,6 +778,9 @@
     total = own[...]
     for k, block in enumerate(got, 1):
         total = total + swap_lane_blocks(block[...], k, part)
+    norms[...] = jnp.zeros_like(norms)
+    for k, block in enumerate([own] + list(got)):
+        norms[0:2, k * part : (k + 1) * part] = block[4:6, :part]
     mean = total[0:1] / full
     scaling = lax.rsqrt(total[1:2] / full - mean * mean + eps)
     first = total[2:3] / full
@@ -867,9 +867,7 @@
     columns = jnp.concatenate([b[:, width:].astype(f32) for b in [own] + list(got)], axis=0).T
     first = columns[0:1] + columns[1:2]
     cross = columns[2:3] + columns[3:4]
-    columns = stats[...].T
-    mean = columns[0:1] + columns[1:2]
-    scaling = columns[2:3] + columns[3:4]
+    mean, scaling = stats[0:1], stats[1:2]
     grad = dot_t(weight[...], gb[...])
     value = jnp.concatenate([att[j].astype(f32) for j in range(blocks)], axis=0)
     normed = (value - mean) * scaling
@@ -912,7 +910,7 @@
     for i in range(blocks // group):
         mine = range(i * group, (i + 1) * group)
         query = jnp.concatenate([got[j, :HD, :] for j in mine], axis=1) * bf16(HD**-0.5)
-        ids_row = jnp.concatenate([got[j, 3 * HD : 3 * HD + 1, :] for j in mine], axis=1).astype(f32)
+        ids_row = jnp.concatenate([got[j, 3 * HD : 3 * HD + 16, :].astype(f32)[:1] for j in mine], axis=1)
         go = jnp.concatenate([grads[j, :HD, :] for j in mine], axis=1)
         span = slice(i * width, (i + 1) * width)
         delta = jnp.sum(go.astype(f32) * mixed[:, span], axis=0, keepdims=True)
@@ -935,17 +933,23 @@
         out[j, 2 * HD :, :] = gv[:, span].astype(bf16)
 
 
-def input_back_kernel(parts, step, got, w0, w1, w2, own_out, *pieces):
+def input_back_kernel(parts, got, *refs):
+    weights, own_out, pieces = refs[:6], refs[6], refs[7:]
     part, width = own_out.shape
+    half = width // 2
     grads = []
     for c in range(3):
         here = slice(c * HD, (c + 1) * HD)
         grad = jnp.concatenate([got[j, here, :].astype(f32) for j in range(got.shape[0])], axis=0)
         grads.append(grad.T.astype(bf16))
-    result = dot_t(grads[0], w0[0]) + dot_t(grads[1], w1[0]) + dot_t(grads[2], w2[0])
-    own_out[...] = result[:part]
-    for k, piece in enumerate(pieces, 1):
-        piece[...] = result[k * part : (k + 1) * part].astype(bf16)
+    totals = [0.0, 0.0]
+    for n, weight in enumerate(weights):
+        totals[n % 2] = totals[n % 2] + dot_t(grads[n // 2], weight[0])
+    for h, result in enumerate(totals):
+        here = slice(h * half, (h + 1) * half)
+        own_out[:, here] = result[:part]
+        for k, piece in enumerate(pieces, 1):
+            piece[:, here] = result[k * part : (k + 1) * part].astype(bf16)
 
 
 def final_kernel(parts, own, *refs):
@@ -1074,20 +1078,23 @@
 
 
 def outputs_kernel(parts, ids, *refs):
-    blocks, (y_even, y_odd, out, y, first, second) = refs[:parts], refs[parts:]
+    blocks, (out, first, second) = refs[:parts], refs[parts:]
     part, width = blocks[0].shape[0], out.shape[1]
     for k in range(parts):
         out[block_at(ids[0], k, part), :] = blocks[-k % parts][:, :width]
-        both = y_odd if k % 2 else y_even
-        y[block_at(ids[0], k, part), :] = both[k // 2 * part : (k // 2 + 1) * part, :]
     out.send()
-    y.send()
     count = first.shape[1] // 128
     total = sum(b[:, width:].astype(f32) for b in blocks)
     total = total[: 2 * count] + total[2 * count : 4 * count]
     for i in range(count):
         first[:, i * 128 : (i + 1) * 128] = total[i : i + 1]
         second[:, i * 128 : (i + 1) * 128] = total[count + i : count + i + 1]
+
+
+def layer_output_kernel(ids, even, odd, out):
+    part = even.shape[0] // 2
+    for k in range(4):
+        out[block_at(ids[0], k, part), :] = (odd if k % 2 else even)[k // 2 * part : (k // 2 + 1) * part, :]
 
 
 def body(
@@ -1154,6 +1161,8 @@
 
     cols, first_rows = lambda i, *_: (0, i), lambda i, *_: (i, 0)
     origin2, origin3 = lambda i, *_: (0, 0), lambda i, *_: (0, 0, 0)
+    sixth = lambda c, h: lambda ids: (pl.ds(c, 1), pl.ds(h * width // 2, width // 2), slice(None))
+    weight_sixths = [Far(weight3, (1, width // 2, head_width), sixth(c, h)) for c in range(3) for h in range(2)]
     weight_thirds = [Far(weight3, (1, width, head_width), third(c)) for c in range(3)]
 
     pair, gy_x, sent = call(
@@ -1181,7 +1190,7 @@
 
     own, *pieces, near_att = call(
         functools.partial(out_kernel, T),
-        piece_shapes(width + 256) + [Near(shape((C, HD, rows), bf16))],
+        piece_shapes(wide_part) + [Near(shape((C, HD, rows), bf16))],
         [att, near_heads, near_out],
     )
     (grad_hid,) = call(
@@ -1191,9 +1200,9 @@
         [pl.BlockSpec((rows, step), cols)],
         grid=(hidden // step,), after=[own], mb=10, cost=3,
     )
-    x1, u_own, gain_row = call(
+    x1, u_own, gain_row, norms = call(
         functools.partial(middle_kernel, T, head_width),
-        [Near(shape((part, width), f32)), shape((part, wide_part), bf16), Near(shape((1, width), f32))],
+        [Near(shape((part, width), f32)), shape((part, width), bf16), Near(shape((1, width), f32)), Near(shape((8, 128), f32))],
         [own, *exchange(pieces), near_x, near_mid], after=[grad_hid],
     )
     u_blocks = [u_own] + spread(u_own)
@@ -1204,16 +1213,16 @@
         scratch=[pltpu.SemaphoreType.DMA((width // 256,))], after=[u_own], mb=6,
     )
 
-    act, slope, u_cols, stats, near_tail = call(
+    act, slope, u_cols, stats = call(
         functools.partial(up_kernel, T, step),
         [Near(shape((rows, hidden), f32)), Near(shape((rows, hidden), f32)), Near(shape((C, rows, wide), bf16)),
-         shape((8, rows), f32), Near(shape((rows, 128), f32))],
-        [*u_blocks, near_up, grad_hid, near_hid],
+         shape((8, rows), f32)],
+        [*u_blocks, near_up, grad_hid, near_hid, norms],
         scratch=[pltpu.VMEM((rows, width), bf16)], mb=8, after=[near_flip],
     )
-    gh, both, own, *pieces = call(
+    gh, both, norms, own, *pieces = call(
         functools.partial(hidden_back_kernel, T, FF, step),
-        [Far(shape((rows, hidden), bf16)), Far(shape((C, rows, wide + high), bf16))] + piece_shapes(width),
+        [Far(shape((rows, hidden), bf16)), Far(shape((C, rows, wide + high), bf16)), Near(shape((8, rows), f32))] + piece_shapes(width),
         [stats, *spread(stats), act, slope, grad_hid, near_hid, near_flip, u_cols], mb=10,
     )
     gu_got = exchange(pieces)
@@ -1263,7 +1272,7 @@
     sent, gb, y_odd = call(
         functools.partial(heads_back_kernel, T),
         [Far(shape((C, 2 * HD, rows), bf16)), Far(shape((rows, width), bf16))],
-        [*gb_blocks, near_tail, near_att, near_heads, near_out], after=[Pin(both_got)], carry=[y_odd],
+        [*gb_blocks, norms, near_att, near_heads, near_out], after=[Pin(both_got)], carry=[y_odd],
     )
     y_got = swap_tp(y_odd, 1)
     gb_all = lax.all_gather(gb, "cp", axis=0)
@@ -1289,7 +1298,7 @@
     y_even = swap_tp(y_low, 2)
     (grad_qkv,) = product(gq_sent, early, False, 0, 0, 3 * HD, [y_low])
     own, *pieces = call(
-        functools.partial(input_back_kernel, T, step), piece_shapes(width), [gq, *weight_thirds], mb=10, cost=10,
+        functools.partial(input_back_kernel, T), piece_shapes(width), [gq, *weight_sixths], mb=10, cost=10,
     )
     ga_got = exchange(pieces)
     (y_even,) = call(join_kernel, [shape((2 * part, width), bf16)], [y_low, y_even], after=[own])
@@ -1310,10 +1319,14 @@
     )
     final_blocks = [final] + spread(final)
     grad_out, heads_gain_grad = product(z, gb_all, False, None, 0, HD, [final], out_weight, gain_heads)
-    grad_input, layer_output, input_gain_grad, middle_gain_grad = call(
+    (layer_output,) = call(
+        layer_output_kernel, [Far(shape((rows, width), bf16))], [ids, y_even, y_odd], [scalars(), whole(), whole()],
+        after=[final],
+    )
+    grad_input, input_gain_grad, middle_gain_grad = call(
         functools.partial(outputs_kernel, T),
-        [Far(shape((rows, width), bf16))] * 2 + [shape((1, wide), f32), shape((1, wide), f32)],
-        [ids, *final_blocks, y_even, y_odd], [scalars()] + [whole()] * (T + 2), after=[Pin(grad_out)],
+        [Far(shape((rows, width), bf16)), shape((1, wide), f32), shape((1, wide), f32)],
+        [ids, *final_blocks], [scalars()] + [whole()] * T, after=[Pin(grad_out), Pin(layer_output)],
     )
     return (
         layer_output.reshape(layer_input.shape),

time: 191 us -> 188 us (0.984)
  waiting for transfers between devices: 35.5 us -> 33.1 us
    pallas_call x26 -> x27, Pallas kernels: 74.9 us -> 75.6 us  [call(): pl.pallas_call(run, out_shape=tuple((result(t) for t in outs)) + tuple((r...]
  transfers between devices with their start and end apart: 33 -> 33, of which waited for: 13 -> 13; matrix products, arithmetic and copies ran while one was open for 0% -> 0% of each run, Pallas kernels for 33% -> 34%
where the time goes in v5:
time: 188 us
  Pallas kernels  75.6 us (40%)
  starting transfers between devices  55.7 us (30%)
  waiting for transfers between devices  33.1 us (18%)
  between operations  14.1 us (8%)
  blocking collectives  8.82 us (5%)
    pallas_call x27, Pallas kernels, call(): pl.pallas_call(run, out_shape=tuple((result(t) for t in outs)) + tuple((r...  75.6 us
    ppermute x25, starting transfers between devices, swap_tp(): return lax.ppermute(value, 'tp', pairs(lax.axis_size('tp'), k))  34.9 us
    all_to_all x5, starting transfers between devices, to_cp(): return lax.all_to_all(value, 'cp', 0, 0, tiled=True)  20.5 us
    ppermute x25, waiting for transfers between devices, swap_tp(): return lax.ppermute(value, 'tp', pairs(lax.axis_size('tp'), k))  18.5 us
    all_to_all x5, waiting for transfers between devices, to_cp(): return lax.all_to_all(value, 'cp', 0, 0, tiled=True)  10.5 us
    all_to_all x1, blocking collectives, to_cp(): return lax.all_to_all(value, 'cp', 0, 0, tiled=True)  8.82 us
  transfers between devices with their start and end apart: 33, of which 13 were waited for; matrix products, arithmetic and copies ran while one was open for 0% of the time, Pallas kernels for 34%

profile of v5, /device:TPU:0, one launch (start us, length us, event | category | flops | bytes accessed | tf_op | source)
XLA Modules:
  0.0 187.5 jit_solution(3868389623445011872)
XLA Ops:
  7.3 5.8 %shard_map.213 = (bf16[2,128,2048]{2,1,0:T(8,128)(2,1)}, bf16[128,2048]{1,0:T(8,128)(2,1)}, bf16[8,208,128]{2,1,0:T(8,128)(2,1)}) custom-call(s32[2]{0:T(128)S(1)} %pad_add_fusion.refs_0_, bf16[128,2048]{1,0:T(8,128)(2,1)} %bitcast.39, f32[1,2048]{1,0:T(1,128)} %bitcast.20, bf16[128,2048]{1,0:T(8,128)(2,1)} %bitcast.41, ...), custom_call_target="tpu_custom_call" | custom-call | flops 300000000 | tf_op jit(solution)/shard_map/pallas_call | solution.py:466
  13.1 5.2 %all-to-all-start = ((bf16[8,208,128]{2,1,0:T(8,128)(2,1)}), bf16[8,208,128]{2,1,0:T(8,128)(2,1)S(1)}, u32[]{:S(2)}, u32[]{:S(2)}) async-start(bf16[8,208,128]{2,1,0:T(8,128)(2,1)} %get-tuple-element.77.refs_8_), calls=%async_computation | async-start | bytes 851968 | tf_op jit(solution)/shard_map/all_to_all | solution.py:1151
  20.5 6.4 %all-to-all-done.refs_1_ = bf16[8,208,128]{2,1,0:T(8,128)(2,1)S(1)} async-done(((bf16[8,208,128]{2,1,0:T(8,128)(2,1)}), bf16[8,208,128]{2,1,0:T(8,128)(2,1)S(1)}, u32[]{:S(2)}, u32[]{:S(2)}) %all-to-all-start) | async-done | bytes 426016 | tf_op jit(solution)/shard_map/all_to_all | solution.py:1151
  26.9 3.2 %shard_map.215 = (bf16[8,64,128]{2,1,0:T(8,128)(2,1)}, f32[64,1024]{1,0:T(8,128)}, f32[1,1024]{1,0:T(1,128)}, bf16[8,208,128]{2,1,0:T(8,128)(2,1)}, bf16[2,128,2048]{2,1,0:T(8,128)(2,1)}) custom-call(s32[2]{0:T(128)S(1)} %pad_add_fusion.refs_0_, bf16[8,208,128]{2,1,0:T(8,128)(2,1)S(1)} %all-to-all-done.refs_1_, ...), custom_call_target="tpu_custom_call", output_to_operand_aliasing={{4}: (3, {})} | custom-call | flops 300000000 | tf_op jit(solution)/shard_map/pallas_call | solution.py:466
  30.2 8.8 %all_to_all.30.refs_0_ = bf16[8,64,128]{2,1,0:T(8,128)(2,1)S(1)} all-to-all(bf16[8,64,128]{2,1,0:T(8,128)(2,1)} %get-tuple-element.80), channel_id=1, replica_groups=mesh['tp'=4,'cp'=8] {'cp'}, dimensions={0} | all-to-all | bytes 262144 | tf_op jit(solution)/shard_map/all_to_all | solution.py:1151
  39.7 3.7 %collective-permute-start = (bf16[32,2176]{1,0:T(8,128)(2,1)S(1)}, bf16[32,2176]{1,0:T(8,128)(2,1)S(1)}, u32[]{:S(2)}, u32[]{:S(2)}) collective-permute-start(bf16[32,2176]{1,0:T(8,128)(2,1)S(1)} %get-tuple-element.83), channel_id=1, source_target_pairs={{0,24},{8,16},{16,8},{24,0},{1,25},{9,17},{17,9},{25,1},{2,26},{10... | collective-permute-start | bytes 417800 | tf_op jit(solution)/shard_map/ppermute | solution.py:39
  44.1 6.0 %shard_map.217.refs_6_.refs_5_ = f32[128,2048]{1,0:T(8,128)S(1)} custom-call(bf16[128,2048]{1,0:T(8,128)(2,1)} %get-tuple-element.88.refs_0_, bf16[2048,2048]{1,0:T(8,128)(2,1)} %refs_3_.5, f32[32,2176]{1,0:T(8,128)S(1)} %get-tuple-element.82.refs_2_.refs_0_), custom_call_target="tpu_custom_call" | custom-call | flops 3000000000 | tf_op jit(solution)/shard_map/pallas_call | solution.py:466
  50.1 4.8 %collective-permute-done.1.refs_2_ = bf16[32,2176]{1,0:T(8,128)(2,1)S(1)} collective-permute-done((bf16[32,2176]{1,0:T(8,128)(2,1)S(1)}, bf16[32,2176]{1,0:T(8,128)(2,1)S(1)}, u32[]{:S(2)}, u32[]{:S(2)}) %collective-permute-start.1) | collective-permute-done | bytes 139296 | tf_op jit(solution)/shard_map/ppermute | solution.py:39
  59.9 4.1 %shard_map.219 = (bf16[2048,2048]{1,0:T(8,128)(2,1)S(1)}, bf16[2048,2048]{1,0:T(8,128)(2,1)S(1)}) custom-call(bf16[2048,2048]{1,0:T(8,128)(2,1)} %refs_3_.6, bf16[32,2048]{1,0:T(8,128)(2,1)S(1)} %get-tuple-element.89.refs_1_.refs_0_), custom_call_target="tpu_custom_call" | custom-call | flops 300000000 | tf_op jit(solution)/shard_map/pallas_call | solution.py:466
  64.0 4.0 %collective-permute-done.4.refs_2_ = bf16[32,2048]{1,0:T(8,128)(2,1)S(1)} collective-permute-done((bf16[32,2048]{1,0:T(8,128)(2,1)S(1)}, bf16[32,2048]{1,0:T(8,128)(2,1)S(1)}, u32[]{:S(2)}, u32[]{:S(2)}) %collective-permute-start.4) | collective-permute-done | bytes 131104 | tf_op jit(solution)/shard_map/ppermute | solution.py:39
  83.6 4.2 %all-to-all-start.2 = ((bf16[8,128,512]{2,1,0:T(8,128)(2,1)}), bf16[8,128,512]{2,1,0:T(8,128)(2,1)}, u32[]{:S(2)}, u32[]{:S(2)}) async-start(bf16[8,128,512]{2,1,0:T(8,128)(2,1)} %get-tuple-element.98.refs_0_), calls=%async_computation.2 | async-start | bytes 2097152 | tf_op jit(solution)/shard_map/all_to_all | solution.py:1151
  95.8 5.0 %shard_map.223 = (f32[32,2048]{1,0:T(8,128)}, f32[32,2048]{1,0:T(8,128)}, bf16[64,2048]{1,0:T(8,128)(2,1)}) custom-call(bf16[8,128,512]{2,1,0:T(8,128)(2,1)} %get-tuple-element.98.refs_0_, bf16[2048,2048]{1,0:T(8,128)(2,1)} %refs_3_.5, bf16[2048,2048]{1,0:T(8,128)(2,1)} %refs_3_.5, bf16[2048,2048]{1,0:T(8,128)(2,1)} %refs_3_.5, bf16[2048,2048]{1,0:T(8,128)(2,1)} %refs_3_.5, ...), custom_call_target="tpu_custom_call" | custom-call | flops 20000000000 | tf_op jit(solution)/shard_map/pallas_call | solution.py:466
  105.8 3.0 %all-to-all-done.2.refs_8_.refs_1_ = bf16[8,128,512]{2,1,0:T(8,128)(2,1)} async-done(((bf16[8,128,512]{2,1,0:T(8,128)(2,1)}), bf16[8,128,512]{2,1,0:T(8,128)(2,1)}, u32[]{:S(2)}, u32[]{:S(2)}) %all-to-all-start.2) | async-done | bytes 1048608 | tf_op jit(solution)/shard_map/all_to_all | solution.py:1151
  110.8 3.4 %all-to-all-start.3 = ((bf16[8,128,128]{2,1,0:T(8,128)(2,1)}), bf16[8,128,128]{2,1,0:T(8,128)(2,1)S(1)}, u32[]{:S(2)}, u32[]{:S(2)}) async-start(bf16[8,128,128]{2,1,0:T(8,128)(2,1)} %get-tuple-element.113.refs_2_.refs_6_.refs_5_), calls=%async_computation.3 | async-start | bytes 524288 | tf_op jit(solution)/shard_map/all_to_all | solution.py:1151
  119.0 5.9 %shard_map.228 = (f32[256,2048]{1,0:T(8,128)}, f32[1,256]{1,0:T(1,128)}) custom-call(s32[2]{0:T(128)S(1)} %pad_add_fusion.refs_0_, bf16[8,128,512]{2,1,0:T(8,128)(2,1)} %all-to-all-done.2.refs_8_.refs_1_, bf16[8,2,128,2048]{3,2,1,0:T(8,128)(2,1)} %bitcast.45, bf16[2048,2048]{1,0:T(8,128)(2,1)} %refs_3_.5, f32[1,2048]{1,0:T(1,128)S(1)} %bitcast.24, ...), custom_call_target="tpu_custom_call" | custom-call | flops 20000000000 | tf_op jit(solution)/shard_map/pallas_call | solution.py:466
  124.9 3.7 %shard_map.229 = (bf16[8,192,128]{2,1,0:T(8,128)(2,1)}, bf16[8,64,128]{2,1,0:T(8,128)(2,1)}) custom-call(s32[2]{0:T(128)S(1)} %pad_add_fusion.refs_0_, bf16[8,208,128]{2,1,0:T(8,128)(2,1)S(1)} %get-tuple-element.117.refs_1_, bf16[8,128,128]{2,1,0:T(8,128)(2,1)S(1)} %all-to-all-done.3.refs_2_, f32[64,1024]{1,0:T(8,128)S(1)} %get-tuple-element.118.refs_3_, ...), custom_call_target="tpu_custom_call" | custom-call | flops 8000000000 | tf_op jit(solution)/shard_map/pallas_call | solution.py:466
  128.7 4.1 %all-to-all-start.4 = ((bf16[8,192,128]{2,1,0:T(8,128)(2,1)}), bf16[8,192,128]{2,1,0:T(8,128)(2,1)S(1)}, u32[]{:S(2)}, u32[]{:S(2)}) async-start(bf16[8,192,128]{2,1,0:T(8,128)(2,1)} %get-tuple-element.124.refs_4_.refs_1_), calls=%async_computation.4 | async-start | bytes 786432 | tf_op jit(solution)/shard_map/all_to_all | solution.py:1151
  133.8 4.5 %shard_map.233 = bf16[8,192,256]{2,1,0:T(8,128)(2,1)} custom-call(s32[2]{0:T(128)S(1)} %pad_add_fusion.refs_0_, bf16[8,192,128]{2,1,0:T(8,128)(2,1)} %get-tuple-element.124.refs_4_.refs_1_, bf16[8,2,128,2048]{3,2,1,0:T(8,128)(2,1)} %bitcast.46, bf16[32,2048]{1,0:T(8,128)(2,1)S(1)} %shard_map.230.refs_0_.refs_3_), custom_call_target="tpu_custom_call" | custom-call | flops 20000000000 | tf_op jit(solution)/shard_map/pallas_call | solution.py:466
  141.1 3.5 %all-to-all-start.5 = ((bf16[8,192,256]{2,1,0:T(8,128)(2,1)}), bf16[8,192,256]{2,1,0:T(8,128)(2,1)S(1)}, u32[]{:S(2)}, u32[]{:S(2)}) async-start(bf16[8,192,256]{2,1,0:T(8,128)(2,1)} %shard_map.233), calls=%async_computation.5 | async-start | bytes 1572864 | tf_op jit(solution)/shard_map/all_to_all | solution.py:1151
  144.7 4.4 %shard_map.231 = (f32[32,2048]{1,0:T(8,128)S(1)}, bf16[32,2048]{1,0:T(8,128)(2,1)S(1)}, bf16[32,2048]{1,0:T(8,128)(2,1)S(1)}, bf16[32,2048]{1,0:T(8,128)(2,1)S(1)}) custom-call(bf16[8,192,128]{2,1,0:T(8,128)(2,1)S(1)} %all-to-all-done.4.refs_0_, bf16[3,2048,512]{2,1,0:T(8,128)(2,1)} %bitcast.32, bf16[3,2048,512]{2,1,0:T(8,128)(2,1)} %bitcast.33, ...), custom_call_target="tpu_custom_call" | custom-call | flops 10000000000 | tf_op jit(solution)/shard_map/pallas_call | solution.py:466
  154.2 5.4 %shard_map.234 = (f32[256,2048]{1,0:T(8,128)}, f32[1,256]{1,0:T(1,128)S(1)}) custom-call(s32[2]{0:T(128)S(1)} %pad_add_fusion.refs_0_, bf16[8,128,512]{2,1,0:T(8,128)(2,1)} %all-to-all-done.2.refs_8_.refs_1_, bf16[8,128,2048]{2,1,0:T(8,128)(2,1)} %bitcast.47, bf16[2048,2048]{1,0:T(8,128)(2,1)} %refs_3_.6, f32[1,2048]{1,0:T(1,128)S(1)} %bitcast.26, ...), custom_call_target="tpu_custom_call" | custom-call | flops 20000000000 | tf_op jit(solution)/shard_map/pallas_call | solution.py:466
  159.6 3.1 %shard_map.235 = (f32[3,256,512]{2,1,0:T(8,128)}, f32[8,256]{1,0:T(8,128)S(1)}) custom-call(s32[2]{0:T(128)S(1)} %pad_add_fusion.refs_0_, bf16[8,192,256]{2,1,0:T(8,128)(2,1)S(1)} %all-to-all-done.5.refs_1_, bf16[3,2048,512]{2,1,0:T(8,128)(2,1)} %bitcast.38, f32[1,2048]{1,0:T(1,128)S(1)} %bitcast.22, f32[1,256]{1,0:T(1,128)S(1)} %get-tuple-element.132.refs_4_, ...), custom_call_target="tpu_custom_call" | custom-call | flops 20000000000 | tf_op jit(solution)/shard_map/pallas_call | solution.py:466
  169.2 3.6 %all-gather.11.cloned.1.call-done = bf16[1024,2048]{1,0:T(8,128)(2,1)} async-done(((bf16[128,2048]{1,0:T(8,128)(2,1)}), bf16[1024,2048]{1,0:T(8,128)(2,1)}) %all-gather.11.cloned.1.call-update) | async-done | bytes 4194320 | tf_op jit(solution)/shard_map/all_gather | solution.py:1278
  172.8 4.8 %shard_map.238 = (f32[64,2048]{1,0:T(8,128)}, f32[1,64]{1,0:T(1,128)}) custom-call(s32[2]{0:T(128)S(1)} %pad_add_fusion.refs_0_, bf16[8,64,128]{2,1,0:T(8,128)(2,1)} %get-tuple-element.135.refs_1_, bf16[8,128,2048]{2,1,0:T(8,128)(2,1)} %bitcast.48, bf16[512,2048]{1,0:T(8,128)(2,1)} %refs_3_.7, f32[1,512]{1,0:T(1,128)S(1)} %bitcast.28, ...), custom_call_target="tpu_custom_call" | custom-call | flops 20000000000 | tf_op jit(solution)/shard_map/pallas_call | solution.py:466
  (86 shorter events, 62.7 us)
Async XLA Ops:
  13.1 13.9 %all-to-all-start = ((bf16[8,208,128]{2,1,0:T(8,128)(2,1)}), bf16[8,208,128]{2,1,0:T(8,128)(2,1)S(1)}, u32[]{:S(2)}, u32[]{:S(2)}) async-start(bf16[8,208,128]{2,1,0:T(8,128)(2,1)} %get-tuple-element.77.refs_8_), calls=%async_computation | async-start | bytes 851968 | tf_op jit(solution)/shard_map/all_to_all | solution.py:1151
  18.2 100.8 %all-gather.7.cloned.1.call-start = ((), (), s32[]{:S(2)}) async-start(), calls=%async_computation.6 | async-start | bytes 9437184 | tf_op jit(solution)/shard_map/all_gather | solution.py:1189
  30.2 124.0 %all-gather.9.cloned.1.call-start = ((), (), s32[]{:S(2)}) async-start(), calls=%async_computation.7 | async-start | bytes 4718592 | tf_op jit(solution)/shard_map/all_gather | solution.py:1230
  39.7 10.4 %collective-permute-start = (bf16[32,2176]{1,0:T(8,128)(2,1)S(1)}, bf16[32,2176]{1,0:T(8,128)(2,1)S(1)}, u32[]{:S(2)}, u32[]{:S(2)}) collective-permute-start(bf16[32,2176]{1,0:T(8,128)(2,1)S(1)} %get-tuple-element.83), channel_id=1, source_target_pairs={{0,24},{8,16},{16,8},{24,0},{1,25},{9,17},{17,9},{25,1},{2,26},{10... | collective-permute-start | bytes 417800 | tf_op jit(solution)/shard_map/ppermute | solution.py:39
  43.3 11.6 %collective-permute-start.1 = (bf16[32,2176]{1,0:T(8,128)(2,1)S(1)}, bf16[32,2176]{1,0:T(8,128)(2,1)S(1)}, u32[]{:S(2)}, u32[]{:S(2)}) collective-permute-start(bf16[32,2176]{1,0:T(8,128)(2,1)S(1)} %get-tuple-element.84), channel_id=1, source_target_pairs={{0,16},{8,24},{16,0},{24,8},{1,17},{9,25},{17,1},{25,9},{2,18},{10... | collective-permute-start | bytes 417800 | tf_op jit(solution)/shard_map/ppermute | solution.py:39
  43.3 11.6 %collective-permute-start.2 = (bf16[32,2176]{1,0:T(8,128)(2,1)S(1)}, bf16[32,2176]{1,0:T(8,128)(2,1)S(1)}, u32[]{:S(2)}, u32[]{:S(2)}) collective-permute-start(bf16[32,2176]{1,0:T(8,128)(2,1)S(1)} %get-tuple-element.85), channel_id=1, source_target_pairs={{0,8},{8,0},{16,24},{24,16},{1,9},{9,1},{17,25},{25,17},{2,10},{10... | collective-permute-start | bytes 417800 | tf_op jit(solution)/shard_map/ppermute | solution.py:39
  79.1 10.3 %collective-permute-start.10 = (bf16[32,2048]{1,0:T(8,128)(2,1)S(1)}, bf16[32,2048]{1,0:T(8,128)(2,1)S(1)}, u32[]{:S(2)}, u32[]{:S(2)}) collective-permute-start(bf16[32,2048]{1,0:T(8,128)(2,1)S(1)} %get-tuple-element.101), channel_id=1, source_target_pairs={{0,16},{8,24},{16,0},{24,8},{1,17},{9,25},{17,1},{25,9},{2,18},{10... | collective-permute-start | bytes 393224 | tf_op jit(solution)/shard_map/ppermute | solution.py:39
  83.6 25.3 %all-to-all-start.2 = ((bf16[8,128,512]{2,1,0:T(8,128)(2,1)}), bf16[8,128,512]{2,1,0:T(8,128)(2,1)}, u32[]{:S(2)}, u32[]{:S(2)}) async-start(bf16[8,128,512]{2,1,0:T(8,128)(2,1)} %get-tuple-element.98.refs_0_), calls=%async_computation.2 | async-start | bytes 2097152 | tf_op jit(solution)/shard_map/all_to_all | solution.py:1151
  91.3 11.6 %collective-permute-start.12 = (bf16[32,2176]{1,0:T(8,128)(2,1)S(1)}, bf16[32,2176]{1,0:T(8,128)(2,1)S(1)}, u32[]{:S(2)}, u32[]{:S(2)}) collective-permute-start(bf16[32,2176]{1,0:T(8,128)(2,1)S(1)} %get-tuple-element.106.refs_5_.refs_2_.refs_0_), channel_id=1, source_target_pairs={{0,24},{8,16},{16,8},{24,0},{1,25},{9,17},{17,9},{25,1},{2,26},{10... | collective-permute-start | bytes 417800 | tf_op jit(solution)/shard_map/ppermute | solution.py:39
  93.5 12.3 %collective-permute-start.13 = (bf16[32,2176]{1,0:T(8,128)(2,1)S(1)}, bf16[32,2176]{1,0:T(8,128)(2,1)S(1)}, u32[]{:S(2)}, u32[]{:S(2)}) collective-permute-start(bf16[32,2176]{1,0:T(8,128)(2,1)S(1)} %get-tuple-element.106.refs_5_.refs_2_.refs_0_), channel_id=1, source_target_pairs={{0,16},{8,24},{16,0},{24,8},{1,17},{9,25},{17,1},{25,9},{2,18},{10... | collective-permute-start | bytes 417800 | tf_op jit(solution)/shard_map/ppermute | solution.py:39
  95.4 10.4 %collective-permute-start.14 = (bf16[32,2176]{1,0:T(8,128)(2,1)S(1)}, bf16[32,2176]{1,0:T(8,128)(2,1)S(1)}, u32[]{:S(2)}, u32[]{:S(2)}) collective-permute-start(bf16[32,2176]{1,0:T(8,128)(2,1)S(1)} %get-tuple-element.106.refs_5_.refs_2_.refs_0_), channel_id=1, source_target_pairs={{0,8},{8,0},{16,24},{24,16},{1,9},{9,1},{17,25},{25,17},{2,10},{10... | collective-permute-start | bytes 417800 | tf_op jit(solution)/shard_map/ppermute | solution.py:39
  110.8 14.1 %all-to-all-start.3 = ((bf16[8,128,128]{2,1,0:T(8,128)(2,1)}), bf16[8,128,128]{2,1,0:T(8,128)(2,1)S(1)}, u32[]{:S(2)}, u32[]{:S(2)}) async-start(bf16[8,128,128]{2,1,0:T(8,128)(2,1)} %get-tuple-element.113.refs_2_.refs_6_.refs_5_), calls=%async_computation.3 | async-start | bytes 524288 | tf_op jit(solution)/shard_map/all_to_all | solution.py:1151
  114.2 58.6 %all-gather.11.cloned.1.call-start = ((), (), s32[]{:S(2)}) async-start(), calls=%async_computation.8 | async-start | bytes 4718592 | tf_op jit(solution)/shard_map/all_gather | solution.py:1278
  118.1 14.7 %collective-permute-start.16 = (bf16[32,2048]{1,0:T(8,128)(2,1)S(1)}, bf16[32,2048]{1,0:T(8,128)(2,1)S(1)}, u32[]{:S(2)}, u32[]{:S(2)}) collective-permute-start(bf16[32,2048]{1,0:T(8,128)(2,1)S(1)} %shard_map.226.refs_8_), channel_id=1, source_target_pairs={{0,16},{8,24},{16,0},{24,8},{1,17},{9,25},{17,1},{25,9},{2,18},{10... | collective-permute-start | bytes 393224 | tf_op jit(solution)/shard_map/ppermute | solution.py:39
  128.7 12.4 %all-to-all-start.4 = ((bf16[8,192,128]{2,1,0:T(8,128)(2,1)}), bf16[8,192,128]{2,1,0:T(8,128)(2,1)S(1)}, u32[]{:S(2)}, u32[]{:S(2)}) async-start(bf16[8,192,128]{2,1,0:T(8,128)(2,1)} %get-tuple-element.124.refs_4_.refs_1_), calls=%async_computation.4 | async-start | bytes 786432 | tf_op jit(solution)/shard_map/all_to_all | solution.py:1151
  138.3 15.2 %collective-permute-start.17 = (bf16[32,2048]{1,0:T(8,128)(2,1)S(1)}, bf16[32,2048]{1,0:T(8,128)(2,1)S(1)}, u32[]{:S(2)}, u32[]{:S(2)}) collective-permute-start(bf16[32,2048]{1,0:T(8,128)(2,1)S(1)} %shard_map.230.refs_0_.refs_3_), channel_id=1, source_target_pairs={{0,16},{8,24},{16,0},{24,8},{1,17},{9,25},{17,1},{25,9},{2,18},{10... | collective-permute-start | bytes 393224 | tf_op jit(solution)/shard_map/ppermute | solution.py:39
  141.1 18.5 %all-to-all-start.5 = ((bf16[8,192,256]{2,1,0:T(8,128)(2,1)}), bf16[8,192,256]{2,1,0:T(8,128)(2,1)S(1)}, u32[]{:S(2)}, u32[]{:S(2)}) async-start(bf16[8,192,256]{2,1,0:T(8,128)(2,1)} %shard_map.233), calls=%async_computation.5 | async-start | bytes 1572864 | tf_op jit(solution)/shard_map/all_to_all | solution.py:1151
  149.0 13.7 %collective-permute-start.19 = (bf16[32,2048]{1,0:T(8,128)(2,1)S(1)}, bf16[32,2048]{1,0:T(8,128)(2,1)S(1)}, u32[]{:S(2)}, u32[]{:S(2)}) collective-permute-start(bf16[32,2048]{1,0:T(8,128)(2,1)S(1)} %get-tuple-element.126), channel_id=1, source_target_pairs={{0,24},{8,16},{16,8},{24,0},{1,25},{9,17},{17,9},{25,1},{2,26},{10... | collective-permute-start | bytes 393224 | tf_op jit(solution)/shard_map/ppermute | solution.py:39
  152.1 12.3 %collective-permute-start.20 = (bf16[32,2048]{1,0:T(8,128)(2,1)S(1)}, bf16[32,2048]{1,0:T(8,128)(2,1)S(1)}, u32[]{:S(2)}, u32[]{:S(2)}) collective-permute-start(bf16[32,2048]{1,0:T(8,128)(2,1)S(1)} %get-tuple-element.127), channel_id=1, source_target_pairs={{0,16},{8,24},{16,0},{24,8},{1,17},{9,25},{17,1},{25,9},{2,18},{10... | collective-permute-start | bytes 393224 | tf_op jit(solution)/shard_map/ppermute | solution.py:39
  152.1 12.3 %collective-permute-start.21 = (bf16[32,2048]{1,0:T(8,128)(2,1)S(1)}, bf16[32,2048]{1,0:T(8,128)(2,1)S(1)}, u32[]{:S(2)}, u32[]{:S(2)}) collective-permute-start(bf16[32,2048]{1,0:T(8,128)(2,1)S(1)} %get-tuple-element.128), channel_id=1, source_target_pairs={{0,8},{8,0},{16,24},{24,16},{1,9},{9,1},{17,25},{25,17},{2,10},{10... | collective-permute-start | bytes 393224 | tf_op jit(solution)/shard_map/ppermute | solution.py:39
  153.5 24.1 %collective-permute-start.18 = (bf16[64,2048]{1,0:T(8,128)(2,1)S(1)}, bf16[64,2048]{1,0:T(8,128)(2,1)S(1)}, u32[]{:S(2)}, u32[]{:S(2)}) collective-permute-start(bf16[64,2048]{1,0:T(8,128)(2,1)S(1)} %shard_map.232.refs_1_), channel_id=1, source_target_pairs={{0,8},{8,0},{16,24},{24,16},{1,9},{9,1},{17,25},{25,17},{2,10},{10... | collective-permute-start | bytes 786440 | tf_op jit(solution)/shard_map/ppermute | solution.py:39
  164.7 14.3 %collective-permute-start.22 = (bf16[32,2176]{1,0:T(8,128)(2,1)S(1)}, bf16[32,2176]{1,0:T(8,128)(2,1)S(1)}, u32[]{:S(2)}, u32[]{:S(2)}) collective-permute-start(bf16[32,2176]{1,0:T(8,128)(2,1)S(1)} %shard_map.236.refs_3_.refs_5_.refs_1_), channel_id=1, source_target_pairs={{0,24},{8,16},{16,8},{24,0},{1,25},{9,17},{17,9},{25,1},{2,26},{10... | collective-permute-start | bytes 417800 | tf_op jit(solution)/shard_map/ppermute | solution.py:39
  166.5 12.6 %collective-permute-start.23 = (bf16[32,2176]{1,0:T(8,128)(2,1)S(1)}, bf16[32,2176]{1,0:T(8,128)(2,1)S(1)}, u32[]{:S(2)}, u32[]{:S(2)}) collective-permute-start(bf16[32,2176]{1,0:T(8,128)(2,1)S(1)} %shard_map.236.refs_3_.refs_5_.refs_1_), channel_id=1, source_target_pairs={{0,16},{8,24},{16,0},{24,8},{1,17},{9,25},{17,1},{25,9},{2,18},{10... | collective-permute-start | bytes 417800 | tf_op jit(solution)/shard_map/ppermute | solution.py:39
  166.5 12.6 %collective-permute-start.24 = (bf16[32,2176]{1,0:T(8,128)(2,1)S(1)}, bf16[32,2176]{1,0:T(8,128)(2,1)S(1)}, u32[]{:S(2)}, u32[]{:S(2)}) collective-permute-start(bf16[32,2176]{1,0:T(8,128)(2,1)S(1)} %shard_map.236.refs_3_.refs_5_.refs_1_), channel_id=1, source_target_pairs={{0,8},{8,0},{16,24},{24,16},{1,9},{9,1},{17,25},{25,17},{2,10},{10... | collective-permute-start | bytes 417800 | tf_op jit(solution)/shard_map/ppermute | solution.py:39
  (15 other events, 144.2 us)
Sparse Core Ops, SparseCore 0:
  30.3 53.7 all-gather.6
  86.5 43.4 all-gather.8
  132.5 40.2 all-gather.10

commit v6 on v5

--- a/solution.py
+++ b/solution.py
@@ -511,10 +511,6 @@
     return out
 
 
-def pair_sum(block, i):
-    return block[:, i : i + 1].astype(f32) + block[:, i + 1 : i + 2].astype(f32)
-
-
 def own_order(me, part, index):
     return ((index // part) ^ me) * part + index % part
 
@@ -544,7 +540,7 @@
     return of(np.arange(local_len)), of(np.arange(cp_count) * local_len)
 
 
-def project_kernel(parts, ids, x, gain, gy, inner, base, seg, w0, w1, w2, pair, gy_out, out):
+def project_kernel(parts, ids, x, gain, gy, inner, base, seg, w0, w1, w2, pair, out):
     me, mine = ids[0], ids[1]
     rows, width = pair.shape[1:]
     part = rows // parts
@@ -555,11 +551,8 @@
         pair[0, k * part : (k + 1) * part, :] = (normed * gain[...]).astype(bf16)
     gy.ready()
     for k in range(parts):
-        block = gy.ref[block_at(me, k, part), :]
-        pair[1, k * part : (k + 1) * part, :] = block
-        gy_out[k * part : (k + 1) * part, :] = block
+        pair[1, k * part : (k + 1) * part, :] = gy.ref[block_at(me, k, part), :]
     pair.send()
-    gy_out.send()
     inner.ready()
     here = [base[kind, pl.ds(mine, 1), :] for kind in range(4)]
     table = [
@@ -642,16 +635,6 @@
     out.send()
 
 
-def store_pieces(total, own, pieces, part, extra=None):
-    own[:, : total.shape[1]] = total[:part]
-    for k, piece in enumerate(pieces, 1):
-        piece[:, : total.shape[1]] = total[k * part : (k + 1) * part].astype(bf16)
-    if extra is not None:
-        own[:, total.shape[1] :] = extra[:part]
-        for k, piece in enumerate(pieces, 1):
-            piece[:, total.shape[1] :] = extra[k * part : (k + 1) * part].astype(bf16)
-
-
 def out_kernel(parts, att, gain, weight, own, *refs):
     pieces, kept = refs[:-1], refs[-1]
     kept[...] = att[...]
@@ -710,7 +693,7 @@
 
 
 def grad_hidden_kernel(gy, weight, grad):
-    grad[...] = dot_t(gy[...], weight[...])
+    grad[...] = dot_t(gy[0], weight[...])
 
 
 def prepare_kernel(step, up, near_up, flipped, up_sems):
@@ -971,13 +954,6 @@
 def output_kernel(own, got, last, x1, out):
     total = own[...] + x1[...] + got[: out.shape[0], :].astype(f32)
     out[...] = (total + last[...].astype(f32)).astype(bf16)
-
-
-def natural_kernel(ids, *refs):
-    blocks, out = refs[:-1], refs[-1]
-    part = blocks[0].shape[0]
-    for k, block in enumerate(blocks):
-        out[block_at(ids[0], k, part), :] = block[...]
 
 
 def own_row(gain, index, own):
@@ -1165,9 +1141,9 @@
     weight_sixths = [Far(weight3, (1, width // 2, head_width), sixth(c, h)) for c in range(3) for h in range(2)]
     weight_thirds = [Far(weight3, (1, width, head_width), third(c)) for c in range(3)]
 
-    pair, gy_x, sent = call(
+    pair, sent = call(
         functools.partial(project_kernel, T),
-        [Far(shape((2, rows, width), bf16)), Far(shape((rows, width), bf16)), Far(shape((C, 3 * HD + 16, rows), bf16))],
+        [Far(shape((2, rows, width), bf16)), Far(shape((C, 3 * HD + 16, rows), bf16))],
         [ids, Far(x), Far(gain_in), Far(gy), Far(inner2), Far(base2), Far(segment_ids.reshape(1, rows)), *weight_thirds],
         [scalars()] + [whole()] * 9, mb=14,
     )
@@ -1195,8 +1171,8 @@
     )
     (grad_hid,) = call(
         grad_hidden_kernel, [Near(shape((rows, hidden), f32))],
-        [Pin(gy_x), Pin(down_weight)],
-        [fixed((rows, width)), pl.BlockSpec((step, width), first_rows)],
+        [Pin(pair), Pin(down_weight)],
+        [pl.BlockSpec((1, rows, width), lambda i: (1, 0, 0)), pl.BlockSpec((step, width), first_rows)],
         [pl.BlockSpec((rows, step), cols)],
         grid=(hidden // step,), after=[own], mb=10, cost=3,
     )

time: 188 us -> 188 us (level)
  transfers between devices with their start and end apart: 33 -> 33, of which waited for: 13 -> 13; matrix products, arithmetic and copies ran while one was open for 0% -> 0% of each run, Pallas kernels for 34% -> 35%
where the time goes in v6:
time: 188 us; the launch traced here: 187 us
  Pallas kernels  75.6 us (40%)
  starting transfers between devices  55.7 us (30%)
  waiting for transfers between devices  33.1 us (18%)
  between operations  14.1 us (8%)
  blocking collectives  8.82 us (5%)
    pallas_call x27, Pallas kernels, call(): pl.pallas_call(run, out_shape=tuple((result(t) for t in outs)) + tuple((r...  75.6 us
    ppermute x25, starting transfers between devices, swap_tp(): return lax.ppermute(value, 'tp', pairs(lax.axis_size('tp'), k))  34.8 us
    all_to_all x5, starting transfers between devices, to_cp(): return lax.all_to_all(value, 'cp', 0, 0, tiled=True)  20.5 us
    ppermute x25, waiting for transfers between devices, swap_tp(): return lax.ppermute(value, 'tp', pairs(lax.axis_size('tp'), k))  18.5 us
    all_to_all x5, waiting for transfers between devices, to_cp(): return lax.all_to_all(value, 'cp', 0, 0, tiled=True)  10.5 us
    all_to_all x1, blocking collectives, to_cp(): return lax.all_to_all(value, 'cp', 0, 0, tiled=True)  8.82 us
  transfers between devices with their start and end apart: 33, of which 13 were waited for; matrix products, arithmetic and copies ran while one was open for 0% of the time, Pallas kernels for 35%

profile of v6, /device:TPU:0, one launch (start us, length us, event | category | flops | bytes accessed | tf_op | source)
XLA Modules:
  0.0 187.4 jit_solution(10130740495441694569)
XLA Ops:
  7.3 5.7 %shard_map.213 = (bf16[2,128,2048]{2,1,0:T(8,128)(2,1)}, bf16[8,208,128]{2,1,0:T(8,128)(2,1)}) custom-call(s32[2]{0:T(128)S(1)} %pad_add_fusion.refs_0_, bf16[128,2048]{1,0:T(8,128)(2,1)} %bitcast.39, f32[1,2048]{1,0:T(1,128)} %bitcast.20, bf16[128,2048]{1,0:T(8,128)(2,1)} %bitcast.41, f32[4,128,128]{2,1,0:T(8,128)} %constant.14.clone.refs_4_, ...), custom_call_target="tpu_custom_call" | custom-call | flops 300000000 | tf_op jit(solution)/shard_map/pallas_call | solution.py:466
  13.0 5.2 %all-to-all-start = ((bf16[8,208,128]{2,1,0:T(8,128)(2,1)}), bf16[8,208,128]{2,1,0:T(8,128)(2,1)S(1)}, u32[]{:S(2)}, u32[]{:S(2)}) async-start(bf16[8,208,128]{2,1,0:T(8,128)(2,1)} %get-tuple-element.76.refs_8_), calls=%async_computation | async-start | bytes 851968 | tf_op jit(solution)/shard_map/all_to_all | solution.py:1127
  20.4 6.4 %all-to-all-done.refs_1_ = bf16[8,208,128]{2,1,0:T(8,128)(2,1)S(1)} async-done(((bf16[8,208,128]{2,1,0:T(8,128)(2,1)}), bf16[8,208,128]{2,1,0:T(8,128)(2,1)S(1)}, u32[]{:S(2)}, u32[]{:S(2)}) %all-to-all-start) | async-done | bytes 426016 | tf_op jit(solution)/shard_map/all_to_all | solution.py:1127
  26.8 3.2 %shard_map.215 = (bf16[8,64,128]{2,1,0:T(8,128)(2,1)}, f32[64,1024]{1,0:T(8,128)}, f32[1,1024]{1,0:T(1,128)}, bf16[8,208,128]{2,1,0:T(8,128)(2,1)}, bf16[2,128,2048]{2,1,0:T(8,128)(2,1)}) custom-call(s32[2]{0:T(128)S(1)} %pad_add_fusion.refs_0_, bf16[8,208,128]{2,1,0:T(8,128)(2,1)S(1)} %all-to-all-done.refs_1_, ...), custom_call_target="tpu_custom_call", output_to_operand_aliasing={{4}: (3, {})} | custom-call | flops 300000000 | tf_op jit(solution)/shard_map/pallas_call | solution.py:466
  30.1 8.8 %all_to_all.30.refs_0_ = bf16[8,64,128]{2,1,0:T(8,128)(2,1)S(1)} all-to-all(bf16[8,64,128]{2,1,0:T(8,128)(2,1)} %get-tuple-element.79), channel_id=1, replica_groups=mesh['tp'=4,'cp'=8] {'cp'}, dimensions={0} | all-to-all | bytes 262144 | tf_op jit(solution)/shard_map/all_to_all | solution.py:1127
  39.6 3.7 %collective-permute-start = (bf16[32,2176]{1,0:T(8,128)(2,1)S(1)}, bf16[32,2176]{1,0:T(8,128)(2,1)S(1)}, u32[]{:S(2)}, u32[]{:S(2)}) collective-permute-start(bf16[32,2176]{1,0:T(8,128)(2,1)S(1)} %get-tuple-element.82), channel_id=1, source_target_pairs={{0,24},{8,16},{16,8},{24,0},{1,25},{9,17},{17,9},{25,1},{2,26},{10... | collective-permute-start | bytes 417800 | tf_op jit(solution)/shard_map/ppermute | solution.py:39
  44.0 6.0 %shard_map.217.refs_6_.refs_5_ = f32[128,2048]{1,0:T(8,128)S(1)} custom-call(bf16[2,128,2048]{2,1,0:T(8,128)(2,1)} %get-tuple-element.87.refs_0_, bf16[2048,2048]{1,0:T(8,128)(2,1)} %refs_3_.5, f32[32,2176]{1,0:T(8,128)S(1)} %get-tuple-element.81.refs_2_.refs_0_), custom_call_target="tpu_custom_call" | custom-call | flops 3000000000 | tf_op jit(solution)/shard_map/pallas_call | solution.py:466
  50.0 4.8 %collective-permute-done.1.refs_2_ = bf16[32,2176]{1,0:T(8,128)(2,1)S(1)} collective-permute-done((bf16[32,2176]{1,0:T(8,128)(2,1)S(1)}, bf16[32,2176]{1,0:T(8,128)(2,1)S(1)}, u32[]{:S(2)}, u32[]{:S(2)}) %collective-permute-start.1) | collective-permute-done | bytes 139296 | tf_op jit(solution)/shard_map/ppermute | solution.py:39
  59.8 4.1 %shard_map.219 = (bf16[2048,2048]{1,0:T(8,128)(2,1)S(1)}, bf16[2048,2048]{1,0:T(8,128)(2,1)S(1)}) custom-call(bf16[2048,2048]{1,0:T(8,128)(2,1)} %refs_3_.6, bf16[32,2048]{1,0:T(8,128)(2,1)S(1)} %get-tuple-element.88.refs_1_.refs_0_), custom_call_target="tpu_custom_call" | custom-call | flops 300000000 | tf_op jit(solution)/shard_map/pallas_call | solution.py:466
  63.9 4.0 %collective-permute-done.4.refs_2_ = bf16[32,2048]{1,0:T(8,128)(2,1)S(1)} collective-permute-done((bf16[32,2048]{1,0:T(8,128)(2,1)S(1)}, bf16[32,2048]{1,0:T(8,128)(2,1)S(1)}, u32[]{:S(2)}, u32[]{:S(2)}) %collective-permute-start.4) | collective-permute-done | bytes 131104 | tf_op jit(solution)/shard_map/ppermute | solution.py:39
  83.4 4.2 %all-to-all-start.2 = ((bf16[8,128,512]{2,1,0:T(8,128)(2,1)}), bf16[8,128,512]{2,1,0:T(8,128)(2,1)}, u32[]{:S(2)}, u32[]{:S(2)}) async-start(bf16[8,128,512]{2,1,0:T(8,128)(2,1)} %get-tuple-element.97.refs_0_), calls=%async_computation.2 | async-start | bytes 2097152 | tf_op jit(solution)/shard_map/all_to_all | solution.py:1127
  95.7 5.0 %shard_map.223 = (f32[32,2048]{1,0:T(8,128)}, f32[32,2048]{1,0:T(8,128)}, bf16[64,2048]{1,0:T(8,128)(2,1)}) custom-call(bf16[8,128,512]{2,1,0:T(8,128)(2,1)} %get-tuple-element.97.refs_0_, bf16[2048,2048]{1,0:T(8,128)(2,1)} %refs_3_.5, bf16[2048,2048]{1,0:T(8,128)(2,1)} %refs_3_.5, bf16[2048,2048]{1,0:T(8,128)(2,1)} %refs_3_.5, bf16[2048,2048]{1,0:T(8,128)(2,1)} %refs_3_.5, ...), custom_call_target="tpu_custom_call" | custom-call | flops 20000000000 | tf_op jit(solution)/shard_map/pallas_call | solution.py:466
  105.7 3.1 %all-to-all-done.2.refs_8_.refs_1_ = bf16[8,128,512]{2,1,0:T(8,128)(2,1)} async-done(((bf16[8,128,512]{2,1,0:T(8,128)(2,1)}), bf16[8,128,512]{2,1,0:T(8,128)(2,1)}, u32[]{:S(2)}, u32[]{:S(2)}) %all-to-all-start.2) | async-done | bytes 1048608 | tf_op jit(solution)/shard_map/all_to_all | solution.py:1127
  110.7 3.4 %all-to-all-start.3 = ((bf16[8,128,128]{2,1,0:T(8,128)(2,1)}), bf16[8,128,128]{2,1,0:T(8,128)(2,1)S(1)}, u32[]{:S(2)}, u32[]{:S(2)}) async-start(bf16[8,128,128]{2,1,0:T(8,128)(2,1)} %get-tuple-element.112.refs_2_.refs_6_.refs_5_), calls=%async_computation.3 | async-start | bytes 524288 | tf_op jit(solution)/shard_map/all_to_all | solution.py:1127
  118.9 5.9 %shard_map.228 = (f32[256,2048]{1,0:T(8,128)}, f32[1,256]{1,0:T(1,128)}) custom-call(s32[2]{0:T(128)S(1)} %pad_add_fusion.refs_0_, bf16[8,128,512]{2,1,0:T(8,128)(2,1)} %all-to-all-done.2.refs_8_.refs_1_, bf16[8,2,128,2048]{3,2,1,0:T(8,128)(2,1)} %bitcast.45, bf16[2048,2048]{1,0:T(8,128)(2,1)} %refs_3_.5, f32[1,2048]{1,0:T(1,128)S(1)} %bitcast.24, ...), custom_call_target="tpu_custom_call" | custom-call | flops 20000000000 | tf_op jit(solution)/shard_map/pallas_call | solution.py:466
  124.8 3.7 %shard_map.229 = (bf16[8,192,128]{2,1,0:T(8,128)(2,1)}, bf16[8,64,128]{2,1,0:T(8,128)(2,1)}) custom-call(s32[2]{0:T(128)S(1)} %pad_add_fusion.refs_0_, bf16[8,208,128]{2,1,0:T(8,128)(2,1)S(1)} %get-tuple-element.116.refs_1_, bf16[8,128,128]{2,1,0:T(8,128)(2,1)S(1)} %all-to-all-done.3.refs_2_, f32[64,1024]{1,0:T(8,128)S(1)} %get-tuple-element.117.refs_3_, ...), custom_call_target="tpu_custom_call" | custom-call | flops 8000000000 | tf_op jit(solution)/shard_map/pallas_call | solution.py:466
  128.5 4.1 %all-to-all-start.4 = ((bf16[8,192,128]{2,1,0:T(8,128)(2,1)}), bf16[8,192,128]{2,1,0:T(8,128)(2,1)S(1)}, u32[]{:S(2)}, u32[]{:S(2)}) async-start(bf16[8,192,128]{2,1,0:T(8,128)(2,1)} %get-tuple-element.122.refs_4_.refs_1_), calls=%async_computation.4 | async-start | bytes 786432 | tf_op jit(solution)/shard_map/all_to_all | solution.py:1127
  133.7 4.5 %shard_map.233 = bf16[8,192,256]{2,1,0:T(8,128)(2,1)} custom-call(s32[2]{0:T(128)S(1)} %pad_add_fusion.refs_0_, bf16[8,192,128]{2,1,0:T(8,128)(2,1)} %get-tuple-element.122.refs_4_.refs_1_, bf16[8,2,128,2048]{3,2,1,0:T(8,128)(2,1)} %bitcast.46, bf16[32,2048]{1,0:T(8,128)(2,1)S(1)} %shard_map.230.refs_0_.refs_3_), custom_call_target="tpu_custom_call" | custom-call | flops 20000000000 | tf_op jit(solution)/shard_map/pallas_call | solution.py:466
  141.0 3.5 %all-to-all-start.5 = ((bf16[8,192,256]{2,1,0:T(8,128)(2,1)}), bf16[8,192,256]{2,1,0:T(8,128)(2,1)S(1)}, u32[]{:S(2)}, u32[]{:S(2)}) async-start(bf16[8,192,256]{2,1,0:T(8,128)(2,1)} %shard_map.233), calls=%async_computation.5 | async-start | bytes 1572864 | tf_op jit(solution)/shard_map/all_to_all | solution.py:1127
  144.5 4.4 %shard_map.231 = (f32[32,2048]{1,0:T(8,128)S(1)}, bf16[32,2048]{1,0:T(8,128)(2,1)S(1)}, bf16[32,2048]{1,0:T(8,128)(2,1)S(1)}, bf16[32,2048]{1,0:T(8,128)(2,1)S(1)}) custom-call(bf16[8,192,128]{2,1,0:T(8,128)(2,1)S(1)} %all-to-all-done.4.refs_0_, bf16[3,2048,512]{2,1,0:T(8,128)(2,1)} %bitcast.32, bf16[3,2048,512]{2,1,0:T(8,128)(2,1)} %bitcast.33, ...), custom_call_target="tpu_custom_call" | custom-call | flops 10000000000 | tf_op jit(solution)/shard_map/pallas_call | solution.py:466
  154.1 5.4 %shard_map.234 = (f32[256,2048]{1,0:T(8,128)}, f32[1,256]{1,0:T(1,128)S(1)}) custom-call(s32[2]{0:T(128)S(1)} %pad_add_fusion.refs_0_, bf16[8,128,512]{2,1,0:T(8,128)(2,1)} %all-to-all-done.2.refs_8_.refs_1_, bf16[8,128,2048]{2,1,0:T(8,128)(2,1)} %bitcast.47, bf16[2048,2048]{1,0:T(8,128)(2,1)} %refs_3_.6, f32[1,2048]{1,0:T(1,128)S(1)} %bitcast.26, ...), custom_call_target="tpu_custom_call" | custom-call | flops 20000000000 | tf_op jit(solution)/shard_map/pallas_call | solution.py:466
  159.5 3.1 %shard_map.235 = (f32[3,256,512]{2,1,0:T(8,128)}, f32[8,256]{1,0:T(8,128)S(1)}) custom-call(s32[2]{0:T(128)S(1)} %pad_add_fusion.refs_0_, bf16[8,192,256]{2,1,0:T(8,128)(2,1)S(1)} %all-to-all-done.5.refs_1_, bf16[3,2048,512]{2,1,0:T(8,128)(2,1)} %bitcast.38, f32[1,2048]{1,0:T(1,128)S(1)} %bitcast.22, f32[1,256]{1,0:T(1,128)S(1)} %get-tuple-element.130.refs_4_, ...), custom_call_target="tpu_custom_call" | custom-call | flops 20000000000 | tf_op jit(solution)/shard_map/pallas_call | solution.py:466
  169.1 3.6 %all-gather.11.cloned.1.call-done = bf16[1024,2048]{1,0:T(8,128)(2,1)} async-done(((bf16[128,2048]{1,0:T(8,128)(2,1)}), bf16[1024,2048]{1,0:T(8,128)(2,1)}) %all-gather.11.cloned.1.call-update) | async-done | bytes 4194320 | tf_op jit(solution)/shard_map/all_gather | solution.py:1254
  172.7 4.8 %shard_map.238 = (f32[64,2048]{1,0:T(8,128)}, f32[1,64]{1,0:T(1,128)}) custom-call(s32[2]{0:T(128)S(1)} %pad_add_fusion.refs_0_, bf16[8,64,128]{2,1,0:T(8,128)(2,1)} %get-tuple-element.133.refs_1_, bf16[8,128,2048]{2,1,0:T(8,128)(2,1)} %bitcast.48, bf16[512,2048]{1,0:T(8,128)(2,1)} %refs_3_.7, f32[1,512]{1,0:T(1,128)S(1)} %bitcast.28, ...), custom_call_target="tpu_custom_call" | custom-call | flops 20000000000 | tf_op jit(solution)/shard_map/pallas_call | solution.py:466
  (86 shorter events, 62.6 us)
Async XLA Ops:
  13.0 13.9 %all-to-all-start = ((bf16[8,208,128]{2,1,0:T(8,128)(2,1)}), bf16[8,208,128]{2,1,0:T(8,128)(2,1)S(1)}, u32[]{:S(2)}, u32[]{:S(2)}) async-start(bf16[8,208,128]{2,1,0:T(8,128)(2,1)} %get-tuple-element.76.refs_8_), calls=%async_computation | async-start | bytes 851968 | tf_op jit(solution)/shard_map/all_to_all | solution.py:1127
  18.1 100.7 %all-gather.7.cloned.1.call-start = ((), (), s32[]{:S(2)}) async-start(), calls=%async_computation.6 | async-start | bytes 9437184 | tf_op jit(solution)/shard_map/all_gather | solution.py:1165
  30.1 124.0 %all-gather.9.cloned.1.call-start = ((), (), s32[]{:S(2)}) async-start(), calls=%async_computation.7 | async-start | bytes 4718592 | tf_op jit(solution)/shard_map/all_gather | solution.py:1206
  39.6 10.4 %collective-permute-start = (bf16[32,2176]{1,0:T(8,128)(2,1)S(1)}, bf16[32,2176]{1,0:T(8,128)(2,1)S(1)}, u32[]{:S(2)}, u32[]{:S(2)}) collective-permute-start(bf16[32,2176]{1,0:T(8,128)(2,1)S(1)} %get-tuple-element.82), channel_id=1, source_target_pairs={{0,24},{8,16},{16,8},{24,0},{1,25},{9,17},{17,9},{25,1},{2,26},{10... | collective-permute-start | bytes 417800 | tf_op jit(solution)/shard_map/ppermute | solution.py:39
  43.2 11.6 %collective-permute-start.1 = (bf16[32,2176]{1,0:T(8,128)(2,1)S(1)}, bf16[32,2176]{1,0:T(8,128)(2,1)S(1)}, u32[]{:S(2)}, u32[]{:S(2)}) collective-permute-start(bf16[32,2176]{1,0:T(8,128)(2,1)S(1)} %get-tuple-element.83), channel_id=1, source_target_pairs={{0,16},{8,24},{16,0},{24,8},{1,17},{9,25},{17,1},{25,9},{2,18},{10... | collective-permute-start | bytes 417800 | tf_op jit(solution)/shard_map/ppermute | solution.py:39
  43.2 11.6 %collective-permute-start.2 = (bf16[32,2176]{1,0:T(8,128)(2,1)S(1)}, bf16[32,2176]{1,0:T(8,128)(2,1)S(1)}, u32[]{:S(2)}, u32[]{:S(2)}) collective-permute-start(bf16[32,2176]{1,0:T(8,128)(2,1)S(1)} %get-tuple-element.84), channel_id=1, source_target_pairs={{0,8},{8,0},{16,24},{24,16},{1,9},{9,1},{17,25},{25,17},{2,10},{10... | collective-permute-start | bytes 417800 | tf_op jit(solution)/shard_map/ppermute | solution.py:39
  79.0 10.3 %collective-permute-start.10 = (bf16[32,2048]{1,0:T(8,128)(2,1)S(1)}, bf16[32,2048]{1,0:T(8,128)(2,1)S(1)}, u32[]{:S(2)}, u32[]{:S(2)}) collective-permute-start(bf16[32,2048]{1,0:T(8,128)(2,1)S(1)} %get-tuple-element.100), channel_id=1, source_target_pairs={{0,16},{8,24},{16,0},{24,8},{1,17},{9,25},{17,1},{25,9},{2,18},{10... | collective-permute-start | bytes 393224 | tf_op jit(solution)/shard_map/ppermute | solution.py:39
  83.4 25.3 %all-to-all-start.2 = ((bf16[8,128,512]{2,1,0:T(8,128)(2,1)}), bf16[8,128,512]{2,1,0:T(8,128)(2,1)}, u32[]{:S(2)}, u32[]{:S(2)}) async-start(bf16[8,128,512]{2,1,0:T(8,128)(2,1)} %get-tuple-element.97.refs_0_), calls=%async_computation.2 | async-start | bytes 2097152 | tf_op jit(solution)/shard_map/all_to_all | solution.py:1127
  91.3 11.6 %collective-permute-start.12 = (bf16[32,2176]{1,0:T(8,128)(2,1)S(1)}, bf16[32,2176]{1,0:T(8,128)(2,1)S(1)}, u32[]{:S(2)}, u32[]{:S(2)}) collective-permute-start(bf16[32,2176]{1,0:T(8,128)(2,1)S(1)} %get-tuple-element.105.refs_5_.refs_2_.refs_0_), channel_id=1, source_target_pairs={{0,24},{8,16},{16,8},{24,0},{1,25},{9,17},{17,9},{25,1},{2,26},{10... | collective-permute-start | bytes 417800 | tf_op jit(solution)/shard_map/ppermute | solution.py:39
  93.4 12.3 %collective-permute-start.13 = (bf16[32,2176]{1,0:T(8,128)(2,1)S(1)}, bf16[32,2176]{1,0:T(8,128)(2,1)S(1)}, u32[]{:S(2)}, u32[]{:S(2)}) collective-permute-start(bf16[32,2176]{1,0:T(8,128)(2,1)S(1)} %get-tuple-element.105.refs_5_.refs_2_.refs_0_), channel_id=1, source_target_pairs={{0,16},{8,24},{16,0},{24,8},{1,17},{9,25},{17,1},{25,9},{2,18},{10... | collective-permute-start | bytes 417800 | tf_op jit(solution)/shard_map/ppermute | solution.py:39
  95.3 10.4 %collective-permute-start.14 = (bf16[32,2176]{1,0:T(8,128)(2,1)S(1)}, bf16[32,2176]{1,0:T(8,128)(2,1)S(1)}, u32[]{:S(2)}, u32[]{:S(2)}) collective-permute-start(bf16[32,2176]{1,0:T(8,128)(2,1)S(1)} %get-tuple-element.105.refs_5_.refs_2_.refs_0_), channel_id=1, source_target_pairs={{0,8},{8,0},{16,24},{24,16},{1,9},{9,1},{17,25},{25,17},{2,10},{10... | collective-permute-start | bytes 417800 | tf_op jit(solution)/shard_map/ppermute | solution.py:39
  110.7 14.1 %all-to-all-start.3 = ((bf16[8,128,128]{2,1,0:T(8,128)(2,1)}), bf16[8,128,128]{2,1,0:T(8,128)(2,1)S(1)}, u32[]{:S(2)}, u32[]{:S(2)}) async-start(bf16[8,128,128]{2,1,0:T(8,128)(2,1)} %get-tuple-element.112.refs_2_.refs_6_.refs_5_), calls=%async_computation.3 | async-start | bytes 524288 | tf_op jit(solution)/shard_map/all_to_all | solution.py:1127
  114.1 58.6 %all-gather.11.cloned.1.call-start = ((), (), s32[]{:S(2)}) async-start(), calls=%async_computation.8 | async-start | bytes 4718592 | tf_op jit(solution)/shard_map/all_gather | solution.py:1254
  118.0 14.7 %collective-permute-start.16 = (bf16[32,2048]{1,0:T(8,128)(2,1)S(1)}, bf16[32,2048]{1,0:T(8,128)(2,1)S(1)}, u32[]{:S(2)}, u32[]{:S(2)}) collective-permute-start(bf16[32,2048]{1,0:T(8,128)(2,1)S(1)} %shard_map.226.refs_8_), channel_id=1, source_target_pairs={{0,16},{8,24},{16,0},{24,8},{1,17},{9,25},{17,1},{25,9},{2,18},{10... | collective-permute-start | bytes 393224 | tf_op jit(solution)/shard_map/ppermute | solution.py:39
  128.5 12.5 %all-to-all-start.4 = ((bf16[8,192,128]{2,1,0:T(8,128)(2,1)}), bf16[8,192,128]{2,1,0:T(8,128)(2,1)S(1)}, u32[]{:S(2)}, u32[]{:S(2)}) async-start(bf16[8,192,128]{2,1,0:T(8,128)(2,1)} %get-tuple-element.122.refs_4_.refs_1_), calls=%async_computation.4 | async-start | bytes 786432 | tf_op jit(solution)/shard_map/all_to_all | solution.py:1127
  138.2 15.2 %collective-permute-start.17 = (bf16[32,2048]{1,0:T(8,128)(2,1)S(1)}, bf16[32,2048]{1,0:T(8,128)(2,1)S(1)}, u32[]{:S(2)}, u32[]{:S(2)}) collective-permute-start(bf16[32,2048]{1,0:T(8,128)(2,1)S(1)} %shard_map.230.refs_0_.refs_3_), channel_id=1, source_target_pairs={{0,16},{8,24},{16,0},{24,8},{1,17},{9,25},{17,1},{25,9},{2,18},{10... | collective-permute-start | bytes 393224 | tf_op jit(solution)/shard_map/ppermute | solution.py:39
  141.0 18.5 %all-to-all-start.5 = ((bf16[8,192,256]{2,1,0:T(8,128)(2,1)}), bf16[8,192,256]{2,1,0:T(8,128)(2,1)S(1)}, u32[]{:S(2)}, u32[]{:S(2)}) async-start(bf16[8,192,256]{2,1,0:T(8,128)(2,1)} %shard_map.233), calls=%async_computation.5 | async-start | bytes 1572864 | tf_op jit(solution)/shard_map/all_to_all | solution.py:1127
  148.9 13.7 %collective-permute-start.19 = (bf16[32,2048]{1,0:T(8,128)(2,1)S(1)}, bf16[32,2048]{1,0:T(8,128)(2,1)S(1)}, u32[]{:S(2)}, u32[]{:S(2)}) collective-permute-start(bf16[32,2048]{1,0:T(8,128)(2,1)S(1)} %get-tuple-element.124), channel_id=1, source_target_pairs={{0,24},{8,16},{16,8},{24,0},{1,25},{9,17},{17,9},{25,1},{2,26},{10... | collective-permute-start | bytes 393224 | tf_op jit(solution)/shard_map/ppermute | solution.py:39
  152.0 12.3 %collective-permute-start.20 = (bf16[32,2048]{1,0:T(8,128)(2,1)S(1)}, bf16[32,2048]{1,0:T(8,128)(2,1)S(1)}, u32[]{:S(2)}, u32[]{:S(2)}) collective-permute-start(bf16[32,2048]{1,0:T(8,128)(2,1)S(1)} %get-tuple-element.125), channel_id=1, source_target_pairs={{0,16},{8,24},{16,0},{24,8},{1,17},{9,25},{17,1},{25,9},{2,18},{10... | collective-permute-start | bytes 393224 | tf_op jit(solution)/shard_map/ppermute | solution.py:39
  152.0 12.3 %collective-permute-start.21 = (bf16[32,2048]{1,0:T(8,128)(2,1)S(1)}, bf16[32,2048]{1,0:T(8,128)(2,1)S(1)}, u32[]{:S(2)}, u32[]{:S(2)}) collective-permute-start(bf16[32,2048]{1,0:T(8,128)(2,1)S(1)} %get-tuple-element.126), channel_id=1, source_target_pairs={{0,8},{8,0},{16,24},{24,16},{1,9},{9,1},{17,25},{25,17},{2,10},{10... | collective-permute-start | bytes 393224 | tf_op jit(solution)/shard_map/ppermute | solution.py:39
  153.4 24.1 %collective-permute-start.18 = (bf16[64,2048]{1,0:T(8,128)(2,1)S(1)}, bf16[64,2048]{1,0:T(8,128)(2,1)S(1)}, u32[]{:S(2)}, u32[]{:S(2)}) collective-permute-start(bf16[64,2048]{1,0:T(8,128)(2,1)S(1)} %shard_map.232.refs_1_), channel_id=1, source_target_pairs={{0,8},{8,0},{16,24},{24,16},{1,9},{9,1},{17,25},{25,17},{2,10},{10... | collective-permute-start | bytes 786440 | tf_op jit(solution)/shard_map/ppermute | solution.py:39
  164.6 14.3 %collective-permute-start.22 = (bf16[32,2176]{1,0:T(8,128)(2,1)S(1)}, bf16[32,2176]{1,0:T(8,128)(2,1)S(1)}, u32[]{:S(2)}, u32[]{:S(2)}) collective-permute-start(bf16[32,2176]{1,0:T(8,128)(2,1)S(1)} %shard_map.236.refs_3_.refs_5_.refs_1_), channel_id=1, source_target_pairs={{0,24},{8,16},{16,8},{24,0},{1,25},{9,17},{17,9},{25,1},{2,26},{10... | collective-permute-start | bytes 417800 | tf_op jit(solution)/shard_map/ppermute | solution.py:39
  166.4 12.6 %collective-permute-start.23 = (bf16[32,2176]{1,0:T(8,128)(2,1)S(1)}, bf16[32,2176]{1,0:T(8,128)(2,1)S(1)}, u32[]{:S(2)}, u32[]{:S(2)}) collective-permute-start(bf16[32,2176]{1,0:T(8,128)(2,1)S(1)} %shard_map.236.refs_3_.refs_5_.refs_1_), channel_id=1, source_target_pairs={{0,16},{8,24},{16,0},{24,8},{1,17},{9,25},{17,1},{25,9},{2,18},{10... | collective-permute-start | bytes 417800 | tf_op jit(solution)/shard_map/ppermute | solution.py:39
  166.4 12.6 %collective-permute-start.24 = (bf16[32,2176]{1,0:T(8,128)(2,1)S(1)}, bf16[32,2176]{1,0:T(8,128)(2,1)S(1)}, u32[]{:S(2)}, u32[]{:S(2)}) collective-permute-start(bf16[32,2176]{1,0:T(8,128)(2,1)S(1)} %shard_map.236.refs_3_.refs_5_.refs_1_), channel_id=1, source_target_pairs={{0,8},{8,0},{16,24},{24,16},{1,9},{9,1},{17,25},{25,17},{2,10},{10... | collective-permute-start | bytes 417800 | tf_op jit(solution)/shard_map/ppermute | solution.py:39
  (15 other events, 144.3 us)
Sparse Core Ops, SparseCore 0:
  30.2 53.7 all-gather.6
  86.5 43.4 all-gather.8
  132.4 40.2 all-gather.10

commit v7 on v6

--- a/solution.py
+++ b/solution.py
@@ -492,6 +492,16 @@
         [scalars()] + [pl.BlockSpec(memory_space=pl.ANY)] * len(items),
         scratch=[pltpu.SemaphoreType.DMA] * len(items), after=after, carry=carry, mb=2, cost=cost,
     )
+
+
+def in_hbm():
+    return pl.BlockSpec(memory_space=pl.ANY)
+
+
+def started(source, to, sem):
+    copy = pltpu.make_async_copy(source, to, sem)
+    copy.start()
+    return copy
 
 
 def fixed(dims):
@@ -606,10 +616,9 @@
     return same & earlier
 
 
-def attend_kernel(parts, ids, got, out, mixed, lse, kept, keys, ids_col):
+def attend_kernel(parts, ids, got, out, mixed, lse, kept, keys, ids_col, kept_sem):
     me = ids[0]
-    kept[...] = got[...]
-    kept.send()
+    keep = started(got, kept, kept_sem)
     blocks, _, rows = got.shape
     part = rows // parts
     gather_heads(got, keys, ids_col)
@@ -633,6 +642,7 @@
         for n, j in enumerate(mine):
             out[j] = result[:, n * rows : (n + 1) * rows].astype(bf16)
     out.send()
+    keep.wait()
 
 
 def out_kernel(parts, att, gain, weight, own, *refs):
@@ -753,9 +763,9 @@
 def hidden_back_kernel(parts, full, step, own, *refs):
     got, refs = refs[: parts - 1][::-1], refs[parts - 1 :]
     act, slope, grad, gain, weight, u, gh, both, norms, own_out = refs[:10]
-    pieces = refs[10:]
-    first_wide = u.shape[2]
-    both[:, :, :first_wide] = u[...]
+    pieces, (low_all, u_sem, low_sem) = refs[10 : 9 + parts], refs[9 + parts :]
+    first_wide, wide = u.shape[2], low_all.shape[2]
+    copies = [started(u, both.at[:, :, pl.ds(0, first_wide)], u_sem)]
     rows = act.shape[0]
     part = rows // parts
     total = own[...]
@@ -774,16 +784,15 @@
         table = jnp.where(row == i, value, table)
     cols = table.T
     mean, scaling, first, cross = (cols[:, i : i + 1] for i in range(4))
-    wide = both.shape[2] - first_wide
     for i in range(0, act.shape[1], step):
         here = slice(i, i + step)
         normed = (act[:, here] - mean) * scaling
         low = (normed * gain[:, here]).astype(bf16)
         for j in range(0, step, wide):
-            both[(i + j) // wide, :, first_wide:] = low[:, j : j + wide]
+            low_all[(i + j) // wide] = low[:, j : j + wide]
         value = scaling * (grad[:, here] * gain[:, here] - first - normed * cross) * slope[:, here]
         gh[:, here] = value.astype(bf16)
-    both.send()
+    copies.append(started(low_all, both.at[:, :, pl.ds(first_wide, wide)], low_sem))
     gh.send()
     width = weight.shape[1]
     for i in range(0, width, step):
@@ -792,6 +801,8 @@
         own_out[:, here] = result[:part]
         for k, piece in enumerate(pieces, 1):
             piece[:, here] = result[k * part : (k + 1) * part].astype(bf16)
+    for copy in copies:
+        copy.wait()
 
 
 def down_kernel(z2, *refs):
@@ -872,11 +883,9 @@
     return (grad * cosine + swap_pairs(grad, 0) * sine) * factor
 
 
-def attend_back_kernel(parts, ids, got, grads, mixed, lse, inner, base, out, z, keys, values, ids_col, gk, gv):
+def attend_back_kernel(parts, ids, got, grads, mixed, lse, inner, base, out, z, keys, values, ids_col, gk, gv, z_sem):
     me = ids[0]
-    for j in range(grads.shape[0]):
-        z[j] = grads[j, HD:, :]
-    z.send()
+    send_z = started(grads.at[:, pl.ds(HD, HD), :], z, z_sem)
     blocks, _, rows = got.shape
     part = rows // parts
     gather_heads(got, keys, ids_col, values)
@@ -914,6 +923,7 @@
         span = slice(j * rows, (j + 1) * rows)
         out[j, HD : 2 * HD, :] = turn_back(gk[:, span], table, base, j, True).astype(bf16)
         out[j, 2 * HD :, :] = gv[:, span].astype(bf16)
+    send_z.wait()
 
 
 def input_back_kernel(parts, got, *refs):
@@ -1054,23 +1064,30 @@
 
 
 def outputs_kernel(parts, ids, *refs):
-    blocks, (out, first, second) = refs[:parts], refs[parts:]
+    blocks, (out, first, second, sems) = refs[:parts], refs[parts:]
     part, width = blocks[0].shape[0], out.shape[1]
-    for k in range(parts):
-        out[block_at(ids[0], k, part), :] = blocks[-k % parts][:, :width]
-    out.send()
+    copies = [
+        started(blocks[-k % parts].at[:, pl.ds(0, width)], out.at[block_at(ids[0], k, part), :], sems.at[k])
+        for k in range(parts)
+    ]
     count = first.shape[1] // 128
     total = sum(b[:, width:].astype(f32) for b in blocks)
     total = total[: 2 * count] + total[2 * count : 4 * count]
     for i in range(count):
         first[:, i * 128 : (i + 1) * 128] = total[i : i + 1]
         second[:, i * 128 : (i + 1) * 128] = total[count + i : count + i + 1]
-
-
-def layer_output_kernel(ids, even, odd, out):
+    for copy in copies:
+        copy.wait()
+
+
+def layer_output_kernel(ids, even, odd, out, sems):
     part = even.shape[0] // 2
+    copies = []
     for k in range(4):
-        out[block_at(ids[0], k, part), :] = (odd if k % 2 else even)[k // 2 * part : (k // 2 + 1) * part, :]
+        source = (odd if k % 2 else even).at[pl.ds(k // 2 * part, part), :]
+        copies.append(started(source, out.at[block_at(ids[0], k, part), :], sems.at[k]))
+    for copy in copies:
+        copy.wait()
 
 
 def body(
@@ -1156,9 +1173,9 @@
     back, mixed, lse, far_got, pair = call(
         functools.partial(attend_kernel, T),
         [Far(shape((C, HD, rows), bf16)), Far(shape((HD, tokens), f32)), Far(shape((1, tokens), f32)),
-         Far(shape((C, 3 * HD + 16, rows), bf16))],
-        [ids, got], [scalars(), whole()],
-        scratch=[pltpu.VMEM((tokens, HD), bf16), pltpu.VMEM((tokens, 16), f32)],
+         Pin(shape((C, 3 * HD + 16, rows), bf16))],
+        [ids, got], [scalars(), whole()], [whole()] * 3 + [in_hbm()],
+        scratch=[pltpu.VMEM((tokens, HD), bf16), pltpu.VMEM((tokens, 16), f32), pltpu.SemaphoreType.DMA],
         mb=10, after=[near_heads], carry=[pair],
     )
     att = to_cp(back)
@@ -1198,8 +1215,10 @@
     )
     gh, both, norms, own, *pieces = call(
         functools.partial(hidden_back_kernel, T, FF, step),
-        [Far(shape((rows, hidden), bf16)), Far(shape((C, rows, wide + high), bf16)), Near(shape((8, rows), f32))] + piece_shapes(width),
+        [Far(shape((rows, hidden), bf16)), Pin(shape((C, rows, wide + high), bf16)), Near(shape((8, rows), f32))] + piece_shapes(width),
         [stats, *spread(stats), act, slope, grad_hid, near_hid, near_flip, u_cols], mb=10,
+        out_specs=[whole(), in_hbm()] + [whole()] * (T + 1),
+        scratch=[pltpu.VMEM((C, rows, high), bf16), pltpu.SemaphoreType.DMA, pltpu.SemaphoreType.DMA],
     )
     gu_got = exchange(pieces)
     both_got = to_cp(both)
@@ -1261,10 +1280,11 @@
     y_last = swap_tp(y_half, 2)
     gq_sent, z = call(
         functools.partial(attend_back_kernel, T),
-        [Far(shape((C, 3 * HD, rows), bf16)), Far(shape((C, HD, rows), bf16))],
+        [Far(shape((C, 3 * HD, rows), bf16)), Pin(shape((C, HD, rows), bf16))],
         [ids, near_got, grads, near_mixed, near_lse, near_inner, near_base], [scalars()] + [whole()] * 6,
+        [whole(), in_hbm()],
         scratch=[pltpu.VMEM((tokens, HD), bf16), pltpu.VMEM((tokens, HD), bf16), pltpu.VMEM((tokens, 16), f32),
-                 pltpu.VMEM((HD, tokens), f32), pltpu.VMEM((HD, tokens), f32)],
+                 pltpu.VMEM((HD, tokens), f32), pltpu.VMEM((HD, tokens), f32), pltpu.SemaphoreType.DMA],
         mb=12, cost=8, after=[Pin(grad_down), y_half],
     )
     gq = to_cp(gq_sent)
@@ -1296,13 +1316,15 @@
     final_blocks = [final] + spread(final)
     grad_out, heads_gain_grad = product(z, gb_all, False, None, 0, HD, [final], out_weight, gain_heads)
     (layer_output,) = call(
-        layer_output_kernel, [Far(shape((rows, width), bf16))], [ids, y_even, y_odd], [scalars(), whole(), whole()],
+        layer_output_kernel, [Pin(shape((rows, width), bf16))], [ids, y_even, y_odd], [scalars(), whole(), whole()],
+        [in_hbm()], scratch=[pltpu.SemaphoreType.DMA((T,))],
         after=[final],
     )
     grad_input, input_gain_grad, middle_gain_grad = call(
         functools.partial(outputs_kernel, T),
-        [Far(shape((rows, width), bf16)), shape((1, wide), f32), shape((1, wide), f32)],
-        [ids, *final_blocks], [scalars()] + [whole()] * T, after=[Pin(grad_out), Pin(layer_output)],
+        [Pin(shape((rows, width), bf16)), shape((1, wide), f32), shape((1, wide), f32)],
+        [ids, *final_blocks], [scalars()] + [whole()] * T, [in_hbm(), whole(), whole()],
+        scratch=[pltpu.SemaphoreType.DMA((T,))], after=[Pin(grad_out), Pin(layer_output)],
     )
     return (
         layer_output.reshape(layer_input.shape),

time: 188 us -> 188 us (level)
  transfers between devices with their start and end apart: 33 -> 33, of which waited for: 13 -> 13; matrix products, arithmetic and copies ran while one was open for 0% -> 0% of each run, Pallas kernels for 35% -> 34%
where the time goes in v7:
time: 188 us; the launch traced here: 187 us
  Pallas kernels  75.4 us (40%)
  starting transfers between devices  55.7 us (30%)
  waiting for transfers between devices  33.1 us (18%)
  between operations  14.1 us (8%)
  blocking collectives  8.82 us (5%)
    pallas_call x27, Pallas kernels, call(): pl.pallas_call(run, out_shape=tuple((result(t) for t in outs)) + tuple((r...  75.4 us
    ppermute x25, starting transfers between devices, swap_tp(): return lax.ppermute(value, 'tp', pairs(lax.axis_size('tp'), k))  34.8 us
    all_to_all x5, starting transfers between devices, to_cp(): return lax.all_to_all(value, 'cp', 0, 0, tiled=True)  20.5 us
    ppermute x25, waiting for transfers between devices, swap_tp(): return lax.ppermute(value, 'tp', pairs(lax.axis_size('tp'), k))  18.6 us
    all_to_all x5, waiting for transfers between devices, to_cp(): return lax.all_to_all(value, 'cp', 0, 0, tiled=True)  10.4 us
    all_to_all x1, blocking collectives, to_cp(): return lax.all_to_all(value, 'cp', 0, 0, tiled=True)  8.82 us
  transfers between devices with their start and end apart: 33, of which 13 were waited for; matrix products, arithmetic and copies ran while one was open for 0% of the time, Pallas kernels for 34%

profile of v7, /device:TPU:0, one launch (start us, length us, event | category | flops | bytes accessed | tf_op | source)
XLA Modules:
  0.0 187.3 jit_solution(4960482034853229784)
XLA Ops:
  7.3 5.7 %shard_map.213 = (bf16[2,128,2048]{2,1,0:T(8,128)(2,1)}, bf16[8,208,128]{2,1,0:T(8,128)(2,1)}) custom-call(s32[2]{0:T(128)S(1)} %pad_add_fusion.refs_0_, bf16[128,2048]{1,0:T(8,128)(2,1)} %bitcast.39, f32[1,2048]{1,0:T(1,128)} %bitcast.20, bf16[128,2048]{1,0:T(8,128)(2,1)} %bitcast.41, f32[4,128,128]{2,1,0:T(8,128)} %constant.14.clone.refs_4_, ...), custom_call_target="tpu_custom_call" | custom-call | flops 300000000 | tf_op jit(solution)/shard_map/pallas_call | solution.py:466
  13.0 5.2 %all-to-all-start = ((bf16[8,208,128]{2,1,0:T(8,128)(2,1)}), bf16[8,208,128]{2,1,0:T(8,128)(2,1)S(1)}, u32[]{:S(2)}, u32[]{:S(2)}) async-start(bf16[8,208,128]{2,1,0:T(8,128)(2,1)} %get-tuple-element.76.refs_8_), calls=%async_computation | async-start | bytes 851968 | tf_op jit(solution)/shard_map/all_to_all | solution.py:1144
  20.4 6.4 %all-to-all-done.refs_1_ = bf16[8,208,128]{2,1,0:T(8,128)(2,1)S(1)} async-done(((bf16[8,208,128]{2,1,0:T(8,128)(2,1)}), bf16[8,208,128]{2,1,0:T(8,128)(2,1)S(1)}, u32[]{:S(2)}, u32[]{:S(2)}) %all-to-all-start) | async-done | bytes 426016 | tf_op jit(solution)/shard_map/all_to_all | solution.py:1144
  26.8 3.2 %shard_map.215 = (bf16[8,64,128]{2,1,0:T(8,128)(2,1)}, f32[64,1024]{1,0:T(8,128)}, f32[1,1024]{1,0:T(1,128)}, bf16[8,208,128]{2,1,0:T(8,128)(2,1)}, bf16[2,128,2048]{2,1,0:T(8,128)(2,1)}) custom-call(s32[2]{0:T(128)S(1)} %pad_add_fusion.refs_0_, bf16[8,208,128]{2,1,0:T(8,128)(2,1)S(1)} %all-to-all-done.refs_1_, ...), custom_call_target="tpu_custom_call", output_to_operand_aliasing={{4}: (3, {})} | custom-call | flops 300000000 | tf_op jit(solution)/shard_map/pallas_call | solution.py:466
  30.1 8.8 %all_to_all.30.refs_0_ = bf16[8,64,128]{2,1,0:T(8,128)(2,1)S(1)} all-to-all(bf16[8,64,128]{2,1,0:T(8,128)(2,1)} %get-tuple-element.79), channel_id=1, replica_groups=mesh['tp'=4,'cp'=8] {'cp'}, dimensions={0} | all-to-all | bytes 262144 | tf_op jit(solution)/shard_map/all_to_all | solution.py:1144
  39.6 3.7 %collective-permute-start = (bf16[32,2176]{1,0:T(8,128)(2,1)S(1)}, bf16[32,2176]{1,0:T(8,128)(2,1)S(1)}, u32[]{:S(2)}, u32[]{:S(2)}) collective-permute-start(bf16[32,2176]{1,0:T(8,128)(2,1)S(1)} %get-tuple-element.82), channel_id=1, source_target_pairs={{0,24},{8,16},{16,8},{24,0},{1,25},{9,17},{17,9},{25,1},{2,26},{10... | collective-permute-start | bytes 417800 | tf_op jit(solution)/shard_map/ppermute | solution.py:39
  44.0 6.0 %shard_map.217.refs_6_.refs_5_ = f32[128,2048]{1,0:T(8,128)S(1)} custom-call(bf16[2,128,2048]{2,1,0:T(8,128)(2,1)} %get-tuple-element.87.refs_0_, bf16[2048,2048]{1,0:T(8,128)(2,1)} %refs_3_.5, f32[32,2176]{1,0:T(8,128)S(1)} %get-tuple-element.81.refs_2_.refs_0_), custom_call_target="tpu_custom_call" | custom-call | flops 3000000000 | tf_op jit(solution)/shard_map/pallas_call | solution.py:466
  50.0 4.8 %collective-permute-done.1.refs_2_ = bf16[32,2176]{1,0:T(8,128)(2,1)S(1)} collective-permute-done((bf16[32,2176]{1,0:T(8,128)(2,1)S(1)}, bf16[32,2176]{1,0:T(8,128)(2,1)S(1)}, u32[]{:S(2)}, u32[]{:S(2)}) %collective-permute-start.1) | collective-permute-done | bytes 139296 | tf_op jit(solution)/shard_map/ppermute | solution.py:39
  59.8 4.1 %shard_map.219 = (bf16[2048,2048]{1,0:T(8,128)(2,1)S(1)}, bf16[2048,2048]{1,0:T(8,128)(2,1)S(1)}) custom-call(bf16[2048,2048]{1,0:T(8,128)(2,1)} %refs_3_.6, bf16[32,2048]{1,0:T(8,128)(2,1)S(1)} %get-tuple-element.88.refs_1_.refs_0_), custom_call_target="tpu_custom_call" | custom-call | flops 300000000 | tf_op jit(solution)/shard_map/pallas_call | solution.py:466
  63.9 4.0 %collective-permute-done.4.refs_2_ = bf16[32,2048]{1,0:T(8,128)(2,1)S(1)} collective-permute-done((bf16[32,2048]{1,0:T(8,128)(2,1)S(1)}, bf16[32,2048]{1,0:T(8,128)(2,1)S(1)}, u32[]{:S(2)}, u32[]{:S(2)}) %collective-permute-start.4) | collective-permute-done | bytes 131104 | tf_op jit(solution)/shard_map/ppermute | solution.py:39
  83.3 4.2 %all-to-all-start.2 = ((bf16[8,128,512]{2,1,0:T(8,128)(2,1)}), bf16[8,128,512]{2,1,0:T(8,128)(2,1)}, u32[]{:S(2)}, u32[]{:S(2)}) async-start(bf16[8,128,512]{2,1,0:T(8,128)(2,1)} %get-tuple-element.97.refs_0_), calls=%async_computation.2 | async-start | bytes 2097152 | tf_op jit(solution)/shard_map/all_to_all | solution.py:1144
  95.6 5.0 %shard_map.223 = (f32[32,2048]{1,0:T(8,128)}, f32[32,2048]{1,0:T(8,128)}, bf16[64,2048]{1,0:T(8,128)(2,1)}) custom-call(bf16[8,128,512]{2,1,0:T(8,128)(2,1)} %get-tuple-element.97.refs_0_, bf16[2048,2048]{1,0:T(8,128)(2,1)} %refs_3_.5, bf16[2048,2048]{1,0:T(8,128)(2,1)} %refs_3_.5, bf16[2048,2048]{1,0:T(8,128)(2,1)} %refs_3_.5, bf16[2048,2048]{1,0:T(8,128)(2,1)} %refs_3_.5, ...), custom_call_target="tpu_custom_call" | custom-call | flops 20000000000 | tf_op jit(solution)/shard_map/pallas_call | solution.py:466
  110.5 3.4 %all-to-all-start.3 = ((bf16[8,128,128]{2,1,0:T(8,128)(2,1)}), bf16[8,128,128]{2,1,0:T(8,128)(2,1)S(1)}, u32[]{:S(2)}, u32[]{:S(2)}) async-start(bf16[8,128,128]{2,1,0:T(8,128)(2,1)} %get-tuple-element.112.refs_2_.refs_6_.refs_5_), calls=%async_computation.3 | async-start | bytes 524288 | tf_op jit(solution)/shard_map/all_to_all | solution.py:1144
  118.7 5.9 %shard_map.228 = (f32[256,2048]{1,0:T(8,128)}, f32[1,256]{1,0:T(1,128)}) custom-call(s32[2]{0:T(128)S(1)} %pad_add_fusion.refs_0_, bf16[8,128,512]{2,1,0:T(8,128)(2,1)} %all-to-all-done.2.refs_8_.refs_1_, bf16[8,2,128,2048]{3,2,1,0:T(8,128)(2,1)} %bitcast.45, bf16[2048,2048]{1,0:T(8,128)(2,1)} %refs_3_.5, f32[1,2048]{1,0:T(1,128)S(1)} %bitcast.24, ...), custom_call_target="tpu_custom_call" | custom-call | flops 20000000000 | tf_op jit(solution)/shard_map/pallas_call | solution.py:466
  124.6 3.7 %shard_map.229 = (bf16[8,192,128]{2,1,0:T(8,128)(2,1)}, bf16[8,64,128]{2,1,0:T(8,128)(2,1)}) custom-call(s32[2]{0:T(128)S(1)} %pad_add_fusion.refs_0_, bf16[8,208,128]{2,1,0:T(8,128)(2,1)S(1)} %get-tuple-element.116.refs_1_, bf16[8,128,128]{2,1,0:T(8,128)(2,1)S(1)} %all-to-all-done.3.refs_2_, f32[64,1024]{1,0:T(8,128)S(1)} %get-tuple-element.117.refs_3_, ...), custom_call_target="tpu_custom_call" | custom-call | flops 8000000000 | tf_op jit(solution)/shard_map/pallas_call | solution.py:466
  128.3 4.1 %all-to-all-start.4 = ((bf16[8,192,128]{2,1,0:T(8,128)(2,1)}), bf16[8,192,128]{2,1,0:T(8,128)(2,1)S(1)}, u32[]{:S(2)}, u32[]{:S(2)}) async-start(bf16[8,192,128]{2,1,0:T(8,128)(2,1)} %get-tuple-element.122.refs_4_.refs_1_), calls=%async_computation.4 | async-start | bytes 786432 | tf_op jit(solution)/shard_map/all_to_all | solution.py:1144
  133.5 4.5 %shard_map.233 = bf16[8,192,256]{2,1,0:T(8,128)(2,1)} custom-call(s32[2]{0:T(128)S(1)} %pad_add_fusion.refs_0_, bf16[8,192,128]{2,1,0:T(8,128)(2,1)} %get-tuple-element.122.refs_4_.refs_1_, bf16[8,2,128,2048]{3,2,1,0:T(8,128)(2,1)} %bitcast.46, bf16[32,2048]{1,0:T(8,128)(2,1)S(1)} %shard_map.230.refs_0_.refs_3_), custom_call_target="tpu_custom_call" | custom-call | flops 20000000000 | tf_op jit(solution)/shard_map/pallas_call | solution.py:466
  140.8 3.5 %all-to-all-start.5 = ((bf16[8,192,256]{2,1,0:T(8,128)(2,1)}), bf16[8,192,256]{2,1,0:T(8,128)(2,1)S(1)}, u32[]{:S(2)}, u32[]{:S(2)}) async-start(bf16[8,192,256]{2,1,0:T(8,128)(2,1)} %shard_map.233), calls=%async_computation.5 | async-start | bytes 1572864 | tf_op jit(solution)/shard_map/all_to_all | solution.py:1144
  144.4 4.4 %shard_map.231 = (f32[32,2048]{1,0:T(8,128)S(1)}, bf16[32,2048]{1,0:T(8,128)(2,1)S(1)}, bf16[32,2048]{1,0:T(8,128)(2,1)S(1)}, bf16[32,2048]{1,0:T(8,128)(2,1)S(1)}) custom-call(bf16[8,192,128]{2,1,0:T(8,128)(2,1)S(1)} %all-to-all-done.4.refs_0_, bf16[3,2048,512]{2,1,0:T(8,128)(2,1)} %bitcast.32, bf16[3,2048,512]{2,1,0:T(8,128)(2,1)} %bitcast.33, ...), custom_call_target="tpu_custom_call" | custom-call | flops 10000000000 | tf_op jit(solution)/shard_map/pallas_call | solution.py:466
  148.7 3.1 %collective-permute-start.19 = (bf16[32,2048]{1,0:T(8,128)(2,1)S(1)}, bf16[32,2048]{1,0:T(8,128)(2,1)S(1)}, u32[]{:S(2)}, u32[]{:S(2)}) collective-permute-start(bf16[32,2048]{1,0:T(8,128)(2,1)S(1)} %get-tuple-element.124), channel_id=1, source_target_pairs={{0,24},{8,16},{16,8},{24,0},{1,25},{9,17},{17,9},{25,1},{2,26},{10... | collective-permute-start | bytes 393224 | tf_op jit(solution)/shard_map/ppermute | solution.py:39
  154.0 5.4 %shard_map.234 = (f32[256,2048]{1,0:T(8,128)}, f32[1,256]{1,0:T(1,128)S(1)}) custom-call(s32[2]{0:T(128)S(1)} %pad_add_fusion.refs_0_, bf16[8,128,512]{2,1,0:T(8,128)(2,1)} %all-to-all-done.2.refs_8_.refs_1_, bf16[8,128,2048]{2,1,0:T(8,128)(2,1)} %bitcast.47, bf16[2048,2048]{1,0:T(8,128)(2,1)} %refs_3_.6, f32[1,2048]{1,0:T(1,128)S(1)} %bitcast.26, ...), custom_call_target="tpu_custom_call" | custom-call | flops 20000000000 | tf_op jit(solution)/shard_map/pallas_call | solution.py:466
  159.4 3.1 %shard_map.235 = (f32[3,256,512]{2,1,0:T(8,128)}, f32[8,256]{1,0:T(8,128)S(1)}) custom-call(s32[2]{0:T(128)S(1)} %pad_add_fusion.refs_0_, bf16[8,192,256]{2,1,0:T(8,128)(2,1)S(1)} %all-to-all-done.5.refs_1_, bf16[3,2048,512]{2,1,0:T(8,128)(2,1)} %bitcast.38, f32[1,2048]{1,0:T(1,128)S(1)} %bitcast.22, f32[1,256]{1,0:T(1,128)S(1)} %get-tuple-element.130.refs_4_, ...), custom_call_target="tpu_custom_call" | custom-call | flops 20000000000 | tf_op jit(solution)/shard_map/pallas_call | solution.py:466
  169.0 3.7 %all-gather.11.cloned.1.call-done = bf16[1024,2048]{1,0:T(8,128)(2,1)} async-done(((bf16[128,2048]{1,0:T(8,128)(2,1)}), bf16[1024,2048]{1,0:T(8,128)(2,1)}) %all-gather.11.cloned.1.call-update) | async-done | bytes 4194320 | tf_op jit(solution)/shard_map/all_gather | solution.py:1273
  172.6 4.8 %shard_map.238 = (f32[64,2048]{1,0:T(8,128)}, f32[1,64]{1,0:T(1,128)}) custom-call(s32[2]{0:T(128)S(1)} %pad_add_fusion.refs_0_, bf16[8,64,128]{2,1,0:T(8,128)(2,1)} %get-tuple-element.133.refs_1_, bf16[8,128,2048]{2,1,0:T(8,128)(2,1)} %bitcast.48, bf16[512,2048]{1,0:T(8,128)(2,1)} %refs_3_.7, f32[1,512]{1,0:T(1,128)S(1)} %bitcast.28, ...), custom_call_target="tpu_custom_call" | custom-call | flops 20000000000 | tf_op jit(solution)/shard_map/pallas_call | solution.py:466
  (86 shorter events, 62.4 us)
Async XLA Ops:
  13.0 13.9 %all-to-all-start = ((bf16[8,208,128]{2,1,0:T(8,128)(2,1)}), bf16[8,208,128]{2,1,0:T(8,128)(2,1)S(1)}, u32[]{:S(2)}, u32[]{:S(2)}) async-start(bf16[8,208,128]{2,1,0:T(8,128)(2,1)} %get-tuple-element.76.refs_8_), calls=%async_computation | async-start | bytes 851968 | tf_op jit(solution)/shard_map/all_to_all | solution.py:1144
  18.1 100.5 %all-gather.7.cloned.1.call-start = ((), (), s32[]{:S(2)}) async-start(), calls=%async_computation.6 | async-start | bytes 9437184 | tf_op jit(solution)/shard_map/all_gather | solution.py:1182
  30.1 123.9 %all-gather.9.cloned.1.call-start = ((), (), s32[]{:S(2)}) async-start(), calls=%async_computation.7 | async-start | bytes 4718592 | tf_op jit(solution)/shard_map/all_gather | solution.py:1225
  39.6 10.4 %collective-permute-start = (bf16[32,2176]{1,0:T(8,128)(2,1)S(1)}, bf16[32,2176]{1,0:T(8,128)(2,1)S(1)}, u32[]{:S(2)}, u32[]{:S(2)}) collective-permute-start(bf16[32,2176]{1,0:T(8,128)(2,1)S(1)} %get-tuple-element.82), channel_id=1, source_target_pairs={{0,24},{8,16},{16,8},{24,0},{1,25},{9,17},{17,9},{25,1},{2,26},{10... | collective-permute-start | bytes 417800 | tf_op jit(solution)/shard_map/ppermute | solution.py:39
  43.2 11.6 %collective-permute-start.1 = (bf16[32,2176]{1,0:T(8,128)(2,1)S(1)}, bf16[32,2176]{1,0:T(8,128)(2,1)S(1)}, u32[]{:S(2)}, u32[]{:S(2)}) collective-permute-start(bf16[32,2176]{1,0:T(8,128)(2,1)S(1)} %get-tuple-element.83), channel_id=1, source_target_pairs={{0,16},{8,24},{16,0},{24,8},{1,17},{9,25},{17,1},{25,9},{2,18},{10... | collective-permute-start | bytes 417800 | tf_op jit(solution)/shard_map/ppermute | solution.py:39
  43.2 11.6 %collective-permute-start.2 = (bf16[32,2176]{1,0:T(8,128)(2,1)S(1)}, bf16[32,2176]{1,0:T(8,128)(2,1)S(1)}, u32[]{:S(2)}, u32[]{:S(2)}) collective-permute-start(bf16[32,2176]{1,0:T(8,128)(2,1)S(1)} %get-tuple-element.84), channel_id=1, source_target_pairs={{0,8},{8,0},{16,24},{24,16},{1,9},{9,1},{17,25},{25,17},{2,10},{10... | collective-permute-start | bytes 417800 | tf_op jit(solution)/shard_map/ppermute | solution.py:39
  78.9 10.3 %collective-permute-start.10 = (bf16[32,2048]{1,0:T(8,128)(2,1)S(1)}, bf16[32,2048]{1,0:T(8,128)(2,1)S(1)}, u32[]{:S(2)}, u32[]{:S(2)}) collective-permute-start(bf16[32,2048]{1,0:T(8,128)(2,1)S(1)} %get-tuple-element.100), channel_id=1, source_target_pairs={{0,16},{8,24},{16,0},{24,8},{1,17},{9,25},{17,1},{25,9},{2,18},{10... | collective-permute-start | bytes 393224 | tf_op jit(solution)/shard_map/ppermute | solution.py:39
  83.3 25.3 %all-to-all-start.2 = ((bf16[8,128,512]{2,1,0:T(8,128)(2,1)}), bf16[8,128,512]{2,1,0:T(8,128)(2,1)}, u32[]{:S(2)}, u32[]{:S(2)}) async-start(bf16[8,128,512]{2,1,0:T(8,128)(2,1)} %get-tuple-element.97.refs_0_), calls=%async_computation.2 | async-start | bytes 2097152 | tf_op jit(solution)/shard_map/all_to_all | solution.py:1144
  91.1 11.6 %collective-permute-start.12 = (bf16[32,2176]{1,0:T(8,128)(2,1)S(1)}, bf16[32,2176]{1,0:T(8,128)(2,1)S(1)}, u32[]{:S(2)}, u32[]{:S(2)}) collective-permute-start(bf16[32,2176]{1,0:T(8,128)(2,1)S(1)} %get-tuple-element.105.refs_5_.refs_2_.refs_0_), channel_id=1, source_target_pairs={{0,24},{8,16},{16,8},{24,0},{1,25},{9,17},{17,9},{25,1},{2,26},{10... | collective-permute-start | bytes 417800 | tf_op jit(solution)/shard_map/ppermute | solution.py:39
  93.3 12.3 %collective-permute-start.13 = (bf16[32,2176]{1,0:T(8,128)(2,1)S(1)}, bf16[32,2176]{1,0:T(8,128)(2,1)S(1)}, u32[]{:S(2)}, u32[]{:S(2)}) collective-permute-start(bf16[32,2176]{1,0:T(8,128)(2,1)S(1)} %get-tuple-element.105.refs_5_.refs_2_.refs_0_), channel_id=1, source_target_pairs={{0,16},{8,24},{16,0},{24,8},{1,17},{9,25},{17,1},{25,9},{2,18},{10... | collective-permute-start | bytes 417800 | tf_op jit(solution)/shard_map/ppermute | solution.py:39
  95.2 10.4 %collective-permute-start.14 = (bf16[32,2176]{1,0:T(8,128)(2,1)S(1)}, bf16[32,2176]{1,0:T(8,128)(2,1)S(1)}, u32[]{:S(2)}, u32[]{:S(2)}) collective-permute-start(bf16[32,2176]{1,0:T(8,128)(2,1)S(1)} %get-tuple-element.105.refs_5_.refs_2_.refs_0_), channel_id=1, source_target_pairs={{0,8},{8,0},{16,24},{24,16},{1,9},{9,1},{17,25},{25,17},{2,10},{10... | collective-permute-start | bytes 417800 | tf_op jit(solution)/shard_map/ppermute | solution.py:39
  110.5 14.1 %all-to-all-start.3 = ((bf16[8,128,128]{2,1,0:T(8,128)(2,1)}), bf16[8,128,128]{2,1,0:T(8,128)(2,1)S(1)}, u32[]{:S(2)}, u32[]{:S(2)}) async-start(bf16[8,128,128]{2,1,0:T(8,128)(2,1)} %get-tuple-element.112.refs_2_.refs_6_.refs_5_), calls=%async_computation.3 | async-start | bytes 524288 | tf_op jit(solution)/shard_map/all_to_all | solution.py:1144
  113.9 58.7 %all-gather.11.cloned.1.call-start = ((), (), s32[]{:S(2)}) async-start(), calls=%async_computation.8 | async-start | bytes 4718592 | tf_op jit(solution)/shard_map/all_gather | solution.py:1273
  117.9 14.6 %collective-permute-start.16 = (bf16[32,2048]{1,0:T(8,128)(2,1)S(1)}, bf16[32,2048]{1,0:T(8,128)(2,1)S(1)}, u32[]{:S(2)}, u32[]{:S(2)}) collective-permute-start(bf16[32,2048]{1,0:T(8,128)(2,1)S(1)} %shard_map.226.refs_8_), channel_id=1, source_target_pairs={{0,16},{8,24},{16,0},{24,8},{1,17},{9,25},{17,1},{25,9},{2,18},{10... | collective-permute-start | bytes 393224 | tf_op jit(solution)/shard_map/ppermute | solution.py:39
  128.3 12.5 %all-to-all-start.4 = ((bf16[8,192,128]{2,1,0:T(8,128)(2,1)}), bf16[8,192,128]{2,1,0:T(8,128)(2,1)S(1)}, u32[]{:S(2)}, u32[]{:S(2)}) async-start(bf16[8,192,128]{2,1,0:T(8,128)(2,1)} %get-tuple-element.122.refs_4_.refs_1_), calls=%async_computation.4 | async-start | bytes 786432 | tf_op jit(solution)/shard_map/all_to_all | solution.py:1144
  138.0 15.2 %collective-permute-start.17 = (bf16[32,2048]{1,0:T(8,128)(2,1)S(1)}, bf16[32,2048]{1,0:T(8,128)(2,1)S(1)}, u32[]{:S(2)}, u32[]{:S(2)}) collective-permute-start(bf16[32,2048]{1,0:T(8,128)(2,1)S(1)} %shard_map.230.refs_0_.refs_3_), channel_id=1, source_target_pairs={{0,16},{8,24},{16,0},{24,8},{1,17},{9,25},{17,1},{25,9},{2,18},{10... | collective-permute-start | bytes 393224 | tf_op jit(solution)/shard_map/ppermute | solution.py:39
  140.8 18.6 %all-to-all-start.5 = ((bf16[8,192,256]{2,1,0:T(8,128)(2,1)}), bf16[8,192,256]{2,1,0:T(8,128)(2,1)S(1)}, u32[]{:S(2)}, u32[]{:S(2)}) async-start(bf16[8,192,256]{2,1,0:T(8,128)(2,1)} %shard_map.233), calls=%async_computation.5 | async-start | bytes 1572864 | tf_op jit(solution)/shard_map/all_to_all | solution.py:1144
  148.7 13.8 %collective-permute-start.19 = (bf16[32,2048]{1,0:T(8,128)(2,1)S(1)}, bf16[32,2048]{1,0:T(8,128)(2,1)S(1)}, u32[]{:S(2)}, u32[]{:S(2)}) collective-permute-start(bf16[32,2048]{1,0:T(8,128)(2,1)S(1)} %get-tuple-element.124), channel_id=1, source_target_pairs={{0,24},{8,16},{16,8},{24,0},{1,25},{9,17},{17,9},{25,1},{2,26},{10... | collective-permute-start | bytes 393224 | tf_op jit(solution)/shard_map/ppermute | solution.py:39
  151.9 12.3 %collective-permute-start.20 = (bf16[32,2048]{1,0:T(8,128)(2,1)S(1)}, bf16[32,2048]{1,0:T(8,128)(2,1)S(1)}, u32[]{:S(2)}, u32[]{:S(2)}) collective-permute-start(bf16[32,2048]{1,0:T(8,128)(2,1)S(1)} %get-tuple-element.125), channel_id=1, source_target_pairs={{0,16},{8,24},{16,0},{24,8},{1,17},{9,25},{17,1},{25,9},{2,18},{10... | collective-permute-start | bytes 393224 | tf_op jit(solution)/shard_map/ppermute | solution.py:39
  151.9 12.3 %collective-permute-start.21 = (bf16[32,2048]{1,0:T(8,128)(2,1)S(1)}, bf16[32,2048]{1,0:T(8,128)(2,1)S(1)}, u32[]{:S(2)}, u32[]{:S(2)}) collective-permute-start(bf16[32,2048]{1,0:T(8,128)(2,1)S(1)} %get-tuple-element.126), channel_id=1, source_target_pairs={{0,8},{8,0},{16,24},{24,16},{1,9},{9,1},{17,25},{25,17},{2,10},{10... | collective-permute-start | bytes 393224 | tf_op jit(solution)/shard_map/ppermute | solution.py:39
  153.2 24.2 %collective-permute-start.18 = (bf16[64,2048]{1,0:T(8,128)(2,1)S(1)}, bf16[64,2048]{1,0:T(8,128)(2,1)S(1)}, u32[]{:S(2)}, u32[]{:S(2)}) collective-permute-start(bf16[64,2048]{1,0:T(8,128)(2,1)S(1)} %shard_map.232.refs_1_), channel_id=1, source_target_pairs={{0,8},{8,0},{16,24},{24,16},{1,9},{9,1},{17,25},{25,17},{2,10},{10... | collective-permute-start | bytes 786440 | tf_op jit(solution)/shard_map/ppermute | solution.py:39
  164.5 14.3 %collective-permute-start.22 = (bf16[32,2176]{1,0:T(8,128)(2,1)S(1)}, bf16[32,2176]{1,0:T(8,128)(2,1)S(1)}, u32[]{:S(2)}, u32[]{:S(2)}) collective-permute-start(bf16[32,2176]{1,0:T(8,128)(2,1)S(1)} %shard_map.236.refs_3_.refs_5_.refs_1_), channel_id=1, source_target_pairs={{0,24},{8,16},{16,8},{24,0},{1,25},{9,17},{17,9},{25,1},{2,26},{10... | collective-permute-start | bytes 417800 | tf_op jit(solution)/shard_map/ppermute | solution.py:39
  166.3 12.5 %collective-permute-start.23 = (bf16[32,2176]{1,0:T(8,128)(2,1)S(1)}, bf16[32,2176]{1,0:T(8,128)(2,1)S(1)}, u32[]{:S(2)}, u32[]{:S(2)}) collective-permute-start(bf16[32,2176]{1,0:T(8,128)(2,1)S(1)} %shard_map.236.refs_3_.refs_5_.refs_1_), channel_id=1, source_target_pairs={{0,16},{8,24},{16,0},{24,8},{1,17},{9,25},{17,1},{25,9},{2,18},{10... | collective-permute-start | bytes 417800 | tf_op jit(solution)/shard_map/ppermute | solution.py:39
  166.3 12.5 %collective-permute-start.24 = (bf16[32,2176]{1,0:T(8,128)(2,1)S(1)}, bf16[32,2176]{1,0:T(8,128)(2,1)S(1)}, u32[]{:S(2)}, u32[]{:S(2)}) collective-permute-start(bf16[32,2176]{1,0:T(8,128)(2,1)S(1)} %shard_map.236.refs_3_.refs_5_.refs_1_), channel_id=1, source_target_pairs={{0,8},{8,0},{16,24},{24,16},{1,9},{9,1},{17,25},{25,17},{2,10},{10... | collective-permute-start | bytes 417800 | tf_op jit(solution)/shard_map/ppermute | solution.py:39
  (15 other events, 144.1 us)
Sparse Core Ops, SparseCore 0:
  30.2 53.7 all-gather.6
  86.4 43.3 all-gather.8
  132.3 40.2 all-gather.10
